TPU v7x, 32 devices: a whole 2x2x4 slice. The times are simulated.
32 devices in a mesh: dp: 2 (over y), ctx: 16 (over z, x, core).
Axes of the slice: x: 2, y: 2, z: 4, core: 2. Of those that a mesh axis runs over, the one named last changes fastest.
Arguments:
- embeds: bfloat16 [2, 65536, 128], P('dp', 'ctx'), may hold values from -6 to 6
- perturb: bfloat16 [2, 65536, 128], P('dp', 'ctx'), may hold values from -1.5 to 1.5
- cotangent: bfloat16 [2, 65536, 128], P('dp', 'ctx'), may hold values from -6 to 6
- filter_spectrum: float32 [2, 256, 256, 128], P(None, 'ctx'), may hold values from -4.2 to 4.2
- skip_gain: float32 [128], replicated, may hold values from 0.25 to 1.75
Outputs:
- clean_output: bfloat16 [2, 65536, 128], P('dp', 'ctx')
- filter_grad: float32 [2, 256, 256, 128], P(None, 'ctx', 'dp')
All inputs are finite; a program needn't handle non-finite values.
Results may differ from a plain program's by a relative error of at most 0.022.
Values may be sent and summed in bfloat16 or wider, within the bound.
No kernel may reach another device: no remote copies, remote signals or barrier semaphores. Data moves between devices by JAX's collectives and lax.ppermute only.
A program may use at most 128 MiB of HBM per device.

v0:
```python
import jax
import jax.numpy as jnp
from jax import lax
from jax.sharding import PartitionSpec as P

N1 = 256
N2 = 256


two_pi = 6.283185307179586
smart_weight = 2.0


def trig_table(period):
    row_ids = jnp.arange(period, dtype=jnp.int32)
    exponent = row_ids[:, None] * row_ids[None, :] % period
    phase_angle = exponent.astype(jnp.float32) * (two_pi / period)
    return (jnp.cos(phase_angle).astype(jnp.bfloat16), jnp.sin(phase_angle).astype(jnp.bfloat16))


def twiddle(row_first, row_count, col_first, col_count):
    row_ids = row_first + jnp.arange(row_count, dtype=jnp.int32)
    col_ids = col_first + jnp.arange(col_count, dtype=jnp.int32)
    exponent = row_ids[:, None] * col_ids[None, :] % (N1 * N2)
    phase_angle = exponent.astype(jnp.float32) * (two_pi / (N1 * N2))
    return (jnp.cos(phase_angle)[:, :, None], jnp.sin(phase_angle)[:, :, None])


def first_section(values, col_start):
    cos_table, sin_table = trig_table(N1)
    part_real = jnp.einsum("kn,snmc->skmc", cos_table, values, preferred_element_type=jnp.float32)
    part_imag = -jnp.einsum("kn,snmc->skmc", sin_table, values, preferred_element_type=jnp.float32)
    tw_cos, tw_sin = twiddle(0, N1, col_start, values.shape[2])
    out_real = part_real * tw_cos + part_imag * tw_sin
    out_imag = part_imag * tw_cos - part_real * tw_sin
    return jnp.stack([out_real, out_imag], 1).astype(jnp.bfloat16)


def second_section(section_rows):
    cos_table, sin_table = trig_table(N2)
    with_cos = jnp.einsum(
        "sprnc,kn->sprkc", section_rows, cos_table, preferred_element_type=jnp.float32
    )
    with_sin = jnp.einsum(
        "sprnc,kn->sprkc", section_rows, sin_table, preferred_element_type=jnp.float32
    )
    return jnp.stack([with_cos[:, 0] + with_sin[:, 1], with_cos[:, 1] - with_sin[:, 0]], 1)


def spectral_inverse(product, row_start):
    cos_table, sin_table = trig_table(N2)
    with_cos = jnp.einsum("sprkc,nk->sprnc", product, cos_table, preferred_element_type=jnp.float32)
    with_sin = jnp.einsum("sprkc,nk->sprnc", product, sin_table, preferred_element_type=jnp.float32)
    part_real = with_cos[:, 0] - with_sin[:, 1]
    part_imag = with_cos[:, 1] + with_sin[:, 0]
    tw_cos, tw_sin = twiddle(row_start, product.shape[2], 0, N2)
    out_real = part_real * tw_cos - part_imag * tw_sin
    out_imag = part_imag * tw_cos + part_real * tw_sin
    return jnp.stack([out_real, out_imag], 1).astype(jnp.bfloat16)


def column_inverse(mixed_cols):
    cos_table, sin_table = trig_table(N1)
    with_cos = jnp.einsum(
        "nk,skmc->snmc", cos_table, mixed_cols[:, 0], preferred_element_type=jnp.float32
    )
    with_sin = jnp.einsum(
        "nk,skmc->snmc", sin_table, mixed_cols[:, 1], preferred_element_type=jnp.float32
    )
    return ((with_cos - with_sin) * (1.0 / (N1 * N2))).astype(jnp.bfloat16)


def to_spectrum(section_cols):
    return second_section(
        lax.all_to_all(section_cols, "ctx", split_axis=2, concat_axis=3, tiled=True)
    )


def error_terms(signal, filtered, skip_gain, cotangent_view):
    signal_wide = signal.astype(jnp.float32)
    filtered_wide = lax.optimization_barrier(filtered).astype(jnp.float32)
    outputs = signal_wide * filtered_wide + skip_gain * signal_wide
    clean_y = outputs[0]
    smooth_gap = outputs[1] - clean_y
    err_clean = signal_wide[0] * (cotangent_view.astype(jnp.float32) - smart_weight * smooth_gap)
    err_shift = signal_wide[1] * (smart_weight * smooth_gap)
    return (clean_y, jnp.stack([err_clean, err_shift], 0).astype(jnp.bfloat16))


def body(embeds, perturb, cotangent, filter_spectrum, skip_gain):
    ctx_size = lax.axis_size("ctx")
    ctx_index = lax.axis_index("ctx")
    channels = embeds.shape[2]
    row_count = N1 // ctx_size
    col_count = N2 // ctx_size
    row_start = ctx_index * row_count
    col_start = ctx_index * col_count
    clean_rows = embeds[0].reshape(row_count, N2, channels)
    perturb_rows = perturb[0].reshape(row_count, N2, channels)
    shifted = (clean_rows.astype(jnp.float32) + perturb_rows.astype(jnp.float32)).astype(
        jnp.bfloat16
    )
    inputs = jnp.stack([clean_rows, shifted], 0)
    signal_cols = lax.all_to_all(inputs, "ctx", split_axis=2, concat_axis=1, tiled=True)
    section_cols, signal_cols = (first_section(signal_cols, col_start), signal_cols)
    spectra = to_spectrum(section_cols)
    filter_real = filter_spectrum[0]
    filter_imag = filter_spectrum[1]
    spectrum_real = spectra[:, 0]
    spectrum_imag = spectra[:, 1]
    product = jnp.stack(
        [
            filter_real * spectrum_real - filter_imag * spectrum_imag,
            filter_real * spectrum_imag + filter_imag * spectrum_real,
        ],
        1,
    ).astype(jnp.bfloat16)
    mixed_rows = spectral_inverse(product, row_start)
    filtered = column_inverse(
        lax.all_to_all(mixed_rows, "ctx", split_axis=3, concat_axis=2, tiled=True)
    )
    cotangent_rows = cotangent[0].reshape(row_count, N2, channels)
    filtered_rows = lax.all_to_all(filtered, "ctx", split_axis=1, concat_axis=2, tiled=True)
    clean_y, errors = error_terms(inputs, filtered_rows, skip_gain, cotangent_rows)
    clean_output = clean_y.astype(jnp.bfloat16)
    error_section = first_section(
        lax.all_to_all(errors, "ctx", split_axis=2, concat_axis=1, tiled=True), col_start
    )
    error_spec = to_spectrum(error_section)
    error_real = error_spec[:, 0]
    error_imag = error_spec[:, 1]
    term_real = error_real * spectrum_real + error_imag * spectrum_imag
    term_imag = error_imag * spectrum_real - error_real * spectrum_imag
    local_grad = jnp.stack([term_real[0] + term_real[1], term_imag[0] + term_imag[1]], 0) * (
        1.0 / (N1 * N2)
    )
    grad_shard = lax.psum_scatter(
        local_grad.astype(jnp.bfloat16), "dp", scatter_dimension=2, tiled=True
    ).astype(jnp.float32)
    return (clean_output.reshape(1, row_count * N2, channels), grad_shard)


def solution(mesh):
    return jax.shard_map(
        body,
        mesh=mesh,
        in_specs=(
            P("dp", "ctx", None),
            P("dp", "ctx", None),
            P("dp", "ctx", None),
            P(None, "ctx", None, None),
            P(),
        ),
        out_specs=(P("dp", "ctx", None), P(None, "ctx", "dp", None)),
        check_vma=False,
    )
```

profile of v0, /device:TPU:0, one launch (start us, length us, event | category | flops | bytes accessed | tf_op | source)
XLA Modules:
  0.0 628.3 jit_solution(12935674254373948272)
XLA Ops:
  9.0 3.6 fusion.113
  15.3 7.4 %all-to-all-start = ((bf16[2,16,256,128]{3,1,0,2:T(8,128)(2,1)}), bf16[2,16,256,128]{3,1,0,2:T(8,128)(2,1)S(1)}, u32[]{:S(2)}, u32[]{:S(2)}) async-start(bf16[2,16,256,128]{3,1,0,2:T(8,128)(2,1)} %copy.47), calls=%async_computation | async-start | bytes 4194304 | tf_op jit(solution)/shard_map/all_to_all | solution.py:104
  22.8 40.9 %all-to-all-done = bf16[2,16,256,128]{3,1,0,2:T(8,128)(2,1)S(1)} async-done(((bf16[2,16,256,128]{3,1,0,2:T(8,128)(2,1)}), bf16[2,16,256,128]{3,1,0,2:T(8,128)(2,1)S(1)}, u32[]{:S(2)}, u32[]{:S(2)}) %all-to-all-start) | async-done | bytes 2097184 | tf_op jit(solution)/shard_map/all_to_all | solution.py:104
  65.9 3.0 copy.50
  75.5 7.9 %copy.52 = bf16[2,2,256,16,128]{4,3,0,1,2:T(8,128)(2,1)} copy(bf16[2,2,256,16,128]{2,4,3,0,1:T(8,128)(2,1)} %pad_maximum_fusion) | data formatting | bytes 8388608 | tf_op jit(solution)/shard_map/stack | solution.py:36
  83.4 11.3 %all-to-all-start.1 = ((bf16[2,2,256,16,128]{4,3,0,1,2:T(8,128)(2,1)}), bf16[2,2,256,16,128]{4,3,0,1,2:T(8,128)(2,1)}, u32[]{:S(2)}, u32[]{:S(2)}) async-start(bf16[2,2,256,16,128]{4,3,0,1,2:T(8,128)(2,1)} %copy.52), calls=%async_computation.1 | async-start | bytes 8388608 | tf_op jit(solution)/shard_map/all_to_all | solution.py:75
  95.2 3.9 slice_bitcast_fusion.1
  99.1 73.3 %all-to-all-done.1 = bf16[2,2,256,16,128]{4,3,0,1,2:T(8,128)(2,1)} async-done(((bf16[2,2,256,16,128]{4,3,0,1,2:T(8,128)(2,1)}), bf16[2,2,256,16,128]{4,3,0,1,2:T(8,128)(2,1)}, u32[]{:S(2)}, u32[]{:S(2)}) %all-to-all-start.1) | async-done | bytes 4194336 | tf_op jit(solution)/shard_map/all_to_all | solution.py:75
  172.4 3.4 copy.54
  178.0 5.4 convolution_bitcast_fusion.5
  183.4 6.0 subtract_convert_fusion.1
  189.3 4.6 add_convert_fusion.1
  204.2 111.9 %all_to_all.108 = bf16[2,2,16,256,128]{4,2,1,0,3:T(8,128)(2,1)S(1)} all-to-all(bf16[2,2,16,256,128]{4,2,1,0,3:T(8,128)(2,1)S(1)} %copy.55), channel_id=1, replica_groups=mesh['dp'=2,'ctx'=16] {'ctx'}, dimensions={3} | all-to-all | bytes 8388608 | tf_op jit(solution)/shard_map/all_to_all | solution.py:120
  316.0 4.9 copy.57
  325.7 3.0 copy.81
  333.4 3.4 copy.60
  336.8 52.7 %all_to_all.109 = bf16[2,256,16,128]{3,2,0,1:T(8,128)(2,1)S(1)} all-to-all(bf16[2,256,16,128]{3,2,0,1:T(8,128)(2,1)S(1)} %copy.60), channel_id=1, replica_groups=mesh['dp'=2,'ctx'=16] {'ctx'}, dimensions={1} | all-to-all | bytes 4194304 | tf_op jit(solution)/shard_map/all_to_all | solution.py:123
  396.7 52.2 %all_to_all.110 = bf16[2,16,256,128]{3,1,0,2:T(8,128)(2,1)S(1)} all-to-all(bf16[2,16,256,128]{3,1,0,2:T(8,128)(2,1)S(1)} %copy.63), channel_id=1, replica_groups=mesh['dp'=2,'ctx'=16] {'ctx'}, dimensions={2} | all-to-all | bytes 4194304 | tf_op jit(solution)/shard_map/all_to_all | solution.py:127
  451.0 3.0 copy.66
  460.6 7.9 %copy.68 = bf16[2,2,256,16,128]{4,3,0,1,2:T(8,128)(2,1)} copy(bf16[2,2,256,16,128]{2,4,3,0,1:T(8,128)(2,1)} %pad_maximum_fusion.3) | data formatting | bytes 8388608 | tf_op jit(solution)/shard_map/stack | solution.py:36
  468.5 97.6 %all_to_all.111 = bf16[2,2,256,16,128]{4,3,0,1,2:T(8,128)(2,1)S(1)} all-to-all(bf16[2,2,256,16,128]{4,3,0,1,2:T(8,128)(2,1)} %copy.68), channel_id=1, replica_groups=mesh['dp'=2,'ctx'=16] {'ctx'}, dimensions={2} | all-to-all | bytes 8388608 | tf_op jit(solution)/shard_map/all_to_all | solution.py:75
  569.5 5.4 convolution_bitcast_fusion.1
  574.9 6.2 multiply_add_fusion
  588.6 29.8 %reduce-scatter.2.cloned.1.call-done = bf16[2,16,128,128]{3,2,1,0:T(8,128)(2,1)} async-done(((bf16[2,16,256,128]{3,2,1,0:T(8,128)(2,1)}), bf16[2,16,128,128]{3,2,1,0:T(8,128)(2,1)}) %reduce-scatter.2.cloned.1.call-update) | async-done | bytes 1048592 | tf_op jit(solution)/shard_map/reduce_scatter | solution.py:137
  (62 shorter events, 64.9 us)
Async XLA Ops:
  15.3 48.5 %all-to-all-start = ((bf16[2,16,256,128]{3,1,0,2:T(8,128)(2,1)}), bf16[2,16,256,128]{3,1,0,2:T(8,128)(2,1)S(1)}, u32[]{:S(2)}, u32[]{:S(2)}) async-start(bf16[2,16,256,128]{3,1,0,2:T(8,128)(2,1)} %copy.47), calls=%async_computation | async-start | bytes 4194304 | tf_op jit(solution)/shard_map/all_to_all | solution.py:104
  83.4 89.0 %all-to-all-start.1 = ((bf16[2,2,256,16,128]{4,3,0,1,2:T(8,128)(2,1)}), bf16[2,2,256,16,128]{4,3,0,1,2:T(8,128)(2,1)}, u32[]{:S(2)}, u32[]{:S(2)}) async-start(bf16[2,2,256,16,128]{4,3,0,1,2:T(8,128)(2,1)} %copy.52), calls=%async_computation.1 | async-start | bytes 8388608 | tf_op jit(solution)/shard_map/all_to_all | solution.py:75
  94.7 523.7 %reduce-scatter.2.cloned.1.call-start = ((), (), s32[]{:S(2)}) async-start(), calls=%async_computation.7 | async-start | bytes 3145728 | tf_op jit(solution)/shard_map/reduce_scatter | solution.py:137
  177.9 5.4 copy-start.5
  189.3 4.6 copy-start
  189.3 4.6 copy-start.2
  189.3 5.1 copy-start.6
  194.5 2.2 copy-start.7
  328.7 1.7 copy-start.10
  336.8 53.4 %copy-start.9 = (bf16[1,4096,128]{2,1,0:T(8,128)(2,1)S(1)}, bf16[1,4096,128]{2,1,0:T(8,128)(2,1)}, u32[]{:S(2)}) copy-start(bf16[1,4096,128]{2,1,0:T(8,128)(2,1)} %param.5) | copy-start | bytes 3145732
  336.8 53.4 %copy-start.12 = (f32[128]{0:T(128)S(1)}, f32[128]{0:T(128)}, u32[]{:S(2)}) copy-start(f32[128]{0:T(128)} %param.9) | copy-start | bytes 1540
  390.2 3.3 copy-start.8
  390.2 4.0 copy-start.11
  391.0 4.1 copy-start.4
  569.5 5.4 copy-start.1
  569.5 5.4 copy-start.3
Sparse Core Ops, SparseCore 0:
  585.9 32.4 reduce-scatter.1
where the time goes:
time: 635 us; the launch traced here: 628 us
  blocking collectives  314 us (49%)
  waiting for transfers between devices  144 us (23%)
  local copies, waits for them, and re-layouts  64.6 us (10%)
  other arithmetic  39.1 us (6%)
  matrix products  32.5 us (5%)
  starting transfers between devices  19 us (3%)
  between operations  14.6 us (2%)
    all_to_all x1, blocking collectives, body(): lax.all_to_all(mixed_rows, 'ctx', split_axis=3, concat_axis=2, tiled=True)  112 us
    all_to_all x1, blocking collectives, to_spectrum(): lax.all_to_all(section_cols, 'ctx', split_axis=2, concat_axis=3, tiled=True)  97.6 us
    all_to_all x1, waiting for transfers between devices, to_spectrum(): lax.all_to_all(section_cols, 'ctx', split_axis=2, concat_axis=3, tiled=True)  73.3 us
    all_to_all x1, blocking collectives, body(): lax.all_to_all(filtered, 'ctx', split_axis=1, concat_axis=2, tiled=True)  52.7 us
    all_to_all x1, blocking collectives, body(): lax.all_to_all(errors, 'ctx', split_axis=2, concat_axis=1, tiled=True)  52.2 us
    all_to_all x1, waiting for transfers between devices, body(): lax.all_to_all(inputs, 'ctx', split_axis=2, concat_axis=1, tiled=True)  40.9 us
    reduce_scatter x1, waiting for transfers between devices, body(): lax.psum_scatter(local_grad.astype(jnp.bfloat16), 'dp', scatter_dimension...  29.8 us
    another operation x2, local copies, waits for them, and re-layouts, first_section(): return jnp.stack([out_real, out_imag], 1).astype(jnp.bfloat16)  15.9 us
  transfers between devices with their start and end apart: 3, of which 3 were waited for; matrix products, arithmetic and copies ran while one was open for 1% of the time, Pallas kernels for 0%

commit v1 on v0

--- a/solution.py
+++ b/solution.py
@@ -1,14 +1,203 @@
 import jax
 import jax.numpy as jnp
+import numpy as np
 from jax import lax
+from jax.experimental import pallas as pl
+from jax.experimental.pallas import tpu as pltpu
 from jax.sharding import PartitionSpec as P
 
 N1 = 256
 N2 = 256
-
+BF16 = jnp.bfloat16
+F32 = jnp.float32
 
 two_pi = 6.283185307179586
 smart_weight = 2.0
+
+
+def tables():
+    ids = np.arange(N1)
+    phase = (ids[:, None] * ids[None, :] % N1) * (two_pi / N1)
+    cos_table, sin_table = np.cos(phase), np.sin(phase)
+    split_rows = np.concatenate([cos_table, -sin_table], 0)
+    forward = np.block([[cos_table, -sin_table], [sin_table, cos_table]])
+    inverse = np.block([[cos_table, sin_table], [-sin_table, cos_table]])
+    join_rows = np.concatenate([cos_table, -sin_table], 1) / (N1 * N2)
+    angle = (ids[:, None] * ids[None, :]) * (two_pi / (N1 * N2))
+    twiddle = np.stack([np.cos(angle), np.sin(angle)], 0)
+    small = [jnp.asarray(t.astype(jnp.bfloat16)) for t in (split_rows, forward, inverse, join_rows)]
+    return (*small, jnp.asarray(twiddle.astype(np.float32)))
+
+
+def dot(a, b):
+    return jnp.dot(a, b, preferred_element_type=F32)
+
+
+def half_forward(rows, tw_cos, tw_sin):
+    part_real, part_imag = rows[:N1], rows[N1:]
+    out_real = part_real * tw_cos + part_imag * tw_sin
+    out_imag = part_imag * tw_cos - part_real * tw_sin
+    return jnp.concatenate([out_real.astype(BF16), out_imag.astype(BF16)], 1)
+
+
+def conv_kernel(
+    gain_ref, ep_ref, filt_ref, split_ref, fwd_ref, inv_ref, join_ref, tw_ref,
+    send_ref, gap_ref, spec_ref, grad_ref,
+):
+    q, d = pl.program_id(0), pl.program_id(1)
+    tw_cos, tw_sin = tw_ref[0], tw_ref[1]
+    clean = ep_ref[0, :, 0, 0].reshape(N1, N2)
+    clean_wide = clean.astype(F32)
+    shifted = (clean_wide + ep_ref[0, :, 1, 0].reshape(N1, N2).astype(F32)).astype(BF16)
+    shifted_wide = shifted.astype(F32)
+    half = [half_forward(dot(split_ref[...], x), tw_cos, tw_sin) for x in (clean, shifted)]
+    spec = [dot(h, fwd_ref[...]) for h in half]
+    spec_ref[0, 0] = spec[0]
+    filter_real = filt_ref[0, :, 0, 0].reshape(N1, N2).astype(F32)
+    filter_imag = filt_ref[1, :, 0, 0].reshape(N1, N2).astype(F32)
+    gain = gain_ref[q]
+    ys = []
+    for x_wide, x_spec in zip((clean_wide, shifted_wide), spec):
+        real, imag = x_spec[:, :N2], x_spec[:, N2:]
+        prod_real = (filter_real * real - filter_imag * imag).astype(BF16)
+        prod_imag = (filter_real * imag + filter_imag * real).astype(BF16)
+        back = dot(jnp.concatenate([prod_real, prod_imag], 1), inv_ref[...])
+        back_real, back_imag = back[:, :N2], back[:, N2:]
+        mixed_real = (back_real * tw_cos - back_imag * tw_sin).astype(BF16)
+        mixed_imag = (back_imag * tw_cos + back_real * tw_sin).astype(BF16)
+        conv = dot(join_ref[...], jnp.concatenate([mixed_real, mixed_imag], 0))
+        conv = conv.astype(BF16).astype(F32)
+        ys.append(x_wide * conv + gain * x_wide)
+    send_ref[0, :, 0, 0] = ys[0].astype(BF16).reshape(send_ref.shape[1], -1, N2)
+    gap = smart_weight * (ys[1] - ys[0])
+    gap_ref[0, 0] = gap
+    err = (shifted_wide * gap).astype(BF16)
+    err_spec = dot(half_forward(dot(split_ref[...], err), tw_cos, tw_sin), fwd_ref[...])
+    add_grad(grad_ref, d, err_spec, spec[1])
+
+
+def add_grad(grad_ref, d, err_spec, spec):
+    err_real, err_imag = err_spec[:, :N2], err_spec[:, N2:]
+    real, imag = spec[:, :N2], spec[:, N2:]
+    term_real = err_real * real + err_imag * imag
+    term_imag = err_imag * real - err_real * imag
+
+    @pl.when(d == 0)
+    def _():
+        grad_ref[0, 0] = term_real
+        grad_ref[0, 1] = term_imag
+
+    @pl.when(d != 0)
+    def _():
+        grad_ref[0, 0] += term_real
+        grad_ref[0, 1] += term_imag
+
+
+def grad_kernel(
+    ep_ref, cot_ref, gap_ref, spec_ref, part_ref, split_ref, fwd_ref, tw_ref, _, send_ref, sum_ref
+):
+    d = pl.program_id(1)
+    tw_cos, tw_sin = tw_ref[0], tw_ref[1]
+    clean = ep_ref[0, :, 0, 0].reshape(N1, N2).astype(F32)
+    cot = cot_ref[0, :, 0].reshape(N1, N2).astype(F32)
+    err = (clean * (cot - gap_ref[0, 0])).astype(BF16)
+    err_spec = dot(half_forward(dot(split_ref[...], err), tw_cos, tw_sin), fwd_ref[...])
+    add_grad(sum_ref, d, err_spec, spec_ref[0, 0])
+
+    @pl.when(d == pl.num_programs(1) - 1)
+    def _():
+        total = ((sum_ref[0] + part_ref[0]) * (1.0 / (N1 * N2))).astype(BF16)
+        count = send_ref.shape[0]
+        width = N2 // count
+        for i in range(count):
+            cols = jnp.concatenate([total[0, :, i * width : (i + 1) * width], total[1, :, i * width : (i + 1) * width]], 1)
+            send_ref[i, :, 0, 0] = cols.reshape(send_ref.shape[1], -1, 2 * width)
+
+
+def whole(x):
+    return pl.BlockSpec(x.shape, lambda q, d: (0,) * x.ndim)
+
+
+def conv_call(gain, received, tabs):
+    dp, ctx, _, per, rows, _ = received.shape
+    split_rows, forward, inverse, join_rows, twiddle = tabs
+    return pl.pallas_call(
+        conv_kernel,
+        grid=(per, dp),
+        in_specs=[
+            pl.BlockSpec(memory_space=pltpu.SMEM),
+            pl.BlockSpec((1, ctx, 2, 1, rows, N2), lambda q, d: (d, 0, 0, q, 0, 0)),
+            pl.BlockSpec((dp, ctx, 1, 1, rows, N2), lambda q, d: (0, 0, 2, q, 0, 0)),
+            *[whole(t) for t in tabs],
+        ],
+        out_specs=[
+            pl.BlockSpec((1, ctx, 1, 1, rows, N2), lambda q, d: (d, 0, 0, q, 0, 0)),
+            pl.BlockSpec((1, 1, N1, N2), lambda q, d: (q, d, 0, 0)),
+            pl.BlockSpec((1, 1, N1, 2 * N2), lambda q, d: (q, d, 0, 0)),
+            pl.BlockSpec((1, 2, N1, N2), lambda q, d: (q, 0, 0, 0)),
+        ],
+        out_shape=[
+            jax.ShapeDtypeStruct((dp, ctx, 2, per, rows, N2), BF16),
+            jax.ShapeDtypeStruct((per, dp, N1, N2), F32),
+            jax.ShapeDtypeStruct((per, dp, N1, 2 * N2), F32),
+            jax.ShapeDtypeStruct((per, 2, N1, N2), F32),
+        ],
+        compiler_params=pltpu.CompilerParams(vmem_limit_bytes=40 << 20),
+        cost_estimate=pl.CostEstimate(flops=8 * per * dp * N1 * N1 * N1 * 12, bytes_accessed=20 << 20, transcendentals=0),
+        name="conv",
+    )(gain, received, received, split_rows, forward, inverse, join_rows, twiddle)
+
+
+def grad_call(received, cot, gap, spec, part, tabs, send):
+    dp, ctx, _, per, rows, _ = received.shape
+    split_rows, forward, _, _, twiddle = tabs
+    return pl.pallas_call(
+        grad_kernel,
+        grid=(per, dp),
+        in_specs=[
+            pl.BlockSpec((1, ctx, 1, 1, rows, N2), lambda q, d: (d, 0, 0, q, 0, 0)),
+            pl.BlockSpec((1, ctx, 1, rows, N2), lambda q, d: (d, 0, q, 0, 0)),
+            pl.BlockSpec((1, 1, N1, N2), lambda q, d: (q, d, 0, 0)),
+            pl.BlockSpec((1, 1, N1, 2 * N2), lambda q, d: (q, d, 0, 0)),
+            pl.BlockSpec((1, 2, N1, N2), lambda q, d: (q, 0, 0, 0)),
+            whole(split_rows),
+            whole(forward),
+            whole(twiddle),
+            pl.BlockSpec(memory_space=pl.ANY),
+        ],
+        out_specs=pl.BlockSpec((dp, ctx, 1, 1, rows, N2), lambda q, d: (0, 0, 1, q, 0, 0)),
+        out_shape=jax.ShapeDtypeStruct(send.shape, BF16),
+        scratch_shapes=[pltpu.VMEM((1, 2, N1, N2), F32)],
+        input_output_aliases={8: 0},
+        compiler_params=pltpu.CompilerParams(vmem_limit_bytes=40 << 20),
+        cost_estimate=pl.CostEstimate(flops=2 * per * dp * N1 * N1 * N1 * 6, bytes_accessed=12 << 20, transcendentals=0),
+        name="grad",
+    )(received, cot, gap, spec, part, split_rows, forward, twiddle, send)
+
+
+def by_channel_body(embeds, perturb, cotangent, filter_spectrum, skip_gain):
+    dp, ctx = lax.axis_size("dp"), lax.axis_size("ctx")
+    d, c = lax.axis_index("dp"), lax.axis_index("ctx")
+    axes = ("dp", "ctx")
+    channels = embeds.shape[2]
+    rows = N1 // ctx
+    per = channels // (dp * ctx)
+    tabs = tables()
+
+    def outward(x):
+        return x.reshape(rows * N2, channels).T.reshape(dp * ctx, per, rows, N2)
+
+    filter_part = lax.dynamic_index_in_dim(filter_spectrum, d, 0, keepdims=False).astype(BF16)
+    first = jnp.stack([outward(embeds), outward(perturb), outward(filter_part)], 1)
+    received = lax.all_to_all(first, axes, 0, 0, tiled=True).reshape(dp, ctx, 3, per, rows, N2)
+    cot = lax.all_to_all(outward(cotangent), axes, 0, 0, tiled=True).reshape(dp, ctx, per, rows, N2)
+    gain = lax.dynamic_slice(skip_gain, ((d * ctx + c) * per,), (per,))
+    send, gap, spec, part = conv_call(gain, received, tabs)
+    send = grad_call(received, cot, gap, spec, part, tabs, send)
+    last = lax.all_to_all(send.reshape(dp * ctx, 2, per, rows, N2), axes, 0, 0, tiled=True)
+    y = last[:, 0].reshape(channels, rows * N2).T.reshape(1, rows * N2, channels)
+    grad = last[:, 1].reshape(channels, rows, 2, N2 // dp).transpose(2, 1, 3, 0).astype(F32)
+    return y, grad
 
 
 def trig_table(period):
@@ -141,16 +330,22 @@
 
 
 def solution(mesh):
-    return jax.shard_map(
-        body,
-        mesh=mesh,
-        in_specs=(
-            P("dp", "ctx", None),
-            P("dp", "ctx", None),
-            P("dp", "ctx", None),
-            P(None, "ctx", None, None),
-            P(),
-        ),
-        out_specs=(P("dp", "ctx", None), P(None, "ctx", "dp", None)),
-        check_vma=False,
-    )
+    dp, ctx = mesh.shape["dp"], mesh.shape["ctx"]
+
+    def run(embeds, *rest):
+        apart = dp == 2 and embeds.shape[2] % (dp * ctx) == 0 and N1 // ctx % 16 == 0
+        return jax.shard_map(
+            by_channel_body if apart else body,
+            mesh=mesh,
+            in_specs=(
+                P("dp", "ctx", None),
+                P("dp", "ctx", None),
+                P("dp", "ctx", None),
+                P(None, "ctx", None, None),
+                P(),
+            ),
+            out_specs=(P("dp", "ctx", None), P(None, "ctx", "dp", None)),
+            check_vma=False,
+        )(embeds, *rest)
+
+    return run

time: 635 us -> 198 us (0.31)
  blocking collectives: 314 us -> 54.4 us
  waiting for transfers between devices: 144 us -> 68.5 us
  other arithmetic: 39.1 us -> 0.7 us
  matrix products: 32.5 us -> 0 us
  local copies, waits for them, and re-layouts: 64.6 us -> 35.9 us
  Pallas kernels: 0 us -> 25.7 us
  between operations: 14.6 us -> 0.78 us
  starting transfers between devices: 19 us -> 10.7 us
    all_to_all x4 -> x1, blocking collectives: 314 us -> 54.4 us  [by_channel_body(): lax.all_to_all(send.reshape(dp * ctx, 2, per, rows, N2), axes, 0, 0, tile...]
    all_to_all x2, waiting for transfers between devices: 114 us -> 68.5 us  [the longest x1 67.7 us: by_channel_body(): lax.all_to_all(first, axes, 0, 0, tiled=True)]
    dot_general x12 -> x0, matrix products: 32.5 us -> none  [the longest x2 10.8 us: second_section(): jnp.einsum('sprnc,kn->sprkc', section_rows, cos_table, preferred_element_...]
    reduce_scatter x1 -> x0, waiting for transfers between devices: 29.8 us -> none  [body(): lax.psum_scatter(local_grad.astype(jnp.bfloat16), 'dp', scatter_dimension...]
    pallas_call x0 -> x2, Pallas kernels: none -> 25.7 us  [the longest x1 18.2 us: conv_call(): pl.pallas_call(conv_kernel, grid=(per, dp), in_specs=[pl.BlockSpec(memory...]
    another operation x5 -> x1, local copies, waits for them, and re-layouts: 22.6 us -> 2.06 us  [by_channel_body(): jnp.stack([outward(embeds), outward(perturb), outward(filter_part)], 1)]
    all_to_all x8 -> x0, local copies, waits for them, and re-layouts: 20.3 us -> none  [the longest x2 5.12 us: body(): lax.all_to_all(inputs, 'ctx', split_axis=2, concat_axis=1, tiled=True)]
    another operation x8 -> x1, other arithmetic: 19 us -> 0.34 us  [by_channel_body(): jnp.stack([outward(embeds), outward(perturb), outward(filter_part)], 1)]
  transfers between devices with their start and end apart: 3 -> 2, of which waited for: 3 -> 2; matrix products, arithmetic and copies ran while one was open for 1% -> 2% of each run, Pallas kernels for 0% -> 9%
where the time goes in v1:
time: 198 us; the launch traced here: 197 us
  waiting for transfers between devices  68.5 us (35%)
  blocking collectives  54.4 us (27%)
  local copies, waits for them, and re-layouts  35.9 us (18%)
  Pallas kernels  25.7 us (13%)
  starting transfers between devices  10.7 us (5%)
    all_to_all x1, waiting for transfers between devices, by_channel_body(): lax.all_to_all(first, axes, 0, 0, tiled=True)  67.7 us
    all_to_all x1, blocking collectives, by_channel_body(): lax.all_to_all(send.reshape(dp * ctx, 2, per, rows, N2), axes, 0, 0, tile...  54.4 us
    unnamed x35, local copies, waits for them, and re-layouts  24.1 us
    pallas_call x1, Pallas kernels, conv_call(): pl.pallas_call(conv_kernel, grid=(per, dp), in_specs=[pl.BlockSpec(memory...  18.2 us
    pallas_call x1, Pallas kernels, grad_call(): pl.pallas_call(grad_kernel, grid=(per, dp), in_specs=[pl.BlockSpec((1, ct...  7.48 us
    all_to_all x1, starting transfers between devices, by_channel_body(): lax.all_to_all(first, axes, 0, 0, tiled=True)  7.3 us
    transpose x3, local copies, waits for them, and re-layouts, outward(): return x.reshape(rows * N2, channels).T.reshape(dp * ctx, per, rows, N2)  5.28 us
  transfers between devices with their start and end apart: 2, of which 2 were waited for; matrix products, arithmetic and copies ran while one was open for 2% of the time, Pallas kernels for 9%

profile of v1, /device:TPU:0, one launch (start us, length us, event | category | flops | bytes accessed | tf_op | source)
XLA Modules:
  0.0 196.6 jit_solution(7981031323381818610)
XLA Ops:
  0.6 1.8 dynamic-slice_convert_fusion
  3.2 1.5 copy.26
  5.0 1.5 copy.27
  7.1 2.1 %copy.29 = bf16[32,3,4,16,256]{4,3,2,1,0:T(8,128)(2,1)} copy(bf16[32,3,4,16,256]{4,3,2,0,1:T(8,128)(2,1)S(1)} %pad_maximum_fusion) | data formatting | bytes 6291456 | tf_op jit(solution)/shard_map/stack | solution.py:191
  9.1 7.3 %all-to-all-start = ((bf16[32,3,4,16,256]{4,3,2,1,0:T(8,128)(2,1)}), bf16[32,3,4,16,256]{4,3,2,1,0:T(8,128)(2,1)S(1)}, u32[]{:S(2)}, u32[]{:S(2)}) async-start(bf16[32,3,4,16,256]{4,3,2,1,0:T(8,128)(2,1)} %copy.29), calls=%async_computation | async-start | bytes 6291456 | tf_op jit(solution)/shard_map/all_to_all | solution.py:192
  16.5 2.3 %copy.30 = bf16[128,4096]{1,0:T(8,128)(2,1)} copy(bf16[128,4096]{0,1:T(8,128)(2,1)} %bitcast.57) | data formatting | bytes 2097152 | tf_op jit(solution)/shard_map/transpose | solution.py:188
  18.8 2.5 %copy.36 = bf16[16,8,16,256]{3,2,1,0:T(8,128)(2,1)} copy(bf16[16,8,16,256]{3,1,2,0:T(8,128)(2,1)} %bitcast.51) | data formatting | bytes 2097152
  21.2 67.7 %all-to-all-done = bf16[32,3,4,16,256]{4,3,2,1,0:T(8,128)(2,1)S(1)} async-done(((bf16[32,3,4,16,256]{4,3,2,1,0:T(8,128)(2,1)}), bf16[32,3,4,16,256]{4,3,2,1,0:T(8,128)(2,1)S(1)}, u32[]{:S(2)}, u32[]{:S(2)}) %all-to-all-start) | async-done | bytes 3145760 | tf_op jit(solution)/shard_map/all_to_all | solution.py:192
  89.0 3.4 %all-to-all-start.1 = ((bf16[32,4,16,256]{3,2,1,0:T(8,128)(2,1)}), bf16[32,4,16,256]{3,2,1,0:T(8,128)(2,1)}, u32[]{:S(2)}, u32[]{:S(2)}) async-start(bf16[32,4,16,256]{3,2,1,0:T(8,128)(2,1)} %bitcast.46), calls=%async_computation.1 | async-start | bytes 2097152 | tf_op jit(solution)/shard_map/all_to_all | solution.py:193
  92.4 1.0 copy-done.6
  93.5 1.0 copy-done.8
  94.5 1.0 copy-done.11
  96.5 18.2 %conv.1 = (bf16[2,16,2,4,16,256]{5,4,3,2,1,0:T(8,128)(2,1)S(1)}, f32[4,2,256,256]{3,2,1,0:T(8,128)S(1)}, f32[4,2,256,512]{3,2,1,0:T(8,128)}, f32[4,2,256,256]{3,2,1,0:T(8,128)S(1)}) custom-call(f32[4]{0:T(128)S(1)} %dynamic_slice.8.gain_ref, bf16[2,16,3,4,16,256]{5,4,3,2,1,0:T(8,128)(2,1)S(1)} %bitcast.39, bf16[2,16,3,4,16,256]{5,4,3,2,1,0:T(8,128)(2,1)S(1)} %bitcast.40, ...), custom_call_target="tpu_custom_call" | custom-call | flops 12884901888 | bytes 20971520 | tf_op jit(solution)/shard_map/conv/pallas_call | solution.py:124
  114.7 1.4 copy-done
  116.1 1.3 copy-done.2
  117.4 1.4 copy-done.4
  119.5 1.6 copy-done.1
  121.1 1.6 copy-done.3
  122.7 1.6 copy-done.5
  126.4 7.5 %grad.1 = bf16[2,16,2,4,16,256]{5,4,3,2,1,0:T(8,128)(2,1)S(1)} custom-call(bf16[2,16,3,4,16,256]{5,4,3,2,1,0:T(8,128)(2,1)S(1)} %bitcast.41, bf16[2,16,4,16,256]{4,3,2,1,0:T(8,128)(2,1)} %bitcast.9.cot_ref, f32[4,2,256,256]{3,2,1,0:T(8,128)S(1)} %copy-done.3, f32[4,2,256,512]{3,2,1,0:T(8,128)} %get-tuple-element.7.spec_ref, ...), custom_call_target="tpu_custom_call", output_to_operand_aliasing={{}: (8, {})} | custom-call | flops 1610612736 | bytes 12582912 | tf_op jit(solution)/shard_map/grad/pallas_call | solution.py:154
  133.9 54.4 %all_to_all.15 = bf16[32,2,4,16,256]{4,3,2,1,0:T(8,128)(2,1)S(1)} all-to-all(bf16[32,2,4,16,256]{4,3,2,1,0:T(8,128)(2,1)S(1)} %bitcast.42), channel_id=1, replica_groups=mesh['dp'=2,'ctx'=16] {'dp','ctx'}, dimensions={0} | all-to-all | bytes 4194304 | tf_op jit(solution)/shard_map/all_to_all | solution.py:197
  188.7 2.1 %reshape.41 = f32[128,16,2,128]{3,2,1,0:T(2,128)} reshape(f32[32,1,4,16,256]{4,3,2,1,0:T(8,128)S(1)} %get-tuple-element.14) | data formatting | bytes 4194304 | tf_op jit(solution)/shard_map/convert_element_type | solution.py:199
  190.8 4.1 %copy.32 = f32[2,16,128,128]{3,2,1,0:T(8,128)} copy(f32[2,16,128,128]{2,0,1,3:T(2,128)} %bitcast.43) | data formatting | bytes 4194304
  195.3 1.3 copy.31
  (28 shorter events, 6.3 us)
Async XLA Ops:
  9.1 79.8 %all-to-all-start = ((bf16[32,3,4,16,256]{4,3,2,1,0:T(8,128)(2,1)}), bf16[32,3,4,16,256]{4,3,2,1,0:T(8,128)(2,1)S(1)}, u32[]{:S(2)}, u32[]{:S(2)}) async-start(bf16[32,3,4,16,256]{4,3,2,1,0:T(8,128)(2,1)} %copy.29), calls=%async_computation | async-start | bytes 6291456 | tf_op jit(solution)/shard_map/all_to_all | solution.py:192
  16.4 75.9 %copy-start.13 = (f32[128]{0:T(128)S(1)}, f32[128]{0:T(128)}, u32[]{:S(2)}) copy-start(f32[128]{0:T(128)} %param.14) | copy-start | bytes 1540
  16.4 76.0 %copy-start.10 = (bf16[512,256]{1,0:T(8,128)(2,1)S(1)}, bf16[512,256]{1,0:T(8,128)(2,1)}, u32[]{:S(2)}) copy-start(bf16[512,256]{1,0:T(8,128)(2,1)} %constant.32.clone.split_ref) | copy-start | bytes 786436
  89.0 30.6 %all-to-all-start.1 = ((bf16[32,4,16,256]{3,2,1,0:T(8,128)(2,1)}), bf16[32,4,16,256]{3,2,1,0:T(8,128)(2,1)}, u32[]{:S(2)}, u32[]{:S(2)}) async-start(bf16[32,4,16,256]{3,2,1,0:T(8,128)(2,1)} %bitcast.46), calls=%async_computation.1 | async-start | bytes 2097152 | tf_op jit(solution)/shard_map/all_to_all | solution.py:193
  92.4 1.0 copy-start.6
  93.5 1.0 copy-start.8
  94.5 1.0 copy-start.11
  95.6 0.9 copy-start.12
  114.7 1.4 copy-start
  116.1 1.3 copy-start.2
  117.4 1.4 copy-start.4
  119.5 1.6 copy-start.1
  121.1 1.6 copy-start.3
  122.7 1.6 copy-start.5
  124.3 1.0 copy-start.7
  125.3 1.0 copy-start.9

commit v2 on v1

--- a/solution.py
+++ b/solution.py
@@ -10,6 +10,7 @@
 N2 = 256
 BF16 = jnp.bfloat16
 F32 = jnp.float32
+VMEM = 60 << 20
 
 two_pi = 6.283185307179586
 smart_weight = 2.0
@@ -94,28 +95,34 @@
 
 
 def grad_kernel(
-    ep_ref, cot_ref, gap_ref, spec_ref, part_ref, split_ref, fwd_ref, tw_ref, _, send_ref, sum_ref
+    ep_ref, cot_ref, gap_ref, spec_ref, part_ref, split_ref, fwd_ref, tw_ref, _, send_ref
 ):
-    d = pl.program_id(1)
     tw_cos, tw_sin = tw_ref[0], tw_ref[1]
-    clean = ep_ref[0, :, 0, 0].reshape(N1, N2).astype(F32)
-    cot = cot_ref[0, :, 0].reshape(N1, N2).astype(F32)
-    err = (clean * (cot - gap_ref[0, 0])).astype(BF16)
-    err_spec = dot(half_forward(dot(split_ref[...], err), tw_cos, tw_sin), fwd_ref[...])
-    add_grad(sum_ref, d, err_spec, spec_ref[0, 0])
-
-    @pl.when(d == pl.num_programs(1) - 1)
-    def _():
-        total = ((sum_ref[0] + part_ref[0]) * (1.0 / (N1 * N2))).astype(BF16)
-        count = send_ref.shape[0]
-        width = N2 // count
-        for i in range(count):
-            cols = jnp.concatenate([total[0, :, i * width : (i + 1) * width], total[1, :, i * width : (i + 1) * width]], 1)
-            send_ref[i, :, 0, 0] = cols.reshape(send_ref.shape[1], -1, 2 * width)
+    count = send_ref.shape[0]
+    halves = []
+    for d in range(count):
+        clean = ep_ref[d, :, 0, 0].reshape(N1, N2).astype(F32)
+        cot = cot_ref[d, :, 0].reshape(N1, N2).astype(F32)
+        err = (clean * (cot - gap_ref[0, d])).astype(BF16)
+        halves.append(half_forward(dot(split_ref[...], err), tw_cos, tw_sin))
+    total_real, total_imag = part_ref[0, 0], part_ref[0, 1]
+    for d in range(count):
+        err_spec = dot(halves[d], fwd_ref[...])
+        err_real, err_imag = err_spec[:, :N2], err_spec[:, N2:]
+        real, imag = spec_ref[0, d, :, :N2], spec_ref[0, d, :, N2:]
+        total_real += err_real * real + err_imag * imag
+        total_imag += err_imag * real - err_real * imag
+    scale = 1.0 / (N1 * N2)
+    total_real, total_imag = (total_real * scale).astype(BF16), (total_imag * scale).astype(BF16)
+    width = N2 // count
+    for i in range(count):
+        cols = slice(i * width, (i + 1) * width)
+        pair = jnp.concatenate([total_real[:, cols], total_imag[:, cols]], 1)
+        send_ref[i, :, 0, 0] = pair.reshape(send_ref.shape[1], -1, 2 * width)
 
 
 def whole(x):
-    return pl.BlockSpec(x.shape, lambda q, d: (0,) * x.ndim)
+    return pl.BlockSpec(x.shape, lambda *_: (0,) * x.ndim)
 
 
 def conv_call(gain, received, tabs):
@@ -142,7 +149,7 @@
             jax.ShapeDtypeStruct((per, dp, N1, 2 * N2), F32),
             jax.ShapeDtypeStruct((per, 2, N1, N2), F32),
         ],
-        compiler_params=pltpu.CompilerParams(vmem_limit_bytes=40 << 20),
+        compiler_params=pltpu.CompilerParams(vmem_limit_bytes=VMEM),
         cost_estimate=pl.CostEstimate(flops=8 * per * dp * N1 * N1 * N1 * 12, bytes_accessed=20 << 20, transcendentals=0),
         name="conv",
     )(gain, received, received, split_rows, forward, inverse, join_rows, twiddle)
@@ -153,26 +160,93 @@
     split_rows, forward, _, _, twiddle = tabs
     return pl.pallas_call(
         grad_kernel,
-        grid=(per, dp),
+        grid=(per,),
         in_specs=[
-            pl.BlockSpec((1, ctx, 1, 1, rows, N2), lambda q, d: (d, 0, 0, q, 0, 0)),
-            pl.BlockSpec((1, ctx, 1, rows, N2), lambda q, d: (d, 0, q, 0, 0)),
-            pl.BlockSpec((1, 1, N1, N2), lambda q, d: (q, d, 0, 0)),
-            pl.BlockSpec((1, 1, N1, 2 * N2), lambda q, d: (q, d, 0, 0)),
-            pl.BlockSpec((1, 2, N1, N2), lambda q, d: (q, 0, 0, 0)),
+            pl.BlockSpec((dp, ctx, 1, 1, rows, N2), lambda q: (0, 0, 0, q, 0, 0)),
+            pl.BlockSpec((dp, ctx, 1, rows, N2), lambda q: (0, 0, q, 0, 0)),
+            pl.BlockSpec((1, dp, N1, N2), lambda q: (q, 0, 0, 0)),
+            pl.BlockSpec((1, dp, N1, 2 * N2), lambda q: (q, 0, 0, 0)),
+            pl.BlockSpec((1, 2, N1, N2), lambda q: (q, 0, 0, 0)),
             whole(split_rows),
             whole(forward),
             whole(twiddle),
             pl.BlockSpec(memory_space=pl.ANY),
         ],
-        out_specs=pl.BlockSpec((dp, ctx, 1, 1, rows, N2), lambda q, d: (0, 0, 1, q, 0, 0)),
+        out_specs=pl.BlockSpec((dp, ctx, 1, 1, rows, N2), lambda q: (0, 0, 1, q, 0, 0)),
         out_shape=jax.ShapeDtypeStruct(send.shape, BF16),
-        scratch_shapes=[pltpu.VMEM((1, 2, N1, N2), F32)],
         input_output_aliases={8: 0},
-        compiler_params=pltpu.CompilerParams(vmem_limit_bytes=40 << 20),
+        compiler_params=pltpu.CompilerParams(vmem_limit_bytes=VMEM),
         cost_estimate=pl.CostEstimate(flops=2 * per * dp * N1 * N1 * N1 * 6, bytes_accessed=12 << 20, transcendentals=0),
         name="grad",
     )(received, cot, gap, spec, part, split_rows, forward, twiddle, send)
+
+
+def outward_kernel(index_ref, *refs):
+    *in_refs, out_ref, rows_ref = refs
+    count, _, per, rows, width = out_ref.shape
+    channels = count * per
+    for t, in_ref in enumerate(in_refs):
+        for r in range(rows):
+            block = in_ref[0, r].astype(F32).T
+            rows_ref[pl.ds(r, channels, stride=rows), :] = block
+        out_ref[:, t] = rows_ref[...].astype(BF16).reshape(count, per, rows, width)
+
+
+def outward(index, arrays, count):
+    _, rows, _, channels = arrays[0].shape
+    per = channels // count
+    width = 128
+    picks = [(lambda h, s: (s[0], 0, h, 0)) if a.shape[0] > 1 else (lambda h, s: (0, 0, h, 0)) for a in arrays]
+    return pl.pallas_call(
+        outward_kernel,
+        grid_spec=pltpu.PrefetchScalarGridSpec(
+            num_scalar_prefetch=1,
+            grid=(N2 // width,),
+            in_specs=[pl.BlockSpec((1, rows, width, channels), pick) for pick in picks],
+            out_specs=pl.BlockSpec((count, len(arrays), per, rows, width), lambda h, s: (0, 0, 0, 0, h)),
+            scratch_shapes=[pltpu.VMEM((channels * rows, width), F32)],
+        ),
+        out_shape=jax.ShapeDtypeStruct((count, len(arrays), per, rows, N2), BF16),
+        compiler_params=pltpu.CompilerParams(vmem_limit_bytes=VMEM),
+        cost_estimate=pl.CostEstimate(flops=0, bytes_accessed=(4 * len(arrays)) << 20, transcendentals=0),
+        name="outward",
+    )(index, *arrays)
+
+
+def homeward_kernel(last_ref, y_ref, grad_ref, rows_ref):
+    count, _, per, rows, width = last_ref.shape
+    channels = count * per
+    for t in range(2):
+        rows_ref[...] = last_ref[:, t].astype(F32).reshape(channels * rows, width)
+        for r in range(rows):
+            block = rows_ref[pl.ds(r, channels, stride=rows), :].T
+            if t == 0:
+                y_ref[r] = block.astype(BF16)
+            else:
+                grad_ref[0, r] = block
+
+
+def homeward(last):
+    count, _, per, rows, _ = last.shape
+    channels = count * per
+    width = 128
+    return pl.pallas_call(
+        homeward_kernel,
+        grid=(N2 // width,),
+        in_specs=[pl.BlockSpec((count, 2, per, rows, width), lambda h: (0, 0, 0, 0, h))],
+        out_specs=[
+            pl.BlockSpec((rows, width, channels), lambda h: (0, h, 0)),
+            pl.BlockSpec((1, rows, width, channels), lambda h: (h, 0, 0, 0)),
+        ],
+        out_shape=[
+            jax.ShapeDtypeStruct((rows, N2, channels), BF16),
+            jax.ShapeDtypeStruct((2, rows, width, channels), F32),
+        ],
+        scratch_shapes=[pltpu.VMEM((channels * rows, width), F32)],
+        compiler_params=pltpu.CompilerParams(vmem_limit_bytes=VMEM),
+        cost_estimate=pl.CostEstimate(flops=0, bytes_accessed=5 << 20, transcendentals=0),
+        name="homeward",
+    )(last)
 
 
 def by_channel_body(embeds, perturb, cotangent, filter_spectrum, skip_gain):
@@ -183,21 +257,21 @@
     rows = N1 // ctx
     per = channels // (dp * ctx)
     tabs = tables()
-
-    def outward(x):
-        return x.reshape(rows * N2, channels).T.reshape(dp * ctx, per, rows, N2)
-
-    filter_part = lax.dynamic_index_in_dim(filter_spectrum, d, 0, keepdims=False).astype(BF16)
-    first = jnp.stack([outward(embeds), outward(perturb), outward(filter_part)], 1)
+    index = d.reshape(1)
+
+    def matrix(x):
+        return x.reshape(1, rows, N2, channels)
+
+    first = outward(index, [matrix(embeds), matrix(perturb), filter_spectrum], dp * ctx)
     received = lax.all_to_all(first, axes, 0, 0, tiled=True).reshape(dp, ctx, 3, per, rows, N2)
-    cot = lax.all_to_all(outward(cotangent), axes, 0, 0, tiled=True).reshape(dp, ctx, per, rows, N2)
+    second = outward(index, [matrix(cotangent)], dp * ctx)
+    cot = lax.all_to_all(second, axes, 0, 0, tiled=True).reshape(dp, ctx, per, rows, N2)
     gain = lax.dynamic_slice(skip_gain, ((d * ctx + c) * per,), (per,))
     send, gap, spec, part = conv_call(gain, received, tabs)
     send = grad_call(received, cot, gap, spec, part, tabs, send)
     last = lax.all_to_all(send.reshape(dp * ctx, 2, per, rows, N2), axes, 0, 0, tiled=True)
-    y = last[:, 0].reshape(channels, rows * N2).T.reshape(1, rows * N2, channels)
-    grad = last[:, 1].reshape(channels, rows, 2, N2 // dp).transpose(2, 1, 3, 0).astype(F32)
-    return y, grad
+    y, grad = homeward(last)
+    return y.reshape(1, rows * N2, channels), grad
 
 
 def trig_table(period):
@@ -333,7 +407,7 @@
     dp, ctx = mesh.shape["dp"], mesh.shape["ctx"]
 
     def run(embeds, *rest):
-        apart = dp == 2 and embeds.shape[2] % (dp * ctx) == 0 and N1 // ctx % 16 == 0
+        apart = dp == 2 and embeds.shape[2] % (dp * ctx) == 0 and N1 // ctx == 16
         return jax.shard_map(
             by_channel_body if apart else body,
             mesh=mesh,

time: 198 us -> 181 us (0.914)
  local copies, waits for them, and re-layouts: 35.9 us -> 0.62 us
  Pallas kernels: 25.7 us -> 38.2 us
  waiting for transfers between devices: 68.5 us -> 77.1 us
    unnamed x35 -> x4, local copies, waits for them, and re-layouts: 24.1 us -> 0.01 us
    pallas_call x1 -> x4, Pallas kernels: 7.48 us -> 18.9 us  [the longest x2 7.65 us: outward(): pl.pallas_call(outward_kernel, grid_spec=pltpu.PrefetchScalarGridSpec(num...]
    all_to_all x1, waiting for transfers between devices: 0.78 us -> 7.28 us  [by_channel_body(): lax.all_to_all(second, axes, 0, 0, tiled=True)]
    transpose x3 -> x0, local copies, waits for them, and re-layouts: 5.28 us -> none  [outward(): return x.reshape(rows * N2, channels).T.reshape(dp * ctx, per, rows, N2)]
    convert_element_type x3 -> x0, local copies, waits for them, and re-layouts: 4.41 us -> none  [the longest x2 2.31 us: by_channel_body(): lax.dynamic_index_in_dim(filter_spectrum, d, 0, keepdims=False).astype(BF16)]
    all_to_all x1, waiting for transfers between devices: 67.7 us -> 69.9 us  [by_channel_body(): lax.all_to_all(first, axes, 0, 0, tiled=True)]
    another operation x1 -> x0, local copies, waits for them, and re-layouts: 2.06 us -> none  [by_channel_body(): jnp.stack([outward(embeds), outward(perturb), outward(filter_part)], 1)]
  transfers between devices with their start and end apart: 2 -> 2, of which waited for: 2 -> 2; matrix products, arithmetic and copies ran while one was open for 2% -> 0% of each run, Pallas kernels for 9% -> 12%
where the time goes in v2:
time: 181 us; the launch traced here: 180 us
  waiting for transfers between devices  77.1 us (43%)
  blocking collectives  53.1 us (29%)
  Pallas kernels  38.2 us (21%)
  starting transfers between devices  10.7 us (6%)
    all_to_all x1, waiting for transfers between devices, by_channel_body(): lax.all_to_all(first, axes, 0, 0, tiled=True)  69.9 us
    all_to_all x1, blocking collectives, by_channel_body(): lax.all_to_all(send.reshape(dp * ctx, 2, per, rows, N2), axes, 0, 0, tile...  53.1 us
    pallas_call x1, Pallas kernels, conv_call(): pl.pallas_call(conv_kernel, grid=(per, dp), in_specs=[pl.BlockSpec(memory...  19.3 us
    pallas_call x2, Pallas kernels, outward(): pl.pallas_call(outward_kernel, grid_spec=pltpu.PrefetchScalarGridSpec(num...  7.65 us
    pallas_call x1, Pallas kernels, grad_call(): pl.pallas_call(grad_kernel, grid=(per,), in_specs=[pl.BlockSpec((dp, ctx,...  7.33 us
    all_to_all x1, starting transfers between devices, by_channel_body(): lax.all_to_all(first, axes, 0, 0, tiled=True)  7.3 us
    all_to_all x1, waiting for transfers between devices, by_channel_body(): lax.all_to_all(second, axes, 0, 0, tiled=True)  7.28 us
    pallas_call x1, Pallas kernels, homeward(): pl.pallas_call(homeward_kernel, grid=(N2 // width,), in_specs=[pl.BlockSp...  3.93 us
  transfers between devices with their start and end apart: 2, of which 2 were waited for; matrix products, arithmetic and copies ran while one was open for 0% of the time, Pallas kernels for 12%

profile of v2, /device:TPU:0, one launch (start us, length us, event | category | flops | bytes accessed | tf_op | source)
XLA Modules:
  0.0 180.4 jit_solution(5906307999099834139)
XLA Ops:
  0.6 5.0 %outward.2 = bf16[32,3,4,16,256]{4,3,2,1,0:T(8,128)(2,1)} custom-call(s32[1]{0:T(128)} %bitcast.index_ref, bf16[1,16,256,128]{3,2,1,0:T(8,128)(2,1)} %bitcast.12, bf16[1,16,256,128]{3,2,1,0:T(8,128)(2,1)} %bitcast.13, f32[2,16,256,128]{3,2,1,0:T(8,128)} %refs_2_.1), custom_call_target="tpu_custom_call" | custom-call | bytes 12582912 | tf_op jit(solution)/shard_map/outward/pallas_call | solution.py:200
  5.6 7.3 %all-to-all-start = ((bf16[32,3,4,16,256]{4,3,2,1,0:T(8,128)(2,1)}), bf16[32,3,4,16,256]{4,3,2,1,0:T(8,128)(2,1)S(1)}, u32[]{:S(2)}, u32[]{:S(2)}) async-start(bf16[32,3,4,16,256]{4,3,2,1,0:T(8,128)(2,1)} %outward.2), calls=%async_computation | async-start | bytes 6291456 | tf_op jit(solution)/shard_map/all_to_all | solution.py:266
  12.9 0.0 copy-start.1
  13.0 2.6 %outward.3 = bf16[32,1,4,16,256]{4,3,2,1,0:T(8,128)(2,1)} custom-call(s32[1]{0:T(128)} %bitcast.index_ref, bf16[1,16,256,128]{3,2,1,0:T(8,128)(2,1)} %bitcast.14), custom_call_target="tpu_custom_call" | custom-call | bytes 4194304 | tf_op jit(solution)/shard_map/outward/pallas_call | solution.py:200
  15.6 69.9 %all-to-all-done = bf16[32,3,4,16,256]{4,3,2,1,0:T(8,128)(2,1)S(1)} async-done(((bf16[32,3,4,16,256]{4,3,2,1,0:T(8,128)(2,1)}), bf16[32,3,4,16,256]{4,3,2,1,0:T(8,128)(2,1)S(1)}, u32[]{:S(2)}, u32[]{:S(2)}) %all-to-all-start) | async-done | bytes 3145760 | tf_op jit(solution)/shard_map/all_to_all | solution.py:266
  85.5 0.0 copy-start
  85.5 3.4 %all-to-all-start.1 = ((bf16[32,1,4,16,256]{4,3,2,1,0:T(8,128)(2,1)}), bf16[32,1,4,16,256]{4,3,2,1,0:T(8,128)(2,1)}, u32[]{:S(2)}, u32[]{:S(2)}) async-start(bf16[32,1,4,16,256]{4,3,2,1,0:T(8,128)(2,1)} %outward.3), calls=%async_computation.1 | async-start | bytes 2097152 | tf_op jit(solution)/shard_map/all_to_all | solution.py:268
  88.9 0.0 copy-done.1
  88.9 0.6 dynamic_slice.3.gain_ref
  89.5 0.0 copy-done
  89.5 19.3 %conv.1 = (bf16[2,16,2,4,16,256]{5,4,3,2,1,0:T(8,128)(2,1)}, f32[4,2,256,256]{3,2,1,0:T(8,128)}, f32[4,2,256,512]{3,2,1,0:T(8,128)}, f32[4,2,256,256]{3,2,1,0:T(8,128)}) custom-call(f32[4]{0:T(128)} %dynamic_slice.3.gain_ref, bf16[2,16,3,4,16,256]{5,4,3,2,1,0:T(8,128)(2,1)} %bitcast.8, bf16[2,16,3,4,16,256]{5,4,3,2,1,0:T(8,128)(2,1)} %bitcast.9, ...), custom_call_target="tpu_custom_call" | custom-call | flops 12884901888 | bytes 20971520 | tf_op jit(solution)/shard_map/conv/pallas_call | solution.py:131
  108.8 7.3 %all-to-all-done.1 = bf16[32,1,4,16,256]{4,3,2,1,0:T(8,128)(2,1)} async-done(((bf16[32,1,4,16,256]{4,3,2,1,0:T(8,128)(2,1)}), bf16[32,1,4,16,256]{4,3,2,1,0:T(8,128)(2,1)}, u32[]{:S(2)}, u32[]{:S(2)}) %all-to-all-start.1) | async-done | bytes 1048608 | tf_op jit(solution)/shard_map/all_to_all | solution.py:268
  116.1 7.3 %grad.1 = bf16[2,16,2,4,16,256]{5,4,3,2,1,0:T(8,128)(2,1)} custom-call(bf16[2,16,3,4,16,256]{5,4,3,2,1,0:T(8,128)(2,1)} %bitcast.10, bf16[2,16,4,16,256]{4,3,2,1,0:T(8,128)(2,1)} %bitcast.5.cot_ref, f32[4,2,256,256]{3,2,1,0:T(8,128)} %get-tuple-element.8.gap_ref, f32[4,2,256,512]{3,2,1,0:T(8,128)} %get-tuple-element.9.spec_ref, ...), custom_call_target="tpu_custom_call", output_to_operand_aliasing={{}: (8, {})} | custom-call | flops 1610612736 | bytes 12582912 | tf_op jit(solution)/shard_map/grad/pallas_call | solution.py:161
  123.4 53.1 %all_to_all.15.last_ref = bf16[32,2,4,16,256]{4,3,2,1,0:T(8,128)(2,1)} all-to-all(bf16[32,2,4,16,256]{4,3,2,1,0:T(8,128)(2,1)} %bitcast.11), channel_id=1, replica_groups=mesh['dp'=2,'ctx'=16] {'dp','ctx'}, dimensions={0} | all-to-all | bytes 4194304 | tf_op jit(solution)/shard_map/all_to_all | solution.py:272
  176.5 3.9 %homeward.1 = (bf16[16,256,128]{2,1,0:T(8,128)(2,1)}, f32[2,16,128,128]{3,2,1,0:T(8,128)}) custom-call(bf16[32,2,4,16,256]{4,3,2,1,0:T(8,128)(2,1)} %all_to_all.15.last_ref), custom_call_target="tpu_custom_call" | custom-call | bytes 5242880 | tf_op jit(solution)/shard_map/homeward/pallas_call | solution.py:233
Async XLA Ops:
  5.6 79.8 %all-to-all-start = ((bf16[32,3,4,16,256]{4,3,2,1,0:T(8,128)(2,1)}), bf16[32,3,4,16,256]{4,3,2,1,0:T(8,128)(2,1)S(1)}, u32[]{:S(2)}, u32[]{:S(2)}) async-start(bf16[32,3,4,16,256]{4,3,2,1,0:T(8,128)(2,1)} %outward.2), calls=%async_computation | async-start | bytes 6291456 | tf_op jit(solution)/shard_map/all_to_all | solution.py:266
  12.9 76.0 %copy-start.1 = (f32[128]{0:T(128)S(1)}, f32[128]{0:T(128)}, u32[]{:S(2)}) copy-start(f32[128]{0:T(128)} %param.14) | copy-start | bytes 1540
  85.5 4.1 %copy-start = (bf16[32,3,4,16,256]{4,3,2,1,0:T(8,128)(2,1)}, bf16[32,3,4,16,256]{4,3,2,1,0:T(8,128)(2,1)S(1)}, u32[]{:S(2)}) copy-start(bf16[32,3,4,16,256]{4,3,2,1,0:T(8,128)(2,1)S(1)} %all-to-all-done) | copy-start | bytes 9437188
  85.5 30.6 %all-to-all-start.1 = ((bf16[32,1,4,16,256]{4,3,2,1,0:T(8,128)(2,1)}), bf16[32,1,4,16,256]{4,3,2,1,0:T(8,128)(2,1)}, u32[]{:S(2)}, u32[]{:S(2)}) async-start(bf16[32,1,4,16,256]{4,3,2,1,0:T(8,128)(2,1)} %outward.3), calls=%async_computation.1 | async-start | bytes 2097152 | tf_op jit(solution)/shard_map/all_to_all | solution.py:268

commit v3 on v0

--- a/solution.py
+++ b/solution.py
@@ -1,14 +1,333 @@
+import functools
+
 import jax
 import jax.numpy as jnp
+import numpy as np
 from jax import lax
+from jax.experimental import pallas as pl
+from jax.experimental.pallas import tpu as pltpu
 from jax.sharding import PartitionSpec as P
 
 N1 = 256
 N2 = 256
-
+BF16 = jnp.bfloat16
+F32 = jnp.float32
+HALF = 144
+VMEM = 26 << 20
 
 two_pi = 6.283185307179586
 smart_weight = 2.0
+
+
+def tables():
+    ids = np.arange(N1)
+    phase = (ids[:, None] * ids[None, :] % N1) * (two_pi / N1)
+    cos_table, sin_table = np.cos(phase), np.sin(phase)
+    split_rows = np.concatenate([cos_table[:HALF], -sin_table[:HALF]], 0)
+    forward_table = np.block([[cos_table, -sin_table], [sin_table, cos_table]])
+    weight = np.where(ids[: N1 // 2] == 0, 1.0, 2.0) / (N1 * N2)
+    join_rows = np.concatenate([cos_table[:, : N1 // 2] * weight, -sin_table[:, : N1 // 2] * weight], 1)
+    mirror_rows = np.zeros((HALF, N1))
+    mirror_rows[ids[:HALF], -ids[:HALF] % N1] = 1
+    mirror_cols = np.eye(N2)[::-1]
+    lower_rows = np.zeros((N1 // 2, HALF))
+    lower_rows[ids[: N1 // 2], N1 // 2 - ids[: N1 // 2]] = 1
+    angle = (ids[:HALF, None] * ids[None, :]) * (two_pi / (N1 * N2))
+    twiddle = np.stack([np.cos(angle), np.sin(angle)], 0)
+    small = (split_rows, forward_table, join_rows, mirror_rows, mirror_cols, lower_rows)
+    small = [jnp.asarray(t.astype(jnp.bfloat16)) for t in small]
+    return (*small, jnp.asarray(twiddle.astype(np.float32)))
+
+
+def dot(a, b):
+    return jnp.dot(a, b, preferred_element_type=F32)
+
+
+def near_device(place_ref, j, hop, plane, hops):
+    far = (place_ref[0] ^ (j // plane)) * hops + (place_ref[1] ^ hop)
+    return far * plane + (place_ref[2] ^ (j % plane))
+
+
+def forward(signals, split_ref, fwd_ref, tw_cos, tw_sin):
+    halves = []
+    for x in signals:
+        part = dot(split_ref[...], x)
+        part_real, part_imag = part[:HALF], part[HALF:]
+        out_real = part_real * tw_cos + part_imag * tw_sin
+        out_imag = part_imag * tw_cos - part_real * tw_sin
+        halves.append(jnp.concatenate([out_real.astype(BF16), out_imag.astype(BF16)], 1))
+    spectra = dot(jnp.concatenate(halves, 0), fwd_ref[...])
+    return [spectra[i * HALF : (i + 1) * HALF] for i in range(len(signals))]
+
+
+def hermitian_part(filter_real, filter_imag, mirror_rows, mirror_cols):
+    rows = dot(mirror_rows, jnp.concatenate([filter_real, filter_imag], 1)).astype(BF16)
+    flipped = dot(jnp.concatenate([rows[:, :N2], rows[:, N2:]], 0), mirror_cols)
+    out = []
+    for part, other, sign in ((filter_real, flipped[:HALF], 0.5), (filter_imag, flipped[HALF:], -0.5)):
+        top = other[:8]
+        row = lax.broadcasted_iota(jnp.int32, top.shape, 0)
+        top = jnp.where(row == 0, pltpu.roll(top, 1, 1), top)
+        other = jnp.concatenate([top, other[8:]], 0)
+        out.append(0.5 * part[:HALF].astype(F32) + sign * other)
+    return out
+
+
+def channel_kernel(place_ref, gain_ref, recv_ref, *refs, hops):
+    cot_refs, refs = refs[:hops], refs[hops:]
+    split_ref, fwd_ref, join_ref, mirror_ref, cols_ref, lower_ref, tw_ref, send_ref, cot_rows = refs
+    count, ctx = recv_ref.shape[:2]
+    plane = ctx // hops
+    q = pl.program_id(0)
+    for hop, cot_ref in enumerate(cot_refs):
+        for j in range(count * plane):
+            cot_rows[near_device(place_ref, j, hop, plane, hops)] = cot_ref[j, q]
+    tw_cos, tw_sin = tw_ref[0], tw_ref[1]
+    signals = []
+    for d in range(count):
+        clean = recv_ref[d, :, 0, q].reshape(N1, N2)
+        perturb = recv_ref[d, :, 1, q].reshape(N1, N2)
+        signals += [clean, (clean.astype(F32) + perturb.astype(F32)).astype(BF16)]
+    spectra = forward(signals, split_ref, fwd_ref, tw_cos, tw_sin)
+    filter_real, filter_imag = hermitian_part(
+        recv_ref[0, :, 2, q].reshape(N1, N2), recv_ref[1, :, 2, q].reshape(N1, N2), mirror_ref[...], cols_ref[...]
+    )
+    products = []
+    for spec in spectra:
+        real, imag = spec[:, :N2], spec[:, N2:]
+        prod_real = (filter_real * real - filter_imag * imag).astype(BF16)
+        minus_imag = (-filter_real * imag - filter_imag * real).astype(BF16)
+        products.append(jnp.concatenate([prod_real, minus_imag], 1))
+    back = dot(jnp.concatenate(products, 0), fwd_ref[...])
+    mixed, middle = [], []
+    for i in range(2 * count):
+        back_real, minus_imag = back[i * HALF : (i + 1) * HALF, :N2], back[i * HALF : (i + 1) * HALF, N2:]
+        mixed_real = (back_real * tw_cos + minus_imag * tw_sin).astype(BF16)
+        mixed_imag = (back_real * tw_sin - minus_imag * tw_cos).astype(BF16)
+        mixed.append(jnp.concatenate([mixed_real[: N1 // 2], mixed_imag[: N1 // 2]], 0))
+        middle.append(mixed_real[N1 // 2 :].astype(F32)[:1])
+    conv = dot(join_ref[...], jnp.concatenate(mixed, 1))
+    parity = lax.broadcasted_iota(jnp.int32, (N1, N2), 0) % 2
+    alternate = (1 - 2 * parity).astype(F32) * (1.0 / (N1 * N2))
+    gain = gain_ref[q]
+    errors = []
+    for d in range(count):
+        pair = []
+        for i in range(2):
+            k = 2 * d + i
+            wide = signals[k].astype(F32)
+            filtered = conv[:, k * N2 : (k + 1) * N2] + alternate * middle[k]
+            pair.append((wide, wide * filtered.astype(BF16).astype(F32) + gain * wide))
+        (clean, clean_y), (shifted, shifted_y) = pair
+        send_ref[d, :, 0, q] = clean_y.astype(BF16).reshape(ctx, -1, N2)
+        gap = smart_weight * (shifted_y - clean_y)
+        cot = cot_rows[d * ctx : (d + 1) * ctx].reshape(N1, N2).astype(F32)
+        errors += [(clean * (cot - gap)).astype(BF16), (shifted * gap).astype(BF16)]
+    total_real = total_imag = 0.0
+    for err_spec, spec in zip(forward(errors, split_ref, fwd_ref, tw_cos, tw_sin), spectra):
+        err_real, err_imag = err_spec[:, :N2], err_spec[:, N2:]
+        real, imag = spec[:, :N2], spec[:, N2:]
+        total_real += err_real * real + err_imag * imag
+        total_imag += err_imag * real - err_real * imag
+    scale = 1.0 / (N1 * N2)
+    upper = jnp.concatenate([(total_real * scale).astype(BF16), (total_imag * scale).astype(BF16)], 1)
+    lower = dot(lower_ref[...], upper).astype(BF16)
+    lower = dot(jnp.concatenate([lower[:, :N2], lower[:, N2:]], 0), cols_ref[...])
+    lower_real, lower_imag = lower[: N1 // 2].astype(BF16), (-lower[N1 // 2 :]).astype(BF16)
+    width = N2 // count
+    for i in range(count):
+        first = upper[: N1 // 2, i * width : (i + 1) * width]
+        second = upper[: N1 // 2, N2 + i * width : N2 + (i + 1) * width]
+        upper_pair = jnp.concatenate([first, second], 1)
+        cols = slice(i * width, (i + 1) * width)
+        lower_pair = jnp.concatenate([lower_real[:, cols], lower_imag[:, cols]], 1)
+        send_ref[i, : ctx // 2, 1, q] = upper_pair.reshape(ctx // 2, -1, 2 * width)
+        send_ref[i, ctx // 2 :, 1, q] = lower_pair.reshape(ctx // 2, -1, 2 * width)
+
+
+def whole(x):
+    return pl.BlockSpec(x.shape, lambda *_: (0,) * x.ndim)
+
+
+def near(x):
+    return pltpu.with_memory_space_constraint(x, pltpu.VMEM)
+
+
+def far(x):
+    return pltpu.with_memory_space_constraint(x, pltpu.HBM)
+
+
+def channel_call(place, gain, received, cots, tabs):
+    dp, ctx, _, per, rows, _ = received.shape
+    here = pl.BlockSpec(memory_space=pltpu.VMEM)
+    return pl.pallas_call(
+        functools.partial(channel_kernel, hops=len(cots)),
+        grid=(per,),
+        in_specs=[
+            pl.BlockSpec(memory_space=pltpu.SMEM),
+            pl.BlockSpec(memory_space=pltpu.SMEM),
+            here,
+            *[whole(x) for x in cots],
+            *[whole(t) for t in tabs],
+        ],
+        out_specs=here,
+        out_shape=pltpu.VMEM((dp, ctx, 2, per, rows, N2), BF16),
+        scratch_shapes=[pltpu.VMEM((dp * ctx, rows, N2), BF16)],
+        compiler_params=pltpu.CompilerParams(vmem_limit_bytes=VMEM),
+        cost_estimate=pl.CostEstimate(flops=per * dp * 6 * 12 * N1**3, bytes_accessed=8 << 20, transcendentals=0),
+        name="channels",
+    )(place, gain, near(received), *[far(x) for x in cots], *[far(t) for t in tabs])
+
+
+def outward_kernel(index_ref, *refs):
+    *in_refs, out_ref, rows_ref = refs
+    count, _, per, rows, width = out_ref.shape
+    channels = count * per
+    for t, in_ref in enumerate(in_refs):
+        for r in range(rows):
+            block = in_ref[0, r].astype(F32).T
+            rows_ref[pl.ds(r, channels, stride=rows), :] = block
+        out_ref[:, t] = rows_ref[...].astype(BF16).reshape(count, per, rows, width)
+
+
+def outward(index, arrays, count):
+    _, rows, _, channels = arrays[0].shape
+    per = channels // count
+    width = 128
+    picks = [(lambda h, s: (s[0], 0, h, 0)) if a.shape[0] > 1 else (lambda h, s: (0, 0, h, 0)) for a in arrays]
+    return pl.pallas_call(
+        outward_kernel,
+        grid_spec=pltpu.PrefetchScalarGridSpec(
+            num_scalar_prefetch=1,
+            grid=(N2 // width,),
+            in_specs=[pl.BlockSpec((1, rows, width, channels), pick) for pick in picks],
+            out_specs=pl.BlockSpec((count, len(arrays), per, rows, width), lambda h, s: (0, 0, 0, 0, h)),
+            scratch_shapes=[pltpu.VMEM((channels * rows, width), F32)],
+        ),
+        out_shape=jax.ShapeDtypeStruct((count, len(arrays), per, rows, N2), BF16),
+        compiler_params=pltpu.CompilerParams(vmem_limit_bytes=VMEM),
+        cost_estimate=pl.CostEstimate(flops=0, bytes_accessed=(4 * len(arrays)) << 20, transcendentals=0),
+        name="outward",
+    )(index, *arrays)
+
+
+def outward_near_kernel(place_ref, in_ref, *refs, hops, plane):
+    *out_refs, rows_ref = refs
+    _, per, rows, width = out_refs[0].shape
+    channels = in_ref.shape[3]
+    for r in range(rows):
+        rows_ref[pl.ds(r, channels, stride=rows), :] = in_ref[0, r].astype(F32).T
+    for j, out_ref in enumerate(out_refs):
+        for hop in range(hops):
+            block = near_device(place_ref, j, hop, plane, hops) * (per * rows)
+            rows_here = rows_ref[pl.ds(pl.multiple_of(block, per * rows), per * rows), :]
+            out_ref[hop] = rows_here.astype(BF16).reshape(per, rows, width)
+
+
+def outward_near(place, x, count, hops, plane):
+    _, rows, _, channels = x.shape
+    per = channels // count
+    width = 128
+    return pl.pallas_call(
+        functools.partial(outward_near_kernel, hops=hops, plane=plane),
+        grid=(N2 // width,),
+        in_specs=[
+            pl.BlockSpec(memory_space=pltpu.SMEM),
+            pl.BlockSpec((1, rows, width, channels), lambda h: (0, 0, h, 0)),
+        ],
+        out_specs=[pl.BlockSpec((hops, per, rows, width), lambda h: (0, 0, 0, h))] * (count // hops),
+        out_shape=[jax.ShapeDtypeStruct((hops, per, rows, N2), BF16)] * (count // hops),
+        scratch_shapes=[pltpu.VMEM((channels * rows, width), F32)],
+        compiler_params=pltpu.CompilerParams(vmem_limit_bytes=VMEM),
+        cost_estimate=pl.CostEstimate(flops=0, bytes_accessed=2 << 20, transcendentals=0),
+        name="outward_near",
+    )(place, x)
+
+
+def regroup_kernel(*refs, count):
+    for i, in_ref in enumerate(refs[:count]):
+        for j, out_ref in enumerate(refs[count:]):
+            out_ref[i] = in_ref[j]
+
+
+def regroup(arrays):
+    hops, *block = arrays[0].shape
+    return pl.pallas_call(
+        functools.partial(regroup_kernel, count=len(arrays)),
+        out_shape=[jax.ShapeDtypeStruct((len(arrays), *block), BF16)] * hops,
+        compiler_params=pltpu.CompilerParams(vmem_limit_bytes=VMEM),
+        cost_estimate=pl.CostEstimate(flops=0, bytes_accessed=2 << 20, transcendentals=0),
+        name="regroup",
+    )(*arrays)
+
+
+def homeward_kernel(last_ref, y_ref, grad_ref, rows_ref):
+    count, _, per, rows, _ = last_ref.shape
+    channels = count * per
+    width = rows_ref.shape[1]
+    lanes = pl.ds(pl.multiple_of(pl.program_id(0) * width, width), width)
+    for t in range(2):
+        rows_ref[...] = last_ref[:, t, :, :, lanes].astype(F32).reshape(channels * rows, width)
+        for r in range(rows):
+            block = rows_ref[pl.ds(r, channels, stride=rows), :].T
+            if t == 0:
+                y_ref[r] = block.astype(BF16)
+            else:
+                grad_ref[0, r] = block
+
+
+def homeward(last):
+    count, _, per, rows, _ = last.shape
+    channels = count * per
+    width = 128
+    return pl.pallas_call(
+        homeward_kernel,
+        grid=(N2 // width,),
+        in_specs=[pl.BlockSpec(memory_space=pltpu.VMEM)],
+        out_specs=[
+            pl.BlockSpec((rows, width, channels), lambda h: (0, h, 0)),
+            pl.BlockSpec((1, rows, width, channels), lambda h: (h, 0, 0, 0)),
+        ],
+        out_shape=[
+            jax.ShapeDtypeStruct((rows, N2, channels), BF16),
+            jax.ShapeDtypeStruct((2, rows, width, channels), F32),
+        ],
+        scratch_shapes=[pltpu.VMEM((channels * rows, width), F32)],
+        compiler_params=pltpu.CompilerParams(vmem_limit_bytes=VMEM),
+        cost_estimate=pl.CostEstimate(flops=0, bytes_accessed=5 << 20, transcendentals=0),
+        name="homeward",
+    )(near(last))
+
+
+def by_channel_body(embeds, perturb, cotangent, filter_spectrum, skip_gain):
+    dp, ctx = lax.axis_size("dp"), lax.axis_size("ctx")
+    d, c = lax.axis_index("dp"), lax.axis_index("ctx")
+    axes = ("dp", "ctx")
+    count = dp * ctx
+    channels = embeds.shape[2]
+    rows = N1 // ctx
+    per = channels // count
+    plane = 4
+    hops = ctx // plane
+    tabs = tables()
+    place = jnp.stack([d, c // plane, c % plane])
+
+    def matrix(x):
+        return far(x.reshape(1, rows, N2, channels))
+
+    def exchange(x, mask):
+        return lax.ppermute(x, axes, [(i, i ^ mask) for i in range(count)]) if mask else x
+
+    first = outward(place, [matrix(embeds), matrix(perturb), far(filter_spectrum)], count)
+    received = lax.all_to_all(first, axes, 0, 0, tiled=True).reshape(dp, ctx, 3, per, rows, N2)
+    cots = outward_near(place, matrix(cotangent), count, hops, plane)
+    cots = regroup([exchange(x, j // plane * ctx + j % plane) for j, x in enumerate(cots)])
+    cots = [exchange(x, hop * plane) for hop, x in enumerate(cots)]
+    gain = lax.dynamic_slice(skip_gain, ((d * ctx + c) * per,), (per,))
+    send = channel_call(place, gain, received, cots, tabs)
+    last = lax.all_to_all(send.reshape(count, 2, per, rows, N2), axes, 0, 0, tiled=True)
+    y, grad = homeward(last)
+    return y.reshape(1, rows * N2, channels), grad
 
 
 def trig_table(period):
@@ -141,16 +460,22 @@
 
 
 def solution(mesh):
-    return jax.shard_map(
-        body,
-        mesh=mesh,
-        in_specs=(
-            P("dp", "ctx", None),
-            P("dp", "ctx", None),
-            P("dp", "ctx", None),
-            P(None, "ctx", None, None),
-            P(),
-        ),
-        out_specs=(P("dp", "ctx", None), P(None, "ctx", "dp", None)),
-        check_vma=False,
-    )
+    dp, ctx = mesh.shape["dp"], mesh.shape["ctx"]
+
+    def run(embeds, *rest):
+        apart = dp == 2 and embeds.shape[2] % (dp * ctx) == 0 and N1 // ctx == 16 and embeds.shape[2] // (dp * ctx) > 1
+        return jax.shard_map(
+            by_channel_body if apart else body,
+            mesh=mesh,
+            in_specs=(
+                P("dp", "ctx", None),
+                P("dp", "ctx", None),
+                P("dp", "ctx", None),
+                P(None, "ctx", None, None),
+                P(),
+            ),
+            out_specs=(P("dp", "ctx", None), P(None, "ctx", "dp", None)),
+            check_vma=False,
+        )(embeds, *rest)
+
+    return run

time: 635 us -> 176 us (0.28); the launches traced: 628 us -> 176 us
  blocking collectives: 314 us -> 57.2 us
  waiting for transfers between devices: 144 us -> 71.7 us
  local copies, waits for them, and re-layouts: 64.6 us -> 0.78 us
  other arithmetic: 39.1 us -> 0.08 us
  matrix products: 32.5 us -> 0 us
  Pallas kernels: 0 us -> 24.5 us
  between operations: 14.6 us -> 0.69 us
    all_to_all x4 -> x1, blocking collectives: 314 us -> 57.2 us  [by_channel_body(): lax.all_to_all(send.reshape(count, 2, per, rows, N2), axes, 0, 0, tiled=T...]
    all_to_all x2 -> x1, waiting for transfers between devices: 114 us -> 0.01 us  [by_channel_body(): lax.all_to_all(first, axes, 0, 0, tiled=True)]
    ppermute x0 -> x10, waiting for transfers between devices: none -> 71.7 us  [exchange(): lax.ppermute(x, axes, [(i, i ^ mask) for i in range(count)])]
    dot_general x12 -> x0, matrix products: 32.5 us -> none  [the longest x2 10.8 us: second_section(): jnp.einsum('sprnc,kn->sprkc', section_rows, cos_table, preferred_element_...]
    reduce_scatter x1 -> x0, waiting for transfers between devices: 29.8 us -> none  [body(): lax.psum_scatter(local_grad.astype(jnp.bfloat16), 'dp', scatter_dimension...]
    pallas_call x0 -> x5, Pallas kernels: none -> 24.5 us  [the longest x1 13.2 us: channel_call(): pl.pallas_call(functools.partial(channel_kernel, hops=len(cots)), grid=(p...]
    another operation x5 -> x0, local copies, waits for them, and re-layouts: 22.6 us -> none  [the longest x2 15.9 us: first_section(): return jnp.stack([out_real, out_imag], 1).astype(jnp.bfloat16)]
    all_to_all x8 -> x0, local copies, waits for them, and re-layouts: 20.3 us -> none  [the longest x2 5.12 us: body(): lax.all_to_all(inputs, 'ctx', split_axis=2, concat_axis=1, tiled=True)]
  transfers between devices with their start and end apart: 3 -> 11, of which waited for: 3 -> 6; matrix products, arithmetic and copies ran while one was open for 1% -> 0% of each run, Pallas kernels for 0% -> 2%
where the time goes in v3:
time: 176 us
  waiting for transfers between devices  71.7 us (41%)
  blocking collectives  57.2 us (32%)
  Pallas kernels  24.5 us (14%)
  starting transfers between devices  20.8 us (12%)
    ppermute x10, waiting for transfers between devices, exchange(): lax.ppermute(x, axes, [(i, i ^ mask) for i in range(count)])  71.7 us
    all_to_all x1, blocking collectives, by_channel_body(): lax.all_to_all(send.reshape(count, 2, per, rows, N2), axes, 0, 0, tiled=T...  57.2 us
    ppermute x10, starting transfers between devices, exchange(): lax.ppermute(x, axes, [(i, i ^ mask) for i in range(count)])  13.5 us
    pallas_call x1, Pallas kernels, channel_call(): pl.pallas_call(functools.partial(channel_kernel, hops=len(cots)), grid=(p...  13.2 us
    all_to_all x1, starting transfers between devices, by_channel_body(): lax.all_to_all(first, axes, 0, 0, tiled=True)  7.3 us
    pallas_call x1, Pallas kernels, outward(): pl.pallas_call(outward_kernel, grid_spec=pltpu.PrefetchScalarGridSpec(num...  5.57 us
  transfers between devices with their start and end apart: 11, of which 6 were waited for; matrix products, arithmetic and copies ran while one was open for 0% of the time, Pallas kernels for 2%

profile of v3, /device:TPU:0, one launch (start us, length us, event | category | flops | bytes accessed | tf_op | source)
XLA Modules:
  0.0 175.8 jit_solution(10790233346537409833)
XLA Ops:
  0.7 0.1 pad_add_fusion.index_ref.place_ref
  0.7 5.6 %outward.1 = bf16[32,3,4,16,256]{4,3,2,1,0:T(8,128)(2,1)} custom-call(s32[3]{0:T(128)S(1)} %pad_add_fusion.index_ref.place_ref, bf16[1,16,256,128]{3,2,1,0:T(8,128)(2,1)} %bitcast.11, bf16[1,16,256,128]{3,2,1,0:T(8,128)(2,1)} %bitcast.12, f32[2,16,256,128]{3,2,1,0:T(8,128)} %refs_2_.1), custom_call_target="tpu_custom_call" | custom-call | bytes 12582912 | tf_op jit(solution)/shard_map/outward/pallas_call | solution.py:198
  6.3 7.3 %all-to-all-start = ((bf16[32,3,4,16,256]{4,3,2,1,0:T(8,128)(2,1)}), bf16[32,3,4,16,256]{4,3,2,1,0:T(8,128)(2,1)S(1)}, u32[]{:S(2)}, u32[]{:S(2)}) async-start(bf16[32,3,4,16,256]{4,3,2,1,0:T(8,128)(2,1)} %outward.1), calls=%async_computation | async-start | bytes 6291456 | tf_op jit(solution)/shard_map/all_to_all | solution.py:322
  13.6 2.1 %outward_near.1 = (bf16[4,4,16,256]{3,2,1,0:T(8,128)(2,1)S(1)}, bf16[4,4,16,256]{3,2,1,0:T(8,128)(2,1)S(1)}, bf16[4,4,16,256]{3,2,1,0:T(8,128)(2,1)S(1)}, bf16[4...) custom-call(s32[3]{0:T(128)S(1)} %pad_add_fusion.index_ref.place_ref, ...), custom_call_target="tpu_custom_call" | custom-call | bytes 2097152 | tf_op jit(solution)/shard_map/outward_near/pallas_call | solution.py:231
  15.7 0.3 collective-permute-start
  16.1 1.7 collective-permute-start.1
  17.7 1.7 collective-permute-start.3
  19.4 0.1 collective-permute-start.4
  19.5 2.6 %collective-permute-start.5 = (bf16[4,4,16,256]{3,2,1,0:T(8,128)(2,1)S(1)}, bf16[4,4,16,256]{3,2,1,0:T(8,128)(2,1)S(1)}, u32[]{:S(2)}, u32[]{:S(2)}) collective-permute-start(bf16[4,4,16,256]{3,2,1,0:T(8,128)(2,1)S(1)} %get-tuple-element.22), channel_id=1, source_target_pairs={{0,18},{1,19},{2,16},{3,17},{4,22},{5,23},{6,20},{7,21},{8,26},{9,... | collective-permute-start | bytes 393224 | tf_op jit(solution)/shard_map/ppermute | solution.py:319
  22.1 15.5 %collective-permute-done.1.refs_2_ = bf16[4,4,16,256]{3,2,1,0:T(8,128)(2,1)S(1)} collective-permute-done((bf16[4,4,16,256]{3,2,1,0:T(8,128)(2,1)S(1)}, bf16[4,4,16,256]{3,2,1,0:T(8,128)(2,1)S(1)}, u32[]{:S(2)}, u32[]{:S(2)}) %collective-permute-start.1) | collective-permute-done | bytes 131104 | tf_op jit(solution)/shard_map/ppermute | solution.py:319
  37.7 2.3 %collective-permute-start.6 = (bf16[4,4,16,256]{3,2,1,0:T(8,128)(2,1)S(1)}, bf16[4,4,16,256]{3,2,1,0:T(8,128)(2,1)S(1)}, u32[]{:S(2)}, u32[]{:S(2)}) collective-permute-start(bf16[4,4,16,256]{3,2,1,0:T(8,128)(2,1)S(1)} %get-tuple-element.23), channel_id=1, source_target_pairs={{0,19},{1,18},{2,17},{3,16},{4,23},{5,22},{6,21},{7,20},{8,27},{9,... | collective-permute-start | bytes 393224 | tf_op jit(solution)/shard_map/ppermute | solution.py:319
  40.0 2.8 %collective-permute-done.2.refs_3_ = bf16[4,4,16,256]{3,2,1,0:T(8,128)(2,1)S(1)} collective-permute-done((bf16[4,4,16,256]{3,2,1,0:T(8,128)(2,1)S(1)}, bf16[4,4,16,256]{3,2,1,0:T(8,128)(2,1)S(1)}, u32[]{:S(2)}, u32[]{:S(2)}) %collective-permute-start.2) | collective-permute-done | bytes 131104 | tf_op jit(solution)/shard_map/ppermute | solution.py:319
  42.8 0.0 collective-permute-done.3.refs_4_
  42.8 9.6 %collective-permute-done.5.refs_6_ = bf16[4,4,16,256]{3,2,1,0:T(8,128)(2,1)S(1)} collective-permute-done((bf16[4,4,16,256]{3,2,1,0:T(8,128)(2,1)S(1)}, bf16[4,4,16,256]{3,2,1,0:T(8,128)(2,1)S(1)}, u32[]{:S(2)}, u32[]{:S(2)}) %collective-permute-start.5) | collective-permute-done | bytes 131104 | tf_op jit(solution)/shard_map/ppermute | solution.py:319
  52.4 2.5 %collective-permute-done.6.refs_7_ = bf16[4,4,16,256]{3,2,1,0:T(8,128)(2,1)S(1)} collective-permute-done((bf16[4,4,16,256]{3,2,1,0:T(8,128)(2,1)S(1)}, bf16[4,4,16,256]{3,2,1,0:T(8,128)(2,1)S(1)}, u32[]{:S(2)}, u32[]{:S(2)}) %collective-permute-start.6) | collective-permute-done | bytes 131104 | tf_op jit(solution)/shard_map/ppermute | solution.py:319
  54.9 0.9 regroup.1
  55.8 0.7 copy-done
  56.5 4.8 %collective-permute-start.8 = (bf16[8,4,16,256]{3,2,1,0:T(8,128)(2,1)}, bf16[8,4,16,256]{3,2,1,0:T(8,128)(2,1)}, u32[]{:S(2)}, u32[]{:S(2)}) collective-permute-start(bf16[8,4,16,256]{3,2,1,0:T(8,128)(2,1)} %get-tuple-element.26), channel_id=1, source_target_pairs={{0,8},{1,9},{2,10},{3,11},{4,12},{5,13},{6,14},{7,15},{8,0},{9,1},... | collective-permute-start | bytes 786440 | tf_op jit(solution)/shard_map/ppermute | solution.py:319
  61.3 0.1 dynamic_slice.3.gain_ref
  61.3 10.7 %collective-permute-done.7.refs_1_ = bf16[8,4,16,256]{3,2,1,0:T(8,128)(2,1)} collective-permute-done((bf16[8,4,16,256]{3,2,1,0:T(8,128)(2,1)}, bf16[8,4,16,256]{3,2,1,0:T(8,128)(2,1)}, u32[]{:S(2)}, u32[]{:S(2)}) %collective-permute-start.7) | collective-permute-done | bytes 262176 | tf_op jit(solution)/shard_map/ppermute | solution.py:319
  72.0 30.6 %collective-permute-done.8.refs_2_ = bf16[8,4,16,256]{3,2,1,0:T(8,128)(2,1)} collective-permute-done((bf16[8,4,16,256]{3,2,1,0:T(8,128)(2,1)}, bf16[8,4,16,256]{3,2,1,0:T(8,128)(2,1)}, u32[]{:S(2)}, u32[]{:S(2)}) %collective-permute-start.8) | collective-permute-done | bytes 262176 | tf_op jit(solution)/shard_map/ppermute | solution.py:319
  102.6 13.2 %channels.1 = bf16[2,16,2,4,16,256]{5,4,3,2,1,0:T(8,128)(2,1)S(1)} custom-call(s32[3]{0:T(128)S(1)} %pad_add_fusion.index_ref.place_ref, f32[4]{0:T(128)S(1)} %dynamic_slice.3.gain_ref, bf16[2,16,3,4,16,256]{5,4,3,2,1,0:T(8,128)(2,1)S(1)} %bitcast.9, bf16[8,4,16,256]{3,2,1,0:T(8,128)(2,1)} %copy-done, ...), custom_call_target="tpu_custom_call" | custom-call | flops 9663676416 | bytes 8388608 | tf_op jit(solution)/shard_map/channels/pallas_call | solution.py:163
  115.8 57.2 %all_to_all.10.last_ref = bf16[32,2,4,16,256]{4,3,2,1,0:T(8,128)(2,1)S(1)} all-to-all(bf16[32,2,4,16,256]{4,3,2,1,0:T(8,128)(2,1)S(1)} %bitcast.10), channel_id=1, replica_groups=mesh['dp'=2,'ctx'=16] {'dp','ctx'}, dimensions={0} | all-to-all | bytes 4194304 | tf_op jit(solution)/shard_map/all_to_all | solution.py:328
  173.0 2.8 %homeward.1 = (bf16[16,256,128]{2,1,0:T(8,128)(2,1)}, f32[2,16,128,128]{3,2,1,0:T(8,128)}) custom-call(bf16[32,2,4,16,256]{4,3,2,1,0:T(8,128)(2,1)S(1)} %all_to_all.10.last_ref), custom_call_target="tpu_custom_call" | custom-call | bytes 5242880 | tf_op jit(solution)/shard_map/homeward/pallas_call | solution.py:283
  (10 shorter events, 0.0 us)
Async XLA Ops:
  6.3 55.0 %copy-start.1 = (f32[128]{0:T(128)S(1)}, f32[128]{0:T(128)}, u32[]{:S(2)}) copy-start(f32[128]{0:T(128)} %param.16) | copy-start | bytes 1540
  6.3 96.3 %all-to-all-start = ((bf16[32,3,4,16,256]{4,3,2,1,0:T(8,128)(2,1)}), bf16[32,3,4,16,256]{4,3,2,1,0:T(8,128)(2,1)S(1)}, u32[]{:S(2)}, u32[]{:S(2)}) async-start(bf16[32,3,4,16,256]{4,3,2,1,0:T(8,128)(2,1)} %outward.1), calls=%async_computation | async-start | bytes 6291456 | tf_op jit(solution)/shard_map/all_to_all | solution.py:322
  15.7 3.8 %collective-permute-start = (bf16[4,4,16,256]{3,2,1,0:T(8,128)(2,1)S(1)}, bf16[4,4,16,256]{3,2,1,0:T(8,128)(2,1)S(1)}, u32[]{:S(2)}, u32[]{:S(2)}) collective-permute-start(bf16[4,4,16,256]{3,2,1,0:T(8,128)(2,1)S(1)} %get-tuple-element.17), channel_id=1, source_target_pairs={{0,1},{1,0},{2,3},{3,2},{4,5},{5,4},{6,7},{7,6},{8,9},{9,8},{10,11... | collective-permute-start | bytes 393224 | tf_op jit(solution)/shard_map/ppermute | solution.py:319
  16.1 21.6 %collective-permute-start.1 = (bf16[4,4,16,256]{3,2,1,0:T(8,128)(2,1)S(1)}, bf16[4,4,16,256]{3,2,1,0:T(8,128)(2,1)S(1)}, u32[]{:S(2)}, u32[]{:S(2)}) collective-permute-start(bf16[4,4,16,256]{3,2,1,0:T(8,128)(2,1)S(1)} %get-tuple-element.18), channel_id=1, source_target_pairs={{0,2},{1,3},{2,0},{3,1},{4,6},{5,7},{6,4},{7,5},{8,10},{9,11},{10,... | collective-permute-start | bytes 393224 | tf_op jit(solution)/shard_map/ppermute | solution.py:319
  17.7 25.1 %collective-permute-start.2 = (bf16[4,4,16,256]{3,2,1,0:T(8,128)(2,1)S(1)}, bf16[4,4,16,256]{3,2,1,0:T(8,128)(2,1)S(1)}, u32[]{:S(2)}, u32[]{:S(2)}) collective-permute-start(bf16[4,4,16,256]{3,2,1,0:T(8,128)(2,1)S(1)} %get-tuple-element.19), channel_id=1, source_target_pairs={{0,3},{1,2},{2,1},{3,0},{4,7},{5,6},{6,5},{7,4},{8,11},{9,10},{10,... | collective-permute-start | bytes 393224 | tf_op jit(solution)/shard_map/ppermute | solution.py:319
  17.7 25.1 %collective-permute-start.3 = (bf16[4,4,16,256]{3,2,1,0:T(8,128)(2,1)S(1)}, bf16[4,4,16,256]{3,2,1,0:T(8,128)(2,1)S(1)}, u32[]{:S(2)}, u32[]{:S(2)}) collective-permute-start(bf16[4,4,16,256]{3,2,1,0:T(8,128)(2,1)S(1)} %get-tuple-element.20), channel_id=1, source_target_pairs={{0,16},{1,17},{2,18},{3,19},{4,20},{5,21},{6,22},{7,23},{8,24},{9,... | collective-permute-start | bytes 393224 | tf_op jit(solution)/shard_map/ppermute | solution.py:319
  19.4 23.4 %collective-permute-start.4 = (bf16[4,4,16,256]{3,2,1,0:T(8,128)(2,1)S(1)}, bf16[4,4,16,256]{3,2,1,0:T(8,128)(2,1)S(1)}, u32[]{:S(2)}, u32[]{:S(2)}) collective-permute-start(bf16[4,4,16,256]{3,2,1,0:T(8,128)(2,1)S(1)} %get-tuple-element.21), channel_id=1, source_target_pairs={{0,17},{1,16},{2,19},{3,18},{4,21},{5,20},{6,23},{7,22},{8,25},{9,... | collective-permute-start | bytes 393224 | tf_op jit(solution)/shard_map/ppermute | solution.py:319
  19.5 32.9 %collective-permute-start.5 = (bf16[4,4,16,256]{3,2,1,0:T(8,128)(2,1)S(1)}, bf16[4,4,16,256]{3,2,1,0:T(8,128)(2,1)S(1)}, u32[]{:S(2)}, u32[]{:S(2)}) collective-permute-start(bf16[4,4,16,256]{3,2,1,0:T(8,128)(2,1)S(1)} %get-tuple-element.22), channel_id=1, source_target_pairs={{0,18},{1,19},{2,16},{3,17},{4,22},{5,23},{6,20},{7,21},{8,26},{9,... | collective-permute-start | bytes 393224 | tf_op jit(solution)/shard_map/ppermute | solution.py:319
  37.7 17.3 %collective-permute-start.6 = (bf16[4,4,16,256]{3,2,1,0:T(8,128)(2,1)S(1)}, bf16[4,4,16,256]{3,2,1,0:T(8,128)(2,1)S(1)}, u32[]{:S(2)}, u32[]{:S(2)}) collective-permute-start(bf16[4,4,16,256]{3,2,1,0:T(8,128)(2,1)S(1)} %get-tuple-element.23), channel_id=1, source_target_pairs={{0,19},{1,18},{2,17},{3,16},{4,23},{5,22},{6,21},{7,20},{8,27},{9,... | collective-permute-start | bytes 393224 | tf_op jit(solution)/shard_map/ppermute | solution.py:319
  55.8 0.7 copy-start
  56.5 15.5 %collective-permute-start.7 = (bf16[8,4,16,256]{3,2,1,0:T(8,128)(2,1)}, bf16[8,4,16,256]{3,2,1,0:T(8,128)(2,1)}, u32[]{:S(2)}, u32[]{:S(2)}) collective-permute-start(bf16[8,4,16,256]{3,2,1,0:T(8,128)(2,1)} %get-tuple-element.25), channel_id=1, source_target_pairs={{0,4},{1,5},{2,6},{3,7},{4,0},{5,1},{6,2},{7,3},{8,12},{9,13},{10,... | collective-permute-start | bytes 786440 | tf_op jit(solution)/shard_map/ppermute | solution.py:319
  56.5 46.1 %collective-permute-start.8 = (bf16[8,4,16,256]{3,2,1,0:T(8,128)(2,1)}, bf16[8,4,16,256]{3,2,1,0:T(8,128)(2,1)}, u32[]{:S(2)}, u32[]{:S(2)}) collective-permute-start(bf16[8,4,16,256]{3,2,1,0:T(8,128)(2,1)} %get-tuple-element.26), channel_id=1, source_target_pairs={{0,8},{1,9},{2,10},{3,11},{4,12},{5,13},{6,14},{7,15},{8,0},{9,1},... | collective-permute-start | bytes 786440 | tf_op jit(solution)/shard_map/ppermute | solution.py:319
  61.3 41.3 %collective-permute-start.9 = (bf16[8,4,16,256]{3,2,1,0:T(8,128)(2,1)S(1)}, bf16[8,4,16,256]{3,2,1,0:T(8,128)(2,1)}, u32[]{:S(2)}, u32[]{:S(2)}) collective-permute-start(bf16[8,4,16,256]{3,2,1,0:T(8,128)(2,1)S(1)} %get-tuple-element.27), channel_id=1, source_target_pairs={{0,12},{1,13},{2,14},{3,15},{4,8},{5,9},{6,10},{7,11},{8,4},{9,5},... | collective-permute-start | bytes 786440 | tf_op jit(solution)/shard_map/ppermute | solution.py:319

commit v4 on v3

--- a/solution.py
+++ b/solution.py
@@ -12,6 +12,7 @@
 N2 = 256
 BF16 = jnp.bfloat16
 F32 = jnp.float32
+KEPT = jnp.float32
 HALF = 144
 VMEM = 26 << 20
 
@@ -73,15 +74,22 @@
     return out
 
 
-def channel_kernel(place_ref, gain_ref, recv_ref, *refs, hops):
-    cot_refs, refs = refs[:hops], refs[hops:]
-    split_ref, fwd_ref, join_ref, mirror_ref, cols_ref, lower_ref, tw_ref, send_ref, cot_rows = refs
+def gradient(err_spectra, spectra):
+    total_real = total_imag = 0.0
+    for err_spec, spec in zip(err_spectra, spectra):
+        err_real, err_imag = err_spec[:, :N2], err_spec[:, N2:]
+        real, imag = spec[:, :N2], spec[:, N2:]
+        total_real += err_real * real + err_imag * imag
+        total_imag += err_imag * real - err_real * imag
+    return total_real, total_imag
+
+
+def conv_kernel(
+    gain_ref, recv_ref, split_ref, fwd_ref, join_ref, mirror_ref, cols_ref, tw_ref,
+    send_ref, gap_ref, spec_ref, part_ref,
+):
     count, ctx = recv_ref.shape[:2]
-    plane = ctx // hops
     q = pl.program_id(0)
-    for hop, cot_ref in enumerate(cot_refs):
-        for j in range(count * plane):
-            cot_rows[near_device(place_ref, j, hop, plane, hops)] = cot_ref[j, q]
     tw_cos, tw_sin = tw_ref[0], tw_ref[1]
     signals = []
     for d in range(count):
@@ -121,14 +129,33 @@
         (clean, clean_y), (shifted, shifted_y) = pair
         send_ref[d, :, 0, q] = clean_y.astype(BF16).reshape(ctx, -1, N2)
         gap = smart_weight * (shifted_y - clean_y)
+        gap_ref[q, d] = gap.astype(gap_ref.dtype)
+        spec_ref[q, d] = spectra[2 * d].astype(spec_ref.dtype)
+        errors.append((shifted * gap).astype(BF16))
+    total_real, total_imag = gradient(forward(errors, split_ref, fwd_ref, tw_cos, tw_sin), spectra[1::2])
+    part_ref[q, 0] = total_real
+    part_ref[q, 1] = total_imag
+
+
+def grad_kernel(place_ref, recv_ref, gap_ref, spec_ref, part_ref, *refs, hops):
+    cot_refs, refs = refs[:hops], refs[hops:]
+    split_ref, fwd_ref, cols_ref, lower_ref, tw_ref, _, send_ref, cot_rows = refs
+    count, ctx = recv_ref.shape[:2]
+    near = cot_refs[0].shape[0]
+    plane = near // count
+    q = pl.program_id(0)
+    for hop, cot_ref in enumerate(cot_refs):
+        for j in range(near):
+            cot_rows[near_device(place_ref, j, hop, plane, hops)] = cot_ref[j, q]
+    errors = []
+    for d in range(count):
+        clean = recv_ref[d, :, 0, q].reshape(N1, N2).astype(F32)
         cot = cot_rows[d * ctx : (d + 1) * ctx].reshape(N1, N2).astype(F32)
-        errors += [(clean * (cot - gap)).astype(BF16), (shifted * gap).astype(BF16)]
-    total_real = total_imag = 0.0
-    for err_spec, spec in zip(forward(errors, split_ref, fwd_ref, tw_cos, tw_sin), spectra):
-        err_real, err_imag = err_spec[:, :N2], err_spec[:, N2:]
-        real, imag = spec[:, :N2], spec[:, N2:]
-        total_real += err_real * real + err_imag * imag
-        total_imag += err_imag * real - err_real * imag
+        errors.append((clean * (cot - gap_ref[q, d].astype(F32))).astype(BF16))
+    spectra = [spec_ref[q, d].astype(F32) for d in range(count)]
+    total_real, total_imag = gradient(forward(errors, split_ref, fwd_ref, tw_ref[0], tw_ref[1]), spectra)
+    total_real += part_ref[q, 0]
+    total_imag += part_ref[q, 1]
     scale = 1.0 / (N1 * N2)
     upper = jnp.concatenate([(total_real * scale).astype(BF16), (total_imag * scale).astype(BF16)], 1)
     lower = dot(lower_ref[...], upper).astype(BF16)
@@ -157,26 +184,55 @@
     return pltpu.with_memory_space_constraint(x, pltpu.HBM)
 
 
-def channel_call(place, gain, received, cots, tabs):
+def conv_call(gain, received, tabs):
     dp, ctx, _, per, rows, _ = received.shape
-    here = pl.BlockSpec(memory_space=pltpu.VMEM)
+    split_rows, forward_table, join_rows, mirror_rows, mirror_cols, _, twiddle = tabs
+    tabs = (split_rows, forward_table, join_rows, mirror_rows, mirror_cols, twiddle)
     return pl.pallas_call(
-        functools.partial(channel_kernel, hops=len(cots)),
+        conv_kernel,
         grid=(per,),
         in_specs=[
             pl.BlockSpec(memory_space=pltpu.SMEM),
+            pl.BlockSpec(memory_space=pltpu.VMEM),
+            *[whole(t) for t in tabs],
+        ],
+        out_specs=[pl.BlockSpec(memory_space=pltpu.VMEM)] * 4,
+        out_shape=[
+            pltpu.VMEM((dp, ctx, 2, per, rows, N2), BF16),
+            pltpu.VMEM((per, dp, N1, N2), KEPT),
+            pltpu.VMEM((per, dp, HALF, 2 * N2), KEPT),
+            pltpu.VMEM((per, 2, HALF, N2), F32),
+        ],
+        compiler_params=pltpu.CompilerParams(vmem_limit_bytes=VMEM),
+        cost_estimate=pl.CostEstimate(flops=per * dp * 5 * 6 * N1**3, bytes_accessed=8 << 20, transcendentals=0),
+        name="conv",
+    )(gain, received, *[far(t) for t in tabs])
+
+
+def grad_call(place, received, kept, cots, tabs, send):
+    dp, ctx, _, per, rows, _ = received.shape
+    split_rows, forward_table, _, _, mirror_cols, lower_rows, twiddle = tabs
+    tabs = (split_rows, forward_table, mirror_cols, lower_rows, twiddle)
+    operands = (place, received, *[near(x) for x in kept], *[near(x) for x in cots], *[far(t) for t in tabs], near(send))
+    return pl.pallas_call(
+        functools.partial(grad_kernel, hops=len(cots)),
+        grid=(per,),
+        in_specs=[
             pl.BlockSpec(memory_space=pltpu.SMEM),
-            here,
-            *[whole(x) for x in cots],
+            pl.BlockSpec(memory_space=pltpu.VMEM),
+            *[pl.BlockSpec(memory_space=pltpu.VMEM)] * 3,
+            *[pl.BlockSpec(memory_space=pltpu.VMEM) for _ in cots],
             *[whole(t) for t in tabs],
-        ],
-        out_specs=here,
-        out_shape=pltpu.VMEM((dp, ctx, 2, per, rows, N2), BF16),
+            pl.BlockSpec(memory_space=pltpu.VMEM),
+        ],
+        out_specs=pl.BlockSpec(memory_space=pltpu.VMEM),
+        out_shape=pltpu.VMEM(send.shape, BF16),
         scratch_shapes=[pltpu.VMEM((dp * ctx, rows, N2), BF16)],
+        input_output_aliases={len(operands) - 1: 0},
         compiler_params=pltpu.CompilerParams(vmem_limit_bytes=VMEM),
-        cost_estimate=pl.CostEstimate(flops=per * dp * 6 * 12 * N1**3, bytes_accessed=8 << 20, transcendentals=0),
-        name="channels",
-    )(place, gain, near(received), *[far(x) for x in cots], *[far(t) for t in tabs])
+        cost_estimate=pl.CostEstimate(flops=per * dp * 6 * N1**3, bytes_accessed=8 << 20, transcendentals=0),
+        name="grad",
+    )(*operands)
 
 
 def outward_kernel(index_ref, *refs):
@@ -322,9 +378,13 @@
     received = lax.all_to_all(first, axes, 0, 0, tiled=True).reshape(dp, ctx, 3, per, rows, N2)
     cots = outward_near(place, matrix(cotangent), count, hops, plane)
     cots = regroup([exchange(x, j // plane * ctx + j % plane) for j, x in enumerate(cots)])
-    cots = [exchange(x, hop * plane) for hop, x in enumerate(cots)]
+    received = near(received)
+    *early, late = cots
+    late, received = lax.optimization_barrier((late, received))
+    cots = [exchange(x, hop * plane) for hop, x in enumerate([*early, late])]
     gain = lax.dynamic_slice(skip_gain, ((d * ctx + c) * per,), (per,))
-    send = channel_call(place, gain, received, cots, tabs)
+    send, *kept = conv_call(gain, received, tabs)
+    send = grad_call(place, received, kept, cots, tabs, send)
     last = lax.all_to_all(send.reshape(count, 2, per, rows, N2), axes, 0, 0, tiled=True)
     y, grad = homeward(last)
     return y.reshape(1, rows * N2, channels), grad

time: 176 us -> 168 us (0.955)
  waiting for transfers between devices: 71.7 us -> 53.6 us
  local copies, waits for them, and re-layouts: 0.78 us -> 6.98 us
  Pallas kernels: 24.5 us -> 28.6 us
    ppermute x10, waiting for transfers between devices: 71.7 us -> 27.8 us  [exchange(): lax.ppermute(x, axes, [(i, i ^ mask) for i in range(count)])]
    all_to_all x1, waiting for transfers between devices: 0.01 us -> 25.8 us  [by_channel_body(): lax.all_to_all(first, axes, 0, 0, tiled=True)]
    unnamed x4 -> x20, local copies, waits for them, and re-layouts: 0.71 us -> 6.91 us
    pallas_call x1 -> x2, Pallas kernels: 13.2 us -> 15.7 us  [the longest x1 10.4 us: conv_call(): pl.pallas_call(conv_kernel, grid=(per,), in_specs=[pl.BlockSpec(memory_sp...]
  transfers between devices with their start and end apart: 11 -> 11, of which waited for: 6 -> 5; matrix products, arithmetic and copies ran while one was open for 0% -> 0% of each run, Pallas kernels for 2% -> 9%
where the time goes in v4:
time: 168 us
  blocking collectives  56.9 us (34%)
  waiting for transfers between devices  53.6 us (32%)
  Pallas kernels  28.6 us (17%)
  starting transfers between devices  20.9 us (12%)
  local copies, waits for them, and re-layouts  6.98 us (4%)
    all_to_all x1, blocking collectives, by_channel_body(): lax.all_to_all(send.reshape(count, 2, per, rows, N2), axes, 0, 0, tiled=T...  56.9 us
    ppermute x10, waiting for transfers between devices, exchange(): lax.ppermute(x, axes, [(i, i ^ mask) for i in range(count)])  27.8 us
    all_to_all x1, waiting for transfers between devices, by_channel_body(): lax.all_to_all(first, axes, 0, 0, tiled=True)  25.8 us
    ppermute x10, starting transfers between devices, exchange(): lax.ppermute(x, axes, [(i, i ^ mask) for i in range(count)])  13.6 us
    pallas_call x1, Pallas kernels, conv_call(): pl.pallas_call(conv_kernel, grid=(per,), in_specs=[pl.BlockSpec(memory_sp...  10.4 us
    all_to_all x1, starting transfers between devices, by_channel_body(): lax.all_to_all(first, axes, 0, 0, tiled=True)  7.3 us
    unnamed x20, local copies, waits for them, and re-layouts  6.91 us
    pallas_call x1, Pallas kernels, outward(): pl.pallas_call(outward_kernel, grid_spec=pltpu.PrefetchScalarGridSpec(num...  5.55 us
  transfers between devices with their start and end apart: 11, of which 5 were waited for; matrix products, arithmetic and copies ran while one was open for 0% of the time, Pallas kernels for 9%

profile of v4, /device:TPU:0, one launch (start us, length us, event | category | flops | bytes accessed | tf_op | source)
XLA Modules:
  0.0 167.7 jit_solution(15045280094210886927)
XLA Ops:
  0.7 5.6 %outward.1 = bf16[32,3,4,16,256]{4,3,2,1,0:T(8,128)(2,1)} custom-call(s32[3]{0:T(128)S(1)} %pad_add_fusion.place_ref.index_ref, bf16[1,16,256,128]{3,2,1,0:T(8,128)(2,1)} %bitcast.12, bf16[1,16,256,128]{3,2,1,0:T(8,128)(2,1)} %bitcast.13, f32[2,16,256,128]{3,2,1,0:T(8,128)} %refs_2_.1), custom_call_target="tpu_custom_call" | custom-call | bytes 12582912 | tf_op jit(solution)/shard_map/outward/pallas_call | solution.py:254
  6.3 7.3 %all-to-all-start = ((bf16[32,3,4,16,256]{4,3,2,1,0:T(8,128)(2,1)}), bf16[32,3,4,16,256]{4,3,2,1,0:T(8,128)(2,1)S(1)}, u32[]{:S(2)}, u32[]{:S(2)}) async-start(bf16[32,3,4,16,256]{4,3,2,1,0:T(8,128)(2,1)} %outward.1), calls=%async_computation | async-start | bytes 6291456 | tf_op jit(solution)/shard_map/all_to_all | solution.py:378
  13.6 2.7 %outward_near.1 = (bf16[4,4,16,256]{3,2,1,0:T(8,128)(2,1)S(1)}, bf16[4,4,16,256]{3,2,1,0:T(8,128)(2,1)S(1)}, bf16[4,4,16,256]{3,2,1,0:T(8,128)(2,1)S(1)}, bf16[4...) custom-call(s32[3]{0:T(128)S(1)} %pad_add_fusion.place_ref.index_ref, ...), custom_call_target="tpu_custom_call" | custom-call | bytes 2097152 | tf_op jit(solution)/shard_map/outward_near/pallas_call | solution.py:287
  16.6 1.7 %collective-permute-start.1 = (bf16[4,4,16,256]{3,2,1,0:T(8,128)(2,1)S(1)}, bf16[4,4,16,256]{3,2,1,0:T(8,128)(2,1)S(1)}, u32[]{:S(2)}, u32[]{:S(2)}) collective-permute-start(bf16[4,4,16,256]{3,2,1,0:T(8,128)(2,1)S(1)} %get-tuple-element.24), channel_id=1, source_target_pairs={{0,2},{1,3},{2,0},{3,1},{4,6},{5,7},{6,4},{7,5},{8,10},{9,11},{10,... | collective-permute-start | bytes 393224 | tf_op jit(solution)/shard_map/ppermute | solution.py:375
  18.3 1.7 %collective-permute-start.3 = (bf16[4,4,16,256]{3,2,1,0:T(8,128)(2,1)}, bf16[4,4,16,256]{3,2,1,0:T(8,128)(2,1)}, u32[]{:S(2)}, u32[]{:S(2)}) collective-permute-start(bf16[4,4,16,256]{3,2,1,0:T(8,128)(2,1)} %get-tuple-element.26), channel_id=1, source_target_pairs={{0,16},{1,17},{2,18},{3,19},{4,20},{5,21},{6,22},{7,23},{8,24},{9,... | collective-permute-start | bytes 393224 | tf_op jit(solution)/shard_map/ppermute | solution.py:375
  20.7 2.6 %collective-permute-start.5 = (bf16[4,4,16,256]{3,2,1,0:T(8,128)(2,1)}, bf16[4,4,16,256]{3,2,1,0:T(8,128)(2,1)S(1)}, u32[]{:S(2)}, u32[]{:S(2)}) collective-permute-start(bf16[4,4,16,256]{3,2,1,0:T(8,128)(2,1)} %get-tuple-element.28), channel_id=1, source_target_pairs={{0,18},{1,19},{2,16},{3,17},{4,22},{5,23},{6,20},{7,21},{8,26},{9,... | collective-permute-start | bytes 393224 | tf_op jit(solution)/shard_map/ppermute | solution.py:375
  23.3 14.3 %collective-permute-done.1.refs_2_ = bf16[4,4,16,256]{3,2,1,0:T(8,128)(2,1)S(1)} collective-permute-done((bf16[4,4,16,256]{3,2,1,0:T(8,128)(2,1)S(1)}, bf16[4,4,16,256]{3,2,1,0:T(8,128)(2,1)S(1)}, u32[]{:S(2)}, u32[]{:S(2)}) %collective-permute-start.1) | collective-permute-done | bytes 131104 | tf_op jit(solution)/shard_map/ppermute | solution.py:375
  38.3 2.4 %collective-permute-start.6 = (bf16[4,4,16,256]{3,2,1,0:T(8,128)(2,1)}, bf16[4,4,16,256]{3,2,1,0:T(8,128)(2,1)S(1)}, u32[]{:S(2)}, u32[]{:S(2)}) collective-permute-start(bf16[4,4,16,256]{3,2,1,0:T(8,128)(2,1)} %get-tuple-element.29), channel_id=1, source_target_pairs={{0,19},{1,18},{2,17},{3,16},{4,23},{5,22},{6,21},{7,20},{8,27},{9,... | collective-permute-start | bytes 393224 | tf_op jit(solution)/shard_map/ppermute | solution.py:375
  40.8 2.1 %collective-permute-done.2.refs_3_ = bf16[4,4,16,256]{3,2,1,0:T(8,128)(2,1)} collective-permute-done((bf16[4,4,16,256]{3,2,1,0:T(8,128)(2,1)}, bf16[4,4,16,256]{3,2,1,0:T(8,128)(2,1)}, u32[]{:S(2)}, u32[]{:S(2)}) %collective-permute-start.2) | collective-permute-done | bytes 131104 | tf_op jit(solution)/shard_map/ppermute | solution.py:375
  42.9 9.5 %collective-permute-done.5.refs_6_ = bf16[4,4,16,256]{3,2,1,0:T(8,128)(2,1)S(1)} collective-permute-done((bf16[4,4,16,256]{3,2,1,0:T(8,128)(2,1)}, bf16[4,4,16,256]{3,2,1,0:T(8,128)(2,1)S(1)}, u32[]{:S(2)}, u32[]{:S(2)}) %collective-permute-start.5) | collective-permute-done | bytes 131104 | tf_op jit(solution)/shard_map/ppermute | solution.py:375
  52.4 0.7 copy-done.4
  53.0 1.9 %collective-permute-done.6.refs_7_ = bf16[4,4,16,256]{3,2,1,0:T(8,128)(2,1)S(1)} collective-permute-done((bf16[4,4,16,256]{3,2,1,0:T(8,128)(2,1)}, bf16[4,4,16,256]{3,2,1,0:T(8,128)(2,1)S(1)}, u32[]{:S(2)}, u32[]{:S(2)}) %collective-permute-start.6) | collective-permute-done | bytes 131104 | tf_op jit(solution)/shard_map/ppermute | solution.py:375
  55.6 0.9 copy-done.1
  56.5 0.9 copy-done.3
  57.4 0.9 copy-done.5
  58.3 0.9 copy-done.7
  59.2 1.9 %regroup.1 = (bf16[8,4,16,256]{3,2,1,0:T(8,128)(2,1)S(1)}, bf16[8,4,16,256]{3,2,1,0:T(8,128)(2,1)}, bf16[8,4,16,256]{3,2,1,0:T(8,128)(2,1)}, bf16[8,4,16,256]{3,2,1,0:T(8,128)(2,1)S(1)}) custom-call(bf16[4,4,16,256]{3,2,1,0:T(8,128)(2,1)S(1)} %get-tuple-element.22.refs_0_, bf16[4,4,16,256]{3,2,1,0:T(8,128)(2,1)S(1)} %copy-done.1, ...), custom_call_target="tpu_custom_call" | custom-call | bytes 2097152 | tf_op jit(solution)/shard_map/regroup/pallas_call | solution.py:311
  61.0 0.7 copy-done.8
  61.7 4.8 %collective-permute-start.8 = (bf16[8,4,16,256]{3,2,1,0:T(8,128)(2,1)}, bf16[8,4,16,256]{3,2,1,0:T(8,128)(2,1)}, u32[]{:S(2)}, u32[]{:S(2)}) collective-permute-start(bf16[8,4,16,256]{3,2,1,0:T(8,128)(2,1)} %get-tuple-element.37), channel_id=1, source_target_pairs={{0,8},{1,9},{2,10},{3,11},{4,12},{5,13},{6,14},{7,15},{8,0},{9,1},... | collective-permute-start | bytes 786440 | tf_op jit(solution)/shard_map/ppermute | solution.py:375
  66.5 25.8 %all-to-all-done = bf16[32,3,4,16,256]{4,3,2,1,0:T(8,128)(2,1)S(1)} async-done(((bf16[32,3,4,16,256]{4,3,2,1,0:T(8,128)(2,1)}), bf16[32,3,4,16,256]{4,3,2,1,0:T(8,128)(2,1)S(1)}, u32[]{:S(2)}, u32[]{:S(2)}) %all-to-all-start) | async-done | bytes 3145760 | tf_op jit(solution)/shard_map/all_to_all | solution.py:378
  92.3 10.4 %conv.1 = (bf16[2,16,2,4,16,256]{5,4,3,2,1,0:T(8,128)(2,1)S(1)}, f32[4,2,256,256]{3,2,1,0:T(8,128)S(1)}, f32[4,2,144,512]{3,2,1,0:T(8,128)S(1)}, f32[4,2,144,256]{3,2,1,0:T(8,128)S(1)}) custom-call(f32[4]{0:T(128)S(1)} %dynamic_slice.3.gain_ref, bf16[2,16,3,4,16,256]{5,4,3,2,1,0:T(8,128)(2,1)S(1)} %bitcast.9, ...), custom_call_target="tpu_custom_call" | custom-call | flops 4026531840 | bytes 8388608 | tf_op jit(solution)/shard_map/conv/pallas_call | solution.py:191
  102.8 5.2 %grad.1 = bf16[2,16,2,4,16,256]{5,4,3,2,1,0:T(8,128)(2,1)S(1)} custom-call(s32[3]{0:T(128)S(1)} %pad_add_fusion.place_ref.index_ref, bf16[2,16,3,4,16,256]{5,4,3,2,1,0:T(8,128)(2,1)S(1)} %bitcast.10, f32[4,2,256,256]{3,2,1,0:T(8,128)S(1)} %get-tuple-element.32.gap_ref, ...), custom_call_target="tpu_custom_call", output_to_operand_aliasing={{}: (14, {})} | custom-call | flops 805306368 | bytes 8388608 | tf_op jit(solution)/shard_map/grad/pallas_call | solution.py:217
  108.0 56.9 %all_to_all.10.last_ref = bf16[32,2,4,16,256]{4,3,2,1,0:T(8,128)(2,1)S(1)} all-to-all(bf16[32,2,4,16,256]{4,3,2,1,0:T(8,128)(2,1)S(1)} %bitcast.11), channel_id=1, replica_groups=mesh['dp'=2,'ctx'=16] {'dp','ctx'}, dimensions={0} | all-to-all | bytes 4194304 | tf_op jit(solution)/shard_map/all_to_all | solution.py:388
  164.9 2.8 %homeward.1 = (bf16[16,256,128]{2,1,0:T(8,128)(2,1)}, f32[2,16,128,128]{3,2,1,0:T(8,128)}) custom-call(bf16[32,2,4,16,256]{4,3,2,1,0:T(8,128)(2,1)S(1)} %all_to_all.10.last_ref), custom_call_target="tpu_custom_call" | custom-call | bytes 5242880 | tf_op jit(solution)/shard_map/homeward/pallas_call | solution.py:339
  (27 shorter events, 2.5 us)
Async XLA Ops:
  6.3 34.5 %copy-start.9 = (f32[128]{0:T(128)S(1)}, f32[128]{0:T(128)}, u32[]{:S(2)}) copy-start(f32[128]{0:T(128)} %param.16) | copy-start | bytes 1540
  6.3 86.0 %all-to-all-start = ((bf16[32,3,4,16,256]{4,3,2,1,0:T(8,128)(2,1)}), bf16[32,3,4,16,256]{4,3,2,1,0:T(8,128)(2,1)S(1)}, u32[]{:S(2)}, u32[]{:S(2)}) async-start(bf16[32,3,4,16,256]{4,3,2,1,0:T(8,128)(2,1)} %outward.1), calls=%async_computation | async-start | bytes 6291456 | tf_op jit(solution)/shard_map/all_to_all | solution.py:378
  16.3 3.8 %collective-permute-start = (bf16[4,4,16,256]{3,2,1,0:T(8,128)(2,1)S(1)}, bf16[4,4,16,256]{3,2,1,0:T(8,128)(2,1)S(1)}, u32[]{:S(2)}, u32[]{:S(2)}) collective-permute-start(bf16[4,4,16,256]{3,2,1,0:T(8,128)(2,1)S(1)} %get-tuple-element.23), channel_id=1, source_target_pairs={{0,1},{1,0},{2,3},{3,2},{4,5},{5,4},{6,7},{7,6},{8,9},{9,8},{10,11... | collective-permute-start | bytes 393224 | tf_op jit(solution)/shard_map/ppermute | solution.py:375
  16.6 21.1 %collective-permute-start.1 = (bf16[4,4,16,256]{3,2,1,0:T(8,128)(2,1)S(1)}, bf16[4,4,16,256]{3,2,1,0:T(8,128)(2,1)S(1)}, u32[]{:S(2)}, u32[]{:S(2)}) collective-permute-start(bf16[4,4,16,256]{3,2,1,0:T(8,128)(2,1)S(1)} %get-tuple-element.24), channel_id=1, source_target_pairs={{0,2},{1,3},{2,0},{3,1},{4,6},{5,7},{6,4},{7,5},{8,10},{9,11},{10,... | collective-permute-start | bytes 393224 | tf_op jit(solution)/shard_map/ppermute | solution.py:375
  18.3 24.6 %collective-permute-start.2 = (bf16[4,4,16,256]{3,2,1,0:T(8,128)(2,1)}, bf16[4,4,16,256]{3,2,1,0:T(8,128)(2,1)}, u32[]{:S(2)}, u32[]{:S(2)}) collective-permute-start(bf16[4,4,16,256]{3,2,1,0:T(8,128)(2,1)} %get-tuple-element.25), channel_id=1, source_target_pairs={{0,3},{1,2},{2,1},{3,0},{4,7},{5,6},{6,5},{7,4},{8,11},{9,10},{10,... | collective-permute-start | bytes 393224 | tf_op jit(solution)/shard_map/ppermute | solution.py:375
  18.3 24.6 %collective-permute-start.3 = (bf16[4,4,16,256]{3,2,1,0:T(8,128)(2,1)}, bf16[4,4,16,256]{3,2,1,0:T(8,128)(2,1)}, u32[]{:S(2)}, u32[]{:S(2)}) collective-permute-start(bf16[4,4,16,256]{3,2,1,0:T(8,128)(2,1)} %get-tuple-element.26), channel_id=1, source_target_pairs={{0,16},{1,17},{2,18},{3,19},{4,20},{5,21},{6,22},{7,23},{8,24},{9,... | collective-permute-start | bytes 393224 | tf_op jit(solution)/shard_map/ppermute | solution.py:375
  20.0 23.0 %collective-permute-start.4 = (bf16[4,4,16,256]{3,2,1,0:T(8,128)(2,1)}, bf16[4,4,16,256]{3,2,1,0:T(8,128)(2,1)}, u32[]{:S(2)}, u32[]{:S(2)}) collective-permute-start(bf16[4,4,16,256]{3,2,1,0:T(8,128)(2,1)} %get-tuple-element.27), channel_id=1, source_target_pairs={{0,17},{1,16},{2,19},{3,18},{4,21},{5,20},{6,23},{7,22},{8,25},{9,... | collective-permute-start | bytes 393224 | tf_op jit(solution)/shard_map/ppermute | solution.py:375
  20.1 0.6 copy-start
  20.7 31.7 %collective-permute-start.5 = (bf16[4,4,16,256]{3,2,1,0:T(8,128)(2,1)}, bf16[4,4,16,256]{3,2,1,0:T(8,128)(2,1)S(1)}, u32[]{:S(2)}, u32[]{:S(2)}) collective-permute-start(bf16[4,4,16,256]{3,2,1,0:T(8,128)(2,1)} %get-tuple-element.28), channel_id=1, source_target_pairs={{0,18},{1,19},{2,16},{3,17},{4,22},{5,23},{6,20},{7,21},{8,26},{9,... | collective-permute-start | bytes 393224 | tf_op jit(solution)/shard_map/ppermute | solution.py:375
  37.6 0.6 copy-start.2
  38.3 16.6 %collective-permute-start.6 = (bf16[4,4,16,256]{3,2,1,0:T(8,128)(2,1)}, bf16[4,4,16,256]{3,2,1,0:T(8,128)(2,1)S(1)}, u32[]{:S(2)}, u32[]{:S(2)}) collective-permute-start(bf16[4,4,16,256]{3,2,1,0:T(8,128)(2,1)} %get-tuple-element.29), channel_id=1, source_target_pairs={{0,19},{1,18},{2,17},{3,16},{4,23},{5,22},{6,21},{7,20},{8,27},{9,... | collective-permute-start | bytes 393224 | tf_op jit(solution)/shard_map/ppermute | solution.py:375
  52.4 0.7 copy-start.4
  54.9 0.7 copy-start.6
  55.6 0.9 copy-start.1
  56.5 0.9 copy-start.3
  57.4 0.9 copy-start.5
  58.3 0.9 copy-start.7
  61.0 0.7 copy-start.8
  61.7 41.0 %collective-permute-start.7 = (bf16[8,4,16,256]{3,2,1,0:T(8,128)(2,1)}, bf16[8,4,16,256]{3,2,1,0:T(8,128)(2,1)}, u32[]{:S(2)}, u32[]{:S(2)}) collective-permute-start(bf16[8,4,16,256]{3,2,1,0:T(8,128)(2,1)} %get-tuple-element.36), channel_id=1, source_target_pairs={{0,4},{1,5},{2,6},{3,7},{4,0},{5,1},{6,2},{7,3},{8,12},{9,13},{10,... | collective-permute-start | bytes 786440 | tf_op jit(solution)/shard_map/ppermute | solution.py:375
  61.7 41.0 %collective-permute-start.8 = (bf16[8,4,16,256]{3,2,1,0:T(8,128)(2,1)}, bf16[8,4,16,256]{3,2,1,0:T(8,128)(2,1)}, u32[]{:S(2)}, u32[]{:S(2)}) collective-permute-start(bf16[8,4,16,256]{3,2,1,0:T(8,128)(2,1)} %get-tuple-element.37), channel_id=1, source_target_pairs={{0,8},{1,9},{2,10},{3,11},{4,12},{5,13},{6,14},{7,15},{8,0},{9,1},... | collective-permute-start | bytes 786440 | tf_op jit(solution)/shard_map/ppermute | solution.py:375
  92.3 10.5 %collective-permute-start.9 = (bf16[8,4,16,256]{3,2,1,0:T(8,128)(2,1)}, bf16[8,4,16,256]{3,2,1,0:T(8,128)(2,1)S(1)}, u32[]{:S(2)}, u32[]{:S(2)}) collective-permute-start(bf16[8,4,16,256]{3,2,1,0:T(8,128)(2,1)} %copy-done.8), channel_id=1, source_target_pairs={{0,12},{1,13},{2,14},{3,15},{4,8},{5,9},{6,10},{7,11},{8,4},{9,5},... | collective-permute-start | bytes 786440 | tf_op jit(solution)/shard_map/ppermute | solution.py:375

commit v5 on v4

--- a/solution.py
+++ b/solution.py
@@ -31,11 +31,9 @@
     mirror_rows = np.zeros((HALF, N1))
     mirror_rows[ids[:HALF], -ids[:HALF] % N1] = 1
     mirror_cols = np.eye(N2)[::-1]
-    lower_rows = np.zeros((N1 // 2, HALF))
-    lower_rows[ids[: N1 // 2], N1 // 2 - ids[: N1 // 2]] = 1
     angle = (ids[:HALF, None] * ids[None, :]) * (two_pi / (N1 * N2))
     twiddle = np.stack([np.cos(angle), np.sin(angle)], 0)
-    small = (split_rows, forward_table, join_rows, mirror_rows, mirror_cols, lower_rows)
+    small = (split_rows, forward_table, join_rows, mirror_rows, mirror_cols)
     small = [jnp.asarray(t.astype(jnp.bfloat16)) for t in small]
     return (*small, jnp.asarray(twiddle.astype(np.float32)))
 
@@ -86,10 +84,16 @@
 
 def conv_kernel(
     gain_ref, recv_ref, split_ref, fwd_ref, join_ref, mirror_ref, cols_ref, tw_ref,
-    send_ref, gap_ref, spec_ref, part_ref,
+    send_ref, gap_ref, spec_ref, part_ref, *held_refs,
 ):
     count, ctx = recv_ref.shape[:2]
     q = pl.program_id(0)
+
+    @pl.when(q == 0)
+    def _():
+        for held_ref, table_ref in zip(held_refs, (split_ref, fwd_ref, tw_ref)):
+            held_ref[...] = table_ref[...]
+
     tw_cos, tw_sin = tw_ref[0], tw_ref[1]
     signals = []
     for d in range(count):
@@ -139,37 +143,42 @@
 
 def grad_kernel(place_ref, recv_ref, gap_ref, spec_ref, part_ref, *refs, hops):
     cot_refs, refs = refs[:hops], refs[hops:]
-    split_ref, fwd_ref, cols_ref, lower_ref, tw_ref, _, send_ref, cot_rows = refs
+    split_ref, fwd_ref, tw_ref, _, send_ref, cot_rows = refs
     count, ctx = recv_ref.shape[:2]
     near = cot_refs[0].shape[0]
     plane = near // count
-    q = pl.program_id(0)
+    per = recv_ref.shape[3]
     for hop, cot_ref in enumerate(cot_refs):
         for j in range(near):
-            cot_rows[near_device(place_ref, j, hop, plane, hops)] = cot_ref[j, q]
+            cot_rows[near_device(place_ref, j, hop, plane, hops)] = cot_ref[j]
     errors = []
-    for d in range(count):
-        clean = recv_ref[d, :, 0, q].reshape(N1, N2).astype(F32)
-        cot = cot_rows[d * ctx : (d + 1) * ctx].reshape(N1, N2).astype(F32)
-        errors.append((clean * (cot - gap_ref[q, d].astype(F32))).astype(BF16))
-    spectra = [spec_ref[q, d].astype(F32) for d in range(count)]
-    total_real, total_imag = gradient(forward(errors, split_ref, fwd_ref, tw_ref[0], tw_ref[1]), spectra)
-    total_real += part_ref[q, 0]
-    total_imag += part_ref[q, 1]
-    scale = 1.0 / (N1 * N2)
-    upper = jnp.concatenate([(total_real * scale).astype(BF16), (total_imag * scale).astype(BF16)], 1)
-    lower = dot(lower_ref[...], upper).astype(BF16)
-    lower = dot(jnp.concatenate([lower[:, :N2], lower[:, N2:]], 0), cols_ref[...])
-    lower_real, lower_imag = lower[: N1 // 2].astype(BF16), (-lower[N1 // 2 :]).astype(BF16)
+    for q in range(per):
+        for d in range(count):
+            clean = recv_ref[d, :, 0, q].reshape(N1, N2).astype(F32)
+            cot = cot_rows[d * ctx : (d + 1) * ctx, q].reshape(N1, N2).astype(F32)
+            errors.append((clean * (cot - gap_ref[q, d])).astype(BF16))
+    err_spectra = forward(errors, split_ref, fwd_ref, tw_ref[0], tw_ref[1])
+    for q in range(per):
+        spectra = [spec_ref[q, d] for d in range(count)]
+        total = gradient(err_spectra[q * count : (q + 1) * count], spectra)
+        send_grad(send_ref, q, *[t + part_ref[q, i] for i, t in enumerate(total)])
+
+
+def send_grad(send_ref, q, total_real, total_imag):
+    count, ctx, _, _, rows, _ = send_ref.shape
+    total = jnp.concatenate([total_real, total_imag], 1) * (1.0 / (N1 * N2))
+    upper, after = total[: N1 // 2], total[rows : N1 // 2 + rows]
+    first = lax.broadcasted_iota(jnp.int32, upper.shape, 0) % rows == 0
+    lower = jnp.where(first, after, upper).astype(BF16)
+    upper = upper.astype(BF16)
     width = N2 // count
     for i in range(count):
-        first = upper[: N1 // 2, i * width : (i + 1) * width]
-        second = upper[: N1 // 2, N2 + i * width : N2 + (i + 1) * width]
-        upper_pair = jnp.concatenate([first, second], 1)
-        cols = slice(i * width, (i + 1) * width)
-        lower_pair = jnp.concatenate([lower_real[:, cols], lower_imag[:, cols]], 1)
-        send_ref[i, : ctx // 2, 1, q] = upper_pair.reshape(ctx // 2, -1, 2 * width)
-        send_ref[i, ctx // 2 :, 1, q] = lower_pair.reshape(ctx // 2, -1, 2 * width)
+        for half, x, side in ((0, upper, i), (1, lower, count - 1 - i)):
+            cols = slice(side * width, (side + 1) * width)
+            pair = jnp.concatenate([x[:, :N2][:, cols], x[:, N2:][:, cols]], 1)
+            for block in range(ctx // 2):
+                target = ctx - 1 - block if half else block
+                send_ref[i, target, 1, q] = pair[block * rows : (block + 1) * rows]
 
 
 def whole(x):
@@ -186,8 +195,8 @@
 
 def conv_call(gain, received, tabs):
     dp, ctx, _, per, rows, _ = received.shape
-    split_rows, forward_table, join_rows, mirror_rows, mirror_cols, _, twiddle = tabs
-    tabs = (split_rows, forward_table, join_rows, mirror_rows, mirror_cols, twiddle)
+    split_rows, forward_table, *_, twiddle = tabs
+    held = [pltpu.VMEM(t.shape, t.dtype) for t in (split_rows, forward_table, twiddle)]
     return pl.pallas_call(
         conv_kernel,
         grid=(per,),
@@ -196,12 +205,13 @@
             pl.BlockSpec(memory_space=pltpu.VMEM),
             *[whole(t) for t in tabs],
         ],
-        out_specs=[pl.BlockSpec(memory_space=pltpu.VMEM)] * 4,
+        out_specs=[pl.BlockSpec(memory_space=pltpu.VMEM)] * 7,
         out_shape=[
             pltpu.VMEM((dp, ctx, 2, per, rows, N2), BF16),
             pltpu.VMEM((per, dp, N1, N2), KEPT),
             pltpu.VMEM((per, dp, HALF, 2 * N2), KEPT),
             pltpu.VMEM((per, 2, HALF, N2), F32),
+            *held,
         ],
         compiler_params=pltpu.CompilerParams(vmem_limit_bytes=VMEM),
         cost_estimate=pl.CostEstimate(flops=per * dp * 5 * 6 * N1**3, bytes_accessed=8 << 20, transcendentals=0),
@@ -209,25 +219,20 @@
     )(gain, received, *[far(t) for t in tabs])
 
 
-def grad_call(place, received, kept, cots, tabs, send):
+def grad_call(place, received, kept, cots, send):
     dp, ctx, _, per, rows, _ = received.shape
-    split_rows, forward_table, _, _, mirror_cols, lower_rows, twiddle = tabs
-    tabs = (split_rows, forward_table, mirror_cols, lower_rows, twiddle)
-    operands = (place, received, *[near(x) for x in kept], *[near(x) for x in cots], *[far(t) for t in tabs], near(send))
+    *kept, split_rows, forward_table, twiddle = [near(x) for x in kept]
+    operands = (place, received, *kept, *[near(x) for x in cots], split_rows, forward_table, twiddle, near(send))
     return pl.pallas_call(
         functools.partial(grad_kernel, hops=len(cots)),
-        grid=(per,),
+        grid=(1,),
         in_specs=[
             pl.BlockSpec(memory_space=pltpu.SMEM),
-            pl.BlockSpec(memory_space=pltpu.VMEM),
-            *[pl.BlockSpec(memory_space=pltpu.VMEM)] * 3,
-            *[pl.BlockSpec(memory_space=pltpu.VMEM) for _ in cots],
-            *[whole(t) for t in tabs],
-            pl.BlockSpec(memory_space=pltpu.VMEM),
+            *[pl.BlockSpec(memory_space=pltpu.VMEM)] * (len(operands) - 1),
         ],
         out_specs=pl.BlockSpec(memory_space=pltpu.VMEM),
         out_shape=pltpu.VMEM(send.shape, BF16),
-        scratch_shapes=[pltpu.VMEM((dp * ctx, rows, N2), BF16)],
+        scratch_shapes=[pltpu.VMEM((dp * ctx, per, rows, N2), BF16)],
         input_output_aliases={len(operands) - 1: 0},
         compiler_params=pltpu.CompilerParams(vmem_limit_bytes=VMEM),
         cost_estimate=pl.CostEstimate(flops=per * dp * 6 * N1**3, bytes_accessed=8 << 20, transcendentals=0),
@@ -235,49 +240,67 @@
     )(*operands)
 
 
-def outward_kernel(index_ref, *refs):
-    *in_refs, out_ref, rows_ref = refs
-    count, _, per, rows, width = out_ref.shape
-    channels = count * per
-    for t, in_ref in enumerate(in_refs):
-        for r in range(rows):
-            block = in_ref[0, r].astype(F32).T
-            rows_ref[pl.ds(r, channels, stride=rows), :] = block
-        out_ref[:, t] = rows_ref[...].astype(BF16).reshape(count, per, rows, width)
-
-
-def outward(index, arrays, count):
+def outward_kernel(place_ref, *refs, count):
+    in_refs, refs = refs[:count], refs[count:]
+    out_ref, refs = refs[0], refs[1:]
+    held_refs, (rows_ref, ready_ref, load_sems, store_sems) = refs[:count], refs[count:]
+    devices, _, per, rows, _ = out_ref.shape
+    pitch = rows_ref.shape[1] // (devices * per)
+    width = rows_ref.shape[2]
+    loads, stores = [], []
+    for t, (in_ref, held_ref) in enumerate(zip(in_refs, held_refs)):
+        source = in_ref.at[place_ref[0] if in_ref.shape[0] > 1 else 0]
+        loads.append(pltpu.make_async_copy(source, held_ref, load_sems.at[t]))
+        loads[t].start()
+    for t, held_ref in enumerate(held_refs):
+        loads[t].wait()
+        for h in range(N2 // width):
+            lanes = slice(h * width, (h + 1) * width)
+            for r in range(rows):
+                block = held_ref[r, lanes].astype(BF16).T.astype(F32)
+                rows_ref[h, pl.ds(r, devices * per, stride=pitch), :] = block
+            block = rows_ref[h].reshape(devices, per, pitch, width)[:, :, :rows].astype(BF16)
+            ready_ref[t, :, :, :, lanes] = block
+        stores.append(pltpu.make_async_copy(ready_ref.at[t], out_ref.at[:, t], store_sems.at[t]))
+        stores[t].start()
+    for store in stores:
+        store.wait()
+
+
+def outward(place, arrays, devices):
     _, rows, _, channels = arrays[0].shape
-    per = channels // count
-    width = 128
-    picks = [(lambda h, s: (s[0], 0, h, 0)) if a.shape[0] > 1 else (lambda h, s: (0, 0, h, 0)) for a in arrays]
+    count, per, width, pitch = len(arrays), channels // devices, 128, rows + 8
+    shape = (devices, count, per, rows, N2)
     return pl.pallas_call(
-        outward_kernel,
-        grid_spec=pltpu.PrefetchScalarGridSpec(
-            num_scalar_prefetch=1,
-            grid=(N2 // width,),
-            in_specs=[pl.BlockSpec((1, rows, width, channels), pick) for pick in picks],
-            out_specs=pl.BlockSpec((count, len(arrays), per, rows, width), lambda h, s: (0, 0, 0, 0, h)),
-            scratch_shapes=[pltpu.VMEM((channels * rows, width), F32)],
-        ),
-        out_shape=jax.ShapeDtypeStruct((count, len(arrays), per, rows, N2), BF16),
+        functools.partial(outward_kernel, count=count),
+        in_specs=[pl.BlockSpec(memory_space=pltpu.SMEM), *[pl.BlockSpec(memory_space=pl.ANY)] * count],
+        out_specs=pl.BlockSpec(memory_space=pl.ANY),
+        out_shape=jax.ShapeDtypeStruct(shape, BF16),
+        scratch_shapes=[
+            *[pltpu.VMEM(a.shape[1:], a.dtype) for a in arrays],
+            pltpu.VMEM((N2 // width, channels * pitch, width), F32),
+            pltpu.VMEM((count, devices, per, rows, N2), BF16),
+            pltpu.SemaphoreType.DMA((count,)),
+            pltpu.SemaphoreType.DMA((count,)),
+        ],
         compiler_params=pltpu.CompilerParams(vmem_limit_bytes=VMEM),
-        cost_estimate=pl.CostEstimate(flops=0, bytes_accessed=(4 * len(arrays)) << 20, transcendentals=0),
+        cost_estimate=pl.CostEstimate(flops=0, bytes_accessed=7 << 20, transcendentals=0),
         name="outward",
-    )(index, *arrays)
+    )(place, *arrays)
 
 
 def outward_near_kernel(place_ref, in_ref, *refs, hops, plane):
     *out_refs, rows_ref = refs
     _, per, rows, width = out_refs[0].shape
     channels = in_ref.shape[3]
+    pitch = rows_ref.shape[0] // channels
     for r in range(rows):
-        rows_ref[pl.ds(r, channels, stride=rows), :] = in_ref[0, r].astype(F32).T
+        rows_ref[pl.ds(r, channels, stride=pitch), :] = in_ref[0, r].T.astype(F32)
     for j, out_ref in enumerate(out_refs):
         for hop in range(hops):
-            block = near_device(place_ref, j, hop, plane, hops) * (per * rows)
-            rows_here = rows_ref[pl.ds(pl.multiple_of(block, per * rows), per * rows), :]
-            out_ref[hop] = rows_here.astype(BF16).reshape(per, rows, width)
+            block = near_device(place_ref, j, hop, plane, hops) * (per * pitch)
+            rows_here = rows_ref[pl.ds(pl.multiple_of(block, per * pitch), per * pitch), :]
+            out_ref[hop] = rows_here.reshape(per, pitch, width)[:, :rows].astype(BF16)
 
 
 def outward_near(place, x, count, hops, plane):
@@ -293,7 +316,7 @@
         ],
         out_specs=[pl.BlockSpec((hops, per, rows, width), lambda h: (0, 0, 0, h))] * (count // hops),
         out_shape=[jax.ShapeDtypeStruct((hops, per, rows, N2), BF16)] * (count // hops),
-        scratch_shapes=[pltpu.VMEM((channels * rows, width), F32)],
+        scratch_shapes=[pltpu.VMEM((channels * (rows + 8), width), F32)],
         compiler_params=pltpu.CompilerParams(vmem_limit_bytes=VMEM),
         cost_estimate=pl.CostEstimate(flops=0, bytes_accessed=2 << 20, transcendentals=0),
         name="outward_near",
@@ -317,42 +340,57 @@
     )(*arrays)
 
 
-def homeward_kernel(last_ref, y_ref, grad_ref, rows_ref):
+def homeward_kernel(place_ref, last_ref, y_hbm, grad_hbm, y_ref, grad_ref, rows_ref, sems):
     count, _, per, rows, _ = last_ref.shape
-    channels = count * per
-    width = rows_ref.shape[1]
-    lanes = pl.ds(pl.multiple_of(pl.program_id(0) * width, width), width)
-    for t in range(2):
-        rows_ref[...] = last_ref[:, t, :, :, lanes].astype(F32).reshape(channels * rows, width)
+    width = rows_ref.shape[2]
+    pitch = rows_ref.shape[1] // (count * per)
+    lower = place_ref[1] >= place_ref[3]
+    row = lax.broadcasted_iota(jnp.int32, (width, width), 0)
+    col = lax.broadcasted_iota(jnp.int32, (width, width), 1)
+    turn = (col == jnp.where(lower, width - 1 - row, row)).astype(F32)
+    copies = []
+    for step, (t, h) in enumerate(((1, 0), (1, 1), (0, 0), (0, 1))):
+        lanes = slice(h * width, (h + 1) * width)
+        block = last_ref[:, t, :, :, lanes].astype(F32)
+        rows_ref.at[step].reshape(count, per, pitch, width)[:, :, :rows] = block
+        sign = jnp.where(lower, -1.0, 1.0) if h else 1.0
+        pick = (turn * sign).astype(BF16)
         for r in range(rows):
-            block = rows_ref[pl.ds(r, channels, stride=rows), :].T
-            if t == 0:
-                y_ref[r] = block.astype(BF16)
+            slot = jnp.where(lower, (rows - r) % rows, r) if t else r
+            block = rows_ref[step, pl.ds(slot, count * per, stride=pitch), :].astype(BF16)
+            if t:
+                grad_ref[h, r] = lax.dot_general(pick, block, (((1,), (1,)), ((), ())), preferred_element_type=F32)
             else:
-                grad_ref[0, r] = block
-
-
-def homeward(last):
+                y_ref[r, lanes] = block.T
+        if t:
+            copies.append(pltpu.make_async_copy(grad_ref.at[h], grad_hbm.at[h], sems.at[step]))
+        else:
+            here = pl.ds(h * width, width)
+            copies.append(pltpu.make_async_copy(y_ref.at[:, here], y_hbm.at[:, here], sems.at[step]))
+        copies[step].start()
+    for copy in copies:
+        copy.wait()
+
+
+def homeward(place, last):
     count, _, per, rows, _ = last.shape
-    channels = count * per
-    width = 128
+    channels, width, pitch = count * per, 128, rows + 8
+    y_shape, grad_shape = (rows, N2, channels), (2, rows, width, channels)
     return pl.pallas_call(
         homeward_kernel,
-        grid=(N2 // width,),
-        in_specs=[pl.BlockSpec(memory_space=pltpu.VMEM)],
-        out_specs=[
-            pl.BlockSpec((rows, width, channels), lambda h: (0, h, 0)),
-            pl.BlockSpec((1, rows, width, channels), lambda h: (h, 0, 0, 0)),
-        ],
-        out_shape=[
-            jax.ShapeDtypeStruct((rows, N2, channels), BF16),
-            jax.ShapeDtypeStruct((2, rows, width, channels), F32),
-        ],
-        scratch_shapes=[pltpu.VMEM((channels * rows, width), F32)],
+        in_specs=[pl.BlockSpec(memory_space=pltpu.SMEM), pl.BlockSpec(memory_space=pltpu.VMEM)],
+        out_specs=[pl.BlockSpec(memory_space=pl.ANY)] * 2,
+        out_shape=[jax.ShapeDtypeStruct(y_shape, BF16), jax.ShapeDtypeStruct(grad_shape, F32)],
+        scratch_shapes=[
+            pltpu.VMEM(y_shape, BF16),
+            pltpu.VMEM(grad_shape, F32),
+            pltpu.VMEM((4, channels * pitch, width), F32),
+            pltpu.SemaphoreType.DMA((4,)),
+        ],
         compiler_params=pltpu.CompilerParams(vmem_limit_bytes=VMEM),
         cost_estimate=pl.CostEstimate(flops=0, bytes_accessed=5 << 20, transcendentals=0),
         name="homeward",
-    )(near(last))
+    )(place, near(last))
 
 
 def by_channel_body(embeds, perturb, cotangent, filter_spectrum, skip_gain):
@@ -366,7 +404,7 @@
     plane = 4
     hops = ctx // plane
     tabs = tables()
-    place = jnp.stack([d, c // plane, c % plane])
+    place = jnp.stack([d, c // plane, c % plane, jnp.int32(hops // 2)])
 
     def matrix(x):
         return far(x.reshape(1, rows, N2, channels))
@@ -384,9 +422,9 @@
     cots = [exchange(x, hop * plane) for hop, x in enumerate([*early, late])]
     gain = lax.dynamic_slice(skip_gain, ((d * ctx + c) * per,), (per,))
     send, *kept = conv_call(gain, received, tabs)
-    send = grad_call(place, received, kept, cots, tabs, send)
+    send = grad_call(place, received, kept, cots, send)
     last = lax.all_to_all(send.reshape(count, 2, per, rows, N2), axes, 0, 0, tiled=True)
-    y, grad = homeward(last)
+    y, grad = homeward(place, last)
     return y.reshape(1, rows * N2, channels), grad
 
 

time: 168 us -> 165 us (0.982)
  Pallas kernels: 28.6 us -> 25.5 us
    pallas_call x3, Pallas kernels: 13.6 us -> 10.7 us  [the longest x1 4.49 us: outward(): pl.pallas_call(functools.partial(outward_kernel, count=count), in_specs=[...]
where the time goes in v5:
time: 165 us
  blocking collectives  56.8 us (34%)
  waiting for transfers between devices  53.8 us (33%)
  Pallas kernels  25.5 us (15%)
  starting transfers between devices  20.9 us (13%)
  local copies, waits for them, and re-layouts  6.98 us (4%)
    all_to_all x1, blocking collectives, by_channel_body(): lax.all_to_all(send.reshape(count, 2, per, rows, N2), axes, 0, 0, tiled=T...  56.8 us
    ppermute x10, waiting for transfers between devices, exchange(): lax.ppermute(x, axes, [(i, i ^ mask) for i in range(count)])  28 us
    all_to_all x1, waiting for transfers between devices, by_channel_body(): lax.all_to_all(first, axes, 0, 0, tiled=True)  25.8 us
    ppermute x10, starting transfers between devices, exchange(): lax.ppermute(x, axes, [(i, i ^ mask) for i in range(count)])  13.6 us
    pallas_call x1, Pallas kernels, conv_call(): pl.pallas_call(conv_kernel, grid=(per,), in_specs=[pl.BlockSpec(memory_sp...  10.5 us
    all_to_all x1, starting transfers between devices, by_channel_body(): lax.all_to_all(first, axes, 0, 0, tiled=True)  7.3 us
    unnamed x20, local copies, waits for them, and re-layouts  6.91 us
    pallas_call x1, Pallas kernels, outward(): pl.pallas_call(functools.partial(outward_kernel, count=count), in_specs=[...  4.49 us
  transfers between devices with their start and end apart: 11, of which 5 were waited for; matrix products, arithmetic and copies ran while one was open for 0% of the time, Pallas kernels for 9%

profile of v5, /device:TPU:0, one launch (start us, length us, event | category | flops | bytes accessed | tf_op | source)
XLA Modules:
  0.0 164.8 jit_solution(3537307422314864499)
XLA Ops:
  0.7 4.5 %outward.1 = bf16[32,3,4,16,256]{4,3,2,1,0:T(8,128)(2,1)} custom-call(s32[4]{0:T(128)S(1)} %pad_add_fusion.place_ref, bf16[1,16,256,128]{3,2,1,0:T(8,128)(2,1)} %bitcast.12, bf16[1,16,256,128]{3,2,1,0:T(8,128)(2,1)} %bitcast.13, f32[2,16,256,128]{3,2,1,0:T(8,128)} %refs_2_.1), custom_call_target="tpu_custom_call" | custom-call | bytes 7340032 | tf_op jit(solution)/shard_map/outward/pallas_call | solution.py:274
  5.2 7.3 %all-to-all-start = ((bf16[32,3,4,16,256]{4,3,2,1,0:T(8,128)(2,1)}), bf16[32,3,4,16,256]{4,3,2,1,0:T(8,128)(2,1)S(1)}, u32[]{:S(2)}, u32[]{:S(2)}) async-start(bf16[32,3,4,16,256]{4,3,2,1,0:T(8,128)(2,1)} %outward.1), calls=%async_computation | async-start | bytes 6291456 | tf_op jit(solution)/shard_map/all_to_all | solution.py:416
  12.5 2.5 %outward_near.1 = (bf16[4,4,16,256]{3,2,1,0:T(8,128)(2,1)S(1)}, bf16[4,4,16,256]{3,2,1,0:T(8,128)(2,1)S(1)}, bf16[4,4,16,256]{3,2,1,0:T(8,128)(2,1)S(1)}, bf16[4...) custom-call(s32[4]{0:T(128)S(1)} %pad_add_fusion.place_ref, ...), custom_call_target="tpu_custom_call" | custom-call | bytes 2097152 | tf_op jit(solution)/shard_map/outward_near/pallas_call | solution.py:310
  15.3 1.7 %collective-permute-start.1 = (bf16[4,4,16,256]{3,2,1,0:T(8,128)(2,1)S(1)}, bf16[4,4,16,256]{3,2,1,0:T(8,128)(2,1)S(1)}, u32[]{:S(2)}, u32[]{:S(2)}) collective-permute-start(bf16[4,4,16,256]{3,2,1,0:T(8,128)(2,1)S(1)} %get-tuple-element.27), channel_id=1, source_target_pairs={{0,2},{1,3},{2,0},{3,1},{4,6},{5,7},{6,4},{7,5},{8,10},{9,11},{10,... | collective-permute-start | bytes 393224 | tf_op jit(solution)/shard_map/ppermute | solution.py:413
  17.0 1.7 %collective-permute-start.3 = (bf16[4,4,16,256]{3,2,1,0:T(8,128)(2,1)}, bf16[4,4,16,256]{3,2,1,0:T(8,128)(2,1)}, u32[]{:S(2)}, u32[]{:S(2)}) collective-permute-start(bf16[4,4,16,256]{3,2,1,0:T(8,128)(2,1)} %get-tuple-element.29), channel_id=1, source_target_pairs={{0,16},{1,17},{2,18},{3,19},{4,20},{5,21},{6,22},{7,23},{8,24},{9,... | collective-permute-start | bytes 393224 | tf_op jit(solution)/shard_map/ppermute | solution.py:413
  19.4 2.6 %collective-permute-start.5 = (bf16[4,4,16,256]{3,2,1,0:T(8,128)(2,1)}, bf16[4,4,16,256]{3,2,1,0:T(8,128)(2,1)S(1)}, u32[]{:S(2)}, u32[]{:S(2)}) collective-permute-start(bf16[4,4,16,256]{3,2,1,0:T(8,128)(2,1)} %get-tuple-element.31), channel_id=1, source_target_pairs={{0,18},{1,19},{2,16},{3,17},{4,22},{5,23},{6,20},{7,21},{8,26},{9,... | collective-permute-start | bytes 393224 | tf_op jit(solution)/shard_map/ppermute | solution.py:413
  22.0 14.6 %collective-permute-done.1.refs_2_ = bf16[4,4,16,256]{3,2,1,0:T(8,128)(2,1)S(1)} collective-permute-done((bf16[4,4,16,256]{3,2,1,0:T(8,128)(2,1)S(1)}, bf16[4,4,16,256]{3,2,1,0:T(8,128)(2,1)S(1)}, u32[]{:S(2)}, u32[]{:S(2)}) %collective-permute-start.1) | collective-permute-done | bytes 131104 | tf_op jit(solution)/shard_map/ppermute | solution.py:413
  37.2 2.4 %collective-permute-start.6 = (bf16[4,4,16,256]{3,2,1,0:T(8,128)(2,1)}, bf16[4,4,16,256]{3,2,1,0:T(8,128)(2,1)S(1)}, u32[]{:S(2)}, u32[]{:S(2)}) collective-permute-start(bf16[4,4,16,256]{3,2,1,0:T(8,128)(2,1)} %get-tuple-element.32), channel_id=1, source_target_pairs={{0,19},{1,18},{2,17},{3,16},{4,23},{5,22},{6,21},{7,20},{8,27},{9,... | collective-permute-start | bytes 393224 | tf_op jit(solution)/shard_map/ppermute | solution.py:413
  39.8 2.1 %collective-permute-done.2.refs_3_ = bf16[4,4,16,256]{3,2,1,0:T(8,128)(2,1)} collective-permute-done((bf16[4,4,16,256]{3,2,1,0:T(8,128)(2,1)}, bf16[4,4,16,256]{3,2,1,0:T(8,128)(2,1)}, u32[]{:S(2)}, u32[]{:S(2)}) %collective-permute-start.2) | collective-permute-done | bytes 131104 | tf_op jit(solution)/shard_map/ppermute | solution.py:413
  41.9 9.5 %collective-permute-done.5.refs_6_ = bf16[4,4,16,256]{3,2,1,0:T(8,128)(2,1)S(1)} collective-permute-done((bf16[4,4,16,256]{3,2,1,0:T(8,128)(2,1)}, bf16[4,4,16,256]{3,2,1,0:T(8,128)(2,1)S(1)}, u32[]{:S(2)}, u32[]{:S(2)}) %collective-permute-start.5) | collective-permute-done | bytes 131104 | tf_op jit(solution)/shard_map/ppermute | solution.py:413
  51.3 0.7 copy-done.4
  52.0 1.9 %collective-permute-done.6.refs_7_ = bf16[4,4,16,256]{3,2,1,0:T(8,128)(2,1)S(1)} collective-permute-done((bf16[4,4,16,256]{3,2,1,0:T(8,128)(2,1)}, bf16[4,4,16,256]{3,2,1,0:T(8,128)(2,1)S(1)}, u32[]{:S(2)}, u32[]{:S(2)}) %collective-permute-start.6) | collective-permute-done | bytes 131104 | tf_op jit(solution)/shard_map/ppermute | solution.py:413
  54.5 0.9 copy-done.1
  55.4 0.9 copy-done.3
  56.3 0.9 copy-done.5
  57.2 0.9 copy-done.7
  58.1 1.9 %regroup.1 = (bf16[8,4,16,256]{3,2,1,0:T(8,128)(2,1)S(1)}, bf16[8,4,16,256]{3,2,1,0:T(8,128)(2,1)}, bf16[8,4,16,256]{3,2,1,0:T(8,128)(2,1)}, bf16[8,4,16,256]{3,2,1,0:T(8,128)(2,1)S(1)}) custom-call(bf16[4,4,16,256]{3,2,1,0:T(8,128)(2,1)S(1)} %get-tuple-element.25.refs_0_, bf16[4,4,16,256]{3,2,1,0:T(8,128)(2,1)S(1)} %copy-done.1, ...), custom_call_target="tpu_custom_call" | custom-call | bytes 2097152 | tf_op jit(solution)/shard_map/regroup/pallas_call | solution.py:334
  60.0 0.7 copy-done.8
  60.7 4.8 %collective-permute-start.8 = (bf16[8,4,16,256]{3,2,1,0:T(8,128)(2,1)}, bf16[8,4,16,256]{3,2,1,0:T(8,128)(2,1)}, u32[]{:S(2)}, u32[]{:S(2)}) collective-permute-start(bf16[8,4,16,256]{3,2,1,0:T(8,128)(2,1)} %get-tuple-element.40), channel_id=1, source_target_pairs={{0,8},{1,9},{2,10},{3,11},{4,12},{5,13},{6,14},{7,15},{8,0},{9,1},... | collective-permute-start | bytes 786440 | tf_op jit(solution)/shard_map/ppermute | solution.py:413
  65.5 25.8 %all-to-all-done = bf16[32,3,4,16,256]{4,3,2,1,0:T(8,128)(2,1)S(1)} async-done(((bf16[32,3,4,16,256]{4,3,2,1,0:T(8,128)(2,1)}), bf16[32,3,4,16,256]{4,3,2,1,0:T(8,128)(2,1)S(1)}, u32[]{:S(2)}, u32[]{:S(2)}) %all-to-all-start) | async-done | bytes 3145760 | tf_op jit(solution)/shard_map/all_to_all | solution.py:416
  91.2 10.5 %conv.1 = (bf16[2,16,2,4,16,256]{5,4,3,2,1,0:T(8,128)(2,1)S(1)}, f32[4,2,256,256]{3,2,1,0:T(8,128)S(1)}, f32[4,2,144,512]{3,2,1,0:T(8,128)S(1)}, f32[4,2,144,256...) custom-call(f32[4]{0:T(128)S(1)} %dynamic_slice.3.gain_ref, ...), custom_call_target="tpu_custom_call" | custom-call | flops 4026531840 | bytes 8388608 | tf_op jit(solution)/shard_map/conv/pallas_call | solution.py:200
  101.8 2.7 %grad.1 = bf16[2,16,2,4,16,256]{5,4,3,2,1,0:T(8,128)(2,1)S(1)} custom-call(s32[4]{0:T(128)S(1)} %pad_add_fusion.place_ref, bf16[2,16,3,4,16,256]{5,4,3,2,1,0:T(8,128)(2,1)S(1)} %bitcast.10, f32[4,2,256,256]{3,2,1,0:T(8,128)S(1)} %get-tuple-element.35.gap_ref, f32[4,2,144,512]{3,2,1,0:T(8,128)S(1)} %get-tuple-element.36.spec_ref, ...), custom_call_target="tpu_custom_call", output_to_operand_aliasing={{}: (12, {})} | custom-call | flops 805306368 | bytes 8388608 | tf_op jit(solution)/shard_map/grad/pallas_call | solution.py:226
  104.5 56.8 %all_to_all.10.last_ref = bf16[32,2,4,16,256]{4,3,2,1,0:T(8,128)(2,1)S(1)} all-to-all(bf16[32,2,4,16,256]{4,3,2,1,0:T(8,128)(2,1)S(1)} %bitcast.11), channel_id=1, replica_groups=mesh['dp'=2,'ctx'=16] {'dp','ctx'}, dimensions={0} | all-to-all | bytes 4194304 | tf_op jit(solution)/shard_map/all_to_all | solution.py:426
  161.4 3.5 %homeward.1 = (bf16[16,256,128]{2,1,0:T(8,128)(2,1)}, f32[2,16,128,128]{3,2,1,0:T(8,128)}) custom-call(s32[4]{0:T(128)S(1)} %pad_add_fusion.place_ref, bf16[32,2,4,16,256]{4,3,2,1,0:T(8,128)(2,1)S(1)} %all_to_all.10.last_ref), custom_call_target="tpu_custom_call" | custom-call | bytes 5242880 | tf_op jit(solution)/shard_map/homeward/pallas_call | solution.py:379
  (27 shorter events, 2.5 us)
Async XLA Ops:
  5.2 34.5 %copy-start.9 = (f32[128]{0:T(128)S(1)}, f32[128]{0:T(128)}, u32[]{:S(2)}) copy-start(f32[128]{0:T(128)} %param.15) | copy-start | bytes 1540
  5.2 86.0 %all-to-all-start = ((bf16[32,3,4,16,256]{4,3,2,1,0:T(8,128)(2,1)}), bf16[32,3,4,16,256]{4,3,2,1,0:T(8,128)(2,1)S(1)}, u32[]{:S(2)}, u32[]{:S(2)}) async-start(bf16[32,3,4,16,256]{4,3,2,1,0:T(8,128)(2,1)} %outward.1), calls=%async_computation | async-start | bytes 6291456 | tf_op jit(solution)/shard_map/all_to_all | solution.py:416
  15.0 3.8 %collective-permute-start = (bf16[4,4,16,256]{3,2,1,0:T(8,128)(2,1)S(1)}, bf16[4,4,16,256]{3,2,1,0:T(8,128)(2,1)S(1)}, u32[]{:S(2)}, u32[]{:S(2)}) collective-permute-start(bf16[4,4,16,256]{3,2,1,0:T(8,128)(2,1)S(1)} %get-tuple-element.26), channel_id=1, source_target_pairs={{0,1},{1,0},{2,3},{3,2},{4,5},{5,4},{6,7},{7,6},{8,9},{9,8},{10,11... | collective-permute-start | bytes 393224 | tf_op jit(solution)/shard_map/ppermute | solution.py:413
  15.3 21.3 %collective-permute-start.1 = (bf16[4,4,16,256]{3,2,1,0:T(8,128)(2,1)S(1)}, bf16[4,4,16,256]{3,2,1,0:T(8,128)(2,1)S(1)}, u32[]{:S(2)}, u32[]{:S(2)}) collective-permute-start(bf16[4,4,16,256]{3,2,1,0:T(8,128)(2,1)S(1)} %get-tuple-element.27), channel_id=1, source_target_pairs={{0,2},{1,3},{2,0},{3,1},{4,6},{5,7},{6,4},{7,5},{8,10},{9,11},{10,... | collective-permute-start | bytes 393224 | tf_op jit(solution)/shard_map/ppermute | solution.py:413
  17.0 24.9 %collective-permute-start.2 = (bf16[4,4,16,256]{3,2,1,0:T(8,128)(2,1)}, bf16[4,4,16,256]{3,2,1,0:T(8,128)(2,1)}, u32[]{:S(2)}, u32[]{:S(2)}) collective-permute-start(bf16[4,4,16,256]{3,2,1,0:T(8,128)(2,1)} %get-tuple-element.28), channel_id=1, source_target_pairs={{0,3},{1,2},{2,1},{3,0},{4,7},{5,6},{6,5},{7,4},{8,11},{9,10},{10,... | collective-permute-start | bytes 393224 | tf_op jit(solution)/shard_map/ppermute | solution.py:413
  17.0 24.9 %collective-permute-start.3 = (bf16[4,4,16,256]{3,2,1,0:T(8,128)(2,1)}, bf16[4,4,16,256]{3,2,1,0:T(8,128)(2,1)}, u32[]{:S(2)}, u32[]{:S(2)}) collective-permute-start(bf16[4,4,16,256]{3,2,1,0:T(8,128)(2,1)} %get-tuple-element.29), channel_id=1, source_target_pairs={{0,16},{1,17},{2,18},{3,19},{4,20},{5,21},{6,22},{7,23},{8,24},{9,... | collective-permute-start | bytes 393224 | tf_op jit(solution)/shard_map/ppermute | solution.py:413
  18.7 23.2 %collective-permute-start.4 = (bf16[4,4,16,256]{3,2,1,0:T(8,128)(2,1)}, bf16[4,4,16,256]{3,2,1,0:T(8,128)(2,1)}, u32[]{:S(2)}, u32[]{:S(2)}) collective-permute-start(bf16[4,4,16,256]{3,2,1,0:T(8,128)(2,1)} %get-tuple-element.30), channel_id=1, source_target_pairs={{0,17},{1,16},{2,19},{3,18},{4,21},{5,20},{6,23},{7,22},{8,25},{9,... | collective-permute-start | bytes 393224 | tf_op jit(solution)/shard_map/ppermute | solution.py:413
  18.8 0.6 copy-start
  19.4 31.9 %collective-permute-start.5 = (bf16[4,4,16,256]{3,2,1,0:T(8,128)(2,1)}, bf16[4,4,16,256]{3,2,1,0:T(8,128)(2,1)S(1)}, u32[]{:S(2)}, u32[]{:S(2)}) collective-permute-start(bf16[4,4,16,256]{3,2,1,0:T(8,128)(2,1)} %get-tuple-element.31), channel_id=1, source_target_pairs={{0,18},{1,19},{2,16},{3,17},{4,22},{5,23},{6,20},{7,21},{8,26},{9,... | collective-permute-start | bytes 393224 | tf_op jit(solution)/shard_map/ppermute | solution.py:413
  36.6 0.6 copy-start.2
  37.2 16.6 %collective-permute-start.6 = (bf16[4,4,16,256]{3,2,1,0:T(8,128)(2,1)}, bf16[4,4,16,256]{3,2,1,0:T(8,128)(2,1)S(1)}, u32[]{:S(2)}, u32[]{:S(2)}) collective-permute-start(bf16[4,4,16,256]{3,2,1,0:T(8,128)(2,1)} %get-tuple-element.32), channel_id=1, source_target_pairs={{0,19},{1,18},{2,17},{3,16},{4,23},{5,22},{6,21},{7,20},{8,27},{9,... | collective-permute-start | bytes 393224 | tf_op jit(solution)/shard_map/ppermute | solution.py:413
  51.3 0.7 copy-start.4
  53.9 0.7 copy-start.6
  54.5 0.9 copy-start.1
  55.4 0.9 copy-start.3
  56.3 0.9 copy-start.5
  57.2 0.9 copy-start.7
  60.0 0.7 copy-start.8
  60.7 41.1 %collective-permute-start.7 = (bf16[8,4,16,256]{3,2,1,0:T(8,128)(2,1)}, bf16[8,4,16,256]{3,2,1,0:T(8,128)(2,1)}, u32[]{:S(2)}, u32[]{:S(2)}) collective-permute-start(bf16[8,4,16,256]{3,2,1,0:T(8,128)(2,1)} %get-tuple-element.39), channel_id=1, source_target_pairs={{0,4},{1,5},{2,6},{3,7},{4,0},{5,1},{6,2},{7,3},{8,12},{9,13},{10,... | collective-permute-start | bytes 786440 | tf_op jit(solution)/shard_map/ppermute | solution.py:413
  60.7 41.1 %collective-permute-start.8 = (bf16[8,4,16,256]{3,2,1,0:T(8,128)(2,1)}, bf16[8,4,16,256]{3,2,1,0:T(8,128)(2,1)}, u32[]{:S(2)}, u32[]{:S(2)}) collective-permute-start(bf16[8,4,16,256]{3,2,1,0:T(8,128)(2,1)} %get-tuple-element.40), channel_id=1, source_target_pairs={{0,8},{1,9},{2,10},{3,11},{4,12},{5,13},{6,14},{7,15},{8,0},{9,1},... | collective-permute-start | bytes 786440 | tf_op jit(solution)/shard_map/ppermute | solution.py:413
  91.2 10.5 %collective-permute-start.9 = (bf16[8,4,16,256]{3,2,1,0:T(8,128)(2,1)}, bf16[8,4,16,256]{3,2,1,0:T(8,128)(2,1)S(1)}, u32[]{:S(2)}, u32[]{:S(2)}) collective-permute-start(bf16[8,4,16,256]{3,2,1,0:T(8,128)(2,1)} %copy-done.8), channel_id=1, source_target_pairs={{0,12},{1,13},{2,14},{3,15},{4,8},{5,9},{6,10},{7,11},{8,4},{9,5},... | collective-permute-start | bytes 786440 | tf_op jit(solution)/shard_map/ppermute | solution.py:413

commit v6 on v5

--- a/solution.py
+++ b/solution.py
@@ -42,9 +42,14 @@
     return jnp.dot(a, b, preferred_element_type=F32)
 
 
-def near_device(place_ref, j, hop, plane, hops):
-    far = (place_ref[0] ^ (j // plane)) * hops + (place_ref[1] ^ hop)
-    return far * plane + (place_ref[2] ^ (j % plane))
+def place(plane):
+    c = lax.axis_index("ctx")
+    return lax.axis_index("dp"), c // plane, c % plane
+
+
+def near_device(here, j, hop, plane, hops):
+    far = (here[0] ^ (j // plane)) * hops + (here[1] ^ hop)
+    return far * plane + (here[2] ^ (j % plane))
 
 
 def forward(signals, split_ref, fwd_ref, tw_cos, tw_sin):
@@ -141,16 +146,17 @@
     part_ref[q, 1] = total_imag
 
 
-def grad_kernel(place_ref, recv_ref, gap_ref, spec_ref, part_ref, *refs, hops):
+def grad_kernel(recv_ref, gap_ref, spec_ref, part_ref, *refs, hops):
     cot_refs, refs = refs[:hops], refs[hops:]
     split_ref, fwd_ref, tw_ref, _, send_ref, cot_rows = refs
     count, ctx = recv_ref.shape[:2]
     near = cot_refs[0].shape[0]
     plane = near // count
+    here = place(plane)
     per = recv_ref.shape[3]
     for hop, cot_ref in enumerate(cot_refs):
         for j in range(near):
-            cot_rows[near_device(place_ref, j, hop, plane, hops)] = cot_ref[j]
+            cot_rows[near_device(here, j, hop, plane, hops)] = cot_ref[j]
     errors = []
     for q in range(per):
         for d in range(count):
@@ -219,17 +225,14 @@
     )(gain, received, *[far(t) for t in tabs])
 
 
-def grad_call(place, received, kept, cots, send):
+def grad_call(received, kept, cots, send):
     dp, ctx, _, per, rows, _ = received.shape
     *kept, split_rows, forward_table, twiddle = [near(x) for x in kept]
-    operands = (place, received, *kept, *[near(x) for x in cots], split_rows, forward_table, twiddle, near(send))
+    operands = (received, *kept, *[near(x) for x in cots], split_rows, forward_table, twiddle, near(send))
     return pl.pallas_call(
         functools.partial(grad_kernel, hops=len(cots)),
         grid=(1,),
-        in_specs=[
-            pl.BlockSpec(memory_space=pltpu.SMEM),
-            *[pl.BlockSpec(memory_space=pltpu.VMEM)] * (len(operands) - 1),
-        ],
+        in_specs=[pl.BlockSpec(memory_space=pltpu.VMEM)] * len(operands),
         out_specs=pl.BlockSpec(memory_space=pltpu.VMEM),
         out_shape=pltpu.VMEM(send.shape, BF16),
         scratch_shapes=[pltpu.VMEM((dp * ctx, per, rows, N2), BF16)],
@@ -240,7 +243,7 @@
     )(*operands)
 
 
-def outward_kernel(place_ref, *refs, count):
+def outward_kernel(*refs, count):
     in_refs, refs = refs[:count], refs[count:]
     out_ref, refs = refs[0], refs[1:]
     held_refs, (rows_ref, ready_ref, load_sems, store_sems) = refs[:count], refs[count:]
@@ -249,7 +252,7 @@
     width = rows_ref.shape[2]
     loads, stores = [], []
     for t, (in_ref, held_ref) in enumerate(zip(in_refs, held_refs)):
-        source = in_ref.at[place_ref[0] if in_ref.shape[0] > 1 else 0]
+        source = in_ref.at[lax.axis_index("dp") if in_ref.shape[0] > 1 else 0]
         loads.append(pltpu.make_async_copy(source, held_ref, load_sems.at[t]))
         loads[t].start()
     for t, held_ref in enumerate(held_refs):
@@ -267,15 +270,15 @@
         store.wait()
 
 
-def outward(place, arrays, devices):
+def outward(arrays, devices):
     _, rows, _, channels = arrays[0].shape
     count, per, width, pitch = len(arrays), channels // devices, 128, rows + 8
     shape = (devices, count, per, rows, N2)
     return pl.pallas_call(
         functools.partial(outward_kernel, count=count),
-        in_specs=[pl.BlockSpec(memory_space=pltpu.SMEM), *[pl.BlockSpec(memory_space=pl.ANY)] * count],
+        in_specs=[pl.BlockSpec(memory_space=pl.ANY)] * count,
         out_specs=pl.BlockSpec(memory_space=pl.ANY),
-        out_shape=jax.ShapeDtypeStruct(shape, BF16),
+        out_shape=pltpu.HBM(shape, BF16),
         scratch_shapes=[
             *[pltpu.VMEM(a.shape[1:], a.dtype) for a in arrays],
             pltpu.VMEM((N2 // width, channels * pitch, width), F32),
@@ -286,10 +289,11 @@
         compiler_params=pltpu.CompilerParams(vmem_limit_bytes=VMEM),
         cost_estimate=pl.CostEstimate(flops=0, bytes_accessed=7 << 20, transcendentals=0),
         name="outward",
-    )(place, *arrays)
-
-
-def outward_near_kernel(place_ref, in_ref, *refs, hops, plane):
+    )(*arrays)
+
+
+def outward_near_kernel(in_ref, *refs, hops, plane):
+    here = place(plane)
     *out_refs, rows_ref = refs
     _, per, rows, width = out_refs[0].shape
     channels = in_ref.shape[3]
@@ -298,29 +302,26 @@
         rows_ref[pl.ds(r, channels, stride=pitch), :] = in_ref[0, r].T.astype(F32)
     for j, out_ref in enumerate(out_refs):
         for hop in range(hops):
-            block = near_device(place_ref, j, hop, plane, hops) * (per * pitch)
+            block = near_device(here, j, hop, plane, hops) * (per * pitch)
             rows_here = rows_ref[pl.ds(pl.multiple_of(block, per * pitch), per * pitch), :]
             out_ref[hop] = rows_here.reshape(per, pitch, width)[:, :rows].astype(BF16)
 
 
-def outward_near(place, x, count, hops, plane):
+def outward_near(x, count, hops, plane):
     _, rows, _, channels = x.shape
     per = channels // count
     width = 128
     return pl.pallas_call(
         functools.partial(outward_near_kernel, hops=hops, plane=plane),
         grid=(N2 // width,),
-        in_specs=[
-            pl.BlockSpec(memory_space=pltpu.SMEM),
-            pl.BlockSpec((1, rows, width, channels), lambda h: (0, 0, h, 0)),
-        ],
+        in_specs=[pl.BlockSpec((1, rows, width, channels), lambda h: (0, 0, h, 0))],
         out_specs=[pl.BlockSpec((hops, per, rows, width), lambda h: (0, 0, 0, h))] * (count // hops),
         out_shape=[jax.ShapeDtypeStruct((hops, per, rows, N2), BF16)] * (count // hops),
         scratch_shapes=[pltpu.VMEM((channels * (rows + 8), width), F32)],
         compiler_params=pltpu.CompilerParams(vmem_limit_bytes=VMEM),
         cost_estimate=pl.CostEstimate(flops=0, bytes_accessed=2 << 20, transcendentals=0),
         name="outward_near",
-    )(place, x)
+    )(x)
 
 
 def regroup_kernel(*refs, count):
@@ -340,57 +341,49 @@
     )(*arrays)
 
 
-def homeward_kernel(place_ref, last_ref, y_hbm, grad_hbm, y_ref, grad_ref, rows_ref, sems):
+def homeward_kernel(last_ref, y_ref, grad_ref, rows_ref):
     count, _, per, rows, _ = last_ref.shape
     width = rows_ref.shape[2]
     pitch = rows_ref.shape[1] // (count * per)
-    lower = place_ref[1] >= place_ref[3]
+    h = pl.program_id(0)
+    lanes = pl.ds(pl.multiple_of(h * width, width), width)
+    lower = lax.axis_index("ctx") >= lax.axis_size("ctx") // 2
     row = lax.broadcasted_iota(jnp.int32, (width, width), 0)
     col = lax.broadcasted_iota(jnp.int32, (width, width), 1)
     turn = (col == jnp.where(lower, width - 1 - row, row)).astype(F32)
-    copies = []
-    for step, (t, h) in enumerate(((1, 0), (1, 1), (0, 0), (0, 1))):
-        lanes = slice(h * width, (h + 1) * width)
-        block = last_ref[:, t, :, :, lanes].astype(F32)
-        rows_ref.at[step].reshape(count, per, pitch, width)[:, :, :rows] = block
-        sign = jnp.where(lower, -1.0, 1.0) if h else 1.0
-        pick = (turn * sign).astype(BF16)
-        for r in range(rows):
-            slot = jnp.where(lower, (rows - r) % rows, r) if t else r
-            block = rows_ref[step, pl.ds(slot, count * per, stride=pitch), :].astype(BF16)
-            if t:
-                grad_ref[h, r] = lax.dot_general(pick, block, (((1,), (1,)), ((), ())), preferred_element_type=F32)
-            else:
-                y_ref[r, lanes] = block.T
+    turn = (turn * jnp.where(lower, (1 - 2 * h).astype(F32), 1.0)).astype(BF16)
+    for t in range(2):
+        block = last_ref[:, t, :, :, lanes]
         if t:
-            copies.append(pltpu.make_async_copy(grad_ref.at[h], grad_hbm.at[h], sems.at[step]))
-        else:
-            here = pl.ds(h * width, width)
-            copies.append(pltpu.make_async_copy(y_ref.at[:, here], y_hbm.at[:, here], sems.at[step]))
-        copies[step].start()
-    for copy in copies:
-        copy.wait()
-
-
-def homeward(place, last):
+            block = dot(block.reshape(count * per * rows, width), turn).reshape(block.shape)
+        rows_ref.at[t].reshape(count, per, pitch, width)[:, :, :rows] = block.astype(F32)
+    for r in range(rows):
+        y_ref[r] = rows_ref[0, pl.ds(r, count * per, stride=pitch), :].astype(BF16).T
+    for r in range(rows):
+        target = jnp.where(lower, (rows - r) % rows, r)
+        grad_ref[0, target] = rows_ref[1, pl.ds(r, count * per, stride=pitch), :].T
+
+
+def homeward(last):
     count, _, per, rows, _ = last.shape
     channels, width, pitch = count * per, 128, rows + 8
-    y_shape, grad_shape = (rows, N2, channels), (2, rows, width, channels)
     return pl.pallas_call(
         homeward_kernel,
-        in_specs=[pl.BlockSpec(memory_space=pltpu.SMEM), pl.BlockSpec(memory_space=pltpu.VMEM)],
-        out_specs=[pl.BlockSpec(memory_space=pl.ANY)] * 2,
-        out_shape=[jax.ShapeDtypeStruct(y_shape, BF16), jax.ShapeDtypeStruct(grad_shape, F32)],
-        scratch_shapes=[
-            pltpu.VMEM(y_shape, BF16),
-            pltpu.VMEM(grad_shape, F32),
-            pltpu.VMEM((4, channels * pitch, width), F32),
-            pltpu.SemaphoreType.DMA((4,)),
+        grid=(N2 // width,),
+        in_specs=[pl.BlockSpec(memory_space=pltpu.VMEM)],
+        out_specs=[
+            pl.BlockSpec((rows, width, channels), lambda h: (0, h, 0)),
+            pl.BlockSpec((1, rows, width, channels), lambda h: (h, 0, 0, 0)),
         ],
+        out_shape=[
+            jax.ShapeDtypeStruct((rows, N2, channels), BF16),
+            jax.ShapeDtypeStruct((2, rows, width, channels), F32),
+        ],
+        scratch_shapes=[pltpu.VMEM((2, channels * pitch, width), F32)],
         compiler_params=pltpu.CompilerParams(vmem_limit_bytes=VMEM),
         cost_estimate=pl.CostEstimate(flops=0, bytes_accessed=5 << 20, transcendentals=0),
         name="homeward",
-    )(place, near(last))
+    )(near(last))
 
 
 def by_channel_body(embeds, perturb, cotangent, filter_spectrum, skip_gain):
@@ -404,7 +397,6 @@
     plane = 4
     hops = ctx // plane
     tabs = tables()
-    place = jnp.stack([d, c // plane, c % plane, jnp.int32(hops // 2)])
 
     def matrix(x):
         return far(x.reshape(1, rows, N2, channels))
@@ -412,9 +404,9 @@
     def exchange(x, mask):
         return lax.ppermute(x, axes, [(i, i ^ mask) for i in range(count)]) if mask else x
 
-    first = outward(place, [matrix(embeds), matrix(perturb), far(filter_spectrum)], count)
+    first = outward([matrix(embeds), matrix(perturb), far(filter_spectrum)], count)
     received = lax.all_to_all(first, axes, 0, 0, tiled=True).reshape(dp, ctx, 3, per, rows, N2)
-    cots = outward_near(place, matrix(cotangent), count, hops, plane)
+    cots = outward_near(matrix(cotangent), count, hops, plane)
     cots = regroup([exchange(x, j // plane * ctx + j % plane) for j, x in enumerate(cots)])
     received = near(received)
     *early, late = cots
@@ -422,9 +414,9 @@
     cots = [exchange(x, hop * plane) for hop, x in enumerate([*early, late])]
     gain = lax.dynamic_slice(skip_gain, ((d * ctx + c) * per,), (per,))
     send, *kept = conv_call(gain, received, tabs)
-    send = grad_call(place, received, kept, cots, send)
+    send = grad_call(received, kept, cots, send)
     last = lax.all_to_all(send.reshape(count, 2, per, rows, N2), axes, 0, 0, tiled=True)
-    y, grad = homeward(place, last)
+    y, grad = homeward(last)
     return y.reshape(1, rows * N2, channels), grad
 
 

time: 165 us -> 164 us (level)
  no operation moved by 1% of the time
where the time goes in v6:
time: 164 us; the launch traced here: 163 us
  blocking collectives  56.9 us (35%)
  waiting for transfers between devices  53.8 us (33%)
  Pallas kernels  23.9 us (15%)
  starting transfers between devices  20.9 us (13%)
  local copies, waits for them, and re-layouts  6.98 us (4%)
    all_to_all x1, blocking collectives, by_channel_body(): lax.all_to_all(send.reshape(count, 2, per, rows, N2), axes, 0, 0, tiled=T...  56.9 us
    ppermute x10, waiting for transfers between devices, exchange(): lax.ppermute(x, axes, [(i, i ^ mask) for i in range(count)])  28.1 us
    all_to_all x1, waiting for transfers between devices, by_channel_body(): lax.all_to_all(first, axes, 0, 0, tiled=True)  25.8 us
    ppermute x10, starting transfers between devices, exchange(): lax.ppermute(x, axes, [(i, i ^ mask) for i in range(count)])  13.6 us
    pallas_call x1, Pallas kernels, conv_call(): pl.pallas_call(conv_kernel, grid=(per,), in_specs=[pl.BlockSpec(memory_sp...  10.4 us
    all_to_all x1, starting transfers between devices, by_channel_body(): lax.all_to_all(first, axes, 0, 0, tiled=True)  7.3 us
    unnamed x20, local copies, waits for them, and re-layouts  6.91 us
    pallas_call x1, Pallas kernels, outward(): pl.pallas_call(functools.partial(outward_kernel, count=count), in_specs=[...  3.94 us
  transfers between devices with their start and end apart: 11, of which 5 were waited for; matrix products, arithmetic and copies ran while one was open for 0% of the time, Pallas kernels for 9%

profile of v6, /device:TPU:0, one launch (start us, length us, event | category | flops | bytes accessed | tf_op | source)
XLA Modules:
  0.0 163.2 jit_solution(8226141224684345693)
XLA Ops:
  0.6 3.9 %outward.1 = bf16[32,3,4,16,256]{4,3,2,1,0:T(8,128)(2,1)} custom-call(bf16[1,16,256,128]{3,2,1,0:T(8,128)(2,1)} %bitcast.9, bf16[1,16,256,128]{3,2,1,0:T(8,128)(2,1)} %bitcast.10, f32[2,16,256,128]{3,2,1,0:T(8,128)} %refs_2_.1), custom_call_target="tpu_custom_call" | custom-call | bytes 7340032 | tf_op jit(solution)/shard_map/outward/pallas_call | solution.py:277
  4.6 7.3 %all-to-all-start = ((bf16[32,3,4,16,256]{4,3,2,1,0:T(8,128)(2,1)}), bf16[32,3,4,16,256]{4,3,2,1,0:T(8,128)(2,1)S(1)}, u32[]{:S(2)}, u32[]{:S(2)}) async-start(bf16[32,3,4,16,256]{4,3,2,1,0:T(8,128)(2,1)} %outward.1), calls=%async_computation | async-start | bytes 6291456 | tf_op jit(solution)/shard_map/all_to_all | solution.py:408
  11.9 2.4 %outward_near.1 = (bf16[4,4,16,256]{3,2,1,0:T(8,128)(2,1)S(1)}, bf16[4,4,16,256]{3,2,1,0:T(8,128)(2,1)S(1)}, bf16[4,4,16,256]{3,2,1,0:T(8,128)(2,1)S(1)}, bf16[4...) custom-call(bf16[1,16,256,128]{3,2,1,0:T(8,128)(2,1)} %bitcast.11), custom_call_target="tpu_custom_call" | custom-call | bytes 2097152 | tf_op jit(solution)/shard_map/outward_near/pallas_call | solution.py:314
  14.6 1.7 %collective-permute-start.1 = (bf16[4,4,16,256]{3,2,1,0:T(8,128)(2,1)S(1)}, bf16[4,4,16,256]{3,2,1,0:T(8,128)(2,1)S(1)}, u32[]{:S(2)}, u32[]{:S(2)}) collective-permute-start(bf16[4,4,16,256]{3,2,1,0:T(8,128)(2,1)S(1)} %get-tuple-element.27), channel_id=1, source_target_pairs={{0,2},{1,3},{2,0},{3,1},{4,6},{5,7},{6,4},{7,5},{8,10},{9,11},{10,... | collective-permute-start | bytes 393224 | tf_op jit(solution)/shard_map/ppermute | solution.py:405
  16.3 1.7 %collective-permute-start.3 = (bf16[4,4,16,256]{3,2,1,0:T(8,128)(2,1)}, bf16[4,4,16,256]{3,2,1,0:T(8,128)(2,1)}, u32[]{:S(2)}, u32[]{:S(2)}) collective-permute-start(bf16[4,4,16,256]{3,2,1,0:T(8,128)(2,1)} %get-tuple-element.29), channel_id=1, source_target_pairs={{0,16},{1,17},{2,18},{3,19},{4,20},{5,21},{6,22},{7,23},{8,24},{9,... | collective-permute-start | bytes 393224 | tf_op jit(solution)/shard_map/ppermute | solution.py:405
  18.8 2.6 %collective-permute-start.5 = (bf16[4,4,16,256]{3,2,1,0:T(8,128)(2,1)}, bf16[4,4,16,256]{3,2,1,0:T(8,128)(2,1)S(1)}, u32[]{:S(2)}, u32[]{:S(2)}) collective-permute-start(bf16[4,4,16,256]{3,2,1,0:T(8,128)(2,1)} %get-tuple-element.31), channel_id=1, source_target_pairs={{0,18},{1,19},{2,16},{3,17},{4,22},{5,23},{6,20},{7,21},{8,26},{9,... | collective-permute-start | bytes 393224 | tf_op jit(solution)/shard_map/ppermute | solution.py:405
  21.3 14.6 %collective-permute-done.1.refs_2_ = bf16[4,4,16,256]{3,2,1,0:T(8,128)(2,1)S(1)} collective-permute-done((bf16[4,4,16,256]{3,2,1,0:T(8,128)(2,1)S(1)}, bf16[4,4,16,256]{3,2,1,0:T(8,128)(2,1)S(1)}, u32[]{:S(2)}, u32[]{:S(2)}) %collective-permute-start.1) | collective-permute-done | bytes 131104 | tf_op jit(solution)/shard_map/ppermute | solution.py:405
  36.6 2.4 %collective-permute-start.6 = (bf16[4,4,16,256]{3,2,1,0:T(8,128)(2,1)}, bf16[4,4,16,256]{3,2,1,0:T(8,128)(2,1)S(1)}, u32[]{:S(2)}, u32[]{:S(2)}) collective-permute-start(bf16[4,4,16,256]{3,2,1,0:T(8,128)(2,1)} %get-tuple-element.32), channel_id=1, source_target_pairs={{0,19},{1,18},{2,17},{3,16},{4,23},{5,22},{6,21},{7,20},{8,27},{9,... | collective-permute-start | bytes 393224 | tf_op jit(solution)/shard_map/ppermute | solution.py:405
  39.1 2.1 %collective-permute-done.2.refs_3_ = bf16[4,4,16,256]{3,2,1,0:T(8,128)(2,1)} collective-permute-done((bf16[4,4,16,256]{3,2,1,0:T(8,128)(2,1)}, bf16[4,4,16,256]{3,2,1,0:T(8,128)(2,1)}, u32[]{:S(2)}, u32[]{:S(2)}) %collective-permute-start.2) | collective-permute-done | bytes 131104 | tf_op jit(solution)/shard_map/ppermute | solution.py:405
  41.2 9.5 %collective-permute-done.5.refs_6_ = bf16[4,4,16,256]{3,2,1,0:T(8,128)(2,1)S(1)} collective-permute-done((bf16[4,4,16,256]{3,2,1,0:T(8,128)(2,1)}, bf16[4,4,16,256]{3,2,1,0:T(8,128)(2,1)S(1)}, u32[]{:S(2)}, u32[]{:S(2)}) %collective-permute-start.5) | collective-permute-done | bytes 131104 | tf_op jit(solution)/shard_map/ppermute | solution.py:405
  50.7 0.7 copy-done.4
  51.4 1.9 %collective-permute-done.6.refs_7_ = bf16[4,4,16,256]{3,2,1,0:T(8,128)(2,1)S(1)} collective-permute-done((bf16[4,4,16,256]{3,2,1,0:T(8,128)(2,1)}, bf16[4,4,16,256]{3,2,1,0:T(8,128)(2,1)S(1)}, u32[]{:S(2)}, u32[]{:S(2)}) %collective-permute-start.6) | collective-permute-done | bytes 131104 | tf_op jit(solution)/shard_map/ppermute | solution.py:405
  53.9 0.9 copy-done.1
  54.8 0.9 copy-done.3
  55.7 0.9 copy-done.5
  56.6 0.9 copy-done.7
  57.5 1.9 %regroup.1 = (bf16[8,4,16,256]{3,2,1,0:T(8,128)(2,1)S(1)}, bf16[8,4,16,256]{3,2,1,0:T(8,128)(2,1)}, bf16[8,4,16,256]{3,2,1,0:T(8,128)(2,1)}, bf16[8,4,16,256]{3,2,1,0:T(8,128)(2,1)S(1)}) custom-call(bf16[4,4,16,256]{3,2,1,0:T(8,128)(2,1)S(1)} %get-tuple-element.25.refs_0_, bf16[4,4,16,256]{3,2,1,0:T(8,128)(2,1)S(1)} %copy-done.1, ...), custom_call_target="tpu_custom_call" | custom-call | bytes 2097152 | tf_op jit(solution)/shard_map/regroup/pallas_call | solution.py:335
  59.4 0.7 copy-done.8
  60.1 4.8 %collective-permute-start.8 = (bf16[8,4,16,256]{3,2,1,0:T(8,128)(2,1)}, bf16[8,4,16,256]{3,2,1,0:T(8,128)(2,1)}, u32[]{:S(2)}, u32[]{:S(2)}) collective-permute-start(bf16[8,4,16,256]{3,2,1,0:T(8,128)(2,1)} %get-tuple-element.40), channel_id=1, source_target_pairs={{0,8},{1,9},{2,10},{3,11},{4,12},{5,13},{6,14},{7,15},{8,0},{9,1},... | collective-permute-start | bytes 786440 | tf_op jit(solution)/shard_map/ppermute | solution.py:405
  64.8 25.8 %all-to-all-done = bf16[32,3,4,16,256]{4,3,2,1,0:T(8,128)(2,1)S(1)} async-done(((bf16[32,3,4,16,256]{4,3,2,1,0:T(8,128)(2,1)}), bf16[32,3,4,16,256]{4,3,2,1,0:T(8,128)(2,1)S(1)}, u32[]{:S(2)}, u32[]{:S(2)}) %all-to-all-start) | async-done | bytes 3145760 | tf_op jit(solution)/shard_map/all_to_all | solution.py:408
  90.6 10.4 %conv.1 = (bf16[2,16,2,4,16,256]{5,4,3,2,1,0:T(8,128)(2,1)S(1)}, f32[4,2,256,256]{3,2,1,0:T(8,128)S(1)}, f32[4,2,144,512]{3,2,1,0:T(8,128)S(1)}, f32[4,2,144,256...) custom-call(f32[4]{0:T(128)S(1)} %dynamic_slice.3.gain_ref, ...), custom_call_target="tpu_custom_call" | custom-call | flops 4026531840 | bytes 8388608 | tf_op jit(solution)/shard_map/conv/pallas_call | solution.py:206
  101.1 2.5 %grad.1 = bf16[2,16,2,4,16,256]{5,4,3,2,1,0:T(8,128)(2,1)S(1)} custom-call(bf16[2,16,3,4,16,256]{5,4,3,2,1,0:T(8,128)(2,1)S(1)} %bitcast.7, f32[4,2,256,256]{3,2,1,0:T(8,128)S(1)} %get-tuple-element.35.gap_ref, f32[4,2,144,512]{3,2,1,0:T(8,128)S(1)} %get-tuple-element.36.spec_ref, ...), custom_call_target="tpu_custom_call", output_to_operand_aliasing={{}: (11, {})} | custom-call | flops 805306368 | bytes 8388608 | tf_op jit(solution)/shard_map/grad/pallas_call | solution.py:232
  103.6 56.9 %all_to_all.10.last_ref = bf16[32,2,4,16,256]{4,3,2,1,0:T(8,128)(2,1)S(1)} all-to-all(bf16[32,2,4,16,256]{4,3,2,1,0:T(8,128)(2,1)S(1)} %bitcast.8), channel_id=1, replica_groups=mesh['dp'=2,'ctx'=16] {'dp','ctx'}, dimensions={0} | all-to-all | bytes 4194304 | tf_op jit(solution)/shard_map/all_to_all | solution.py:418
  160.5 2.7 %homeward.1 = (bf16[16,256,128]{2,1,0:T(8,128)(2,1)}, f32[2,16,128,128]{3,2,1,0:T(8,128)}) custom-call(bf16[32,2,4,16,256]{4,3,2,1,0:T(8,128)(2,1)S(1)} %all_to_all.10.last_ref), custom_call_target="tpu_custom_call" | custom-call | bytes 5242880 | tf_op jit(solution)/shard_map/homeward/pallas_call | solution.py:370
  (26 shorter events, 2.4 us)
Async XLA Ops:
  4.6 34.5 %copy-start.9 = (f32[128]{0:T(128)S(1)}, f32[128]{0:T(128)}, u32[]{:S(2)}) copy-start(f32[128]{0:T(128)} %param.15) | copy-start | bytes 1540
  4.6 86.0 %all-to-all-start = ((bf16[32,3,4,16,256]{4,3,2,1,0:T(8,128)(2,1)}), bf16[32,3,4,16,256]{4,3,2,1,0:T(8,128)(2,1)S(1)}, u32[]{:S(2)}, u32[]{:S(2)}) async-start(bf16[32,3,4,16,256]{4,3,2,1,0:T(8,128)(2,1)} %outward.1), calls=%async_computation | async-start | bytes 6291456 | tf_op jit(solution)/shard_map/all_to_all | solution.py:408
  14.3 3.8 %collective-permute-start = (bf16[4,4,16,256]{3,2,1,0:T(8,128)(2,1)S(1)}, bf16[4,4,16,256]{3,2,1,0:T(8,128)(2,1)S(1)}, u32[]{:S(2)}, u32[]{:S(2)}) collective-permute-start(bf16[4,4,16,256]{3,2,1,0:T(8,128)(2,1)S(1)} %get-tuple-element.26), channel_id=1, source_target_pairs={{0,1},{1,0},{2,3},{3,2},{4,5},{5,4},{6,7},{7,6},{8,9},{9,8},{10,11... | collective-permute-start | bytes 393224 | tf_op jit(solution)/shard_map/ppermute | solution.py:405
  14.6 21.3 %collective-permute-start.1 = (bf16[4,4,16,256]{3,2,1,0:T(8,128)(2,1)S(1)}, bf16[4,4,16,256]{3,2,1,0:T(8,128)(2,1)S(1)}, u32[]{:S(2)}, u32[]{:S(2)}) collective-permute-start(bf16[4,4,16,256]{3,2,1,0:T(8,128)(2,1)S(1)} %get-tuple-element.27), channel_id=1, source_target_pairs={{0,2},{1,3},{2,0},{3,1},{4,6},{5,7},{6,4},{7,5},{8,10},{9,11},{10,... | collective-permute-start | bytes 393224 | tf_op jit(solution)/shard_map/ppermute | solution.py:405
  16.3 24.9 %collective-permute-start.2 = (bf16[4,4,16,256]{3,2,1,0:T(8,128)(2,1)}, bf16[4,4,16,256]{3,2,1,0:T(8,128)(2,1)}, u32[]{:S(2)}, u32[]{:S(2)}) collective-permute-start(bf16[4,4,16,256]{3,2,1,0:T(8,128)(2,1)} %get-tuple-element.28), channel_id=1, source_target_pairs={{0,3},{1,2},{2,1},{3,0},{4,7},{5,6},{6,5},{7,4},{8,11},{9,10},{10,... | collective-permute-start | bytes 393224 | tf_op jit(solution)/shard_map/ppermute | solution.py:405
  16.3 24.9 %collective-permute-start.3 = (bf16[4,4,16,256]{3,2,1,0:T(8,128)(2,1)}, bf16[4,4,16,256]{3,2,1,0:T(8,128)(2,1)}, u32[]{:S(2)}, u32[]{:S(2)}) collective-permute-start(bf16[4,4,16,256]{3,2,1,0:T(8,128)(2,1)} %get-tuple-element.29), channel_id=1, source_target_pairs={{0,16},{1,17},{2,18},{3,19},{4,20},{5,21},{6,22},{7,23},{8,24},{9,... | collective-permute-start | bytes 393224 | tf_op jit(solution)/shard_map/ppermute | solution.py:405
  18.0 23.2 %collective-permute-start.4 = (bf16[4,4,16,256]{3,2,1,0:T(8,128)(2,1)}, bf16[4,4,16,256]{3,2,1,0:T(8,128)(2,1)}, u32[]{:S(2)}, u32[]{:S(2)}) collective-permute-start(bf16[4,4,16,256]{3,2,1,0:T(8,128)(2,1)} %get-tuple-element.30), channel_id=1, source_target_pairs={{0,17},{1,16},{2,19},{3,18},{4,21},{5,20},{6,23},{7,22},{8,25},{9,... | collective-permute-start | bytes 393224 | tf_op jit(solution)/shard_map/ppermute | solution.py:405
  18.1 0.6 copy-start
  18.8 31.9 %collective-permute-start.5 = (bf16[4,4,16,256]{3,2,1,0:T(8,128)(2,1)}, bf16[4,4,16,256]{3,2,1,0:T(8,128)(2,1)S(1)}, u32[]{:S(2)}, u32[]{:S(2)}) collective-permute-start(bf16[4,4,16,256]{3,2,1,0:T(8,128)(2,1)} %get-tuple-element.31), channel_id=1, source_target_pairs={{0,18},{1,19},{2,16},{3,17},{4,22},{5,23},{6,20},{7,21},{8,26},{9,... | collective-permute-start | bytes 393224 | tf_op jit(solution)/shard_map/ppermute | solution.py:405
  36.0 0.6 copy-start.2
  36.6 16.6 %collective-permute-start.6 = (bf16[4,4,16,256]{3,2,1,0:T(8,128)(2,1)}, bf16[4,4,16,256]{3,2,1,0:T(8,128)(2,1)S(1)}, u32[]{:S(2)}, u32[]{:S(2)}) collective-permute-start(bf16[4,4,16,256]{3,2,1,0:T(8,128)(2,1)} %get-tuple-element.32), channel_id=1, source_target_pairs={{0,19},{1,18},{2,17},{3,16},{4,23},{5,22},{6,21},{7,20},{8,27},{9,... | collective-permute-start | bytes 393224 | tf_op jit(solution)/shard_map/ppermute | solution.py:405
  50.7 0.7 copy-start.4
  53.2 0.7 copy-start.6
  53.9 0.9 copy-start.1
  54.8 0.9 copy-start.3
  55.7 0.9 copy-start.5
  56.6 0.9 copy-start.7
  59.4 0.7 copy-start.8
  60.1 41.0 %collective-permute-start.7 = (bf16[8,4,16,256]{3,2,1,0:T(8,128)(2,1)}, bf16[8,4,16,256]{3,2,1,0:T(8,128)(2,1)}, u32[]{:S(2)}, u32[]{:S(2)}) collective-permute-start(bf16[8,4,16,256]{3,2,1,0:T(8,128)(2,1)} %get-tuple-element.39), channel_id=1, source_target_pairs={{0,4},{1,5},{2,6},{3,7},{4,0},{5,1},{6,2},{7,3},{8,12},{9,13},{10,... | collective-permute-start | bytes 786440 | tf_op jit(solution)/shard_map/ppermute | solution.py:405
  60.1 41.0 %collective-permute-start.8 = (bf16[8,4,16,256]{3,2,1,0:T(8,128)(2,1)}, bf16[8,4,16,256]{3,2,1,0:T(8,128)(2,1)}, u32[]{:S(2)}, u32[]{:S(2)}) collective-permute-start(bf16[8,4,16,256]{3,2,1,0:T(8,128)(2,1)} %get-tuple-element.40), channel_id=1, source_target_pairs={{0,8},{1,9},{2,10},{3,11},{4,12},{5,13},{6,14},{7,15},{8,0},{9,1},... | collective-permute-start | bytes 786440 | tf_op jit(solution)/shard_map/ppermute | solution.py:405
  90.6 10.5 %collective-permute-start.9 = (bf16[8,4,16,256]{3,2,1,0:T(8,128)(2,1)}, bf16[8,4,16,256]{3,2,1,0:T(8,128)(2,1)S(1)}, u32[]{:S(2)}, u32[]{:S(2)}) collective-permute-start(bf16[8,4,16,256]{3,2,1,0:T(8,128)(2,1)} %copy-done.8), channel_id=1, source_target_pairs={{0,12},{1,13},{2,14},{3,15},{4,8},{5,9},{6,10},{7,11},{8,4},{9,5},... | collective-permute-start | bytes 786440 | tf_op jit(solution)/shard_map/ppermute | solution.py:405

commit v7 on v6

--- a/solution.py
+++ b/solution.py
@@ -12,6 +12,7 @@
 N2 = 256
 BF16 = jnp.bfloat16
 F32 = jnp.float32
+EARLY = 2
 KEPT = jnp.float32
 HALF = 144
 VMEM = 26 << 20
@@ -89,9 +90,13 @@
 
 def conv_kernel(
     gain_ref, recv_ref, split_ref, fwd_ref, join_ref, mirror_ref, cols_ref, tw_ref,
-    send_ref, gap_ref, spec_ref, part_ref, *held_refs,
+    send_ref, gap_ref, spec_ref, part_ref, *refs,
 ):
+    *refs, y_rows = refs
+    held_refs, early_refs = refs[:3], refs[3:]
     count, ctx = recv_ref.shape[:2]
+    hops, near_count = len(early_refs), early_refs[0].shape[0]
+    here = place(near_count // count)
     q = pl.program_id(0)
 
     @pl.when(q == 0)
@@ -136,7 +141,7 @@
             filtered = conv[:, k * N2 : (k + 1) * N2] + alternate * middle[k]
             pair.append((wide, wide * filtered.astype(BF16).astype(F32) + gain * wide))
         (clean, clean_y), (shifted, shifted_y) = pair
-        send_ref[d, :, 0, q] = clean_y.astype(BF16).reshape(ctx, -1, N2)
+        y_rows[d * ctx : (d + 1) * ctx] = clean_y.astype(BF16).reshape(ctx, -1, N2)
         gap = smart_weight * (shifted_y - clean_y)
         gap_ref[q, d] = gap.astype(gap_ref.dtype)
         spec_ref[q, d] = spectra[2 * d].astype(spec_ref.dtype)
@@ -145,10 +150,23 @@
     part_ref[q, 0] = total_real
     part_ref[q, 1] = total_imag
 
+    @pl.when(q < EARLY)
+    def _():
+        for hop, early_ref in enumerate(early_refs):
+            for j in range(near_count):
+                early_ref[j, q] = y_rows[near_device(here, j, hop, near_count // count, hops)]
+
+    @pl.when(q >= EARLY)
+    def _():
+        for d in range(count):
+            send_ref[d, :, q - EARLY] = y_rows[d * ctx : (d + 1) * ctx]
+
 
 def grad_kernel(recv_ref, gap_ref, spec_ref, part_ref, *refs, hops):
     cot_refs, refs = refs[:hops], refs[hops:]
-    split_ref, fwd_ref, tw_ref, _, send_ref, cot_rows = refs
+    split_ref, fwd_ref, tw_ref, y_ref, send_ref, cot_rows, ready_ref, sems = refs
+    copies = [pltpu.make_async_copy(y_ref, send_ref.at[:, :, pl.ds(0, y_ref.shape[2])], sems.at[0])]
+    copies[0].start()
     count, ctx = recv_ref.shape[:2]
     near = cot_refs[0].shape[0]
     plane = near // count
@@ -167,11 +185,15 @@
     for q in range(per):
         spectra = [spec_ref[q, d] for d in range(count)]
         total = gradient(err_spectra[q * count : (q + 1) * count], spectra)
-        send_grad(send_ref, q, *[t + part_ref[q, i] for i, t in enumerate(total)])
-
-
-def send_grad(send_ref, q, total_real, total_imag):
-    count, ctx, _, _, rows, _ = send_ref.shape
+        fill_grad(ready_ref, q, *[t + part_ref[q, i] for i, t in enumerate(total)])
+        copies.append(pltpu.make_async_copy(ready_ref.at[q], send_ref.at[:, :, per - EARLY + q], sems.at[1 + q]))
+        copies[1 + q].start()
+    for copy in copies:
+        copy.wait()
+
+
+def fill_grad(ready_ref, q, total_real, total_imag):
+    _, count, ctx, rows, _ = ready_ref.shape
     total = jnp.concatenate([total_real, total_imag], 1) * (1.0 / (N1 * N2))
     upper, after = total[: N1 // 2], total[rows : N1 // 2 + rows]
     first = lax.broadcasted_iota(jnp.int32, upper.shape, 0) % rows == 0
@@ -184,7 +206,7 @@
             pair = jnp.concatenate([x[:, :N2][:, cols], x[:, N2:][:, cols]], 1)
             for block in range(ctx // 2):
                 target = ctx - 1 - block if half else block
-                send_ref[i, target, 1, q] = pair[block * rows : (block + 1) * rows]
+                ready_ref[q, i, target] = pair[block * rows : (block + 1) * rows]
 
 
 def whole(x):
@@ -199,9 +221,10 @@
     return pltpu.with_memory_space_constraint(x, pltpu.HBM)
 
 
-def conv_call(gain, received, tabs):
+def conv_call(gain, received, tabs, plane):
     dp, ctx, _, per, rows, _ = received.shape
     split_rows, forward_table, *_, twiddle = tabs
+    early = (dp * plane, EARLY, rows, N2)
     held = [pltpu.VMEM(t.shape, t.dtype) for t in (split_rows, forward_table, twiddle)]
     return pl.pallas_call(
         conv_kernel,
@@ -211,14 +234,18 @@
             pl.BlockSpec(memory_space=pltpu.VMEM),
             *[whole(t) for t in tabs],
         ],
-        out_specs=[pl.BlockSpec(memory_space=pltpu.VMEM)] * 7,
+        out_specs=[
+            *[pl.BlockSpec(memory_space=pltpu.VMEM)] * (7 + ctx // plane),
+        ],
         out_shape=[
-            pltpu.VMEM((dp, ctx, 2, per, rows, N2), BF16),
+            pltpu.VMEM((dp, ctx, per - EARLY, rows, N2), BF16),
             pltpu.VMEM((per, dp, N1, N2), KEPT),
             pltpu.VMEM((per, dp, HALF, 2 * N2), KEPT),
             pltpu.VMEM((per, 2, HALF, N2), F32),
             *held,
-        ],
+            *[pltpu.VMEM(early, BF16)] * (ctx // plane),
+        ],
+        scratch_shapes=[pltpu.VMEM((dp * ctx, rows, N2), BF16)],
         compiler_params=pltpu.CompilerParams(vmem_limit_bytes=VMEM),
         cost_estimate=pl.CostEstimate(flops=per * dp * 5 * 6 * N1**3, bytes_accessed=8 << 20, transcendentals=0),
         name="conv",
@@ -233,10 +260,13 @@
         functools.partial(grad_kernel, hops=len(cots)),
         grid=(1,),
         in_specs=[pl.BlockSpec(memory_space=pltpu.VMEM)] * len(operands),
-        out_specs=pl.BlockSpec(memory_space=pltpu.VMEM),
-        out_shape=pltpu.VMEM(send.shape, BF16),
-        scratch_shapes=[pltpu.VMEM((dp * ctx, per, rows, N2), BF16)],
-        input_output_aliases={len(operands) - 1: 0},
+        out_specs=pl.BlockSpec(memory_space=pl.ANY),
+        out_shape=pltpu.HBM((dp, ctx, 2 * per - EARLY, rows, N2), BF16),
+        scratch_shapes=[
+            pltpu.VMEM((dp * ctx, per, rows, N2), BF16),
+            pltpu.VMEM((per, dp, ctx, rows, N2), BF16),
+            pltpu.SemaphoreType.DMA((1 + per,)),
+        ],
         compiler_params=pltpu.CompilerParams(vmem_limit_bytes=VMEM),
         cost_estimate=pl.CostEstimate(flops=per * dp * 6 * N1**3, bytes_accessed=8 << 20, transcendentals=0),
         name="grad",
@@ -341,8 +371,12 @@
     )(*arrays)
 
 
-def homeward_kernel(last_ref, y_ref, grad_ref, rows_ref):
-    count, _, per, rows, _ = last_ref.shape
+def homeward_kernel(last_ref, *refs, per):
+    *early_refs, y_ref, grad_ref, rows_ref = refs
+    count, _, rows, _ = last_ref.shape
+    hops = early_refs[0].shape[0]
+    plane = count // hops // 2
+    here = place(plane)
     width = rows_ref.shape[2]
     pitch = rows_ref.shape[1] // (count * per)
     h = pl.program_id(0)
@@ -352,11 +386,14 @@
     col = lax.broadcasted_iota(jnp.int32, (width, width), 1)
     turn = (col == jnp.where(lower, width - 1 - row, row)).astype(F32)
     turn = (turn * jnp.where(lower, (1 - 2 * h).astype(F32), 1.0)).astype(BF16)
-    for t in range(2):
-        block = last_ref[:, t, :, :, lanes]
-        if t:
-            block = dot(block.reshape(count * per * rows, width), turn).reshape(block.shape)
-        rows_ref.at[t].reshape(count, per, pitch, width)[:, :, :rows] = block.astype(F32)
+    y_rows = rows_ref.at[0].reshape(count, per, pitch, width)
+    grad_rows = rows_ref.at[1].reshape(count, per, pitch, width)
+    for j, early_ref in enumerate(early_refs):
+        for hop in range(hops):
+            y_rows[near_device(here, j, hop, plane, hops), :EARLY, :rows] = early_ref[hop, :, :, lanes].astype(F32)
+    y_rows[:, EARLY:, :rows] = last_ref[:, : per - EARLY, :, lanes].astype(F32)
+    block = last_ref[:, per - EARLY :, :, lanes]
+    grad_rows[:, :, :rows] = dot(block.reshape(count * per * rows, width), turn).reshape(block.shape)
     for r in range(rows):
         y_ref[r] = rows_ref[0, pl.ds(r, count * per, stride=pitch), :].astype(BF16).T
     for r in range(rows):
@@ -364,13 +401,14 @@
         grad_ref[0, target] = rows_ref[1, pl.ds(r, count * per, stride=pitch), :].T
 
 
-def homeward(last):
-    count, _, per, rows, _ = last.shape
+def homeward(last, early):
+    count, slots, rows, _ = last.shape
+    per = (slots + EARLY) // 2
     channels, width, pitch = count * per, 128, rows + 8
     return pl.pallas_call(
-        homeward_kernel,
+        functools.partial(homeward_kernel, per=per),
         grid=(N2 // width,),
-        in_specs=[pl.BlockSpec(memory_space=pltpu.VMEM)],
+        in_specs=[pl.BlockSpec(memory_space=pltpu.VMEM)] * (1 + len(early)),
         out_specs=[
             pl.BlockSpec((rows, width, channels), lambda h: (0, h, 0)),
             pl.BlockSpec((1, rows, width, channels), lambda h: (h, 0, 0, 0)),
@@ -383,7 +421,7 @@
         compiler_params=pltpu.CompilerParams(vmem_limit_bytes=VMEM),
         cost_estimate=pl.CostEstimate(flops=0, bytes_accessed=5 << 20, transcendentals=0),
         name="homeward",
-    )(near(last))
+    )(near(last), *[near(x) for x in early])
 
 
 def by_channel_body(embeds, perturb, cotangent, filter_spectrum, skip_gain):
@@ -413,10 +451,14 @@
     late, received = lax.optimization_barrier((late, received))
     cots = [exchange(x, hop * plane) for hop, x in enumerate([*early, late])]
     gain = lax.dynamic_slice(skip_gain, ((d * ctx + c) * per,), (per,))
-    send, *kept = conv_call(gain, received, tabs)
+    outs = conv_call(gain, received, tabs, plane)
+    (send, *kept), early = outs[:-hops], outs[-hops:]
+    early = [exchange(x, hop * plane) for hop, x in enumerate(early)]
     send = grad_call(received, kept, cots, send)
-    last = lax.all_to_all(send.reshape(count, 2, per, rows, N2), axes, 0, 0, tiled=True)
-    y, grad = homeward(last)
+    send, *early = lax.optimization_barrier((send, *early))
+    last = lax.all_to_all(send.reshape(count, *send.shape[2:]), axes, 0, 0, tiled=True)
+    early = [exchange(x, j // plane * ctx + j % plane) for j, x in enumerate(regroup(early))]
+    y, grad = homeward(last, early)
     return y.reshape(1, rows * N2, channels), grad
 
 

time: 164 us -> 162 us (0.988)
  blocking collectives: 56.9 us -> 0 us
  waiting for transfers between devices: 53.8 us -> 90.2 us
  starting transfers between devices: 20.9 us -> 36.7 us
  local copies, waits for them, and re-layouts: 6.98 us -> 8.95 us
    all_to_all x1 -> x0, blocking collectives: 56.9 us -> none  [by_channel_body(): lax.all_to_all(send.reshape(count, 2, per, rows, N2), axes, 0, 0, tiled=T...]
    ppermute x10 -> x20, waiting for transfers between devices: 28.1 us -> 46.7 us  [exchange(): lax.ppermute(x, axes, [(i, i ^ mask) for i in range(count)])]
    all_to_all x0 -> x1, waiting for transfers between devices: none -> 17.8 us  [by_channel_body(): lax.all_to_all(send.reshape(count, *send.shape[2:]), axes, 0, 0, tiled=True)]
    ppermute x10 -> x20, starting transfers between devices: 13.6 us -> 25.3 us  [exchange(): lax.ppermute(x, axes, [(i, i ^ mask) for i in range(count)])]
    all_to_all x0 -> x1, starting transfers between devices: none -> 4.15 us  [by_channel_body(): lax.all_to_all(send.reshape(count, *send.shape[2:]), axes, 0, 0, tiled=True)]
    unnamed x20 -> x32, local copies, waits for them, and re-layouts: 6.91 us -> 8.88 us
  transfers between devices with their start and end apart: 11 -> 22, of which waited for: 5 -> 11; matrix products, arithmetic and copies ran while one was open for 0% -> 0% of each run, Pallas kernels for 9% -> 11%
where the time goes in v7:
time: 162 us
  waiting for transfers between devices  90.2 us (56%)
  starting transfers between devices  36.7 us (23%)
  Pallas kernels  24.9 us (15%)
  local copies, waits for them, and re-layouts  8.95 us (6%)
    ppermute x20, waiting for transfers between devices, exchange(): lax.ppermute(x, axes, [(i, i ^ mask) for i in range(count)])  46.7 us
    all_to_all x1, waiting for transfers between devices, by_channel_body(): lax.all_to_all(first, axes, 0, 0, tiled=True)  25.8 us
    ppermute x20, starting transfers between devices, exchange(): lax.ppermute(x, axes, [(i, i ^ mask) for i in range(count)])  25.3 us
    all_to_all x1, waiting for transfers between devices, by_channel_body(): lax.all_to_all(send.reshape(count, *send.shape[2:]), axes, 0, 0, tiled=True)  17.8 us
    pallas_call x1, Pallas kernels, conv_call(): pl.pallas_call(conv_kernel, grid=(per,), in_specs=[pl.BlockSpec(memory_sp...  10.6 us
    unnamed x32, local copies, waits for them, and re-layouts  8.88 us
    all_to_all x1, starting transfers between devices, by_channel_body(): lax.all_to_all(first, axes, 0, 0, tiled=True)  7.3 us
    all_to_all x1, starting transfers between devices, by_channel_body(): lax.all_to_all(send.reshape(count, *send.shape[2:]), axes, 0, 0, tiled=True)  4.15 us
  transfers between devices with their start and end apart: 22, of which 11 were waited for; matrix products, arithmetic and copies ran while one was open for 0% of the time, Pallas kernels for 11%

profile of v7, /device:TPU:0, one launch (start us, length us, event | category | flops | bytes accessed | tf_op | source)
XLA Modules:
  0.0 161.6 jit_solution(1990337752733924946)
XLA Ops:
  0.6 4.0 %outward.1 = bf16[32,3,4,16,256]{4,3,2,1,0:T(8,128)(2,1)} custom-call(bf16[1,16,256,128]{3,2,1,0:T(8,128)(2,1)} %bitcast.9, bf16[1,16,256,128]{3,2,1,0:T(8,128)(2,1)} %bitcast.10, f32[2,16,256,128]{3,2,1,0:T(8,128)} %refs_2_.1), custom_call_target="tpu_custom_call" | custom-call | bytes 7340032 | tf_op jit(solution)/shard_map/outward/pallas_call | solution.py:307
  4.7 7.3 %all-to-all-start = ((bf16[32,3,4,16,256]{4,3,2,1,0:T(8,128)(2,1)}), bf16[32,3,4,16,256]{4,3,2,1,0:T(8,128)(2,1)S(1)}, u32[]{:S(2)}, u32[]{:S(2)}) async-start(bf16[32,3,4,16,256]{4,3,2,1,0:T(8,128)(2,1)} %outward.1), calls=%async_computation | async-start | bytes 6291456 | tf_op jit(solution)/shard_map/all_to_all | solution.py:446
  12.0 2.4 %outward_near.1 = (bf16[4,4,16,256]{3,2,1,0:T(8,128)(2,1)S(1)}, bf16[4,4,16,256]{3,2,1,0:T(8,128)(2,1)S(1)}, bf16[4,4,16,256]{3,2,1,0:T(8,128)(2,1)S(1)}, bf16[4...) custom-call(bf16[1,16,256,128]{3,2,1,0:T(8,128)(2,1)} %bitcast.11), custom_call_target="tpu_custom_call" | custom-call | bytes 2097152 | tf_op jit(solution)/shard_map/outward_near/pallas_call | solution.py:344
  16.4 1.7 %collective-permute-start.3 = (bf16[4,4,16,256]{3,2,1,0:T(8,128)(2,1)}, bf16[4,4,16,256]{3,2,1,0:T(8,128)(2,1)}, u32[]{:S(2)}, u32[]{:S(2)}) collective-permute-start(bf16[4,4,16,256]{3,2,1,0:T(8,128)(2,1)} %get-tuple-element.46), channel_id=1, source_target_pairs={{0,16},{1,17},{2,18},{3,19},{4,20},{5,21},{6,22},{7,23},{8,24},{9,... | collective-permute-start | bytes 393224 | tf_op jit(solution)/shard_map/ppermute | solution.py:443
  18.8 2.6 %collective-permute-start.5 = (bf16[4,4,16,256]{3,2,1,0:T(8,128)(2,1)}, bf16[4,4,16,256]{3,2,1,0:T(8,128)(2,1)S(1)}, u32[]{:S(2)}, u32[]{:S(2)}) collective-permute-start(bf16[4,4,16,256]{3,2,1,0:T(8,128)(2,1)} %get-tuple-element.48), channel_id=1, source_target_pairs={{0,18},{1,19},{2,16},{3,17},{4,22},{5,23},{6,20},{7,21},{8,26},{9,... | collective-permute-start | bytes 393224 | tf_op jit(solution)/shard_map/ppermute | solution.py:443
  21.4 14.6 %collective-permute-done.1.refs_2_ = bf16[4,4,16,256]{3,2,1,0:T(8,128)(2,1)S(1)} collective-permute-done((bf16[4,4,16,256]{3,2,1,0:T(8,128)(2,1)S(1)}, bf16[4,4,16,256]{3,2,1,0:T(8,128)(2,1)S(1)}, u32[]{:S(2)}, u32[]{:S(2)}) %collective-permute-start.1) | collective-permute-done | bytes 131104 | tf_op jit(solution)/shard_map/ppermute | solution.py:443
  36.7 2.4 %collective-permute-start.6 = (bf16[4,4,16,256]{3,2,1,0:T(8,128)(2,1)}, bf16[4,4,16,256]{3,2,1,0:T(8,128)(2,1)S(1)}, u32[]{:S(2)}, u32[]{:S(2)}) collective-permute-start(bf16[4,4,16,256]{3,2,1,0:T(8,128)(2,1)} %get-tuple-element.49), channel_id=1, source_target_pairs={{0,19},{1,18},{2,17},{3,16},{4,23},{5,22},{6,21},{7,20},{8,27},{9,... | collective-permute-start | bytes 393224 | tf_op jit(solution)/shard_map/ppermute | solution.py:443
  39.2 2.1 %collective-permute-done.2.refs_3_ = bf16[4,4,16,256]{3,2,1,0:T(8,128)(2,1)} collective-permute-done((bf16[4,4,16,256]{3,2,1,0:T(8,128)(2,1)}, bf16[4,4,16,256]{3,2,1,0:T(8,128)(2,1)}, u32[]{:S(2)}, u32[]{:S(2)}) %collective-permute-start.2) | collective-permute-done | bytes 131104 | tf_op jit(solution)/shard_map/ppermute | solution.py:443
  41.3 9.5 %collective-permute-done.5.refs_6_ = bf16[4,4,16,256]{3,2,1,0:T(8,128)(2,1)S(1)} collective-permute-done((bf16[4,4,16,256]{3,2,1,0:T(8,128)(2,1)}, bf16[4,4,16,256]{3,2,1,0:T(8,128)(2,1)S(1)}, u32[]{:S(2)}, u32[]{:S(2)}) %collective-permute-start.5) | collective-permute-done | bytes 131104 | tf_op jit(solution)/shard_map/ppermute | solution.py:443
  51.4 1.9 %collective-permute-done.6.refs_7_ = bf16[4,4,16,256]{3,2,1,0:T(8,128)(2,1)S(1)} collective-permute-done((bf16[4,4,16,256]{3,2,1,0:T(8,128)(2,1)}, bf16[4,4,16,256]{3,2,1,0:T(8,128)(2,1)S(1)}, u32[]{:S(2)}, u32[]{:S(2)}) %collective-permute-start.6) | collective-permute-done | bytes 131104 | tf_op jit(solution)/shard_map/ppermute | solution.py:443
  57.6 1.9 %regroup.2 = (bf16[8,4,16,256]{3,2,1,0:T(8,128)(2,1)S(1)}, bf16[8,4,16,256]{3,2,1,0:T(8,128)(2,1)}, bf16[8,4,16,256]{3,2,1,0:T(8,128)(2,1)}, bf16[8,4,16,256]{3,2,1,0:T(8,128)(2,1)S(1)}) custom-call(bf16[4,4,16,256]{3,2,1,0:T(8,128)(2,1)S(1)} %get-tuple-element.42.refs_0_, bf16[4,4,16,256]{3,2,1,0:T(8,128)(2,1)S(1)} %copy-done.7, ...), custom_call_target="tpu_custom_call" | custom-call | bytes 2097152 | tf_op jit(solution)/shard_map/regroup/pallas_call | solution.py:365
  60.1 4.8 %collective-permute-start.8 = (bf16[8,4,16,256]{3,2,1,0:T(8,128)(2,1)}, bf16[8,4,16,256]{3,2,1,0:T(8,128)(2,1)}, u32[]{:S(2)}, u32[]{:S(2)}) collective-permute-start(bf16[8,4,16,256]{3,2,1,0:T(8,128)(2,1)} %get-tuple-element.57), channel_id=1, source_target_pairs={{0,8},{1,9},{2,10},{3,11},{4,12},{5,13},{6,14},{7,15},{8,0},{9,1},... | collective-permute-start | bytes 786440 | tf_op jit(solution)/shard_map/ppermute | solution.py:443
  64.9 25.8 %all-to-all-done = bf16[32,3,4,16,256]{4,3,2,1,0:T(8,128)(2,1)S(1)} async-done(((bf16[32,3,4,16,256]{4,3,2,1,0:T(8,128)(2,1)}), bf16[32,3,4,16,256]{4,3,2,1,0:T(8,128)(2,1)S(1)}, u32[]{:S(2)}, u32[]{:S(2)}) %all-to-all-start) | async-done | bytes 3145760 | tf_op jit(solution)/shard_map/all_to_all | solution.py:446
  90.7 10.6 %conv.1 = (bf16[2,16,2,16,256]{4,3,2,1,0:T(8,128)(2,1)S(1)}, f32[4,2,256,256]{3,2,1,0:T(8,128)S(1)}, f32[4,2,144,512]{3,2,1,0:T(8,128)S(1)}, f32[4,2,144,256]{3,...) custom-call(f32[4]{0:T(128)S(1)} %dynamic_slice.3.gain_ref, ...), custom_call_target="tpu_custom_call" | custom-call | flops 4026531840 | bytes 8388608 | tf_op jit(solution)/shard_map/conv/pallas_call | solution.py:229
  101.3 4.4 %collective-permute-start.11 = (bf16[8,2,16,256]{3,2,1,0:T(8,128)(2,1)S(1)}, bf16[8,2,16,256]{3,2,1,0:T(8,128)(2,1)S(1)}, u32[]{:S(2)}, u32[]{:S(2)}) collective-permute-start(bf16[8,2,16,256]{3,2,1,0:T(8,128)(2,1)S(1)} %get-tuple-element.65), channel_id=1, source_target_pairs={{0,8},{1,9},{2,10},{3,11},{4,12},{5,13},{6,14},{7,15},{8,0},{9,1},... | collective-permute-start | bytes 393224 | tf_op jit(solution)/shard_map/ppermute | solution.py:443
  105.7 3.3 %grad.1 = bf16[2,16,6,16,256]{4,3,2,1,0:T(8,128)(2,1)} custom-call(bf16[2,16,3,4,16,256]{5,4,3,2,1,0:T(8,128)(2,1)S(1)} %bitcast.7, f32[4,2,256,256]{3,2,1,0:T(8,128)S(1)} %get-tuple-element.52.gap_ref, f32[4,2,144,512]{3,2,1,0:T(8,128)S(1)} %get-tuple-element.53.spec_ref, f32[4,2,144,256]{3,2,1,0:T(8,128)S(1)} %get-tuple-element.54.part_ref, ...), custom_call_target="tpu_custom_call" | custom-call | flops 805306368 | bytes 8388608 | tf_op jit(solution)/shard_map/grad/pallas_call | solution.py:259
  109.7 5.3 %collective-permute-done.11.refs_2_ = bf16[8,2,16,256]{3,2,1,0:T(8,128)(2,1)S(1)} collective-permute-done((bf16[8,2,16,256]{3,2,1,0:T(8,128)(2,1)S(1)}, bf16[8,2,16,256]{3,2,1,0:T(8,128)(2,1)S(1)}, u32[]{:S(2)}, u32[]{:S(2)}) %collective-permute-start.11) | collective-permute-done | bytes 131104 | tf_op jit(solution)/shard_map/ppermute | solution.py:443
  116.3 4.2 %all-to-all-start.1 = ((bf16[32,6,16,256]{3,2,1,0:T(8,128)(2,1)}), bf16[32,6,16,256]{3,2,1,0:T(8,128)(2,1)S(1)}, u32[]{:S(2)}, u32[]{:S(2)}) async-start(bf16[32,6,16,256]{3,2,1,0:T(8,128)(2,1)} %bitcast.8), calls=%async_computation.1 | async-start | bytes 3145728 | tf_op jit(solution)/shard_map/all_to_all | solution.py:459
  122.6 1.7 %collective-permute-start.16 = (bf16[4,2,16,256]{3,2,1,0:T(8,128)(2,1)S(1)}, bf16[4,2,16,256]{3,2,1,0:T(8,128)(2,1)S(1)}, u32[]{:S(2)}, u32[]{:S(2)}) collective-permute-start(bf16[4,2,16,256]{3,2,1,0:T(8,128)(2,1)S(1)} %get-tuple-element.76), channel_id=1, source_target_pairs={{0,16},{1,17},{2,18},{3,19},{4,20},{5,21},{6,22},{7,23},{8,24},{9,... | collective-permute-start | bytes 196616 | tf_op jit(solution)/shard_map/ppermute | solution.py:443
  124.4 2.6 %collective-permute-start.18 = (bf16[4,2,16,256]{3,2,1,0:T(8,128)(2,1)S(1)}, bf16[4,2,16,256]{3,2,1,0:T(8,128)(2,1)S(1)}, u32[]{:S(2)}, u32[]{:S(2)}) collective-permute-start(bf16[4,2,16,256]{3,2,1,0:T(8,128)(2,1)S(1)} %get-tuple-element.78), channel_id=1, source_target_pairs={{0,18},{1,19},{2,16},{3,17},{4,22},{5,23},{6,20},{7,21},{8,26},{9,... | collective-permute-start | bytes 196616 | tf_op jit(solution)/shard_map/ppermute | solution.py:443
  127.0 6.6 %collective-permute-done.14.refs_2_ = bf16[4,2,16,256]{3,2,1,0:T(8,128)(2,1)S(1)} collective-permute-done((bf16[4,2,16,256]{3,2,1,0:T(8,128)(2,1)S(1)}, bf16[4,2,16,256]{3,2,1,0:T(8,128)(2,1)S(1)}, u32[]{:S(2)}, u32[]{:S(2)}) %collective-permute-start.14) | collective-permute-done | bytes 65568 | tf_op jit(solution)/shard_map/ppermute | solution.py:443
  135.0 5.7 %collective-permute-done.18.refs_6_ = bf16[4,2,16,256]{3,2,1,0:T(8,128)(2,1)S(1)} collective-permute-done((bf16[4,2,16,256]{3,2,1,0:T(8,128)(2,1)S(1)}, bf16[4,2,16,256]{3,2,1,0:T(8,128)(2,1)S(1)}, u32[]{:S(2)}, u32[]{:S(2)}) %collective-permute-start.18) | collective-permute-done | bytes 65568 | tf_op jit(solution)/shard_map/ppermute | solution.py:443
  141.1 17.8 %all-to-all-done.1.last_ref = bf16[32,6,16,256]{3,2,1,0:T(8,128)(2,1)S(1)} async-done(((bf16[32,6,16,256]{3,2,1,0:T(8,128)(2,1)}), bf16[32,6,16,256]{3,2,1,0:T(8,128)(2,1)S(1)}, u32[]{:S(2)}, u32[]{:S(2)}) %all-to-all-start.1) | async-done | bytes 1572896 | tf_op jit(solution)/shard_map/all_to_all | solution.py:459
  158.9 2.7 %homeward.1 = (bf16[16,256,128]{2,1,0:T(8,128)(2,1)}, f32[2,16,128,128]{3,2,1,0:T(8,128)}) custom-call(bf16[32,6,16,256]{3,2,1,0:T(8,128)(2,1)S(1)} %all-to-all-done.1.last_ref, bf16[4,2,16,256]{3,2,1,0:T(8,128)(2,1)S(1)} %get-tuple-element.72.refs_0_, bf16[4,2,16,256]{3,2,1,0:T(8,128)(2,1)S(1)} %collective-permute-done.13.refs_1_, ...), custom_call_target="tpu_custom_call" | custom-call | bytes 5242880 | tf_op jit(solution)/shard_map/homeward/pallas_call | solution.py:408
  (60 shorter events, 15.2 us)
Async XLA Ops:
  4.6 34.5 %copy-start.15 = (f32[128]{0:T(128)S(1)}, f32[128]{0:T(128)}, u32[]{:S(2)}) copy-start(f32[128]{0:T(128)} %param.15) | copy-start | bytes 1540
  4.7 86.0 %all-to-all-start = ((bf16[32,3,4,16,256]{4,3,2,1,0:T(8,128)(2,1)}), bf16[32,3,4,16,256]{4,3,2,1,0:T(8,128)(2,1)S(1)}, u32[]{:S(2)}, u32[]{:S(2)}) async-start(bf16[32,3,4,16,256]{4,3,2,1,0:T(8,128)(2,1)} %outward.1), calls=%async_computation | async-start | bytes 6291456 | tf_op jit(solution)/shard_map/all_to_all | solution.py:446
  14.4 3.8 %collective-permute-start = (bf16[4,4,16,256]{3,2,1,0:T(8,128)(2,1)S(1)}, bf16[4,4,16,256]{3,2,1,0:T(8,128)(2,1)S(1)}, u32[]{:S(2)}, u32[]{:S(2)}) collective-permute-start(bf16[4,4,16,256]{3,2,1,0:T(8,128)(2,1)S(1)} %get-tuple-element.43), channel_id=1, source_target_pairs={{0,1},{1,0},{2,3},{3,2},{4,5},{5,4},{6,7},{7,6},{8,9},{9,8},{10,11... | collective-permute-start | bytes 393224 | tf_op jit(solution)/shard_map/ppermute | solution.py:443
  14.7 21.3 %collective-permute-start.1 = (bf16[4,4,16,256]{3,2,1,0:T(8,128)(2,1)S(1)}, bf16[4,4,16,256]{3,2,1,0:T(8,128)(2,1)S(1)}, u32[]{:S(2)}, u32[]{:S(2)}) collective-permute-start(bf16[4,4,16,256]{3,2,1,0:T(8,128)(2,1)S(1)} %get-tuple-element.44), channel_id=1, source_target_pairs={{0,2},{1,3},{2,0},{3,1},{4,6},{5,7},{6,4},{7,5},{8,10},{9,11},{10,... | collective-permute-start | bytes 393224 | tf_op jit(solution)/shard_map/ppermute | solution.py:443
  16.4 24.9 %collective-permute-start.2 = (bf16[4,4,16,256]{3,2,1,0:T(8,128)(2,1)}, bf16[4,4,16,256]{3,2,1,0:T(8,128)(2,1)}, u32[]{:S(2)}, u32[]{:S(2)}) collective-permute-start(bf16[4,4,16,256]{3,2,1,0:T(8,128)(2,1)} %get-tuple-element.45), channel_id=1, source_target_pairs={{0,3},{1,2},{2,1},{3,0},{4,7},{5,6},{6,5},{7,4},{8,11},{9,10},{10,... | collective-permute-start | bytes 393224 | tf_op jit(solution)/shard_map/ppermute | solution.py:443
  16.4 24.9 %collective-permute-start.3 = (bf16[4,4,16,256]{3,2,1,0:T(8,128)(2,1)}, bf16[4,4,16,256]{3,2,1,0:T(8,128)(2,1)}, u32[]{:S(2)}, u32[]{:S(2)}) collective-permute-start(bf16[4,4,16,256]{3,2,1,0:T(8,128)(2,1)} %get-tuple-element.46), channel_id=1, source_target_pairs={{0,16},{1,17},{2,18},{3,19},{4,20},{5,21},{6,22},{7,23},{8,24},{9,... | collective-permute-start | bytes 393224 | tf_op jit(solution)/shard_map/ppermute | solution.py:443
  18.1 23.2 %collective-permute-start.4 = (bf16[4,4,16,256]{3,2,1,0:T(8,128)(2,1)}, bf16[4,4,16,256]{3,2,1,0:T(8,128)(2,1)}, u32[]{:S(2)}, u32[]{:S(2)}) collective-permute-start(bf16[4,4,16,256]{3,2,1,0:T(8,128)(2,1)} %get-tuple-element.47), channel_id=1, source_target_pairs={{0,17},{1,16},{2,19},{3,18},{4,21},{5,20},{6,23},{7,22},{8,25},{9,... | collective-permute-start | bytes 393224 | tf_op jit(solution)/shard_map/ppermute | solution.py:443
  18.8 31.9 %collective-permute-start.5 = (bf16[4,4,16,256]{3,2,1,0:T(8,128)(2,1)}, bf16[4,4,16,256]{3,2,1,0:T(8,128)(2,1)S(1)}, u32[]{:S(2)}, u32[]{:S(2)}) collective-permute-start(bf16[4,4,16,256]{3,2,1,0:T(8,128)(2,1)} %get-tuple-element.48), channel_id=1, source_target_pairs={{0,18},{1,19},{2,16},{3,17},{4,22},{5,23},{6,20},{7,21},{8,26},{9,... | collective-permute-start | bytes 393224 | tf_op jit(solution)/shard_map/ppermute | solution.py:443
  36.7 16.6 %collective-permute-start.6 = (bf16[4,4,16,256]{3,2,1,0:T(8,128)(2,1)}, bf16[4,4,16,256]{3,2,1,0:T(8,128)(2,1)S(1)}, u32[]{:S(2)}, u32[]{:S(2)}) collective-permute-start(bf16[4,4,16,256]{3,2,1,0:T(8,128)(2,1)} %get-tuple-element.49), channel_id=1, source_target_pairs={{0,19},{1,18},{2,17},{3,16},{4,23},{5,22},{6,21},{7,20},{8,27},{9,... | collective-permute-start | bytes 393224 | tf_op jit(solution)/shard_map/ppermute | solution.py:443
  60.1 45.6 %collective-permute-start.7 = (bf16[8,4,16,256]{3,2,1,0:T(8,128)(2,1)}, bf16[8,4,16,256]{3,2,1,0:T(8,128)(2,1)}, u32[]{:S(2)}, u32[]{:S(2)}) collective-permute-start(bf16[8,4,16,256]{3,2,1,0:T(8,128)(2,1)} %get-tuple-element.56), channel_id=1, source_target_pairs={{0,4},{1,5},{2,6},{3,7},{4,0},{5,1},{6,2},{7,3},{8,12},{9,13},{10,... | collective-permute-start | bytes 786440 | tf_op jit(solution)/shard_map/ppermute | solution.py:443
  60.1 45.6 %collective-permute-start.8 = (bf16[8,4,16,256]{3,2,1,0:T(8,128)(2,1)}, bf16[8,4,16,256]{3,2,1,0:T(8,128)(2,1)}, u32[]{:S(2)}, u32[]{:S(2)}) collective-permute-start(bf16[8,4,16,256]{3,2,1,0:T(8,128)(2,1)} %get-tuple-element.57), channel_id=1, source_target_pairs={{0,8},{1,9},{2,10},{3,11},{4,12},{5,13},{6,14},{7,15},{8,0},{9,1},... | collective-permute-start | bytes 786440 | tf_op jit(solution)/shard_map/ppermute | solution.py:443
  90.7 15.1 %collective-permute-start.9 = (bf16[8,4,16,256]{3,2,1,0:T(8,128)(2,1)}, bf16[8,4,16,256]{3,2,1,0:T(8,128)(2,1)S(1)}, u32[]{:S(2)}, u32[]{:S(2)}) collective-permute-start(bf16[8,4,16,256]{3,2,1,0:T(8,128)(2,1)} %copy-done.14), channel_id=1, source_target_pairs={{0,12},{1,13},{2,14},{3,15},{4,8},{5,9},{6,10},{7,11},{8,4},{9,5},... | collective-permute-start | bytes 786440 | tf_op jit(solution)/shard_map/ppermute | solution.py:443
  101.3 7.8 %collective-permute-start.10 = (bf16[8,2,16,256]{3,2,1,0:T(8,128)(2,1)S(1)}, bf16[8,2,16,256]{3,2,1,0:T(8,128)(2,1)S(1)}, u32[]{:S(2)}, u32[]{:S(2)}) collective-permute-start(bf16[8,2,16,256]{3,2,1,0:T(8,128)(2,1)S(1)} %get-tuple-element.64), channel_id=1, source_target_pairs={{0,4},{1,5},{2,6},{3,7},{4,0},{5,1},{6,2},{7,3},{8,12},{9,13},{10,... | collective-permute-start | bytes 393224 | tf_op jit(solution)/shard_map/ppermute | solution.py:443
  101.3 13.7 %collective-permute-start.11 = (bf16[8,2,16,256]{3,2,1,0:T(8,128)(2,1)S(1)}, bf16[8,2,16,256]{3,2,1,0:T(8,128)(2,1)S(1)}, u32[]{:S(2)}, u32[]{:S(2)}) collective-permute-start(bf16[8,2,16,256]{3,2,1,0:T(8,128)(2,1)S(1)} %get-tuple-element.65), channel_id=1, source_target_pairs={{0,8},{1,9},{2,10},{3,11},{4,12},{5,13},{6,14},{7,15},{8,0},{9,1},... | collective-permute-start | bytes 393224 | tf_op jit(solution)/shard_map/ppermute | solution.py:443
  105.7 10.0 %collective-permute-start.12 = (bf16[8,2,16,256]{3,2,1,0:T(8,128)(2,1)S(1)}, bf16[8,2,16,256]{3,2,1,0:T(8,128)(2,1)S(1)}, u32[]{:S(2)}, u32[]{:S(2)}) collective-permute-start(bf16[8,2,16,256]{3,2,1,0:T(8,128)(2,1)S(1)} %get-tuple-element.66), channel_id=1, source_target_pairs={{0,12},{1,13},{2,14},{3,15},{4,8},{5,9},{6,10},{7,11},{8,4},{9,5},... | collective-permute-start | bytes 393224 | tf_op jit(solution)/shard_map/ppermute | solution.py:443
  115.7 4.8 %copy-start.1 = (bf16[8,2,16,256]{3,2,1,0:T(8,128)(2,1)S(1)}, bf16[8,2,16,256]{3,2,1,0:T(8,128)(2,1)}, u32[]{:S(2)}) copy-start(bf16[8,2,16,256]{3,2,1,0:T(8,128)(2,1)} %copy-done) | copy-start | bytes 393220
  116.3 42.6 %all-to-all-start.1 = ((bf16[32,6,16,256]{3,2,1,0:T(8,128)(2,1)}), bf16[32,6,16,256]{3,2,1,0:T(8,128)(2,1)S(1)}, u32[]{:S(2)}, u32[]{:S(2)}) async-start(bf16[32,6,16,256]{3,2,1,0:T(8,128)(2,1)} %bitcast.8), calls=%async_computation.1 | async-start | bytes 3145728 | tf_op jit(solution)/shard_map/all_to_all | solution.py:459
  120.6 3.8 %collective-permute-start.13 = (bf16[4,2,16,256]{3,2,1,0:T(8,128)(2,1)S(1)}, bf16[4,2,16,256]{3,2,1,0:T(8,128)(2,1)S(1)}, u32[]{:S(2)}, u32[]{:S(2)}) collective-permute-start(bf16[4,2,16,256]{3,2,1,0:T(8,128)(2,1)S(1)} %get-tuple-element.73), channel_id=1, source_target_pairs={{0,1},{1,0},{2,3},{3,2},{4,5},{5,4},{6,7},{7,6},{8,9},{9,8},{10,11... | collective-permute-start | bytes 196616 | tf_op jit(solution)/shard_map/ppermute | solution.py:443
  120.9 12.7 %collective-permute-start.14 = (bf16[4,2,16,256]{3,2,1,0:T(8,128)(2,1)S(1)}, bf16[4,2,16,256]{3,2,1,0:T(8,128)(2,1)S(1)}, u32[]{:S(2)}, u32[]{:S(2)}) collective-permute-start(bf16[4,2,16,256]{3,2,1,0:T(8,128)(2,1)S(1)} %get-tuple-element.74), channel_id=1, source_target_pairs={{0,2},{1,3},{2,0},{3,1},{4,6},{5,7},{6,4},{7,5},{8,10},{9,11},{10,... | collective-permute-start | bytes 196616 | tf_op jit(solution)/shard_map/ppermute | solution.py:443
  122.6 12.4 %collective-permute-start.15 = (bf16[4,2,16,256]{3,2,1,0:T(8,128)(2,1)S(1)}, bf16[4,2,16,256]{3,2,1,0:T(8,128)(2,1)S(1)}, u32[]{:S(2)}, u32[]{:S(2)}) collective-permute-start(bf16[4,2,16,256]{3,2,1,0:T(8,128)(2,1)S(1)} %get-tuple-element.75), channel_id=1, source_target_pairs={{0,3},{1,2},{2,1},{3,0},{4,7},{5,6},{6,5},{7,4},{8,11},{9,10},{10,... | collective-permute-start | bytes 196616 | tf_op jit(solution)/shard_map/ppermute | solution.py:443
  122.6 12.4 %collective-permute-start.16 = (bf16[4,2,16,256]{3,2,1,0:T(8,128)(2,1)S(1)}, bf16[4,2,16,256]{3,2,1,0:T(8,128)(2,1)S(1)}, u32[]{:S(2)}, u32[]{:S(2)}) collective-permute-start(bf16[4,2,16,256]{3,2,1,0:T(8,128)(2,1)S(1)} %get-tuple-element.76), channel_id=1, source_target_pairs={{0,16},{1,17},{2,18},{3,19},{4,20},{5,21},{6,22},{7,23},{8,24},{9,... | collective-permute-start | bytes 196616 | tf_op jit(solution)/shard_map/ppermute | solution.py:443
  124.3 10.7 %collective-permute-start.17 = (bf16[4,2,16,256]{3,2,1,0:T(8,128)(2,1)S(1)}, bf16[4,2,16,256]{3,2,1,0:T(8,128)(2,1)S(1)}, u32[]{:S(2)}, u32[]{:S(2)}) collective-permute-start(bf16[4,2,16,256]{3,2,1,0:T(8,128)(2,1)S(1)} %get-tuple-element.77), channel_id=1, source_target_pairs={{0,17},{1,16},{2,19},{3,18},{4,21},{5,20},{6,23},{7,22},{8,25},{9,... | collective-permute-start | bytes 196616 | tf_op jit(solution)/shard_map/ppermute | solution.py:443
  124.4 16.3 %collective-permute-start.18 = (bf16[4,2,16,256]{3,2,1,0:T(8,128)(2,1)S(1)}, bf16[4,2,16,256]{3,2,1,0:T(8,128)(2,1)S(1)}, u32[]{:S(2)}, u32[]{:S(2)}) collective-permute-start(bf16[4,2,16,256]{3,2,1,0:T(8,128)(2,1)S(1)} %get-tuple-element.78), channel_id=1, source_target_pairs={{0,18},{1,19},{2,16},{3,17},{4,22},{5,23},{6,20},{7,21},{8,26},{9,... | collective-permute-start | bytes 196616 | tf_op jit(solution)/shard_map/ppermute | solution.py:443
  133.5 7.6 %collective-permute-start.19 = (bf16[4,2,16,256]{3,2,1,0:T(8,128)(2,1)S(1)}, bf16[4,2,16,256]{3,2,1,0:T(8,128)(2,1)S(1)}, u32[]{:S(2)}, u32[]{:S(2)}) collective-permute-start(bf16[4,2,16,256]{3,2,1,0:T(8,128)(2,1)S(1)} %get-tuple-element.79), channel_id=1, source_target_pairs={{0,19},{1,18},{2,17},{3,16},{4,23},{5,22},{6,21},{7,20},{8,27},{9,... | collective-permute-start | bytes 196616 | tf_op jit(solution)/shard_map/ppermute | solution.py:443
  (14 other events, 17.2 us)

commit v8 on v7

--- a/solution.py
+++ b/solution.py
@@ -48,9 +48,13 @@
     return lax.axis_index("dp"), c // plane, c % plane
 
 
-def near_device(here, j, hop, plane, hops):
-    far = (here[0] ^ (j // plane)) * hops + (here[1] ^ hop)
-    return far * plane + (here[2] ^ (j % plane))
+def peer(here, j, hop, plane):
+    return here[0] ^ (j // plane), (here[1] ^ hop) * plane + (here[2] ^ (j % plane))
+
+
+def owner(here, j, hop, plane):
+    d, c = peer(here, j, hop, plane)
+    return c * lax.axis_size("dp") + d
 
 
 def forward(signals, split_ref, fwd_ref, tw_cos, tw_sin):
@@ -94,7 +98,7 @@
 ):
     *refs, y_rows = refs
     held_refs, early_refs = refs[:3], refs[3:]
-    count, ctx = recv_ref.shape[:2]
+    ctx, count = recv_ref.shape[:2]
     hops, near_count = len(early_refs), early_refs[0].shape[0]
     here = place(near_count // count)
     q = pl.program_id(0)
@@ -107,12 +111,12 @@
     tw_cos, tw_sin = tw_ref[0], tw_ref[1]
     signals = []
     for d in range(count):
-        clean = recv_ref[d, :, 0, q].reshape(N1, N2)
-        perturb = recv_ref[d, :, 1, q].reshape(N1, N2)
+        clean = recv_ref[:, d, 0, q].reshape(N1, N2)
+        perturb = recv_ref[:, d, 1, q].reshape(N1, N2)
         signals += [clean, (clean.astype(F32) + perturb.astype(F32)).astype(BF16)]
     spectra = forward(signals, split_ref, fwd_ref, tw_cos, tw_sin)
     filter_real, filter_imag = hermitian_part(
-        recv_ref[0, :, 2, q].reshape(N1, N2), recv_ref[1, :, 2, q].reshape(N1, N2), mirror_ref[...], cols_ref[...]
+        recv_ref[:, 0, 2, q].reshape(N1, N2), recv_ref[:, 1, 2, q].reshape(N1, N2), mirror_ref[...], cols_ref[...]
     )
     products = []
     for spec in spectra:
@@ -154,12 +158,13 @@
     def _():
         for hop, early_ref in enumerate(early_refs):
             for j in range(near_count):
-                early_ref[j, q] = y_rows[near_device(here, j, hop, near_count // count, hops)]
+                side, block = peer(here, j, hop, near_count // count)
+                early_ref[j, q] = y_rows[side * ctx + block]
 
     @pl.when(q >= EARLY)
     def _():
         for d in range(count):
-            send_ref[d, :, q - EARLY] = y_rows[d * ctx : (d + 1) * ctx]
+            send_ref[:, d, q - EARLY] = y_rows[d * ctx : (d + 1) * ctx]
 
 
 def grad_kernel(recv_ref, gap_ref, spec_ref, part_ref, *refs, hops):
@@ -167,18 +172,19 @@
     split_ref, fwd_ref, tw_ref, y_ref, send_ref, cot_rows, ready_ref, sems = refs
     copies = [pltpu.make_async_copy(y_ref, send_ref.at[:, :, pl.ds(0, y_ref.shape[2])], sems.at[0])]
     copies[0].start()
-    count, ctx = recv_ref.shape[:2]
+    ctx, count = recv_ref.shape[:2]
     near = cot_refs[0].shape[0]
     plane = near // count
     here = place(plane)
     per = recv_ref.shape[3]
     for hop, cot_ref in enumerate(cot_refs):
         for j in range(near):
-            cot_rows[near_device(here, j, hop, plane, hops)] = cot_ref[j]
+            side, block = peer(here, j, hop, plane)
+            cot_rows[side * ctx + block] = cot_ref[j]
     errors = []
     for q in range(per):
         for d in range(count):
-            clean = recv_ref[d, :, 0, q].reshape(N1, N2).astype(F32)
+            clean = recv_ref[:, d, 0, q].reshape(N1, N2).astype(F32)
             cot = cot_rows[d * ctx : (d + 1) * ctx, q].reshape(N1, N2).astype(F32)
             errors.append((clean * (cot - gap_ref[q, d])).astype(BF16))
     err_spectra = forward(errors, split_ref, fwd_ref, tw_ref[0], tw_ref[1])
@@ -193,7 +199,7 @@
 
 
 def fill_grad(ready_ref, q, total_real, total_imag):
-    _, count, ctx, rows, _ = ready_ref.shape
+    _, ctx, count, rows, _ = ready_ref.shape
     total = jnp.concatenate([total_real, total_imag], 1) * (1.0 / (N1 * N2))
     upper, after = total[: N1 // 2], total[rows : N1 // 2 + rows]
     first = lax.broadcasted_iota(jnp.int32, upper.shape, 0) % rows == 0
@@ -206,7 +212,7 @@
             pair = jnp.concatenate([x[:, :N2][:, cols], x[:, N2:][:, cols]], 1)
             for block in range(ctx // 2):
                 target = ctx - 1 - block if half else block
-                ready_ref[q, i, target] = pair[block * rows : (block + 1) * rows]
+                ready_ref[q, target, i] = pair[block * rows : (block + 1) * rows]
 
 
 def whole(x):
@@ -222,7 +228,7 @@
 
 
 def conv_call(gain, received, tabs, plane):
-    dp, ctx, _, per, rows, _ = received.shape
+    ctx, dp, _, per, rows, _ = received.shape
     split_rows, forward_table, *_, twiddle = tabs
     early = (dp * plane, EARLY, rows, N2)
     held = [pltpu.VMEM(t.shape, t.dtype) for t in (split_rows, forward_table, twiddle)]
@@ -238,7 +244,7 @@
             *[pl.BlockSpec(memory_space=pltpu.VMEM)] * (7 + ctx // plane),
         ],
         out_shape=[
-            pltpu.VMEM((dp, ctx, per - EARLY, rows, N2), BF16),
+            pltpu.VMEM((ctx, dp, per - EARLY, rows, N2), BF16),
             pltpu.VMEM((per, dp, N1, N2), KEPT),
             pltpu.VMEM((per, dp, HALF, 2 * N2), KEPT),
             pltpu.VMEM((per, 2, HALF, N2), F32),
@@ -253,7 +259,7 @@
 
 
 def grad_call(received, kept, cots, send):
-    dp, ctx, _, per, rows, _ = received.shape
+    ctx, dp, _, per, rows, _ = received.shape
     *kept, split_rows, forward_table, twiddle = [near(x) for x in kept]
     operands = (received, *kept, *[near(x) for x in cots], split_rows, forward_table, twiddle, near(send))
     return pl.pallas_call(
@@ -261,10 +267,10 @@
         grid=(1,),
         in_specs=[pl.BlockSpec(memory_space=pltpu.VMEM)] * len(operands),
         out_specs=pl.BlockSpec(memory_space=pl.ANY),
-        out_shape=pltpu.HBM((dp, ctx, 2 * per - EARLY, rows, N2), BF16),
+        out_shape=pltpu.HBM((ctx, dp, 2 * per - EARLY, rows, N2), BF16),
         scratch_shapes=[
             pltpu.VMEM((dp * ctx, per, rows, N2), BF16),
-            pltpu.VMEM((per, dp, ctx, rows, N2), BF16),
+            pltpu.VMEM((per, ctx, dp, rows, N2), BF16),
             pltpu.SemaphoreType.DMA((1 + per,)),
         ],
         compiler_params=pltpu.CompilerParams(vmem_limit_bytes=VMEM),
@@ -332,7 +338,7 @@
         rows_ref[pl.ds(r, channels, stride=pitch), :] = in_ref[0, r].T.astype(F32)
     for j, out_ref in enumerate(out_refs):
         for hop in range(hops):
-            block = near_device(here, j, hop, plane, hops) * (per * pitch)
+            block = owner(here, j, hop, plane) * (per * pitch)
             rows_here = rows_ref[pl.ds(pl.multiple_of(block, per * pitch), per * pitch), :]
             out_ref[hop] = rows_here.reshape(per, pitch, width)[:, :rows].astype(BF16)
 
@@ -390,7 +396,7 @@
     grad_rows = rows_ref.at[1].reshape(count, per, pitch, width)
     for j, early_ref in enumerate(early_refs):
         for hop in range(hops):
-            y_rows[near_device(here, j, hop, plane, hops), :EARLY, :rows] = early_ref[hop, :, :, lanes].astype(F32)
+            y_rows[owner(here, j, hop, plane), :EARLY, :rows] = early_ref[hop, :, :, lanes].astype(F32)
     y_rows[:, EARLY:, :rows] = last_ref[:, : per - EARLY, :, lanes].astype(F32)
     block = last_ref[:, per - EARLY :, :, lanes]
     grad_rows[:, :, :rows] = dot(block.reshape(count * per * rows, width), turn).reshape(block.shape)
@@ -427,7 +433,7 @@
 def by_channel_body(embeds, perturb, cotangent, filter_spectrum, skip_gain):
     dp, ctx = lax.axis_size("dp"), lax.axis_size("ctx")
     d, c = lax.axis_index("dp"), lax.axis_index("ctx")
-    axes = ("dp", "ctx")
+    axes, order = ("dp", "ctx"), ("ctx", "dp")
     count = dp * ctx
     channels = embeds.shape[2]
     rows = N1 // ctx
@@ -443,20 +449,20 @@
         return lax.ppermute(x, axes, [(i, i ^ mask) for i in range(count)]) if mask else x
 
     first = outward([matrix(embeds), matrix(perturb), far(filter_spectrum)], count)
-    received = lax.all_to_all(first, axes, 0, 0, tiled=True).reshape(dp, ctx, 3, per, rows, N2)
+    received = lax.all_to_all(first, order, 0, 0, tiled=True).reshape(ctx, dp, 3, per, rows, N2)
     cots = outward_near(matrix(cotangent), count, hops, plane)
     cots = regroup([exchange(x, j // plane * ctx + j % plane) for j, x in enumerate(cots)])
     received = near(received)
     *early, late = cots
     late, received = lax.optimization_barrier((late, received))
     cots = [exchange(x, hop * plane) for hop, x in enumerate([*early, late])]
-    gain = lax.dynamic_slice(skip_gain, ((d * ctx + c) * per,), (per,))
+    gain = lax.dynamic_slice(skip_gain, ((c * dp + d) * per,), (per,))
     outs = conv_call(gain, received, tabs, plane)
     (send, *kept), early = outs[:-hops], outs[-hops:]
     early = [exchange(x, hop * plane) for hop, x in enumerate(early)]
     send = grad_call(received, kept, cots, send)
     send, *early = lax.optimization_barrier((send, *early))
-    last = lax.all_to_all(send.reshape(count, *send.shape[2:]), axes, 0, 0, tiled=True)
+    last = lax.all_to_all(send.reshape(count, *send.shape[2:]), order, 0, 0, tiled=True)
     early = [exchange(x, j // plane * ctx + j % plane) for j, x in enumerate(regroup(early))]
     y, grad = homeward(last, early)
     return y.reshape(1, rows * N2, channels), grad

time: 162 us -> 161 us (level)
  waiting for transfers between devices: 90.2 us -> 73.4 us
  starting transfers between devices: 36.7 us -> 52.5 us
    ppermute x20, starting transfers between devices: 25.3 us -> 40.7 us  [exchange(): lax.ppermute(x, axes, [(i, i ^ mask) for i in range(count)])]
    ppermute x20, waiting for transfers between devices: 46.7 us -> 37.4 us  [exchange(): lax.ppermute(x, axes, [(i, i ^ mask) for i in range(count)])]
    all_to_all x2, waiting for transfers between devices: 43.6 us -> 36 us  [the longest x1 21.1 us: by_channel_body(): lax.all_to_all(first, order, 0, 0, tiled=True)]
  transfers between devices with their start and end apart: 22 -> 22, of which waited for: 11 -> 10; matrix products, arithmetic and copies ran while one was open for 0% -> 0% of each run, Pallas kernels for 11% -> 11%
where the time goes in v8:
time: 161 us
  waiting for transfers between devices  73.4 us (46%)
  starting transfers between devices  52.5 us (33%)
  Pallas kernels  24.9 us (15%)
  local copies, waits for them, and re-layouts  8.95 us (6%)
    ppermute x20, starting transfers between devices, exchange(): lax.ppermute(x, axes, [(i, i ^ mask) for i in range(count)])  40.7 us
    ppermute x20, waiting for transfers between devices, exchange(): lax.ppermute(x, axes, [(i, i ^ mask) for i in range(count)])  37.4 us
    all_to_all x1, waiting for transfers between devices, by_channel_body(): lax.all_to_all(first, order, 0, 0, tiled=True)  21.1 us
    all_to_all x1, waiting for transfers between devices, by_channel_body(): lax.all_to_all(send.reshape(count, *send.shape[2:]), order, 0, 0, tiled=T...  14.9 us
    pallas_call x1, Pallas kernels, conv_call(): pl.pallas_call(conv_kernel, grid=(per,), in_specs=[pl.BlockSpec(memory_sp...  10.6 us
    unnamed x32, local copies, waits for them, and re-layouts  8.88 us
    all_to_all x1, starting transfers between devices, by_channel_body(): lax.all_to_all(first, order, 0, 0, tiled=True)  7.3 us
    all_to_all x1, starting transfers between devices, by_channel_body(): lax.all_to_all(send.reshape(count, *send.shape[2:]), order, 0, 0, tiled=T...  4.45 us
  transfers between devices with their start and end apart: 22, of which 10 were waited for; matrix products, arithmetic and copies ran while one was open for 0% of the time, Pallas kernels for 11%

profile of v8, /device:TPU:0, one launch (start us, length us, event | category | flops | bytes accessed | tf_op | source)
XLA Modules:
  0.0 160.6 jit_solution(17557503602984435202)
XLA Ops:
  0.6 4.0 %outward.1 = bf16[32,3,4,16,256]{4,3,2,1,0:T(8,128)(2,1)} custom-call(bf16[1,16,256,128]{3,2,1,0:T(8,128)(2,1)} %bitcast.9, bf16[1,16,256,128]{3,2,1,0:T(8,128)(2,1)} %bitcast.10, f32[2,16,256,128]{3,2,1,0:T(8,128)} %refs_2_.1), custom_call_target="tpu_custom_call" | custom-call | bytes 7340032 | tf_op jit(solution)/shard_map/outward/pallas_call | solution.py:313
  4.7 7.3 %all-to-all-start = ((bf16[32,3,4,16,256]{4,3,2,1,0:T(8,128)(2,1)}), bf16[32,3,4,16,256]{4,3,2,1,0:T(8,128)(2,1)S(1)}, u32[]{:S(2)}, u32[]{:S(2)}) async-start(bf16[32,3,4,16,256]{4,3,2,1,0:T(8,128)(2,1)} %outward.1), calls=%async_computation | async-start | bytes 6291456 | tf_op jit(solution)/shard_map/all_to_all | solution.py:452
  12.0 2.4 %outward_near.1 = (bf16[4,4,16,256]{3,2,1,0:T(8,128)(2,1)S(1)}, bf16[4,4,16,256]{3,2,1,0:T(8,128)(2,1)S(1)}, bf16[4,4,16,256]{3,2,1,0:T(8,128)(2,1)S(1)}, bf16[4...) custom-call(bf16[1,16,256,128]{3,2,1,0:T(8,128)(2,1)} %bitcast.11), custom_call_target="tpu_custom_call" | custom-call | bytes 2097152 | tf_op jit(solution)/shard_map/outward_near/pallas_call | solution.py:350
  16.4 1.7 %collective-permute-start.3 = (bf16[4,4,16,256]{3,2,1,0:T(8,128)(2,1)}, bf16[4,4,16,256]{3,2,1,0:T(8,128)(2,1)}, u32[]{:S(2)}, u32[]{:S(2)}) collective-permute-start(bf16[4,4,16,256]{3,2,1,0:T(8,128)(2,1)} %get-tuple-element.46), channel_id=1, source_target_pairs={{0,16},{1,17},{2,18},{3,19},{4,20},{5,21},{6,22},{7,23},{8,24},{9,... | collective-permute-start | bytes 393224 | tf_op jit(solution)/shard_map/ppermute | solution.py:449
  18.8 2.6 %collective-permute-start.5 = (bf16[4,4,16,256]{3,2,1,0:T(8,128)(2,1)}, bf16[4,4,16,256]{3,2,1,0:T(8,128)(2,1)S(1)}, u32[]{:S(2)}, u32[]{:S(2)}) collective-permute-start(bf16[4,4,16,256]{3,2,1,0:T(8,128)(2,1)} %get-tuple-element.48), channel_id=1, source_target_pairs={{0,18},{1,19},{2,16},{3,17},{4,22},{5,23},{6,20},{7,21},{8,26},{9,... | collective-permute-start | bytes 393224 | tf_op jit(solution)/shard_map/ppermute | solution.py:449
  21.4 11.4 %collective-permute-done.1.refs_2_ = bf16[4,4,16,256]{3,2,1,0:T(8,128)(2,1)S(1)} collective-permute-done((bf16[4,4,16,256]{3,2,1,0:T(8,128)(2,1)S(1)}, bf16[4,4,16,256]{3,2,1,0:T(8,128)(2,1)S(1)}, u32[]{:S(2)}, u32[]{:S(2)}) %collective-permute-start.1) | collective-permute-done | bytes 131104 | tf_op jit(solution)/shard_map/ppermute | solution.py:449
  33.5 13.3 %collective-permute-start.6 = (bf16[4,4,16,256]{3,2,1,0:T(8,128)(2,1)}, bf16[4,4,16,256]{3,2,1,0:T(8,128)(2,1)S(1)}, u32[]{:S(2)}, u32[]{:S(2)}) collective-permute-start(bf16[4,4,16,256]{3,2,1,0:T(8,128)(2,1)} %get-tuple-element.49), channel_id=1, source_target_pairs={{0,19},{1,18},{2,17},{3,16},{4,23},{5,22},{6,21},{7,20},{8,27},{9,... | collective-permute-start | bytes 393224 | tf_op jit(solution)/shard_map/ppermute | solution.py:449
  46.8 4.9 %collective-permute-done.5.refs_6_ = bf16[4,4,16,256]{3,2,1,0:T(8,128)(2,1)S(1)} collective-permute-done((bf16[4,4,16,256]{3,2,1,0:T(8,128)(2,1)}, bf16[4,4,16,256]{3,2,1,0:T(8,128)(2,1)S(1)}, u32[]{:S(2)}, u32[]{:S(2)}) %collective-permute-start.5) | collective-permute-done | bytes 131104 | tf_op jit(solution)/shard_map/ppermute | solution.py:449
  52.4 3.6 %collective-permute-done.6.refs_7_ = bf16[4,4,16,256]{3,2,1,0:T(8,128)(2,1)S(1)} collective-permute-done((bf16[4,4,16,256]{3,2,1,0:T(8,128)(2,1)}, bf16[4,4,16,256]{3,2,1,0:T(8,128)(2,1)S(1)}, u32[]{:S(2)}, u32[]{:S(2)}) %collective-permute-start.6) | collective-permute-done | bytes 131104 | tf_op jit(solution)/shard_map/ppermute | solution.py:449
  60.3 1.9 %regroup.2 = (bf16[8,4,16,256]{3,2,1,0:T(8,128)(2,1)S(1)}, bf16[8,4,16,256]{3,2,1,0:T(8,128)(2,1)}, bf16[8,4,16,256]{3,2,1,0:T(8,128)(2,1)}, bf16[8,4,16,256]{3,2,1,0:T(8,128)(2,1)S(1)}) custom-call(bf16[4,4,16,256]{3,2,1,0:T(8,128)(2,1)S(1)} %get-tuple-element.42.refs_0_, bf16[4,4,16,256]{3,2,1,0:T(8,128)(2,1)S(1)} %copy-done.7, ...), custom_call_target="tpu_custom_call" | custom-call | bytes 2097152 | tf_op jit(solution)/shard_map/regroup/pallas_call | solution.py:371
  62.8 5.4 %collective-permute-start.8 = (bf16[8,4,16,256]{3,2,1,0:T(8,128)(2,1)}, bf16[8,4,16,256]{3,2,1,0:T(8,128)(2,1)}, u32[]{:S(2)}, u32[]{:S(2)}) collective-permute-start(bf16[8,4,16,256]{3,2,1,0:T(8,128)(2,1)} %get-tuple-element.57), channel_id=1, source_target_pairs={{0,8},{1,9},{2,10},{3,11},{4,12},{5,13},{6,14},{7,15},{8,0},{9,1},... | collective-permute-start | bytes 786440 | tf_op jit(solution)/shard_map/ppermute | solution.py:449
  68.2 21.1 %all-to-all-done = bf16[32,3,4,16,256]{4,3,2,1,0:T(8,128)(2,1)S(1)} async-done(((bf16[32,3,4,16,256]{4,3,2,1,0:T(8,128)(2,1)}), bf16[32,3,4,16,256]{4,3,2,1,0:T(8,128)(2,1)S(1)}, u32[]{:S(2)}, u32[]{:S(2)}) %all-to-all-start) | async-done | bytes 3145760 | tf_op jit(solution)/shard_map/all_to_all | solution.py:452
  90.3 10.6 %conv.1 = (bf16[16,2,2,16,256]{4,3,2,1,0:T(8,128)(2,1)S(1)}, f32[4,2,256,256]{3,2,1,0:T(8,128)S(1)}, f32[4,2,144,512]{3,2,1,0:T(8,128)S(1)}, f32[4,2,144,256]{3,...) custom-call(f32[4]{0:T(128)S(1)} %dynamic_slice.3.gain_ref, ...), custom_call_target="tpu_custom_call" | custom-call | flops 4026531840 | bytes 8388608 | tf_op jit(solution)/shard_map/conv/pallas_call | solution.py:235
  101.0 3.4 %collective-permute-start.11 = (bf16[8,2,16,256]{3,2,1,0:T(8,128)(2,1)S(1)}, bf16[8,2,16,256]{3,2,1,0:T(8,128)(2,1)S(1)}, u32[]{:S(2)}, u32[]{:S(2)}) collective-permute-start(bf16[8,2,16,256]{3,2,1,0:T(8,128)(2,1)S(1)} %get-tuple-element.65), channel_id=1, source_target_pairs={{0,8},{1,9},{2,10},{3,11},{4,12},{5,13},{6,14},{7,15},{8,0},{9,1},... | collective-permute-start | bytes 393224 | tf_op jit(solution)/shard_map/ppermute | solution.py:449
  105.4 3.3 %grad.1 = bf16[16,2,6,16,256]{4,3,2,1,0:T(8,128)(2,1)} custom-call(bf16[16,2,3,4,16,256]{5,4,3,2,1,0:T(8,128)(2,1)S(1)} %bitcast.7, f32[4,2,256,256]{3,2,1,0:T(8,128)S(1)} %get-tuple-element.52.gap_ref, f32[4,2,144,512]{3,2,1,0:T(8,128)S(1)} %get-tuple-element.53.spec_ref, f32[4,2,144,256]{3,2,1,0:T(8,128)S(1)} %get-tuple-element.54.part_ref, ...), custom_call_target="tpu_custom_call" | custom-call | flops 805306368 | bytes 8388608 | tf_op jit(solution)/shard_map/grad/pallas_call | solution.py:265
  109.3 5.3 %collective-permute-done.11.refs_2_ = bf16[8,2,16,256]{3,2,1,0:T(8,128)(2,1)S(1)} collective-permute-done((bf16[8,2,16,256]{3,2,1,0:T(8,128)(2,1)S(1)}, bf16[8,2,16,256]{3,2,1,0:T(8,128)(2,1)S(1)}, u32[]{:S(2)}, u32[]{:S(2)}) %collective-permute-start.11) | collective-permute-done | bytes 131104 | tf_op jit(solution)/shard_map/ppermute | solution.py:449
  116.0 4.4 %all-to-all-start.1 = ((bf16[32,6,16,256]{3,2,1,0:T(8,128)(2,1)}), bf16[32,6,16,256]{3,2,1,0:T(8,128)(2,1)S(1)}, u32[]{:S(2)}, u32[]{:S(2)}) async-start(bf16[32,6,16,256]{3,2,1,0:T(8,128)(2,1)} %bitcast.8), calls=%async_computation.1 | async-start | bytes 3145728 | tf_op jit(solution)/shard_map/all_to_all | solution.py:465
  122.5 1.7 %collective-permute-start.16 = (bf16[4,2,16,256]{3,2,1,0:T(8,128)(2,1)S(1)}, bf16[4,2,16,256]{3,2,1,0:T(8,128)(2,1)S(1)}, u32[]{:S(2)}, u32[]{:S(2)}) collective-permute-start(bf16[4,2,16,256]{3,2,1,0:T(8,128)(2,1)S(1)} %get-tuple-element.76), channel_id=1, source_target_pairs={{0,16},{1,17},{2,18},{3,19},{4,20},{5,21},{6,22},{7,23},{8,24},{9,... | collective-permute-start | bytes 196616 | tf_op jit(solution)/shard_map/ppermute | solution.py:449
  124.3 2.6 %collective-permute-start.18 = (bf16[4,2,16,256]{3,2,1,0:T(8,128)(2,1)S(1)}, bf16[4,2,16,256]{3,2,1,0:T(8,128)(2,1)S(1)}, u32[]{:S(2)}, u32[]{:S(2)}) collective-permute-start(bf16[4,2,16,256]{3,2,1,0:T(8,128)(2,1)S(1)} %get-tuple-element.78), channel_id=1, source_target_pairs={{0,18},{1,19},{2,16},{3,17},{4,22},{5,23},{6,20},{7,21},{8,26},{9,... | collective-permute-start | bytes 196616 | tf_op jit(solution)/shard_map/ppermute | solution.py:449
  126.9 5.1 %collective-permute-done.14.refs_2_ = bf16[4,2,16,256]{3,2,1,0:T(8,128)(2,1)S(1)} collective-permute-done((bf16[4,2,16,256]{3,2,1,0:T(8,128)(2,1)S(1)}, bf16[4,2,16,256]{3,2,1,0:T(8,128)(2,1)S(1)}, u32[]{:S(2)}, u32[]{:S(2)}) %collective-permute-start.14) | collective-permute-done | bytes 65568 | tf_op jit(solution)/shard_map/ppermute | solution.py:449
  132.0 4.0 %collective-permute-start.19 = (bf16[4,2,16,256]{3,2,1,0:T(8,128)(2,1)S(1)}, bf16[4,2,16,256]{3,2,1,0:T(8,128)(2,1)S(1)}, u32[]{:S(2)}, u32[]{:S(2)}) collective-permute-start(bf16[4,2,16,256]{3,2,1,0:T(8,128)(2,1)S(1)} %get-tuple-element.79), channel_id=1, source_target_pairs={{0,19},{1,18},{2,17},{3,16},{4,23},{5,22},{6,21},{7,20},{8,27},{9,... | collective-permute-start | bytes 196616 | tf_op jit(solution)/shard_map/ppermute | solution.py:449
  136.6 5.8 %collective-permute-done.18.refs_6_ = bf16[4,2,16,256]{3,2,1,0:T(8,128)(2,1)S(1)} collective-permute-done((bf16[4,2,16,256]{3,2,1,0:T(8,128)(2,1)S(1)}, bf16[4,2,16,256]{3,2,1,0:T(8,128)(2,1)S(1)}, u32[]{:S(2)}, u32[]{:S(2)}) %collective-permute-start.18) | collective-permute-done | bytes 65568 | tf_op jit(solution)/shard_map/ppermute | solution.py:449
  143.0 14.9 %all-to-all-done.1.last_ref = bf16[32,6,16,256]{3,2,1,0:T(8,128)(2,1)S(1)} async-done(((bf16[32,6,16,256]{3,2,1,0:T(8,128)(2,1)}), bf16[32,6,16,256]{3,2,1,0:T(8,128)(2,1)S(1)}, u32[]{:S(2)}, u32[]{:S(2)}) %all-to-all-start.1) | async-done | bytes 1572896 | tf_op jit(solution)/shard_map/all_to_all | solution.py:465
  157.9 2.7 %homeward.1 = (bf16[16,256,128]{2,1,0:T(8,128)(2,1)}, f32[2,16,128,128]{3,2,1,0:T(8,128)}) custom-call(bf16[32,6,16,256]{3,2,1,0:T(8,128)(2,1)S(1)} %all-to-all-done.1.last_ref, bf16[4,2,16,256]{3,2,1,0:T(8,128)(2,1)S(1)} %get-tuple-element.72.refs_0_, bf16[4,2,16,256]{3,2,1,0:T(8,128)(2,1)S(1)} %collective-permute-done.13.refs_1_, ...), custom_call_target="tpu_custom_call" | custom-call | bytes 5242880 | tf_op jit(solution)/shard_map/homeward/pallas_call | solution.py:414
  (60 shorter events, 16.4 us)
Async XLA Ops:
  4.6 42.1 %copy-start.15 = (f32[128]{0:T(128)S(1)}, f32[128]{0:T(128)}, u32[]{:S(2)}) copy-start(f32[128]{0:T(128)} %param.15) | copy-start | bytes 1540
  4.7 84.7 %all-to-all-start = ((bf16[32,3,4,16,256]{4,3,2,1,0:T(8,128)(2,1)}), bf16[32,3,4,16,256]{4,3,2,1,0:T(8,128)(2,1)S(1)}, u32[]{:S(2)}, u32[]{:S(2)}) async-start(bf16[32,3,4,16,256]{4,3,2,1,0:T(8,128)(2,1)} %outward.1), calls=%async_computation | async-start | bytes 6291456 | tf_op jit(solution)/shard_map/all_to_all | solution.py:452
  14.4 3.8 %collective-permute-start = (bf16[4,4,16,256]{3,2,1,0:T(8,128)(2,1)S(1)}, bf16[4,4,16,256]{3,2,1,0:T(8,128)(2,1)S(1)}, u32[]{:S(2)}, u32[]{:S(2)}) collective-permute-start(bf16[4,4,16,256]{3,2,1,0:T(8,128)(2,1)S(1)} %get-tuple-element.43), channel_id=1, source_target_pairs={{0,1},{1,0},{2,3},{3,2},{4,5},{5,4},{6,7},{7,6},{8,9},{9,8},{10,11... | collective-permute-start | bytes 393224 | tf_op jit(solution)/shard_map/ppermute | solution.py:449
  14.7 18.1 %collective-permute-start.1 = (bf16[4,4,16,256]{3,2,1,0:T(8,128)(2,1)S(1)}, bf16[4,4,16,256]{3,2,1,0:T(8,128)(2,1)S(1)}, u32[]{:S(2)}, u32[]{:S(2)}) collective-permute-start(bf16[4,4,16,256]{3,2,1,0:T(8,128)(2,1)S(1)} %get-tuple-element.44), channel_id=1, source_target_pairs={{0,2},{1,3},{2,0},{3,1},{4,6},{5,7},{6,4},{7,5},{8,10},{9,11},{10,... | collective-permute-start | bytes 393224 | tf_op jit(solution)/shard_map/ppermute | solution.py:449
  16.4 30.4 %collective-permute-start.2 = (bf16[4,4,16,256]{3,2,1,0:T(8,128)(2,1)}, bf16[4,4,16,256]{3,2,1,0:T(8,128)(2,1)}, u32[]{:S(2)}, u32[]{:S(2)}) collective-permute-start(bf16[4,4,16,256]{3,2,1,0:T(8,128)(2,1)} %get-tuple-element.45), channel_id=1, source_target_pairs={{0,3},{1,2},{2,1},{3,0},{4,7},{5,6},{6,5},{7,4},{8,11},{9,10},{10,... | collective-permute-start | bytes 393224 | tf_op jit(solution)/shard_map/ppermute | solution.py:449
  16.4 30.4 %collective-permute-start.3 = (bf16[4,4,16,256]{3,2,1,0:T(8,128)(2,1)}, bf16[4,4,16,256]{3,2,1,0:T(8,128)(2,1)}, u32[]{:S(2)}, u32[]{:S(2)}) collective-permute-start(bf16[4,4,16,256]{3,2,1,0:T(8,128)(2,1)} %get-tuple-element.46), channel_id=1, source_target_pairs={{0,16},{1,17},{2,18},{3,19},{4,20},{5,21},{6,22},{7,23},{8,24},{9,... | collective-permute-start | bytes 393224 | tf_op jit(solution)/shard_map/ppermute | solution.py:449
  18.1 28.7 %collective-permute-start.4 = (bf16[4,4,16,256]{3,2,1,0:T(8,128)(2,1)}, bf16[4,4,16,256]{3,2,1,0:T(8,128)(2,1)}, u32[]{:S(2)}, u32[]{:S(2)}) collective-permute-start(bf16[4,4,16,256]{3,2,1,0:T(8,128)(2,1)} %get-tuple-element.47), channel_id=1, source_target_pairs={{0,17},{1,16},{2,19},{3,18},{4,21},{5,20},{6,23},{7,22},{8,25},{9,... | collective-permute-start | bytes 393224 | tf_op jit(solution)/shard_map/ppermute | solution.py:449
  18.8 32.9 %collective-permute-start.5 = (bf16[4,4,16,256]{3,2,1,0:T(8,128)(2,1)}, bf16[4,4,16,256]{3,2,1,0:T(8,128)(2,1)S(1)}, u32[]{:S(2)}, u32[]{:S(2)}) collective-permute-start(bf16[4,4,16,256]{3,2,1,0:T(8,128)(2,1)} %get-tuple-element.48), channel_id=1, source_target_pairs={{0,18},{1,19},{2,16},{3,17},{4,22},{5,23},{6,20},{7,21},{8,26},{9,... | collective-permute-start | bytes 393224 | tf_op jit(solution)/shard_map/ppermute | solution.py:449
  33.5 22.5 %collective-permute-start.6 = (bf16[4,4,16,256]{3,2,1,0:T(8,128)(2,1)}, bf16[4,4,16,256]{3,2,1,0:T(8,128)(2,1)S(1)}, u32[]{:S(2)}, u32[]{:S(2)}) collective-permute-start(bf16[4,4,16,256]{3,2,1,0:T(8,128)(2,1)} %get-tuple-element.49), channel_id=1, source_target_pairs={{0,19},{1,18},{2,17},{3,16},{4,23},{5,22},{6,21},{7,20},{8,27},{9,... | collective-permute-start | bytes 393224 | tf_op jit(solution)/shard_map/ppermute | solution.py:449
  62.8 41.6 %collective-permute-start.7 = (bf16[8,4,16,256]{3,2,1,0:T(8,128)(2,1)}, bf16[8,4,16,256]{3,2,1,0:T(8,128)(2,1)}, u32[]{:S(2)}, u32[]{:S(2)}) collective-permute-start(bf16[8,4,16,256]{3,2,1,0:T(8,128)(2,1)} %get-tuple-element.56), channel_id=1, source_target_pairs={{0,4},{1,5},{2,6},{3,7},{4,0},{5,1},{6,2},{7,3},{8,12},{9,13},{10,... | collective-permute-start | bytes 786440 | tf_op jit(solution)/shard_map/ppermute | solution.py:449
  62.8 42.5 %collective-permute-start.8 = (bf16[8,4,16,256]{3,2,1,0:T(8,128)(2,1)}, bf16[8,4,16,256]{3,2,1,0:T(8,128)(2,1)}, u32[]{:S(2)}, u32[]{:S(2)}) collective-permute-start(bf16[8,4,16,256]{3,2,1,0:T(8,128)(2,1)} %get-tuple-element.57), channel_id=1, source_target_pairs={{0,8},{1,9},{2,10},{3,11},{4,12},{5,13},{6,14},{7,15},{8,0},{9,1},... | collective-permute-start | bytes 786440 | tf_op jit(solution)/shard_map/ppermute | solution.py:449
  89.4 16.0 %collective-permute-start.9 = (bf16[8,4,16,256]{3,2,1,0:T(8,128)(2,1)}, bf16[8,4,16,256]{3,2,1,0:T(8,128)(2,1)S(1)}, u32[]{:S(2)}, u32[]{:S(2)}) collective-permute-start(bf16[8,4,16,256]{3,2,1,0:T(8,128)(2,1)} %copy-done.14), channel_id=1, source_target_pairs={{0,12},{1,13},{2,14},{3,15},{4,8},{5,9},{6,10},{7,11},{8,4},{9,5},... | collective-permute-start | bytes 786440 | tf_op jit(solution)/shard_map/ppermute | solution.py:449
  100.9 7.8 %collective-permute-start.10 = (bf16[8,2,16,256]{3,2,1,0:T(8,128)(2,1)S(1)}, bf16[8,2,16,256]{3,2,1,0:T(8,128)(2,1)S(1)}, u32[]{:S(2)}, u32[]{:S(2)}) collective-permute-start(bf16[8,2,16,256]{3,2,1,0:T(8,128)(2,1)S(1)} %get-tuple-element.64), channel_id=1, source_target_pairs={{0,4},{1,5},{2,6},{3,7},{4,0},{5,1},{6,2},{7,3},{8,12},{9,13},{10,... | collective-permute-start | bytes 393224 | tf_op jit(solution)/shard_map/ppermute | solution.py:449
  101.0 13.7 %collective-permute-start.11 = (bf16[8,2,16,256]{3,2,1,0:T(8,128)(2,1)S(1)}, bf16[8,2,16,256]{3,2,1,0:T(8,128)(2,1)S(1)}, u32[]{:S(2)}, u32[]{:S(2)}) collective-permute-start(bf16[8,2,16,256]{3,2,1,0:T(8,128)(2,1)S(1)} %get-tuple-element.65), channel_id=1, source_target_pairs={{0,8},{1,9},{2,10},{3,11},{4,12},{5,13},{6,14},{7,15},{8,0},{9,1},... | collective-permute-start | bytes 393224 | tf_op jit(solution)/shard_map/ppermute | solution.py:449
  104.4 10.9 %collective-permute-start.12 = (bf16[8,2,16,256]{3,2,1,0:T(8,128)(2,1)S(1)}, bf16[8,2,16,256]{3,2,1,0:T(8,128)(2,1)S(1)}, u32[]{:S(2)}, u32[]{:S(2)}) collective-permute-start(bf16[8,2,16,256]{3,2,1,0:T(8,128)(2,1)S(1)} %get-tuple-element.66), channel_id=1, source_target_pairs={{0,12},{1,13},{2,14},{3,15},{4,8},{5,9},{6,10},{7,11},{8,4},{9,5},... | collective-permute-start | bytes 393224 | tf_op jit(solution)/shard_map/ppermute | solution.py:449
  115.3 5.1 %copy-start.1 = (bf16[8,2,16,256]{3,2,1,0:T(8,128)(2,1)S(1)}, bf16[8,2,16,256]{3,2,1,0:T(8,128)(2,1)}, u32[]{:S(2)}) copy-start(bf16[8,2,16,256]{3,2,1,0:T(8,128)(2,1)} %copy-done) | copy-start | bytes 393220
  116.0 41.9 %all-to-all-start.1 = ((bf16[32,6,16,256]{3,2,1,0:T(8,128)(2,1)}), bf16[32,6,16,256]{3,2,1,0:T(8,128)(2,1)S(1)}, u32[]{:S(2)}, u32[]{:S(2)}) async-start(bf16[32,6,16,256]{3,2,1,0:T(8,128)(2,1)} %bitcast.8), calls=%async_computation.1 | async-start | bytes 3145728 | tf_op jit(solution)/shard_map/all_to_all | solution.py:465
  120.5 3.8 %collective-permute-start.13 = (bf16[4,2,16,256]{3,2,1,0:T(8,128)(2,1)S(1)}, bf16[4,2,16,256]{3,2,1,0:T(8,128)(2,1)S(1)}, u32[]{:S(2)}, u32[]{:S(2)}) collective-permute-start(bf16[4,2,16,256]{3,2,1,0:T(8,128)(2,1)S(1)} %get-tuple-element.73), channel_id=1, source_target_pairs={{0,1},{1,0},{2,3},{3,2},{4,5},{5,4},{6,7},{7,6},{8,9},{9,8},{10,11... | collective-permute-start | bytes 196616 | tf_op jit(solution)/shard_map/ppermute | solution.py:449
  120.8 11.1 %collective-permute-start.14 = (bf16[4,2,16,256]{3,2,1,0:T(8,128)(2,1)S(1)}, bf16[4,2,16,256]{3,2,1,0:T(8,128)(2,1)S(1)}, u32[]{:S(2)}, u32[]{:S(2)}) collective-permute-start(bf16[4,2,16,256]{3,2,1,0:T(8,128)(2,1)S(1)} %get-tuple-element.74), channel_id=1, source_target_pairs={{0,2},{1,3},{2,0},{3,1},{4,6},{5,7},{6,4},{7,5},{8,10},{9,11},{10,... | collective-permute-start | bytes 196616 | tf_op jit(solution)/shard_map/ppermute | solution.py:449
  122.5 14.1 %collective-permute-start.15 = (bf16[4,2,16,256]{3,2,1,0:T(8,128)(2,1)S(1)}, bf16[4,2,16,256]{3,2,1,0:T(8,128)(2,1)S(1)}, u32[]{:S(2)}, u32[]{:S(2)}) collective-permute-start(bf16[4,2,16,256]{3,2,1,0:T(8,128)(2,1)S(1)} %get-tuple-element.75), channel_id=1, source_target_pairs={{0,3},{1,2},{2,1},{3,0},{4,7},{5,6},{6,5},{7,4},{8,11},{9,10},{10,... | collective-permute-start | bytes 196616 | tf_op jit(solution)/shard_map/ppermute | solution.py:449
  122.5 14.1 %collective-permute-start.16 = (bf16[4,2,16,256]{3,2,1,0:T(8,128)(2,1)S(1)}, bf16[4,2,16,256]{3,2,1,0:T(8,128)(2,1)S(1)}, u32[]{:S(2)}, u32[]{:S(2)}) collective-permute-start(bf16[4,2,16,256]{3,2,1,0:T(8,128)(2,1)S(1)} %get-tuple-element.76), channel_id=1, source_target_pairs={{0,16},{1,17},{2,18},{3,19},{4,20},{5,21},{6,22},{7,23},{8,24},{9,... | collective-permute-start | bytes 196616 | tf_op jit(solution)/shard_map/ppermute | solution.py:449
  124.2 12.4 %collective-permute-start.17 = (bf16[4,2,16,256]{3,2,1,0:T(8,128)(2,1)S(1)}, bf16[4,2,16,256]{3,2,1,0:T(8,128)(2,1)S(1)}, u32[]{:S(2)}, u32[]{:S(2)}) collective-permute-start(bf16[4,2,16,256]{3,2,1,0:T(8,128)(2,1)S(1)} %get-tuple-element.77), channel_id=1, source_target_pairs={{0,17},{1,16},{2,19},{3,18},{4,21},{5,20},{6,23},{7,22},{8,25},{9,... | collective-permute-start | bytes 196616 | tf_op jit(solution)/shard_map/ppermute | solution.py:449
  124.3 18.1 %collective-permute-start.18 = (bf16[4,2,16,256]{3,2,1,0:T(8,128)(2,1)S(1)}, bf16[4,2,16,256]{3,2,1,0:T(8,128)(2,1)S(1)}, u32[]{:S(2)}, u32[]{:S(2)}) collective-permute-start(bf16[4,2,16,256]{3,2,1,0:T(8,128)(2,1)S(1)} %get-tuple-element.78), channel_id=1, source_target_pairs={{0,18},{1,19},{2,16},{3,17},{4,22},{5,23},{6,20},{7,21},{8,26},{9,... | collective-permute-start | bytes 196616 | tf_op jit(solution)/shard_map/ppermute | solution.py:449
  132.0 11.1 %collective-permute-start.19 = (bf16[4,2,16,256]{3,2,1,0:T(8,128)(2,1)S(1)}, bf16[4,2,16,256]{3,2,1,0:T(8,128)(2,1)S(1)}, u32[]{:S(2)}, u32[]{:S(2)}) collective-permute-start(bf16[4,2,16,256]{3,2,1,0:T(8,128)(2,1)S(1)} %get-tuple-element.79), channel_id=1, source_target_pairs={{0,19},{1,18},{2,17},{3,16},{4,23},{5,22},{6,21},{7,20},{8,27},{9,... | collective-permute-start | bytes 196616 | tf_op jit(solution)/shard_map/ppermute | solution.py:449
  (14 other events, 17.8 us)

commit v9 on v8

--- a/solution.py
+++ b/solution.py
@@ -462,8 +462,9 @@
     early = [exchange(x, hop * plane) for hop, x in enumerate(early)]
     send = grad_call(received, kept, cots, send)
     send, *early = lax.optimization_barrier((send, *early))
+    send, *early = lax.optimization_barrier((send, *regroup(early)))
     last = lax.all_to_all(send.reshape(count, *send.shape[2:]), order, 0, 0, tiled=True)
-    early = [exchange(x, j // plane * ctx + j % plane) for j, x in enumerate(regroup(early))]
+    early = [exchange(x, j // plane * ctx + j % plane) for j, x in enumerate(early)]
     y, grad = homeward(last, early)
     return y.reshape(1, rows * N2, channels), grad
 

time: 161 us -> 160 us (level)
  local copies, waits for them, and re-layouts: 8.95 us -> 7.04 us
    unnamed x32 -> x20, local copies, waits for them, and re-layouts: 8.88 us -> 6.96 us
where the time goes in v9:
time: 160 us
  waiting for transfers between devices  74.1 us (46%)
  starting transfers between devices  53.2 us (33%)
  Pallas kernels  24.9 us (16%)
  local copies, waits for them, and re-layouts  7.04 us (4%)
    ppermute x20, starting transfers between devices, exchange(): lax.ppermute(x, axes, [(i, i ^ mask) for i in range(count)])  40.7 us
    ppermute x20, waiting for transfers between devices, exchange(): lax.ppermute(x, axes, [(i, i ^ mask) for i in range(count)])  38.1 us
    all_to_all x1, waiting for transfers between devices, by_channel_body(): lax.all_to_all(first, order, 0, 0, tiled=True)  21.1 us
    all_to_all x1, waiting for transfers between devices, by_channel_body(): lax.all_to_all(send.reshape(count, *send.shape[2:]), order, 0, 0, tiled=T...  14.9 us
    pallas_call x1, Pallas kernels, conv_call(): pl.pallas_call(conv_kernel, grid=(per,), in_specs=[pl.BlockSpec(memory_sp...  10.6 us
    all_to_all x1, starting transfers between devices, by_channel_body(): lax.all_to_all(first, order, 0, 0, tiled=True)  7.3 us
    unnamed x20, local copies, waits for them, and re-layouts  6.96 us
    all_to_all x1, starting transfers between devices, by_channel_body(): lax.all_to_all(send.reshape(count, *send.shape[2:]), order, 0, 0, tiled=T...  5.1 us
  transfers between devices with their start and end apart: 22, of which 10 were waited for; matrix products, arithmetic and copies ran while one was open for 0% of the time, Pallas kernels for 11%

profile of v9, /device:TPU:0, one launch (start us, length us, event | category | flops | bytes accessed | tf_op | source)
XLA Modules:
  0.0 160.0 jit_solution(8908933218751236273)
XLA Ops:
  0.6 4.0 %outward.1 = bf16[32,3,4,16,256]{4,3,2,1,0:T(8,128)(2,1)} custom-call(bf16[1,16,256,128]{3,2,1,0:T(8,128)(2,1)} %bitcast.9, bf16[1,16,256,128]{3,2,1,0:T(8,128)(2,1)} %bitcast.10, f32[2,16,256,128]{3,2,1,0:T(8,128)} %refs_2_.1), custom_call_target="tpu_custom_call" | custom-call | bytes 7340032 | tf_op jit(solution)/shard_map/outward/pallas_call | solution.py:313
  4.7 7.3 %all-to-all-start = ((bf16[32,3,4,16,256]{4,3,2,1,0:T(8,128)(2,1)}), bf16[32,3,4,16,256]{4,3,2,1,0:T(8,128)(2,1)S(1)}, u32[]{:S(2)}, u32[]{:S(2)}) async-start(bf16[32,3,4,16,256]{4,3,2,1,0:T(8,128)(2,1)} %outward.1), calls=%async_computation | async-start | bytes 6291456 | tf_op jit(solution)/shard_map/all_to_all | solution.py:452
  12.0 2.4 %outward_near.1 = (bf16[4,4,16,256]{3,2,1,0:T(8,128)(2,1)S(1)}, bf16[4,4,16,256]{3,2,1,0:T(8,128)(2,1)S(1)}, bf16[4,4,16,256]{3,2,1,0:T(8,128)(2,1)S(1)}, bf16[4...) custom-call(bf16[1,16,256,128]{3,2,1,0:T(8,128)(2,1)} %bitcast.11), custom_call_target="tpu_custom_call" | custom-call | bytes 2097152 | tf_op jit(solution)/shard_map/outward_near/pallas_call | solution.py:350
  16.4 1.7 %collective-permute-start.3 = (bf16[4,4,16,256]{3,2,1,0:T(8,128)(2,1)}, bf16[4,4,16,256]{3,2,1,0:T(8,128)(2,1)}, u32[]{:S(2)}, u32[]{:S(2)}) collective-permute-start(bf16[4,4,16,256]{3,2,1,0:T(8,128)(2,1)} %get-tuple-element.55), channel_id=1, source_target_pairs={{0,16},{1,17},{2,18},{3,19},{4,20},{5,21},{6,22},{7,23},{8,24},{9,... | collective-permute-start | bytes 393224 | tf_op jit(solution)/shard_map/ppermute | solution.py:449
  18.9 2.6 %collective-permute-start.5 = (bf16[4,4,16,256]{3,2,1,0:T(8,128)(2,1)}, bf16[4,4,16,256]{3,2,1,0:T(8,128)(2,1)S(1)}, u32[]{:S(2)}, u32[]{:S(2)}) collective-permute-start(bf16[4,4,16,256]{3,2,1,0:T(8,128)(2,1)} %get-tuple-element.57), channel_id=1, source_target_pairs={{0,18},{1,19},{2,16},{3,17},{4,22},{5,23},{6,20},{7,21},{8,26},{9,... | collective-permute-start | bytes 393224 | tf_op jit(solution)/shard_map/ppermute | solution.py:449
  21.4 11.4 %collective-permute-done.1.refs_2_ = bf16[4,4,16,256]{3,2,1,0:T(8,128)(2,1)S(1)} collective-permute-done((bf16[4,4,16,256]{3,2,1,0:T(8,128)(2,1)S(1)}, bf16[4,4,16,256]{3,2,1,0:T(8,128)(2,1)S(1)}, u32[]{:S(2)}, u32[]{:S(2)}) %collective-permute-start.1) | collective-permute-done | bytes 131104 | tf_op jit(solution)/shard_map/ppermute | solution.py:449
  33.5 13.3 %collective-permute-start.6 = (bf16[4,4,16,256]{3,2,1,0:T(8,128)(2,1)}, bf16[4,4,16,256]{3,2,1,0:T(8,128)(2,1)S(1)}, u32[]{:S(2)}, u32[]{:S(2)}) collective-permute-start(bf16[4,4,16,256]{3,2,1,0:T(8,128)(2,1)} %get-tuple-element.58), channel_id=1, source_target_pairs={{0,19},{1,18},{2,17},{3,16},{4,23},{5,22},{6,21},{7,20},{8,27},{9,... | collective-permute-start | bytes 393224 | tf_op jit(solution)/shard_map/ppermute | solution.py:449
  46.8 4.9 %collective-permute-done.5.refs_6_ = bf16[4,4,16,256]{3,2,1,0:T(8,128)(2,1)S(1)} collective-permute-done((bf16[4,4,16,256]{3,2,1,0:T(8,128)(2,1)}, bf16[4,4,16,256]{3,2,1,0:T(8,128)(2,1)S(1)}, u32[]{:S(2)}, u32[]{:S(2)}) %collective-permute-start.5) | collective-permute-done | bytes 131104 | tf_op jit(solution)/shard_map/ppermute | solution.py:449
  52.4 3.6 %collective-permute-done.6.refs_7_ = bf16[4,4,16,256]{3,2,1,0:T(8,128)(2,1)S(1)} collective-permute-done((bf16[4,4,16,256]{3,2,1,0:T(8,128)(2,1)}, bf16[4,4,16,256]{3,2,1,0:T(8,128)(2,1)S(1)}, u32[]{:S(2)}, u32[]{:S(2)}) %collective-permute-start.6) | collective-permute-done | bytes 131104 | tf_op jit(solution)/shard_map/ppermute | solution.py:449
  60.3 1.9 %regroup.2 = (bf16[8,4,16,256]{3,2,1,0:T(8,128)(2,1)S(1)}, bf16[8,4,16,256]{3,2,1,0:T(8,128)(2,1)}, bf16[8,4,16,256]{3,2,1,0:T(8,128)(2,1)}, bf16[8,4,16,256]{3,2,1,0:T(8,128)(2,1)S(1)}) custom-call(bf16[4,4,16,256]{3,2,1,0:T(8,128)(2,1)S(1)} %get-tuple-element.51.refs_0_, bf16[4,4,16,256]{3,2,1,0:T(8,128)(2,1)S(1)} %copy-done.1, ...), custom_call_target="tpu_custom_call" | custom-call | bytes 2097152 | tf_op jit(solution)/shard_map/regroup/pallas_call | solution.py:371
  62.9 5.4 %collective-permute-start.8 = (bf16[8,4,16,256]{3,2,1,0:T(8,128)(2,1)}, bf16[8,4,16,256]{3,2,1,0:T(8,128)(2,1)}, u32[]{:S(2)}, u32[]{:S(2)}) collective-permute-start(bf16[8,4,16,256]{3,2,1,0:T(8,128)(2,1)} %get-tuple-element.66), channel_id=1, source_target_pairs={{0,8},{1,9},{2,10},{3,11},{4,12},{5,13},{6,14},{7,15},{8,0},{9,1},... | collective-permute-start | bytes 786440 | tf_op jit(solution)/shard_map/ppermute | solution.py:449
  68.2 21.1 %all-to-all-done = bf16[32,3,4,16,256]{4,3,2,1,0:T(8,128)(2,1)S(1)} async-done(((bf16[32,3,4,16,256]{4,3,2,1,0:T(8,128)(2,1)}), bf16[32,3,4,16,256]{4,3,2,1,0:T(8,128)(2,1)S(1)}, u32[]{:S(2)}, u32[]{:S(2)}) %all-to-all-start) | async-done | bytes 3145760 | tf_op jit(solution)/shard_map/all_to_all | solution.py:452
  90.3 10.6 %conv.1 = (bf16[16,2,2,16,256]{4,3,2,1,0:T(8,128)(2,1)S(1)}, f32[4,2,256,256]{3,2,1,0:T(8,128)S(1)}, f32[4,2,144,512]{3,2,1,0:T(8,128)S(1)}, f32[4,2,144,256]{3,...) custom-call(f32[4]{0:T(128)S(1)} %dynamic_slice.3.gain_ref, ...), custom_call_target="tpu_custom_call" | custom-call | flops 4026531840 | bytes 8388608 | tf_op jit(solution)/shard_map/conv/pallas_call | solution.py:235
  101.0 3.4 %collective-permute-start.11 = (bf16[8,2,16,256]{3,2,1,0:T(8,128)(2,1)S(1)}, bf16[8,2,16,256]{3,2,1,0:T(8,128)(2,1)S(1)}, u32[]{:S(2)}, u32[]{:S(2)}) collective-permute-start(bf16[8,2,16,256]{3,2,1,0:T(8,128)(2,1)S(1)} %get-tuple-element.74), channel_id=1, source_target_pairs={{0,8},{1,9},{2,10},{3,11},{4,12},{5,13},{6,14},{7,15},{8,0},{9,1},... | collective-permute-start | bytes 393224 | tf_op jit(solution)/shard_map/ppermute | solution.py:449
  105.4 3.3 %grad.1 = bf16[16,2,6,16,256]{4,3,2,1,0:T(8,128)(2,1)} custom-call(bf16[16,2,3,4,16,256]{5,4,3,2,1,0:T(8,128)(2,1)S(1)} %bitcast.7, f32[4,2,256,256]{3,2,1,0:T(8,128)S(1)} %get-tuple-element.61.gap_ref, f32[4,2,144,512]{3,2,1,0:T(8,128)S(1)} %get-tuple-element.62.spec_ref, f32[4,2,144,256]{3,2,1,0:T(8,128)S(1)} %get-tuple-element.63.part_ref, ...), custom_call_target="tpu_custom_call" | custom-call | flops 805306368 | bytes 8388608 | tf_op jit(solution)/shard_map/grad/pallas_call | solution.py:265
  108.7 6.0 %collective-permute-done.11.refs_2_ = bf16[8,2,16,256]{3,2,1,0:T(8,128)(2,1)S(1)} collective-permute-done((bf16[8,2,16,256]{3,2,1,0:T(8,128)(2,1)S(1)}, bf16[8,2,16,256]{3,2,1,0:T(8,128)(2,1)S(1)}, u32[]{:S(2)}, u32[]{:S(2)}) %collective-permute-start.11) | collective-permute-done | bytes 131104 | tf_op jit(solution)/shard_map/ppermute | solution.py:449
  114.7 5.1 %all-to-all-start.1 = ((bf16[32,6,16,256]{3,2,1,0:T(8,128)(2,1)}), bf16[32,6,16,256]{3,2,1,0:T(8,128)(2,1)S(1)}, u32[]{:S(2)}, u32[]{:S(2)}) async-start(bf16[32,6,16,256]{3,2,1,0:T(8,128)(2,1)} %bitcast.8), calls=%async_computation.1 | async-start | bytes 3145728 | tf_op jit(solution)/shard_map/all_to_all | solution.py:466
  121.8 1.7 %collective-permute-start.16 = (bf16[4,2,16,256]{3,2,1,0:T(8,128)(2,1)S(1)}, bf16[4,2,16,256]{3,2,1,0:T(8,128)(2,1)S(1)}, u32[]{:S(2)}, u32[]{:S(2)}) collective-permute-start(bf16[4,2,16,256]{3,2,1,0:T(8,128)(2,1)S(1)} %get-tuple-element.94), channel_id=1, source_target_pairs={{0,16},{1,17},{2,18},{3,19},{4,20},{5,21},{6,22},{7,23},{8,24},{9,... | collective-permute-start | bytes 196616 | tf_op jit(solution)/shard_map/ppermute | solution.py:449
  123.6 2.6 %collective-permute-start.18 = (bf16[4,2,16,256]{3,2,1,0:T(8,128)(2,1)S(1)}, bf16[4,2,16,256]{3,2,1,0:T(8,128)(2,1)S(1)}, u32[]{:S(2)}, u32[]{:S(2)}) collective-permute-start(bf16[4,2,16,256]{3,2,1,0:T(8,128)(2,1)S(1)} %get-tuple-element.96), channel_id=1, source_target_pairs={{0,18},{1,19},{2,16},{3,17},{4,22},{5,23},{6,20},{7,21},{8,26},{9,... | collective-permute-start | bytes 196616 | tf_op jit(solution)/shard_map/ppermute | solution.py:449
  126.2 5.1 %collective-permute-done.14.refs_2_ = bf16[4,2,16,256]{3,2,1,0:T(8,128)(2,1)S(1)} collective-permute-done((bf16[4,2,16,256]{3,2,1,0:T(8,128)(2,1)S(1)}, bf16[4,2,16,256]{3,2,1,0:T(8,128)(2,1)S(1)}, u32[]{:S(2)}, u32[]{:S(2)}) %collective-permute-start.14) | collective-permute-done | bytes 65568 | tf_op jit(solution)/shard_map/ppermute | solution.py:449
  131.4 4.0 %collective-permute-start.19 = (bf16[4,2,16,256]{3,2,1,0:T(8,128)(2,1)S(1)}, bf16[4,2,16,256]{3,2,1,0:T(8,128)(2,1)S(1)}, u32[]{:S(2)}, u32[]{:S(2)}) collective-permute-start(bf16[4,2,16,256]{3,2,1,0:T(8,128)(2,1)S(1)} %get-tuple-element.97), channel_id=1, source_target_pairs={{0,19},{1,18},{2,17},{3,16},{4,23},{5,22},{6,21},{7,20},{8,27},{9,... | collective-permute-start | bytes 196616 | tf_op jit(solution)/shard_map/ppermute | solution.py:449
  136.0 5.8 %collective-permute-done.18.refs_6_ = bf16[4,2,16,256]{3,2,1,0:T(8,128)(2,1)S(1)} collective-permute-done((bf16[4,2,16,256]{3,2,1,0:T(8,128)(2,1)S(1)}, bf16[4,2,16,256]{3,2,1,0:T(8,128)(2,1)S(1)}, u32[]{:S(2)}, u32[]{:S(2)}) %collective-permute-start.18) | collective-permute-done | bytes 65568 | tf_op jit(solution)/shard_map/ppermute | solution.py:449
  142.4 14.9 %all-to-all-done.1.last_ref = bf16[32,6,16,256]{3,2,1,0:T(8,128)(2,1)S(1)} async-done(((bf16[32,6,16,256]{3,2,1,0:T(8,128)(2,1)}), bf16[32,6,16,256]{3,2,1,0:T(8,128)(2,1)S(1)}, u32[]{:S(2)}, u32[]{:S(2)}) %all-to-all-start.1) | async-done | bytes 1572896 | tf_op jit(solution)/shard_map/all_to_all | solution.py:466
  157.3 2.7 %homeward.1 = (bf16[16,256,128]{2,1,0:T(8,128)(2,1)}, f32[2,16,128,128]{3,2,1,0:T(8,128)}) custom-call(bf16[32,6,16,256]{3,2,1,0:T(8,128)(2,1)S(1)} %all-to-all-done.1.last_ref, bf16[4,2,16,256]{3,2,1,0:T(8,128)(2,1)S(1)} %get-tuple-element.90.refs_0_, bf16[4,2,16,256]{3,2,1,0:T(8,128)(2,1)S(1)} %collective-permute-done.13.refs_1_, ...), custom_call_target="tpu_custom_call" | custom-call | bytes 5242880 | tf_op jit(solution)/shard_map/homeward/pallas_call | solution.py:414
  (48 shorter events, 14.5 us)
Async XLA Ops:
  4.7 42.1 %copy-start.9 = (f32[128]{0:T(128)S(1)}, f32[128]{0:T(128)}, u32[]{:S(2)}) copy-start(f32[128]{0:T(128)} %param.15) | copy-start | bytes 1540
  4.7 84.7 %all-to-all-start = ((bf16[32,3,4,16,256]{4,3,2,1,0:T(8,128)(2,1)}), bf16[32,3,4,16,256]{4,3,2,1,0:T(8,128)(2,1)S(1)}, u32[]{:S(2)}, u32[]{:S(2)}) async-start(bf16[32,3,4,16,256]{4,3,2,1,0:T(8,128)(2,1)} %outward.1), calls=%async_computation | async-start | bytes 6291456 | tf_op jit(solution)/shard_map/all_to_all | solution.py:452
  14.4 3.8 %collective-permute-start = (bf16[4,4,16,256]{3,2,1,0:T(8,128)(2,1)S(1)}, bf16[4,4,16,256]{3,2,1,0:T(8,128)(2,1)S(1)}, u32[]{:S(2)}, u32[]{:S(2)}) collective-permute-start(bf16[4,4,16,256]{3,2,1,0:T(8,128)(2,1)S(1)} %get-tuple-element.52), channel_id=1, source_target_pairs={{0,1},{1,0},{2,3},{3,2},{4,5},{5,4},{6,7},{7,6},{8,9},{9,8},{10,11... | collective-permute-start | bytes 393224 | tf_op jit(solution)/shard_map/ppermute | solution.py:449
  14.7 18.1 %collective-permute-start.1 = (bf16[4,4,16,256]{3,2,1,0:T(8,128)(2,1)S(1)}, bf16[4,4,16,256]{3,2,1,0:T(8,128)(2,1)S(1)}, u32[]{:S(2)}, u32[]{:S(2)}) collective-permute-start(bf16[4,4,16,256]{3,2,1,0:T(8,128)(2,1)S(1)} %get-tuple-element.53), channel_id=1, source_target_pairs={{0,2},{1,3},{2,0},{3,1},{4,6},{5,7},{6,4},{7,5},{8,10},{9,11},{10,... | collective-permute-start | bytes 393224 | tf_op jit(solution)/shard_map/ppermute | solution.py:449
  16.4 30.4 %collective-permute-start.2 = (bf16[4,4,16,256]{3,2,1,0:T(8,128)(2,1)}, bf16[4,4,16,256]{3,2,1,0:T(8,128)(2,1)}, u32[]{:S(2)}, u32[]{:S(2)}) collective-permute-start(bf16[4,4,16,256]{3,2,1,0:T(8,128)(2,1)} %get-tuple-element.54), channel_id=1, source_target_pairs={{0,3},{1,2},{2,1},{3,0},{4,7},{5,6},{6,5},{7,4},{8,11},{9,10},{10,... | collective-permute-start | bytes 393224 | tf_op jit(solution)/shard_map/ppermute | solution.py:449
  16.4 30.4 %collective-permute-start.3 = (bf16[4,4,16,256]{3,2,1,0:T(8,128)(2,1)}, bf16[4,4,16,256]{3,2,1,0:T(8,128)(2,1)}, u32[]{:S(2)}, u32[]{:S(2)}) collective-permute-start(bf16[4,4,16,256]{3,2,1,0:T(8,128)(2,1)} %get-tuple-element.55), channel_id=1, source_target_pairs={{0,16},{1,17},{2,18},{3,19},{4,20},{5,21},{6,22},{7,23},{8,24},{9,... | collective-permute-start | bytes 393224 | tf_op jit(solution)/shard_map/ppermute | solution.py:449
  18.1 28.8 %collective-permute-start.4 = (bf16[4,4,16,256]{3,2,1,0:T(8,128)(2,1)}, bf16[4,4,16,256]{3,2,1,0:T(8,128)(2,1)}, u32[]{:S(2)}, u32[]{:S(2)}) collective-permute-start(bf16[4,4,16,256]{3,2,1,0:T(8,128)(2,1)} %get-tuple-element.56), channel_id=1, source_target_pairs={{0,17},{1,16},{2,19},{3,18},{4,21},{5,20},{6,23},{7,22},{8,25},{9,... | collective-permute-start | bytes 393224 | tf_op jit(solution)/shard_map/ppermute | solution.py:449
  18.9 32.9 %collective-permute-start.5 = (bf16[4,4,16,256]{3,2,1,0:T(8,128)(2,1)}, bf16[4,4,16,256]{3,2,1,0:T(8,128)(2,1)S(1)}, u32[]{:S(2)}, u32[]{:S(2)}) collective-permute-start(bf16[4,4,16,256]{3,2,1,0:T(8,128)(2,1)} %get-tuple-element.57), channel_id=1, source_target_pairs={{0,18},{1,19},{2,16},{3,17},{4,22},{5,23},{6,20},{7,21},{8,26},{9,... | collective-permute-start | bytes 393224 | tf_op jit(solution)/shard_map/ppermute | solution.py:449
  33.5 22.5 %collective-permute-start.6 = (bf16[4,4,16,256]{3,2,1,0:T(8,128)(2,1)}, bf16[4,4,16,256]{3,2,1,0:T(8,128)(2,1)S(1)}, u32[]{:S(2)}, u32[]{:S(2)}) collective-permute-start(bf16[4,4,16,256]{3,2,1,0:T(8,128)(2,1)} %get-tuple-element.58), channel_id=1, source_target_pairs={{0,19},{1,18},{2,17},{3,16},{4,23},{5,22},{6,21},{7,20},{8,27},{9,... | collective-permute-start | bytes 393224 | tf_op jit(solution)/shard_map/ppermute | solution.py:449
  57.6 0.9 copy-start.3
  62.9 41.6 %collective-permute-start.7 = (bf16[8,4,16,256]{3,2,1,0:T(8,128)(2,1)}, bf16[8,4,16,256]{3,2,1,0:T(8,128)(2,1)}, u32[]{:S(2)}, u32[]{:S(2)}) collective-permute-start(bf16[8,4,16,256]{3,2,1,0:T(8,128)(2,1)} %get-tuple-element.65), channel_id=1, source_target_pairs={{0,4},{1,5},{2,6},{3,7},{4,0},{5,1},{6,2},{7,3},{8,12},{9,13},{10,... | collective-permute-start | bytes 786440 | tf_op jit(solution)/shard_map/ppermute | solution.py:449
  62.9 42.5 %collective-permute-start.8 = (bf16[8,4,16,256]{3,2,1,0:T(8,128)(2,1)}, bf16[8,4,16,256]{3,2,1,0:T(8,128)(2,1)}, u32[]{:S(2)}, u32[]{:S(2)}) collective-permute-start(bf16[8,4,16,256]{3,2,1,0:T(8,128)(2,1)} %get-tuple-element.66), channel_id=1, source_target_pairs={{0,8},{1,9},{2,10},{3,11},{4,12},{5,13},{6,14},{7,15},{8,0},{9,1},... | collective-permute-start | bytes 786440 | tf_op jit(solution)/shard_map/ppermute | solution.py:449
  89.4 16.0 %collective-permute-start.9 = (bf16[8,4,16,256]{3,2,1,0:T(8,128)(2,1)}, bf16[8,4,16,256]{3,2,1,0:T(8,128)(2,1)S(1)}, u32[]{:S(2)}, u32[]{:S(2)}) collective-permute-start(bf16[8,4,16,256]{3,2,1,0:T(8,128)(2,1)} %copy-done.8), channel_id=1, source_target_pairs={{0,12},{1,13},{2,14},{3,15},{4,8},{5,9},{6,10},{7,11},{8,4},{9,5},... | collective-permute-start | bytes 786440 | tf_op jit(solution)/shard_map/ppermute | solution.py:449
  100.9 7.8 %collective-permute-start.10 = (bf16[8,2,16,256]{3,2,1,0:T(8,128)(2,1)S(1)}, bf16[8,2,16,256]{3,2,1,0:T(8,128)(2,1)S(1)}, u32[]{:S(2)}, u32[]{:S(2)}) collective-permute-start(bf16[8,2,16,256]{3,2,1,0:T(8,128)(2,1)S(1)} %get-tuple-element.73), channel_id=1, source_target_pairs={{0,4},{1,5},{2,6},{3,7},{4,0},{5,1},{6,2},{7,3},{8,12},{9,13},{10,... | collective-permute-start | bytes 393224 | tf_op jit(solution)/shard_map/ppermute | solution.py:449
  101.0 13.7 %collective-permute-start.11 = (bf16[8,2,16,256]{3,2,1,0:T(8,128)(2,1)S(1)}, bf16[8,2,16,256]{3,2,1,0:T(8,128)(2,1)S(1)}, u32[]{:S(2)}, u32[]{:S(2)}) collective-permute-start(bf16[8,2,16,256]{3,2,1,0:T(8,128)(2,1)S(1)} %get-tuple-element.74), channel_id=1, source_target_pairs={{0,8},{1,9},{2,10},{3,11},{4,12},{5,13},{6,14},{7,15},{8,0},{9,1},... | collective-permute-start | bytes 393224 | tf_op jit(solution)/shard_map/ppermute | solution.py:449
  104.4 10.2 %collective-permute-start.12 = (bf16[8,2,16,256]{3,2,1,0:T(8,128)(2,1)S(1)}, bf16[8,2,16,256]{3,2,1,0:T(8,128)(2,1)S(1)}, u32[]{:S(2)}, u32[]{:S(2)}) collective-permute-start(bf16[8,2,16,256]{3,2,1,0:T(8,128)(2,1)S(1)} %get-tuple-element.75), channel_id=1, source_target_pairs={{0,12},{1,13},{2,14},{3,15},{4,8},{5,9},{6,10},{7,11},{8,4},{9,5},... | collective-permute-start | bytes 393224 | tf_op jit(solution)/shard_map/ppermute | solution.py:449
  114.7 42.6 %all-to-all-start.1 = ((bf16[32,6,16,256]{3,2,1,0:T(8,128)(2,1)}), bf16[32,6,16,256]{3,2,1,0:T(8,128)(2,1)S(1)}, u32[]{:S(2)}, u32[]{:S(2)}) async-start(bf16[32,6,16,256]{3,2,1,0:T(8,128)(2,1)} %bitcast.8), calls=%async_computation.1 | async-start | bytes 3145728 | tf_op jit(solution)/shard_map/all_to_all | solution.py:466
  119.8 3.8 %collective-permute-start.13 = (bf16[4,2,16,256]{3,2,1,0:T(8,128)(2,1)S(1)}, bf16[4,2,16,256]{3,2,1,0:T(8,128)(2,1)S(1)}, u32[]{:S(2)}, u32[]{:S(2)}) collective-permute-start(bf16[4,2,16,256]{3,2,1,0:T(8,128)(2,1)S(1)} %get-tuple-element.91), channel_id=1, source_target_pairs={{0,1},{1,0},{2,3},{3,2},{4,5},{5,4},{6,7},{7,6},{8,9},{9,8},{10,11... | collective-permute-start | bytes 196616 | tf_op jit(solution)/shard_map/ppermute | solution.py:449
  120.1 11.2 %collective-permute-start.14 = (bf16[4,2,16,256]{3,2,1,0:T(8,128)(2,1)S(1)}, bf16[4,2,16,256]{3,2,1,0:T(8,128)(2,1)S(1)}, u32[]{:S(2)}, u32[]{:S(2)}) collective-permute-start(bf16[4,2,16,256]{3,2,1,0:T(8,128)(2,1)S(1)} %get-tuple-element.92), channel_id=1, source_target_pairs={{0,2},{1,3},{2,0},{3,1},{4,6},{5,7},{6,4},{7,5},{8,10},{9,11},{10,... | collective-permute-start | bytes 196616 | tf_op jit(solution)/shard_map/ppermute | solution.py:449
  121.8 14.2 %collective-permute-start.15 = (bf16[4,2,16,256]{3,2,1,0:T(8,128)(2,1)S(1)}, bf16[4,2,16,256]{3,2,1,0:T(8,128)(2,1)S(1)}, u32[]{:S(2)}, u32[]{:S(2)}) collective-permute-start(bf16[4,2,16,256]{3,2,1,0:T(8,128)(2,1)S(1)} %get-tuple-element.93), channel_id=1, source_target_pairs={{0,3},{1,2},{2,1},{3,0},{4,7},{5,6},{6,5},{7,4},{8,11},{9,10},{10,... | collective-permute-start | bytes 196616 | tf_op jit(solution)/shard_map/ppermute | solution.py:449
  121.8 14.2 %collective-permute-start.16 = (bf16[4,2,16,256]{3,2,1,0:T(8,128)(2,1)S(1)}, bf16[4,2,16,256]{3,2,1,0:T(8,128)(2,1)S(1)}, u32[]{:S(2)}, u32[]{:S(2)}) collective-permute-start(bf16[4,2,16,256]{3,2,1,0:T(8,128)(2,1)S(1)} %get-tuple-element.94), channel_id=1, source_target_pairs={{0,16},{1,17},{2,18},{3,19},{4,20},{5,21},{6,22},{7,23},{8,24},{9,... | collective-permute-start | bytes 196616 | tf_op jit(solution)/shard_map/ppermute | solution.py:449
  123.5 12.5 %collective-permute-start.17 = (bf16[4,2,16,256]{3,2,1,0:T(8,128)(2,1)S(1)}, bf16[4,2,16,256]{3,2,1,0:T(8,128)(2,1)S(1)}, u32[]{:S(2)}, u32[]{:S(2)}) collective-permute-start(bf16[4,2,16,256]{3,2,1,0:T(8,128)(2,1)S(1)} %get-tuple-element.95), channel_id=1, source_target_pairs={{0,17},{1,16},{2,19},{3,18},{4,21},{5,20},{6,23},{7,22},{8,25},{9,... | collective-permute-start | bytes 196616 | tf_op jit(solution)/shard_map/ppermute | solution.py:449
  123.6 18.2 %collective-permute-start.18 = (bf16[4,2,16,256]{3,2,1,0:T(8,128)(2,1)S(1)}, bf16[4,2,16,256]{3,2,1,0:T(8,128)(2,1)S(1)}, u32[]{:S(2)}, u32[]{:S(2)}) collective-permute-start(bf16[4,2,16,256]{3,2,1,0:T(8,128)(2,1)S(1)} %get-tuple-element.96), channel_id=1, source_target_pairs={{0,18},{1,19},{2,16},{3,17},{4,22},{5,23},{6,20},{7,21},{8,26},{9,... | collective-permute-start | bytes 196616 | tf_op jit(solution)/shard_map/ppermute | solution.py:449
  131.4 11.1 %collective-permute-start.19 = (bf16[4,2,16,256]{3,2,1,0:T(8,128)(2,1)S(1)}, bf16[4,2,16,256]{3,2,1,0:T(8,128)(2,1)S(1)}, u32[]{:S(2)}, u32[]{:S(2)}) collective-permute-start(bf16[4,2,16,256]{3,2,1,0:T(8,128)(2,1)S(1)} %get-tuple-element.97), channel_id=1, source_target_pairs={{0,19},{1,18},{2,17},{3,16},{4,23},{5,22},{6,21},{7,20},{8,27},{9,... | collective-permute-start | bytes 196616 | tf_op jit(solution)/shard_map/ppermute | solution.py:449
  (8 other events, 6.1 us)

commit v10 on v9

--- a/solution.py
+++ b/solution.py
@@ -12,8 +12,7 @@
 N2 = 256
 BF16 = jnp.bfloat16
 F32 = jnp.float32
-EARLY = 2
-KEPT = jnp.float32
+EARLY = 3
 HALF = 144
 VMEM = 26 << 20
 
@@ -94,19 +93,19 @@
 
 def conv_kernel(
     gain_ref, recv_ref, split_ref, fwd_ref, join_ref, mirror_ref, cols_ref, tw_ref,
-    send_ref, gap_ref, spec_ref, part_ref, *refs,
+    gap_ref, spec_ref, part_ref, *refs, early,
 ):
     *refs, y_rows = refs
-    held_refs, early_refs = refs[:3], refs[3:]
     ctx, count = recv_ref.shape[:2]
-    hops, near_count = len(early_refs), early_refs[0].shape[0]
-    here = place(near_count // count)
-    q = pl.program_id(0)
-
-    @pl.when(q == 0)
-    def _():
-        for held_ref, table_ref in zip(held_refs, (split_ref, fwd_ref, tw_ref)):
-            held_ref[...] = table_ref[...]
+    step = pl.program_id(0)
+    q = step if early else step + EARLY
+    if early:
+        held_refs, early_refs = refs[:3], refs[3:]
+
+        @pl.when(step == 0)
+        def _():
+            for held_ref, table_ref in zip(held_refs, (split_ref, fwd_ref, tw_ref)):
+                held_ref[...] = table_ref[...]
 
     tw_cos, tw_sin = tw_ref[0], tw_ref[1]
     signals = []
@@ -147,27 +146,27 @@
         (clean, clean_y), (shifted, shifted_y) = pair
         y_rows[d * ctx : (d + 1) * ctx] = clean_y.astype(BF16).reshape(ctx, -1, N2)
         gap = smart_weight * (shifted_y - clean_y)
-        gap_ref[q, d] = gap.astype(gap_ref.dtype)
-        spec_ref[q, d] = spectra[2 * d].astype(spec_ref.dtype)
+        gap_ref[step, d] = gap
+        spec_ref[step, d] = spectra[2 * d]
         errors.append((shifted * gap).astype(BF16))
     total_real, total_imag = gradient(forward(errors, split_ref, fwd_ref, tw_cos, tw_sin), spectra[1::2])
-    part_ref[q, 0] = total_real
-    part_ref[q, 1] = total_imag
-
-    @pl.when(q < EARLY)
-    def _():
+    part_ref[step, 0] = total_real
+    part_ref[step, 1] = total_imag
+    if early:
+        near_count = early_refs[0].shape[0]
+        here = place(near_count // count)
         for hop, early_ref in enumerate(early_refs):
             for j in range(near_count):
                 side, block = peer(here, j, hop, near_count // count)
-                early_ref[j, q] = y_rows[side * ctx + block]
-
-    @pl.when(q >= EARLY)
-    def _():
+                early_ref[j, step] = y_rows[side * ctx + block]
+    else:
+        (send_ref,) = refs
         for d in range(count):
-            send_ref[:, d, q - EARLY] = y_rows[d * ctx : (d + 1) * ctx]
-
-
-def grad_kernel(recv_ref, gap_ref, spec_ref, part_ref, *refs, hops):
+            send_ref[:, d, step] = y_rows[d * ctx : (d + 1) * ctx]
+
+
+def grad_kernel(recv_ref, *refs, hops):
+    first, second, refs = refs[:3], refs[3:6], refs[6:]
     cot_refs, refs = refs[:hops], refs[hops:]
     split_ref, fwd_ref, tw_ref, y_ref, send_ref, cot_rows, ready_ref, sems = refs
     copies = [pltpu.make_async_copy(y_ref, send_ref.at[:, :, pl.ds(0, y_ref.shape[2])], sems.at[0])]
@@ -181,17 +180,18 @@
         for j in range(near):
             side, block = peer(here, j, hop, plane)
             cot_rows[side * ctx + block] = cot_ref[j]
+    kept = [(first, q) if q < EARLY else (second, q - EARLY) for q in range(per)]
     errors = []
-    for q in range(per):
+    for q, ((gap_ref, _, _), i) in enumerate(kept):
         for d in range(count):
             clean = recv_ref[:, d, 0, q].reshape(N1, N2).astype(F32)
             cot = cot_rows[d * ctx : (d + 1) * ctx, q].reshape(N1, N2).astype(F32)
-            errors.append((clean * (cot - gap_ref[q, d])).astype(BF16))
+            errors.append((clean * (cot - gap_ref[i, d])).astype(BF16))
     err_spectra = forward(errors, split_ref, fwd_ref, tw_ref[0], tw_ref[1])
-    for q in range(per):
-        spectra = [spec_ref[q, d] for d in range(count)]
+    for q, ((_, spec_ref, part_ref), i) in enumerate(kept):
+        spectra = [spec_ref[i, d] for d in range(count)]
         total = gradient(err_spectra[q * count : (q + 1) * count], spectra)
-        fill_grad(ready_ref, q, *[t + part_ref[q, i] for i, t in enumerate(total)])
+        fill_grad(ready_ref, q, *[t + part_ref[i, p] for p, t in enumerate(total)])
         copies.append(pltpu.make_async_copy(ready_ref.at[q], send_ref.at[:, :, per - EARLY + q], sems.at[1 + q]))
         copies[1 + q].start()
     for copy in copies:
@@ -227,35 +227,36 @@
     return pltpu.with_memory_space_constraint(x, pltpu.HBM)
 
 
-def conv_call(gain, received, tabs, plane):
+def conv_call(gain, received, tabs, plane, early):
     ctx, dp, _, per, rows, _ = received.shape
     split_rows, forward_table, *_, twiddle = tabs
-    early = (dp * plane, EARLY, rows, N2)
-    held = [pltpu.VMEM(t.shape, t.dtype) for t in (split_rows, forward_table, twiddle)]
+    steps = EARLY if early else per - EARLY
+    here = pl.BlockSpec(memory_space=pltpu.VMEM)
+    if early:
+        tabs, specs = [far(t) for t in tabs], [whole(t) for t in tabs]
+        held = [pltpu.VMEM(t.shape, t.dtype) for t in (split_rows, forward_table, twiddle)]
+        more = [*held, *[pltpu.VMEM((dp * plane, EARLY, rows, N2), BF16)] * (ctx // plane)]
+    else:
+        inside = (True, True, False, False, False, True)
+        specs = [here if held else whole(t) for t, held in zip(tabs, inside)]
+        tabs = [near(t) if held else far(t) for t, held in zip(tabs, inside)]
+        more = [pltpu.VMEM((ctx, dp, steps, rows, N2), BF16)]
     return pl.pallas_call(
-        conv_kernel,
-        grid=(per,),
-        in_specs=[
-            pl.BlockSpec(memory_space=pltpu.SMEM),
-            pl.BlockSpec(memory_space=pltpu.VMEM),
-            *[whole(t) for t in tabs],
-        ],
-        out_specs=[
-            *[pl.BlockSpec(memory_space=pltpu.VMEM)] * (7 + ctx // plane),
-        ],
+        functools.partial(conv_kernel, early=early),
+        grid=(steps,),
+        in_specs=[pl.BlockSpec(memory_space=pltpu.SMEM), here, *specs],
+        out_specs=[here] * (3 + len(more)),
         out_shape=[
-            pltpu.VMEM((ctx, dp, per - EARLY, rows, N2), BF16),
-            pltpu.VMEM((per, dp, N1, N2), KEPT),
-            pltpu.VMEM((per, dp, HALF, 2 * N2), KEPT),
-            pltpu.VMEM((per, 2, HALF, N2), F32),
-            *held,
-            *[pltpu.VMEM(early, BF16)] * (ctx // plane),
+            pltpu.VMEM((steps, dp, N1, N2), F32),
+            pltpu.VMEM((steps, dp, HALF, 2 * N2), F32),
+            pltpu.VMEM((steps, 2, HALF, N2), F32),
+            *more,
         ],
         scratch_shapes=[pltpu.VMEM((dp * ctx, rows, N2), BF16)],
         compiler_params=pltpu.CompilerParams(vmem_limit_bytes=VMEM),
-        cost_estimate=pl.CostEstimate(flops=per * dp * 5 * 6 * N1**3, bytes_accessed=8 << 20, transcendentals=0),
-        name="conv",
-    )(gain, received, *[far(t) for t in tabs])
+        cost_estimate=pl.CostEstimate(flops=steps * dp * 5 * 6 * N1**3, bytes_accessed=4 << 20, transcendentals=0),
+        name="conv_early" if early else "conv_late",
+    )(gain, received, *tabs)
 
 
 def grad_call(received, kept, cots, send):
@@ -457,10 +458,11 @@
     late, received = lax.optimization_barrier((late, received))
     cots = [exchange(x, hop * plane) for hop, x in enumerate([*early, late])]
     gain = lax.dynamic_slice(skip_gain, ((c * dp + d) * per,), (per,))
-    outs = conv_call(gain, received, tabs, plane)
-    (send, *kept), early = outs[:-hops], outs[-hops:]
+    outs = conv_call(gain, received, tabs, plane, True)
+    kept, held, early = outs[:3], outs[3:6], outs[6:]
     early = [exchange(x, hop * plane) for hop, x in enumerate(early)]
-    send = grad_call(received, kept, cots, send)
+    *kept_late, send = conv_call(gain, received, [*held[:2], *tabs[2:5], held[2]], plane, False)
+    send = grad_call(received, [*kept, *kept_late, *held], cots, send)
     send, *early = lax.optimization_barrier((send, *early))
     send, *early = lax.optimization_barrier((send, *regroup(early)))
     last = lax.all_to_all(send.reshape(count, *send.shape[2:]), order, 0, 0, tiled=True)

time: 160 us -> 160 us (level)
  waiting for transfers between devices: 74.1 us -> 71.1 us
  starting transfers between devices: 53.2 us -> 55.3 us
    all_to_all x1, waiting for transfers between devices: 14.9 us -> 7.48 us  [by_channel_body(): lax.all_to_all(send.reshape(count, *send.shape[2:]), order, 0, 0, tiled=T...]
    ppermute x20, waiting for transfers between devices: 38.1 us -> 42.5 us  [exchange(): lax.ppermute(x, axes, [(i, i ^ mask) for i in range(count)])]
    pallas_call x1 -> x2, Pallas kernels: 10.6 us -> 11.5 us  [conv_call(): pl.pallas_call(functools.partial(conv_kernel, early=early), grid=(steps,)...]
  transfers between devices with their start and end apart: 22 -> 22, of which waited for: 10 -> 9; matrix products, arithmetic and copies ran while one was open for 0% -> 0% of each run, Pallas kernels for 11% -> 12%
where the time goes in v10:
time: 160 us
  waiting for transfers between devices  71.1 us (44%)
  starting transfers between devices  55.3 us (35%)
  Pallas kernels  25.8 us (16%)
  local copies, waits for them, and re-layouts  7.01 us (4%)
    ppermute x20, waiting for transfers between devices, exchange(): lax.ppermute(x, axes, [(i, i ^ mask) for i in range(count)])  42.5 us
    ppermute x20, starting transfers between devices, exchange(): lax.ppermute(x, axes, [(i, i ^ mask) for i in range(count)])  41.4 us
    all_to_all x1, waiting for transfers between devices, by_channel_body(): lax.all_to_all(first, order, 0, 0, tiled=True)  21.1 us
    pallas_call x2, Pallas kernels, conv_call(): pl.pallas_call(functools.partial(conv_kernel, early=early), grid=(steps,)...  11.5 us
    all_to_all x1, waiting for transfers between devices, by_channel_body(): lax.all_to_all(send.reshape(count, *send.shape[2:]), order, 0, 0, tiled=T...  7.48 us
    all_to_all x1, starting transfers between devices, by_channel_body(): lax.all_to_all(first, order, 0, 0, tiled=True)  7.3 us
    unnamed x20, local copies, waits for them, and re-layouts  6.94 us
    all_to_all x1, starting transfers between devices, by_channel_body(): lax.all_to_all(send.reshape(count, *send.shape[2:]), order, 0, 0, tiled=T...  6.51 us
  transfers between devices with their start and end apart: 22, of which 9 were waited for; matrix products, arithmetic and copies ran while one was open for 0% of the time, Pallas kernels for 12%

profile of v10, /device:TPU:0, one launch (start us, length us, event | category | flops | bytes accessed | tf_op | source)
XLA Modules:
  0.0 160.0 jit_solution(8687413052865255968)
XLA Ops:
  0.6 4.0 %outward.1 = bf16[32,3,4,16,256]{4,3,2,1,0:T(8,128)(2,1)} custom-call(bf16[1,16,256,128]{3,2,1,0:T(8,128)(2,1)} %bitcast.10, bf16[1,16,256,128]{3,2,1,0:T(8,128)(2,1)} %bitcast.11, f32[2,16,256,128]{3,2,1,0:T(8,128)} %refs_2_.1), custom_call_target="tpu_custom_call" | custom-call | bytes 7340032 | tf_op jit(solution)/shard_map/outward/pallas_call | solution.py:314
  4.6 7.3 %all-to-all-start = ((bf16[32,3,4,16,256]{4,3,2,1,0:T(8,128)(2,1)}), bf16[32,3,4,16,256]{4,3,2,1,0:T(8,128)(2,1)S(1)}, u32[]{:S(2)}, u32[]{:S(2)}) async-start(bf16[32,3,4,16,256]{4,3,2,1,0:T(8,128)(2,1)} %outward.1), calls=%async_computation | async-start | bytes 6291456 | tf_op jit(solution)/shard_map/all_to_all | solution.py:453
  11.9 2.4 %outward_near.1 = (bf16[4,4,16,256]{3,2,1,0:T(8,128)(2,1)S(1)}, bf16[4,4,16,256]{3,2,1,0:T(8,128)(2,1)S(1)}, bf16[4,4,16,256]{3,2,1,0:T(8,128)(2,1)S(1)}, bf16[4...) custom-call(bf16[1,16,256,128]{3,2,1,0:T(8,128)(2,1)} %bitcast.12), custom_call_target="tpu_custom_call" | custom-call | bytes 2097152 | tf_op jit(solution)/shard_map/outward_near/pallas_call | solution.py:351
  16.3 1.7 %collective-permute-start.3 = (bf16[4,4,16,256]{3,2,1,0:T(8,128)(2,1)}, bf16[4,4,16,256]{3,2,1,0:T(8,128)(2,1)}, u32[]{:S(2)}, u32[]{:S(2)}) collective-permute-start(bf16[4,4,16,256]{3,2,1,0:T(8,128)(2,1)} %get-tuple-element.58), channel_id=1, source_target_pairs={{0,16},{1,17},{2,18},{3,19},{4,20},{5,21},{6,22},{7,23},{8,24},{9,... | collective-permute-start | bytes 393224 | tf_op jit(solution)/shard_map/ppermute | solution.py:450
  18.8 2.6 %collective-permute-start.5 = (bf16[4,4,16,256]{3,2,1,0:T(8,128)(2,1)}, bf16[4,4,16,256]{3,2,1,0:T(8,128)(2,1)S(1)}, u32[]{:S(2)}, u32[]{:S(2)}) collective-permute-start(bf16[4,4,16,256]{3,2,1,0:T(8,128)(2,1)} %get-tuple-element.60), channel_id=1, source_target_pairs={{0,18},{1,19},{2,16},{3,17},{4,22},{5,23},{6,20},{7,21},{8,26},{9,... | collective-permute-start | bytes 393224 | tf_op jit(solution)/shard_map/ppermute | solution.py:450
  21.4 11.4 %collective-permute-done.1.refs_2_ = bf16[4,4,16,256]{3,2,1,0:T(8,128)(2,1)S(1)} collective-permute-done((bf16[4,4,16,256]{3,2,1,0:T(8,128)(2,1)S(1)}, bf16[4,4,16,256]{3,2,1,0:T(8,128)(2,1)S(1)}, u32[]{:S(2)}, u32[]{:S(2)}) %collective-permute-start.1) | collective-permute-done | bytes 131104 | tf_op jit(solution)/shard_map/ppermute | solution.py:450
  33.4 13.3 %collective-permute-start.6 = (bf16[4,4,16,256]{3,2,1,0:T(8,128)(2,1)}, bf16[4,4,16,256]{3,2,1,0:T(8,128)(2,1)S(1)}, u32[]{:S(2)}, u32[]{:S(2)}) collective-permute-start(bf16[4,4,16,256]{3,2,1,0:T(8,128)(2,1)} %get-tuple-element.61), channel_id=1, source_target_pairs={{0,19},{1,18},{2,17},{3,16},{4,23},{5,22},{6,21},{7,20},{8,27},{9,... | collective-permute-start | bytes 393224 | tf_op jit(solution)/shard_map/ppermute | solution.py:450
  46.8 4.9 %collective-permute-done.5.refs_6_ = bf16[4,4,16,256]{3,2,1,0:T(8,128)(2,1)S(1)} collective-permute-done((bf16[4,4,16,256]{3,2,1,0:T(8,128)(2,1)}, bf16[4,4,16,256]{3,2,1,0:T(8,128)(2,1)S(1)}, u32[]{:S(2)}, u32[]{:S(2)}) %collective-permute-start.5) | collective-permute-done | bytes 131104 | tf_op jit(solution)/shard_map/ppermute | solution.py:450
  52.3 3.6 %collective-permute-done.6.refs_7_ = bf16[4,4,16,256]{3,2,1,0:T(8,128)(2,1)S(1)} collective-permute-done((bf16[4,4,16,256]{3,2,1,0:T(8,128)(2,1)}, bf16[4,4,16,256]{3,2,1,0:T(8,128)(2,1)S(1)}, u32[]{:S(2)}, u32[]{:S(2)}) %collective-permute-start.6) | collective-permute-done | bytes 131104 | tf_op jit(solution)/shard_map/ppermute | solution.py:450
  60.2 1.9 %regroup.2 = (bf16[8,4,16,256]{3,2,1,0:T(8,128)(2,1)S(1)}, bf16[8,4,16,256]{3,2,1,0:T(8,128)(2,1)}, bf16[8,4,16,256]{3,2,1,0:T(8,128)(2,1)}, bf16[8,4,16,256]{3,2,1,0:T(8,128)(2,1)S(1)}) custom-call(bf16[4,4,16,256]{3,2,1,0:T(8,128)(2,1)S(1)} %get-tuple-element.54.refs_0_, bf16[4,4,16,256]{3,2,1,0:T(8,128)(2,1)S(1)} %copy-done.1, ...), custom_call_target="tpu_custom_call" | custom-call | bytes 2097152 | tf_op jit(solution)/shard_map/regroup/pallas_call | solution.py:372
  62.8 5.4 %collective-permute-start.8 = (bf16[8,4,16,256]{3,2,1,0:T(8,128)(2,1)}, bf16[8,4,16,256]{3,2,1,0:T(8,128)(2,1)}, u32[]{:S(2)}, u32[]{:S(2)}) collective-permute-start(bf16[8,4,16,256]{3,2,1,0:T(8,128)(2,1)} %get-tuple-element.75), channel_id=1, source_target_pairs={{0,8},{1,9},{2,10},{3,11},{4,12},{5,13},{6,14},{7,15},{8,0},{9,1},... | collective-permute-start | bytes 786440 | tf_op jit(solution)/shard_map/ppermute | solution.py:450
  68.2 21.1 %all-to-all-done = bf16[32,3,4,16,256]{4,3,2,1,0:T(8,128)(2,1)S(1)} async-done(((bf16[32,3,4,16,256]{4,3,2,1,0:T(8,128)(2,1)}), bf16[32,3,4,16,256]{4,3,2,1,0:T(8,128)(2,1)S(1)}, u32[]{:S(2)}, u32[]{:S(2)}) %all-to-all-start) | async-done | bytes 3145760 | tf_op jit(solution)/shard_map/all_to_all | solution.py:453
  90.3 8.2 %conv_early.1 = (f32[3,2,256,256]{3,2,1,0:T(8,128)S(1)}, f32[3,2,144,512]{3,2,1,0:T(8,128)S(1)}, f32[3,2,144,256]{3,2,1,0:T(8,128)S(1)}, bf16[288,256]{1,0:T(8,1...) custom-call(f32[4]{0:T(128)S(1)} %dynamic_slice.3.gain_ref, ...), custom_call_target="tpu_custom_call" | custom-call | flops 3019898880 | bytes 4194304 | tf_op jit(solution)/shard_map/conv_early/pallas_call | solution.py:244
  98.6 3.4 %collective-permute-start.11 = (bf16[8,3,16,256]{3,2,1,0:T(8,128)(2,1)S(1)}, bf16[8,3,16,256]{3,2,1,0:T(8,128)(2,1)S(1)}, u32[]{:S(2)}, u32[]{:S(2)}) collective-permute-start(bf16[8,3,16,256]{3,2,1,0:T(8,128)(2,1)S(1)} %get-tuple-element.80), channel_id=1, source_target_pairs={{0,8},{1,9},{2,10},{3,11},{4,12},{5,13},{6,14},{7,15},{8,0},{9,1},... | collective-permute-start | bytes 589832 | tf_op jit(solution)/shard_map/ppermute | solution.py:450
  102.9 3.3 %conv_late.1 = (f32[1,2,256,256]{3,2,1,0:T(8,128)S(1)}, f32[1,2,144,512]{3,2,1,0:T(8,128)S(1)}, f32[1,2,144,256]{3,2,1,0:T(8,128)S(1)}, bf16[16,2,1,16,256]{4,3,2,1,0:T(8,128)(2,1)S(1)}) custom-call(f32[4]{0:T(128)S(1)} %dynamic_slice.3.gain_ref, bf16[16,2,3,4,16,256]{5,4,3,2,1,0:T(8,128)(2,1)S(1)} %bitcast.7, ...), custom_call_target="tpu_custom_call" | custom-call | flops 1006632960 | bytes 4194304 | tf_op jit(solution)/shard_map/conv_late/pallas_call | solution.py:244
  106.2 3.3 %grad.1 = bf16[16,2,5,16,256]{4,3,2,1,0:T(8,128)(2,1)} custom-call(bf16[16,2,3,4,16,256]{5,4,3,2,1,0:T(8,128)(2,1)S(1)} %bitcast.8, f32[3,2,256,256]{3,2,1,0:T(8,128)S(1)} %get-tuple-element.64.refs_0_, f32[3,2,144,512]{3,2,1,0:T(8,128)S(1)} %get-tuple-element.65.refs_1_, f32[3,2,144,256]{3,2,1,0:T(8,128)S(1)} %get-tuple-element.66.refs_2_, ...), custom_call_target="tpu_custom_call" | custom-call | flops 805306368 | bytes 8388608 | tf_op jit(solution)/shard_map/grad/pallas_call | solution.py:266
  109.6 9.3 %collective-permute-done.11.refs_2_ = bf16[8,3,16,256]{3,2,1,0:T(8,128)(2,1)S(1)} collective-permute-done((bf16[8,3,16,256]{3,2,1,0:T(8,128)(2,1)S(1)}, bf16[8,3,16,256]{3,2,1,0:T(8,128)(2,1)S(1)}, u32[]{:S(2)}, u32[]{:S(2)}) %collective-permute-start.11) | collective-permute-done | bytes 196640 | tf_op jit(solution)/shard_map/ppermute | solution.py:450
  118.9 6.5 %all-to-all-start.1 = ((bf16[32,5,16,256]{3,2,1,0:T(8,128)(2,1)}), bf16[32,5,16,256]{3,2,1,0:T(8,128)(2,1)S(1)}, u32[]{:S(2)}, u32[]{:S(2)}) async-start(bf16[32,5,16,256]{3,2,1,0:T(8,128)(2,1)} %bitcast.9), calls=%async_computation.1 | async-start | bytes 2621440 | tf_op jit(solution)/shard_map/all_to_all | solution.py:468
  129.2 2.6 %collective-permute-start.18 = (bf16[4,3,16,256]{3,2,1,0:T(8,128)(2,1)S(1)}, bf16[4,3,16,256]{3,2,1,0:T(8,128)(2,1)S(1)}, u32[]{:S(2)}, u32[]{:S(2)}) collective-permute-start(bf16[4,3,16,256]{3,2,1,0:T(8,128)(2,1)S(1)} %get-tuple-element.102), channel_id=1, source_target_pairs={{0,18},{1,19},{2,16},{3,17},{4,22},{5,23},{6,20},{7,21},{8,26},{9,... | collective-permute-start | bytes 294920 | tf_op jit(solution)/shard_map/ppermute | solution.py:450
  131.8 5.5 %collective-permute-done.14.refs_2_ = bf16[4,3,16,256]{3,2,1,0:T(8,128)(2,1)S(1)} collective-permute-done((bf16[4,3,16,256]{3,2,1,0:T(8,128)(2,1)S(1)}, bf16[4,3,16,256]{3,2,1,0:T(8,128)(2,1)S(1)}, u32[]{:S(2)}, u32[]{:S(2)}) %collective-permute-start.14) | collective-permute-done | bytes 98336 | tf_op jit(solution)/shard_map/ppermute | solution.py:450
  137.3 4.7 %collective-permute-start.19 = (bf16[4,3,16,256]{3,2,1,0:T(8,128)(2,1)S(1)}, bf16[4,3,16,256]{3,2,1,0:T(8,128)(2,1)S(1)}, u32[]{:S(2)}, u32[]{:S(2)}) collective-permute-start(bf16[4,3,16,256]{3,2,1,0:T(8,128)(2,1)S(1)} %get-tuple-element.103), channel_id=1, source_target_pairs={{0,19},{1,18},{2,17},{3,16},{4,23},{5,22},{6,21},{7,20},{8,27},{9,... | collective-permute-start | bytes 294920 | tf_op jit(solution)/shard_map/ppermute | solution.py:450
  142.0 6.3 %collective-permute-done.18.refs_6_ = bf16[4,3,16,256]{3,2,1,0:T(8,128)(2,1)S(1)} collective-permute-done((bf16[4,3,16,256]{3,2,1,0:T(8,128)(2,1)S(1)}, bf16[4,3,16,256]{3,2,1,0:T(8,128)(2,1)S(1)}, u32[]{:S(2)}, u32[]{:S(2)}) %collective-permute-start.18) | collective-permute-done | bytes 98336 | tf_op jit(solution)/shard_map/ppermute | solution.py:450
  149.8 7.5 %all-to-all-done.1.last_ref = bf16[32,5,16,256]{3,2,1,0:T(8,128)(2,1)S(1)} async-done(((bf16[32,5,16,256]{3,2,1,0:T(8,128)(2,1)}), bf16[32,5,16,256]{3,2,1,0:T(8,128)(2,1)S(1)}, u32[]{:S(2)}, u32[]{:S(2)}) %all-to-all-start.1) | async-done | bytes 1310752 | tf_op jit(solution)/shard_map/all_to_all | solution.py:468
  157.3 2.7 %homeward.1 = (bf16[16,256,128]{2,1,0:T(8,128)(2,1)}, f32[2,16,128,128]{3,2,1,0:T(8,128)}) custom-call(bf16[32,5,16,256]{3,2,1,0:T(8,128)(2,1)S(1)} %all-to-all-done.1.last_ref, bf16[4,3,16,256]{3,2,1,0:T(8,128)(2,1)S(1)} %get-tuple-element.96.refs_0_, bf16[4,3,16,256]{3,2,1,0:T(8,128)(2,1)S(1)} %collective-permute-done.13.refs_1_, ...), custom_call_target="tpu_custom_call" | custom-call | bytes 5242880 | tf_op jit(solution)/shard_map/homeward/pallas_call | solution.py:415
  (49 shorter events, 16.4 us)
Async XLA Ops:
  4.6 42.1 %copy-start.9 = (f32[128]{0:T(128)S(1)}, f32[128]{0:T(128)}, u32[]{:S(2)}) copy-start(f32[128]{0:T(128)} %param.15) | copy-start | bytes 1540
  4.6 84.7 %all-to-all-start = ((bf16[32,3,4,16,256]{4,3,2,1,0:T(8,128)(2,1)}), bf16[32,3,4,16,256]{4,3,2,1,0:T(8,128)(2,1)S(1)}, u32[]{:S(2)}, u32[]{:S(2)}) async-start(bf16[32,3,4,16,256]{4,3,2,1,0:T(8,128)(2,1)} %outward.1), calls=%async_computation | async-start | bytes 6291456 | tf_op jit(solution)/shard_map/all_to_all | solution.py:453
  14.4 3.8 %collective-permute-start = (bf16[4,4,16,256]{3,2,1,0:T(8,128)(2,1)S(1)}, bf16[4,4,16,256]{3,2,1,0:T(8,128)(2,1)S(1)}, u32[]{:S(2)}, u32[]{:S(2)}) collective-permute-start(bf16[4,4,16,256]{3,2,1,0:T(8,128)(2,1)S(1)} %get-tuple-element.55), channel_id=1, source_target_pairs={{0,1},{1,0},{2,3},{3,2},{4,5},{5,4},{6,7},{7,6},{8,9},{9,8},{10,11... | collective-permute-start | bytes 393224 | tf_op jit(solution)/shard_map/ppermute | solution.py:450
  14.6 18.1 %collective-permute-start.1 = (bf16[4,4,16,256]{3,2,1,0:T(8,128)(2,1)S(1)}, bf16[4,4,16,256]{3,2,1,0:T(8,128)(2,1)S(1)}, u32[]{:S(2)}, u32[]{:S(2)}) collective-permute-start(bf16[4,4,16,256]{3,2,1,0:T(8,128)(2,1)S(1)} %get-tuple-element.56), channel_id=1, source_target_pairs={{0,2},{1,3},{2,0},{3,1},{4,6},{5,7},{6,4},{7,5},{8,10},{9,11},{10,... | collective-permute-start | bytes 393224 | tf_op jit(solution)/shard_map/ppermute | solution.py:450
  16.3 30.4 %collective-permute-start.2 = (bf16[4,4,16,256]{3,2,1,0:T(8,128)(2,1)}, bf16[4,4,16,256]{3,2,1,0:T(8,128)(2,1)}, u32[]{:S(2)}, u32[]{:S(2)}) collective-permute-start(bf16[4,4,16,256]{3,2,1,0:T(8,128)(2,1)} %get-tuple-element.57), channel_id=1, source_target_pairs={{0,3},{1,2},{2,1},{3,0},{4,7},{5,6},{6,5},{7,4},{8,11},{9,10},{10,... | collective-permute-start | bytes 393224 | tf_op jit(solution)/shard_map/ppermute | solution.py:450
  16.3 30.4 %collective-permute-start.3 = (bf16[4,4,16,256]{3,2,1,0:T(8,128)(2,1)}, bf16[4,4,16,256]{3,2,1,0:T(8,128)(2,1)}, u32[]{:S(2)}, u32[]{:S(2)}) collective-permute-start(bf16[4,4,16,256]{3,2,1,0:T(8,128)(2,1)} %get-tuple-element.58), channel_id=1, source_target_pairs={{0,16},{1,17},{2,18},{3,19},{4,20},{5,21},{6,22},{7,23},{8,24},{9,... | collective-permute-start | bytes 393224 | tf_op jit(solution)/shard_map/ppermute | solution.py:450
  18.0 28.8 %collective-permute-start.4 = (bf16[4,4,16,256]{3,2,1,0:T(8,128)(2,1)}, bf16[4,4,16,256]{3,2,1,0:T(8,128)(2,1)}, u32[]{:S(2)}, u32[]{:S(2)}) collective-permute-start(bf16[4,4,16,256]{3,2,1,0:T(8,128)(2,1)} %get-tuple-element.59), channel_id=1, source_target_pairs={{0,17},{1,16},{2,19},{3,18},{4,21},{5,20},{6,23},{7,22},{8,25},{9,... | collective-permute-start | bytes 393224 | tf_op jit(solution)/shard_map/ppermute | solution.py:450
  18.8 32.9 %collective-permute-start.5 = (bf16[4,4,16,256]{3,2,1,0:T(8,128)(2,1)}, bf16[4,4,16,256]{3,2,1,0:T(8,128)(2,1)S(1)}, u32[]{:S(2)}, u32[]{:S(2)}) collective-permute-start(bf16[4,4,16,256]{3,2,1,0:T(8,128)(2,1)} %get-tuple-element.60), channel_id=1, source_target_pairs={{0,18},{1,19},{2,16},{3,17},{4,22},{5,23},{6,20},{7,21},{8,26},{9,... | collective-permute-start | bytes 393224 | tf_op jit(solution)/shard_map/ppermute | solution.py:450
  33.4 22.5 %collective-permute-start.6 = (bf16[4,4,16,256]{3,2,1,0:T(8,128)(2,1)}, bf16[4,4,16,256]{3,2,1,0:T(8,128)(2,1)S(1)}, u32[]{:S(2)}, u32[]{:S(2)}) collective-permute-start(bf16[4,4,16,256]{3,2,1,0:T(8,128)(2,1)} %get-tuple-element.61), channel_id=1, source_target_pairs={{0,19},{1,18},{2,17},{3,16},{4,23},{5,22},{6,21},{7,20},{8,27},{9,... | collective-permute-start | bytes 393224 | tf_op jit(solution)/shard_map/ppermute | solution.py:450
  56.6 0.9 copy-start.1
  62.8 39.2 %collective-permute-start.7 = (bf16[8,4,16,256]{3,2,1,0:T(8,128)(2,1)}, bf16[8,4,16,256]{3,2,1,0:T(8,128)(2,1)}, u32[]{:S(2)}, u32[]{:S(2)}) collective-permute-start(bf16[8,4,16,256]{3,2,1,0:T(8,128)(2,1)} %get-tuple-element.74), channel_id=1, source_target_pairs={{0,4},{1,5},{2,6},{3,7},{4,0},{5,1},{6,2},{7,3},{8,12},{9,13},{10,... | collective-permute-start | bytes 786440 | tf_op jit(solution)/shard_map/ppermute | solution.py:450
  62.8 43.4 %collective-permute-start.8 = (bf16[8,4,16,256]{3,2,1,0:T(8,128)(2,1)}, bf16[8,4,16,256]{3,2,1,0:T(8,128)(2,1)}, u32[]{:S(2)}, u32[]{:S(2)}) collective-permute-start(bf16[8,4,16,256]{3,2,1,0:T(8,128)(2,1)} %get-tuple-element.75), channel_id=1, source_target_pairs={{0,8},{1,9},{2,10},{3,11},{4,12},{5,13},{6,14},{7,15},{8,0},{9,1},... | collective-permute-start | bytes 786440 | tf_op jit(solution)/shard_map/ppermute | solution.py:450
  89.3 16.9 %collective-permute-start.9 = (bf16[8,4,16,256]{3,2,1,0:T(8,128)(2,1)}, bf16[8,4,16,256]{3,2,1,0:T(8,128)(2,1)S(1)}, u32[]{:S(2)}, u32[]{:S(2)}) collective-permute-start(bf16[8,4,16,256]{3,2,1,0:T(8,128)(2,1)} %copy-done.8), channel_id=1, source_target_pairs={{0,12},{1,13},{2,14},{3,15},{4,8},{5,9},{6,10},{7,11},{8,4},{9,5},... | collective-permute-start | bytes 786440 | tf_op jit(solution)/shard_map/ppermute | solution.py:450
  98.5 11.1 %collective-permute-start.10 = (bf16[8,3,16,256]{3,2,1,0:T(8,128)(2,1)S(1)}, bf16[8,3,16,256]{3,2,1,0:T(8,128)(2,1)S(1)}, u32[]{:S(2)}, u32[]{:S(2)}) collective-permute-start(bf16[8,3,16,256]{3,2,1,0:T(8,128)(2,1)S(1)} %get-tuple-element.79), channel_id=1, source_target_pairs={{0,4},{1,5},{2,6},{3,7},{4,0},{5,1},{6,2},{7,3},{8,12},{9,13},{10,... | collective-permute-start | bytes 589832 | tf_op jit(solution)/shard_map/ppermute | solution.py:450
  98.6 20.3 %collective-permute-start.11 = (bf16[8,3,16,256]{3,2,1,0:T(8,128)(2,1)S(1)}, bf16[8,3,16,256]{3,2,1,0:T(8,128)(2,1)S(1)}, u32[]{:S(2)}, u32[]{:S(2)}) collective-permute-start(bf16[8,3,16,256]{3,2,1,0:T(8,128)(2,1)S(1)} %get-tuple-element.80), channel_id=1, source_target_pairs={{0,8},{1,9},{2,10},{3,11},{4,12},{5,13},{6,14},{7,15},{8,0},{9,1},... | collective-permute-start | bytes 589832 | tf_op jit(solution)/shard_map/ppermute | solution.py:450
  102.0 16.8 %collective-permute-start.12 = (bf16[8,3,16,256]{3,2,1,0:T(8,128)(2,1)S(1)}, bf16[8,3,16,256]{3,2,1,0:T(8,128)(2,1)S(1)}, u32[]{:S(2)}, u32[]{:S(2)}) collective-permute-start(bf16[8,3,16,256]{3,2,1,0:T(8,128)(2,1)S(1)} %get-tuple-element.81), channel_id=1, source_target_pairs={{0,12},{1,13},{2,14},{3,15},{4,8},{5,9},{6,10},{7,11},{8,4},{9,5},... | collective-permute-start | bytes 589832 | tf_op jit(solution)/shard_map/ppermute | solution.py:450
  118.9 38.4 %all-to-all-start.1 = ((bf16[32,5,16,256]{3,2,1,0:T(8,128)(2,1)}), bf16[32,5,16,256]{3,2,1,0:T(8,128)(2,1)S(1)}, u32[]{:S(2)}, u32[]{:S(2)}) async-start(bf16[32,5,16,256]{3,2,1,0:T(8,128)(2,1)} %bitcast.9), calls=%async_computation.1 | async-start | bytes 2621440 | tf_op jit(solution)/shard_map/all_to_all | solution.py:468
  125.4 3.8 %collective-permute-start.13 = (bf16[4,3,16,256]{3,2,1,0:T(8,128)(2,1)S(1)}, bf16[4,3,16,256]{3,2,1,0:T(8,128)(2,1)S(1)}, u32[]{:S(2)}, u32[]{:S(2)}) collective-permute-start(bf16[4,3,16,256]{3,2,1,0:T(8,128)(2,1)S(1)} %get-tuple-element.97), channel_id=1, source_target_pairs={{0,1},{1,0},{2,3},{3,2},{4,5},{5,4},{6,7},{7,6},{8,9},{9,8},{10,11... | collective-permute-start | bytes 294920 | tf_op jit(solution)/shard_map/ppermute | solution.py:450
  125.7 11.6 %collective-permute-start.14 = (bf16[4,3,16,256]{3,2,1,0:T(8,128)(2,1)S(1)}, bf16[4,3,16,256]{3,2,1,0:T(8,128)(2,1)S(1)}, u32[]{:S(2)}, u32[]{:S(2)}) collective-permute-start(bf16[4,3,16,256]{3,2,1,0:T(8,128)(2,1)S(1)} %get-tuple-element.98), channel_id=1, source_target_pairs={{0,2},{1,3},{2,0},{3,1},{4,6},{5,7},{6,4},{7,5},{8,10},{9,11},{10,... | collective-permute-start | bytes 294920 | tf_op jit(solution)/shard_map/ppermute | solution.py:450
  127.4 14.6 %collective-permute-start.15 = (bf16[4,3,16,256]{3,2,1,0:T(8,128)(2,1)S(1)}, bf16[4,3,16,256]{3,2,1,0:T(8,128)(2,1)S(1)}, u32[]{:S(2)}, u32[]{:S(2)}) collective-permute-start(bf16[4,3,16,256]{3,2,1,0:T(8,128)(2,1)S(1)} %get-tuple-element.99), channel_id=1, source_target_pairs={{0,3},{1,2},{2,1},{3,0},{4,7},{5,6},{6,5},{7,4},{8,11},{9,10},{10,... | collective-permute-start | bytes 294920 | tf_op jit(solution)/shard_map/ppermute | solution.py:450
  127.4 14.6 %collective-permute-start.16 = (bf16[4,3,16,256]{3,2,1,0:T(8,128)(2,1)S(1)}, bf16[4,3,16,256]{3,2,1,0:T(8,128)(2,1)S(1)}, u32[]{:S(2)}, u32[]{:S(2)}) collective-permute-start(bf16[4,3,16,256]{3,2,1,0:T(8,128)(2,1)S(1)} %get-tuple-element.100), channel_id=1, source_target_pairs={{0,16},{1,17},{2,18},{3,19},{4,20},{5,21},{6,22},{7,23},{8,24},{9,... | collective-permute-start | bytes 294920 | tf_op jit(solution)/shard_map/ppermute | solution.py:450
  129.1 12.9 %collective-permute-start.17 = (bf16[4,3,16,256]{3,2,1,0:T(8,128)(2,1)S(1)}, bf16[4,3,16,256]{3,2,1,0:T(8,128)(2,1)S(1)}, u32[]{:S(2)}, u32[]{:S(2)}) collective-permute-start(bf16[4,3,16,256]{3,2,1,0:T(8,128)(2,1)S(1)} %get-tuple-element.101), channel_id=1, source_target_pairs={{0,17},{1,16},{2,19},{3,18},{4,21},{5,20},{6,23},{7,22},{8,25},{9,... | collective-permute-start | bytes 294920 | tf_op jit(solution)/shard_map/ppermute | solution.py:450
  129.2 19.1 %collective-permute-start.18 = (bf16[4,3,16,256]{3,2,1,0:T(8,128)(2,1)S(1)}, bf16[4,3,16,256]{3,2,1,0:T(8,128)(2,1)S(1)}, u32[]{:S(2)}, u32[]{:S(2)}) collective-permute-start(bf16[4,3,16,256]{3,2,1,0:T(8,128)(2,1)S(1)} %get-tuple-element.102), channel_id=1, source_target_pairs={{0,18},{1,19},{2,16},{3,17},{4,22},{5,23},{6,20},{7,21},{8,26},{9,... | collective-permute-start | bytes 294920 | tf_op jit(solution)/shard_map/ppermute | solution.py:450
  137.3 12.4 %collective-permute-start.19 = (bf16[4,3,16,256]{3,2,1,0:T(8,128)(2,1)S(1)}, bf16[4,3,16,256]{3,2,1,0:T(8,128)(2,1)S(1)}, u32[]{:S(2)}, u32[]{:S(2)}) collective-permute-start(bf16[4,3,16,256]{3,2,1,0:T(8,128)(2,1)S(1)} %get-tuple-element.103), channel_id=1, source_target_pairs={{0,19},{1,18},{2,17},{3,16},{4,23},{5,22},{6,21},{7,20},{8,27},{9,... | collective-permute-start | bytes 294920 | tf_op jit(solution)/shard_map/ppermute | solution.py:450
  (8 other events, 6.0 us)

commit v11 on v10

--- a/solution.py
+++ b/solution.py
@@ -454,9 +454,11 @@
     cots = outward_near(matrix(cotangent), count, hops, plane)
     cots = regroup([exchange(x, j // plane * ctx + j % plane) for j, x in enumerate(cots)])
     received = near(received)
-    *early, late = cots
-    late, received = lax.optimization_barrier((late, received))
-    cots = [exchange(x, hop * plane) for hop, x in enumerate([*early, late])]
+    cots = list(cots)
+    cots[1] = exchange(cots[1], plane)
+    cots[1], cots[2] = lax.optimization_barrier((cots[1], cots[2]))
+    cots[3], received = lax.optimization_barrier((cots[3], received))
+    cots[2:] = [exchange(x, (2 + i) * plane) for i, x in enumerate(cots[2:])]
     gain = lax.dynamic_slice(skip_gain, ((c * dp + d) * per,), (per,))
     outs = conv_call(gain, received, tabs, plane, True)
     kept, held, early = outs[:3], outs[3:6], outs[6:]

time: 160 us -> 160 us (level)
  waiting for transfers between devices: 71.1 us -> 79.9 us
  local copies, waits for them, and re-layouts: 7.01 us -> 1.47 us
  starting transfers between devices: 55.3 us -> 53.6 us
  Pallas kernels: 25.8 us -> 24.2 us
    ppermute x20, waiting for transfers between devices: 42.5 us -> 58 us  [exchange(): lax.ppermute(x, axes, [(i, i ^ mask) for i in range(count)])]
    all_to_all x1, waiting for transfers between devices: 21.1 us -> 14.5 us  [by_channel_body(): lax.all_to_all(first, order, 0, 0, tiled=True)]
    unnamed x20 -> x6, local copies, waits for them, and re-layouts: 6.94 us -> 1.4 us
    ppermute x20, starting transfers between devices: 41.4 us -> 39.8 us  [exchange(): lax.ppermute(x, axes, [(i, i ^ mask) for i in range(count)])]
  transfers between devices with their start and end apart: 22 -> 22, of which waited for: 9 -> 10; matrix products, arithmetic and copies ran while one was open for 0% -> 0% of each run, Pallas kernels for 12% -> 11%
where the time goes in v11:
time: 160 us
  waiting for transfers between devices  79.9 us (50%)
  starting transfers between devices  53.6 us (34%)
  Pallas kernels  24.2 us (15%)
    ppermute x20, waiting for transfers between devices, exchange(): lax.ppermute(x, axes, [(i, i ^ mask) for i in range(count)])  58 us
    ppermute x20, starting transfers between devices, exchange(): lax.ppermute(x, axes, [(i, i ^ mask) for i in range(count)])  39.8 us
    all_to_all x1, waiting for transfers between devices, by_channel_body(): lax.all_to_all(first, order, 0, 0, tiled=True)  14.5 us
    pallas_call x2, Pallas kernels, conv_call(): pl.pallas_call(functools.partial(conv_kernel, early=early), grid=(steps,)...  11.5 us
    all_to_all x1, waiting for transfers between devices, by_channel_body(): lax.all_to_all(send.reshape(count, *send.shape[2:]), order, 0, 0, tiled=T...  7.48 us
    all_to_all x1, starting transfers between devices, by_channel_body(): lax.all_to_all(first, order, 0, 0, tiled=True)  7.3 us
    all_to_all x1, starting transfers between devices, by_channel_body(): lax.all_to_all(send.reshape(count, *send.shape[2:]), order, 0, 0, tiled=T...  6.47 us
    pallas_call x1, Pallas kernels, outward(): pl.pallas_call(functools.partial(outward_kernel, count=count), in_specs=[...  4.03 us
  transfers between devices with their start and end apart: 22, of which 10 were waited for; matrix products, arithmetic and copies ran while one was open for 0% of the time, Pallas kernels for 11%

profile of v11, /device:TPU:0, one launch (start us, length us, event | category | flops | bytes accessed | tf_op | source)
XLA Modules:
  0.0 160.0 jit_solution(9008475892199203569)
XLA Ops:
  0.6 4.0 %outward.1 = bf16[32,3,4,16,256]{4,3,2,1,0:T(8,128)(2,1)} custom-call(bf16[1,16,256,128]{3,2,1,0:T(8,128)(2,1)} %bitcast.10, bf16[1,16,256,128]{3,2,1,0:T(8,128)(2,1)} %bitcast.11, f32[2,16,256,128]{3,2,1,0:T(8,128)} %refs_2_.1), custom_call_target="tpu_custom_call" | custom-call | bytes 7340032 | tf_op jit(solution)/shard_map/outward/pallas_call | solution.py:314
  4.7 7.3 %all-to-all-start = ((bf16[32,3,4,16,256]{4,3,2,1,0:T(8,128)(2,1)}), bf16[32,3,4,16,256]{4,3,2,1,0:T(8,128)(2,1)S(1)}, u32[]{:S(2)}, u32[]{:S(2)}) async-start(bf16[32,3,4,16,256]{4,3,2,1,0:T(8,128)(2,1)} %outward.1), calls=%async_computation | async-start | bytes 6291456 | tf_op jit(solution)/shard_map/all_to_all | solution.py:453
  12.0 1.9 %outward_near.1 = (bf16[4,4,16,256]{3,2,1,0:T(8,128)(2,1)S(1)}, bf16[4,4,16,256]{3,2,1,0:T(8,128)(2,1)S(1)}, bf16[4,4,16,256]{3,2,1,0:T(8,128)(2,1)S(1)}, bf16[4...) custom-call(bf16[1,16,256,128]{3,2,1,0:T(8,128)(2,1)} %bitcast.12), custom_call_target="tpu_custom_call" | custom-call | bytes 2097152 | tf_op jit(solution)/shard_map/outward_near/pallas_call | solution.py:351
  15.9 1.7 %collective-permute-start.3 = (bf16[4,4,16,256]{3,2,1,0:T(8,128)(2,1)S(1)}, bf16[4,4,16,256]{3,2,1,0:T(8,128)(2,1)S(1)}, u32[]{:S(2)}, u32[]{:S(2)}) collective-permute-start(bf16[4,4,16,256]{3,2,1,0:T(8,128)(2,1)S(1)} %get-tuple-element.60), channel_id=1, source_target_pairs={{0,16},{1,17},{2,18},{3,19},{4,20},{5,21},{6,22},{7,23},{8,24},{9,... | collective-permute-start | bytes 393224 | tf_op jit(solution)/shard_map/ppermute | solution.py:450
  17.7 2.6 %collective-permute-start.5 = (bf16[4,4,16,256]{3,2,1,0:T(8,128)(2,1)S(1)}, bf16[4,4,16,256]{3,2,1,0:T(8,128)(2,1)S(1)}, u32[]{:S(2)}, u32[]{:S(2)}) collective-permute-start(bf16[4,4,16,256]{3,2,1,0:T(8,128)(2,1)S(1)} %get-tuple-element.62), channel_id=1, source_target_pairs={{0,18},{1,19},{2,16},{3,17},{4,22},{5,23},{6,20},{7,21},{8,26},{9,... | collective-permute-start | bytes 393224 | tf_op jit(solution)/shard_map/ppermute | solution.py:450
  20.3 12.6 %collective-permute-done.1.refs_2_ = bf16[4,4,16,256]{3,2,1,0:T(8,128)(2,1)S(1)} collective-permute-done((bf16[4,4,16,256]{3,2,1,0:T(8,128)(2,1)S(1)}, bf16[4,4,16,256]{3,2,1,0:T(8,128)(2,1)S(1)}, u32[]{:S(2)}, u32[]{:S(2)}) %collective-permute-start.1) | collective-permute-done | bytes 131104 | tf_op jit(solution)/shard_map/ppermute | solution.py:450
  32.8 13.1 %collective-permute-start.6 = (bf16[4,4,16,256]{3,2,1,0:T(8,128)(2,1)S(1)}, bf16[4,4,16,256]{3,2,1,0:T(8,128)(2,1)S(1)}, u32[]{:S(2)}, u32[]{:S(2)}) collective-permute-start(bf16[4,4,16,256]{3,2,1,0:T(8,128)(2,1)S(1)} %get-tuple-element.63), channel_id=1, source_target_pairs={{0,19},{1,18},{2,17},{3,16},{4,23},{5,22},{6,21},{7,20},{8,27},{9,... | collective-permute-start | bytes 393224 | tf_op jit(solution)/shard_map/ppermute | solution.py:450
  46.0 5.7 %collective-permute-done.5.refs_6_ = bf16[4,4,16,256]{3,2,1,0:T(8,128)(2,1)S(1)} collective-permute-done((bf16[4,4,16,256]{3,2,1,0:T(8,128)(2,1)S(1)}, bf16[4,4,16,256]{3,2,1,0:T(8,128)(2,1)S(1)}, u32[]{:S(2)}, u32[]{:S(2)}) %collective-permute-start.5) | collective-permute-done | bytes 131104 | tf_op jit(solution)/shard_map/ppermute | solution.py:450
  51.7 4.3 %collective-permute-done.6.refs_7_ = bf16[4,4,16,256]{3,2,1,0:T(8,128)(2,1)S(1)} collective-permute-done((bf16[4,4,16,256]{3,2,1,0:T(8,128)(2,1)S(1)}, bf16[4,4,16,256]{3,2,1,0:T(8,128)(2,1)S(1)}, u32[]{:S(2)}, u32[]{:S(2)}) %collective-permute-start.6) | collective-permute-done | bytes 131104 | tf_op jit(solution)/shard_map/ppermute | solution.py:450
  58.2 12.8 %collective-permute-done.7.refs_7_ = bf16[8,4,16,256]{3,2,1,0:T(8,128)(2,1)} collective-permute-done((bf16[8,4,16,256]{3,2,1,0:T(8,128)(2,1)}, bf16[8,4,16,256]{3,2,1,0:T(8,128)(2,1)}, u32[]{:S(2)}, u32[]{:S(2)}) %collective-permute-start.7) | collective-permute-done | bytes 262176 | tf_op jit(solution)/shard_map/ppermute | solution.py:450
  71.1 3.8 %collective-permute-start.8 = (bf16[8,4,16,256]{3,2,1,0:T(8,128)(2,1)}, bf16[8,4,16,256]{3,2,1,0:T(8,128)(2,1)}, u32[]{:S(2)}, u32[]{:S(2)}) collective-permute-start(bf16[8,4,16,256]{3,2,1,0:T(8,128)(2,1)} %copy-done.1), channel_id=1, source_target_pairs={{0,8},{1,9},{2,10},{3,11},{4,12},{5,13},{6,14},{7,15},{8,0},{9,1},... | collective-permute-start | bytes 786440 | tf_op jit(solution)/shard_map/ppermute | solution.py:450
  74.9 14.5 %all-to-all-done = bf16[32,3,4,16,256]{4,3,2,1,0:T(8,128)(2,1)S(1)} async-done(((bf16[32,3,4,16,256]{4,3,2,1,0:T(8,128)(2,1)}), bf16[32,3,4,16,256]{4,3,2,1,0:T(8,128)(2,1)S(1)}, u32[]{:S(2)}, u32[]{:S(2)}) %all-to-all-start) | async-done | bytes 3145760 | tf_op jit(solution)/shard_map/all_to_all | solution.py:453
  90.4 8.2 %conv_early.1 = (f32[3,2,256,256]{3,2,1,0:T(8,128)S(1)}, f32[3,2,144,512]{3,2,1,0:T(8,128)S(1)}, f32[3,2,144,256]{3,2,1,0:T(8,128)S(1)}, bf16[288,256]{1,0:T(8,1...) custom-call(f32[4]{0:T(128)S(1)} %dynamic_slice.3.gain_ref, ...), custom_call_target="tpu_custom_call" | custom-call | flops 3019898880 | bytes 4194304 | tf_op jit(solution)/shard_map/conv_early/pallas_call | solution.py:244
  98.6 3.4 %collective-permute-start.11 = (bf16[8,3,16,256]{3,2,1,0:T(8,128)(2,1)S(1)}, bf16[8,3,16,256]{3,2,1,0:T(8,128)(2,1)S(1)}, u32[]{:S(2)}, u32[]{:S(2)}) collective-permute-start(bf16[8,3,16,256]{3,2,1,0:T(8,128)(2,1)S(1)} %get-tuple-element.84), channel_id=1, source_target_pairs={{0,8},{1,9},{2,10},{3,11},{4,12},{5,13},{6,14},{7,15},{8,0},{9,1},... | collective-permute-start | bytes 589832 | tf_op jit(solution)/shard_map/ppermute | solution.py:450
  103.0 3.3 %conv_late.1 = (f32[1,2,256,256]{3,2,1,0:T(8,128)S(1)}, f32[1,2,144,512]{3,2,1,0:T(8,128)S(1)}, f32[1,2,144,256]{3,2,1,0:T(8,128)S(1)}, bf16[16,2,1,16,256]{4,3,2,1,0:T(8,128)(2,1)S(1)}) custom-call(f32[4]{0:T(128)S(1)} %dynamic_slice.3.gain_ref, bf16[16,2,3,4,16,256]{5,4,3,2,1,0:T(8,128)(2,1)S(1)} %bitcast.7, ...), custom_call_target="tpu_custom_call" | custom-call | flops 1006632960 | bytes 4194304 | tf_op jit(solution)/shard_map/conv_late/pallas_call | solution.py:244
  106.3 3.3 %grad.1 = bf16[16,2,5,16,256]{4,3,2,1,0:T(8,128)(2,1)} custom-call(bf16[16,2,3,4,16,256]{5,4,3,2,1,0:T(8,128)(2,1)S(1)} %bitcast.8, f32[3,2,256,256]{3,2,1,0:T(8,128)S(1)} %get-tuple-element.66.refs_0_, f32[3,2,144,512]{3,2,1,0:T(8,128)S(1)} %get-tuple-element.67.refs_1_, f32[3,2,144,256]{3,2,1,0:T(8,128)S(1)} %get-tuple-element.68.refs_2_, ...), custom_call_target="tpu_custom_call" | custom-call | flops 805306368 | bytes 8388608 | tf_op jit(solution)/shard_map/grad/pallas_call | solution.py:266
  109.6 9.2 %collective-permute-done.11.refs_2_ = bf16[8,3,16,256]{3,2,1,0:T(8,128)(2,1)S(1)} collective-permute-done((bf16[8,3,16,256]{3,2,1,0:T(8,128)(2,1)S(1)}, bf16[8,3,16,256]{3,2,1,0:T(8,128)(2,1)S(1)}, u32[]{:S(2)}, u32[]{:S(2)}) %collective-permute-start.11) | collective-permute-done | bytes 196640 | tf_op jit(solution)/shard_map/ppermute | solution.py:450
  118.9 6.5 %all-to-all-start.1 = ((bf16[32,5,16,256]{3,2,1,0:T(8,128)(2,1)}), bf16[32,5,16,256]{3,2,1,0:T(8,128)(2,1)S(1)}, u32[]{:S(2)}, u32[]{:S(2)}) async-start(bf16[32,5,16,256]{3,2,1,0:T(8,128)(2,1)} %bitcast.9), calls=%async_computation.1 | async-start | bytes 2621440 | tf_op jit(solution)/shard_map/all_to_all | solution.py:470
  129.2 2.6 %collective-permute-start.18 = (bf16[4,3,16,256]{3,2,1,0:T(8,128)(2,1)S(1)}, bf16[4,3,16,256]{3,2,1,0:T(8,128)(2,1)S(1)}, u32[]{:S(2)}, u32[]{:S(2)}) collective-permute-start(bf16[4,3,16,256]{3,2,1,0:T(8,128)(2,1)S(1)} %get-tuple-element.106), channel_id=1, source_target_pairs={{0,18},{1,19},{2,16},{3,17},{4,22},{5,23},{6,20},{7,21},{8,26},{9,... | collective-permute-start | bytes 294920 | tf_op jit(solution)/shard_map/ppermute | solution.py:450
  131.8 5.5 %collective-permute-done.14.refs_2_ = bf16[4,3,16,256]{3,2,1,0:T(8,128)(2,1)S(1)} collective-permute-done((bf16[4,3,16,256]{3,2,1,0:T(8,128)(2,1)S(1)}, bf16[4,3,16,256]{3,2,1,0:T(8,128)(2,1)S(1)}, u32[]{:S(2)}, u32[]{:S(2)}) %collective-permute-start.14) | collective-permute-done | bytes 98336 | tf_op jit(solution)/shard_map/ppermute | solution.py:450
  137.3 4.7 %collective-permute-start.19 = (bf16[4,3,16,256]{3,2,1,0:T(8,128)(2,1)S(1)}, bf16[4,3,16,256]{3,2,1,0:T(8,128)(2,1)S(1)}, u32[]{:S(2)}, u32[]{:S(2)}) collective-permute-start(bf16[4,3,16,256]{3,2,1,0:T(8,128)(2,1)S(1)} %get-tuple-element.107), channel_id=1, source_target_pairs={{0,19},{1,18},{2,17},{3,16},{4,23},{5,22},{6,21},{7,20},{8,27},{9,... | collective-permute-start | bytes 294920 | tf_op jit(solution)/shard_map/ppermute | solution.py:450
  142.0 6.3 %collective-permute-done.18.refs_6_ = bf16[4,3,16,256]{3,2,1,0:T(8,128)(2,1)S(1)} collective-permute-done((bf16[4,3,16,256]{3,2,1,0:T(8,128)(2,1)S(1)}, bf16[4,3,16,256]{3,2,1,0:T(8,128)(2,1)S(1)}, u32[]{:S(2)}, u32[]{:S(2)}) %collective-permute-start.18) | collective-permute-done | bytes 98336 | tf_op jit(solution)/shard_map/ppermute | solution.py:450
  149.8 7.5 %all-to-all-done.1.last_ref = bf16[32,5,16,256]{3,2,1,0:T(8,128)(2,1)S(1)} async-done(((bf16[32,5,16,256]{3,2,1,0:T(8,128)(2,1)}), bf16[32,5,16,256]{3,2,1,0:T(8,128)(2,1)S(1)}, u32[]{:S(2)}, u32[]{:S(2)}) %all-to-all-start.1) | async-done | bytes 1310752 | tf_op jit(solution)/shard_map/all_to_all | solution.py:470
  157.3 2.7 %homeward.1 = (bf16[16,256,128]{2,1,0:T(8,128)(2,1)}, f32[2,16,128,128]{3,2,1,0:T(8,128)}) custom-call(bf16[32,5,16,256]{3,2,1,0:T(8,128)(2,1)S(1)} %all-to-all-done.1.last_ref, bf16[4,3,16,256]{3,2,1,0:T(8,128)(2,1)S(1)} %get-tuple-element.100.refs_0_, bf16[4,3,16,256]{3,2,1,0:T(8,128)(2,1)S(1)} %collective-permute-done.13.refs_1_, ...), custom_call_target="tpu_custom_call" | custom-call | bytes 5242880 | tf_op jit(solution)/shard_map/homeward/pallas_call | solution.py:415
  (35 shorter events, 11.7 us)
Async XLA Ops:
  4.7 84.7 %all-to-all-start = ((bf16[32,3,4,16,256]{4,3,2,1,0:T(8,128)(2,1)}), bf16[32,3,4,16,256]{4,3,2,1,0:T(8,128)(2,1)S(1)}, u32[]{:S(2)}, u32[]{:S(2)}) async-start(bf16[32,3,4,16,256]{4,3,2,1,0:T(8,128)(2,1)} %outward.1), calls=%async_computation | async-start | bytes 6291456 | tf_op jit(solution)/shard_map/all_to_all | solution.py:453
  12.0 46.2 %copy-start.2 = (f32[128]{0:T(128)S(1)}, f32[128]{0:T(128)}, u32[]{:S(2)}) copy-start(f32[128]{0:T(128)} %param.15) | copy-start | bytes 1540
  13.9 3.8 %collective-permute-start = (bf16[4,4,16,256]{3,2,1,0:T(8,128)(2,1)S(1)}, bf16[4,4,16,256]{3,2,1,0:T(8,128)(2,1)S(1)}, u32[]{:S(2)}, u32[]{:S(2)}) collective-permute-start(bf16[4,4,16,256]{3,2,1,0:T(8,128)(2,1)S(1)} %get-tuple-element.57), channel_id=1, source_target_pairs={{0,1},{1,0},{2,3},{3,2},{4,5},{5,4},{6,7},{7,6},{8,9},{9,8},{10,11... | collective-permute-start | bytes 393224 | tf_op jit(solution)/shard_map/ppermute | solution.py:450
  14.2 18.7 %collective-permute-start.1 = (bf16[4,4,16,256]{3,2,1,0:T(8,128)(2,1)S(1)}, bf16[4,4,16,256]{3,2,1,0:T(8,128)(2,1)S(1)}, u32[]{:S(2)}, u32[]{:S(2)}) collective-permute-start(bf16[4,4,16,256]{3,2,1,0:T(8,128)(2,1)S(1)} %get-tuple-element.58), channel_id=1, source_target_pairs={{0,2},{1,3},{2,0},{3,1},{4,6},{5,7},{6,4},{7,5},{8,10},{9,11},{10,... | collective-permute-start | bytes 393224 | tf_op jit(solution)/shard_map/ppermute | solution.py:450
  15.9 30.1 %collective-permute-start.2 = (bf16[4,4,16,256]{3,2,1,0:T(8,128)(2,1)S(1)}, bf16[4,4,16,256]{3,2,1,0:T(8,128)(2,1)S(1)}, u32[]{:S(2)}, u32[]{:S(2)}) collective-permute-start(bf16[4,4,16,256]{3,2,1,0:T(8,128)(2,1)S(1)} %get-tuple-element.59), channel_id=1, source_target_pairs={{0,3},{1,2},{2,1},{3,0},{4,7},{5,6},{6,5},{7,4},{8,11},{9,10},{10,... | collective-permute-start | bytes 393224 | tf_op jit(solution)/shard_map/ppermute | solution.py:450
  15.9 30.1 %collective-permute-start.3 = (bf16[4,4,16,256]{3,2,1,0:T(8,128)(2,1)S(1)}, bf16[4,4,16,256]{3,2,1,0:T(8,128)(2,1)S(1)}, u32[]{:S(2)}, u32[]{:S(2)}) collective-permute-start(bf16[4,4,16,256]{3,2,1,0:T(8,128)(2,1)S(1)} %get-tuple-element.60), channel_id=1, source_target_pairs={{0,16},{1,17},{2,18},{3,19},{4,20},{5,21},{6,22},{7,23},{8,24},{9,... | collective-permute-start | bytes 393224 | tf_op jit(solution)/shard_map/ppermute | solution.py:450
  17.6 28.4 %collective-permute-start.4 = (bf16[4,4,16,256]{3,2,1,0:T(8,128)(2,1)S(1)}, bf16[4,4,16,256]{3,2,1,0:T(8,128)(2,1)S(1)}, u32[]{:S(2)}, u32[]{:S(2)}) collective-permute-start(bf16[4,4,16,256]{3,2,1,0:T(8,128)(2,1)S(1)} %get-tuple-element.61), channel_id=1, source_target_pairs={{0,17},{1,16},{2,19},{3,18},{4,21},{5,20},{6,23},{7,22},{8,25},{9,... | collective-permute-start | bytes 393224 | tf_op jit(solution)/shard_map/ppermute | solution.py:450
  17.7 34.0 %collective-permute-start.5 = (bf16[4,4,16,256]{3,2,1,0:T(8,128)(2,1)S(1)}, bf16[4,4,16,256]{3,2,1,0:T(8,128)(2,1)S(1)}, u32[]{:S(2)}, u32[]{:S(2)}) collective-permute-start(bf16[4,4,16,256]{3,2,1,0:T(8,128)(2,1)S(1)} %get-tuple-element.62), channel_id=1, source_target_pairs={{0,18},{1,19},{2,16},{3,17},{4,22},{5,23},{6,20},{7,21},{8,26},{9,... | collective-permute-start | bytes 393224 | tf_op jit(solution)/shard_map/ppermute | solution.py:450
  32.8 23.2 %collective-permute-start.6 = (bf16[4,4,16,256]{3,2,1,0:T(8,128)(2,1)S(1)}, bf16[4,4,16,256]{3,2,1,0:T(8,128)(2,1)S(1)}, u32[]{:S(2)}, u32[]{:S(2)}) collective-permute-start(bf16[4,4,16,256]{3,2,1,0:T(8,128)(2,1)S(1)} %get-tuple-element.63), channel_id=1, source_target_pairs={{0,19},{1,18},{2,17},{3,16},{4,23},{5,22},{6,21},{7,20},{8,27},{9,... | collective-permute-start | bytes 393224 | tf_op jit(solution)/shard_map/ppermute | solution.py:450
  57.5 0.7 copy-start.1
  58.2 12.9 %collective-permute-start.7 = (bf16[8,4,16,256]{3,2,1,0:T(8,128)(2,1)}, bf16[8,4,16,256]{3,2,1,0:T(8,128)(2,1)}, u32[]{:S(2)}, u32[]{:S(2)}) collective-permute-start(bf16[8,4,16,256]{3,2,1,0:T(8,128)(2,1)} %get-tuple-element.76), channel_id=1, source_target_pairs={{0,4},{1,5},{2,6},{3,7},{4,0},{5,1},{6,2},{7,3},{8,12},{9,13},{10,... | collective-permute-start | bytes 786440 | tf_op jit(solution)/shard_map/ppermute | solution.py:450
  71.1 35.2 %collective-permute-start.8 = (bf16[8,4,16,256]{3,2,1,0:T(8,128)(2,1)}, bf16[8,4,16,256]{3,2,1,0:T(8,128)(2,1)}, u32[]{:S(2)}, u32[]{:S(2)}) collective-permute-start(bf16[8,4,16,256]{3,2,1,0:T(8,128)(2,1)} %copy-done.1), channel_id=1, source_target_pairs={{0,8},{1,9},{2,10},{3,11},{4,12},{5,13},{6,14},{7,15},{8,0},{9,1},... | collective-permute-start | bytes 786440 | tf_op jit(solution)/shard_map/ppermute | solution.py:450
  89.4 16.9 %collective-permute-start.9 = (bf16[8,4,16,256]{3,2,1,0:T(8,128)(2,1)}, bf16[8,4,16,256]{3,2,1,0:T(8,128)(2,1)S(1)}, u32[]{:S(2)}, u32[]{:S(2)}) collective-permute-start(bf16[8,4,16,256]{3,2,1,0:T(8,128)(2,1)} %copy-done), channel_id=1, source_target_pairs={{0,12},{1,13},{2,14},{3,15},{4,8},{5,9},{6,10},{7,11},{8,4},{9,5},... | collective-permute-start | bytes 786440 | tf_op jit(solution)/shard_map/ppermute | solution.py:450
  98.6 11.1 %collective-permute-start.10 = (bf16[8,3,16,256]{3,2,1,0:T(8,128)(2,1)S(1)}, bf16[8,3,16,256]{3,2,1,0:T(8,128)(2,1)S(1)}, u32[]{:S(2)}, u32[]{:S(2)}) collective-permute-start(bf16[8,3,16,256]{3,2,1,0:T(8,128)(2,1)S(1)} %get-tuple-element.83), channel_id=1, source_target_pairs={{0,4},{1,5},{2,6},{3,7},{4,0},{5,1},{6,2},{7,3},{8,12},{9,13},{10,... | collective-permute-start | bytes 589832 | tf_op jit(solution)/shard_map/ppermute | solution.py:450
  98.6 20.2 %collective-permute-start.11 = (bf16[8,3,16,256]{3,2,1,0:T(8,128)(2,1)S(1)}, bf16[8,3,16,256]{3,2,1,0:T(8,128)(2,1)S(1)}, u32[]{:S(2)}, u32[]{:S(2)}) collective-permute-start(bf16[8,3,16,256]{3,2,1,0:T(8,128)(2,1)S(1)} %get-tuple-element.84), channel_id=1, source_target_pairs={{0,8},{1,9},{2,10},{3,11},{4,12},{5,13},{6,14},{7,15},{8,0},{9,1},... | collective-permute-start | bytes 589832 | tf_op jit(solution)/shard_map/ppermute | solution.py:450
  102.0 16.8 %collective-permute-start.12 = (bf16[8,3,16,256]{3,2,1,0:T(8,128)(2,1)S(1)}, bf16[8,3,16,256]{3,2,1,0:T(8,128)(2,1)S(1)}, u32[]{:S(2)}, u32[]{:S(2)}) collective-permute-start(bf16[8,3,16,256]{3,2,1,0:T(8,128)(2,1)S(1)} %get-tuple-element.85), channel_id=1, source_target_pairs={{0,12},{1,13},{2,14},{3,15},{4,8},{5,9},{6,10},{7,11},{8,4},{9,5},... | collective-permute-start | bytes 589832 | tf_op jit(solution)/shard_map/ppermute | solution.py:450
  118.9 38.3 %all-to-all-start.1 = ((bf16[32,5,16,256]{3,2,1,0:T(8,128)(2,1)}), bf16[32,5,16,256]{3,2,1,0:T(8,128)(2,1)S(1)}, u32[]{:S(2)}, u32[]{:S(2)}) async-start(bf16[32,5,16,256]{3,2,1,0:T(8,128)(2,1)} %bitcast.9), calls=%async_computation.1 | async-start | bytes 2621440 | tf_op jit(solution)/shard_map/all_to_all | solution.py:470
  125.4 3.8 %collective-permute-start.13 = (bf16[4,3,16,256]{3,2,1,0:T(8,128)(2,1)S(1)}, bf16[4,3,16,256]{3,2,1,0:T(8,128)(2,1)S(1)}, u32[]{:S(2)}, u32[]{:S(2)}) collective-permute-start(bf16[4,3,16,256]{3,2,1,0:T(8,128)(2,1)S(1)} %get-tuple-element.101), channel_id=1, source_target_pairs={{0,1},{1,0},{2,3},{3,2},{4,5},{5,4},{6,7},{7,6},{8,9},{9,8},{10,11... | collective-permute-start | bytes 294920 | tf_op jit(solution)/shard_map/ppermute | solution.py:450
  125.7 11.6 %collective-permute-start.14 = (bf16[4,3,16,256]{3,2,1,0:T(8,128)(2,1)S(1)}, bf16[4,3,16,256]{3,2,1,0:T(8,128)(2,1)S(1)}, u32[]{:S(2)}, u32[]{:S(2)}) collective-permute-start(bf16[4,3,16,256]{3,2,1,0:T(8,128)(2,1)S(1)} %get-tuple-element.102), channel_id=1, source_target_pairs={{0,2},{1,3},{2,0},{3,1},{4,6},{5,7},{6,4},{7,5},{8,10},{9,11},{10,... | collective-permute-start | bytes 294920 | tf_op jit(solution)/shard_map/ppermute | solution.py:450
  127.4 14.6 %collective-permute-start.15 = (bf16[4,3,16,256]{3,2,1,0:T(8,128)(2,1)S(1)}, bf16[4,3,16,256]{3,2,1,0:T(8,128)(2,1)S(1)}, u32[]{:S(2)}, u32[]{:S(2)}) collective-permute-start(bf16[4,3,16,256]{3,2,1,0:T(8,128)(2,1)S(1)} %get-tuple-element.103), channel_id=1, source_target_pairs={{0,3},{1,2},{2,1},{3,0},{4,7},{5,6},{6,5},{7,4},{8,11},{9,10},{10,... | collective-permute-start | bytes 294920 | tf_op jit(solution)/shard_map/ppermute | solution.py:450
  127.4 14.6 %collective-permute-start.16 = (bf16[4,3,16,256]{3,2,1,0:T(8,128)(2,1)S(1)}, bf16[4,3,16,256]{3,2,1,0:T(8,128)(2,1)S(1)}, u32[]{:S(2)}, u32[]{:S(2)}) collective-permute-start(bf16[4,3,16,256]{3,2,1,0:T(8,128)(2,1)S(1)} %get-tuple-element.104), channel_id=1, source_target_pairs={{0,16},{1,17},{2,18},{3,19},{4,20},{5,21},{6,22},{7,23},{8,24},{9,... | collective-permute-start | bytes 294920 | tf_op jit(solution)/shard_map/ppermute | solution.py:450
  129.1 12.9 %collective-permute-start.17 = (bf16[4,3,16,256]{3,2,1,0:T(8,128)(2,1)S(1)}, bf16[4,3,16,256]{3,2,1,0:T(8,128)(2,1)S(1)}, u32[]{:S(2)}, u32[]{:S(2)}) collective-permute-start(bf16[4,3,16,256]{3,2,1,0:T(8,128)(2,1)S(1)} %get-tuple-element.105), channel_id=1, source_target_pairs={{0,17},{1,16},{2,19},{3,18},{4,21},{5,20},{6,23},{7,22},{8,25},{9,... | collective-permute-start | bytes 294920 | tf_op jit(solution)/shard_map/ppermute | solution.py:450
  129.2 19.1 %collective-permute-start.18 = (bf16[4,3,16,256]{3,2,1,0:T(8,128)(2,1)S(1)}, bf16[4,3,16,256]{3,2,1,0:T(8,128)(2,1)S(1)}, u32[]{:S(2)}, u32[]{:S(2)}) collective-permute-start(bf16[4,3,16,256]{3,2,1,0:T(8,128)(2,1)S(1)} %get-tuple-element.106), channel_id=1, source_target_pairs={{0,18},{1,19},{2,16},{3,17},{4,22},{5,23},{6,20},{7,21},{8,26},{9,... | collective-permute-start | bytes 294920 | tf_op jit(solution)/shard_map/ppermute | solution.py:450
  137.3 12.4 %collective-permute-start.19 = (bf16[4,3,16,256]{3,2,1,0:T(8,128)(2,1)S(1)}, bf16[4,3,16,256]{3,2,1,0:T(8,128)(2,1)S(1)}, u32[]{:S(2)}, u32[]{:S(2)}) collective-permute-start(bf16[4,3,16,256]{3,2,1,0:T(8,128)(2,1)S(1)} %get-tuple-element.107), channel_id=1, source_target_pairs={{0,19},{1,18},{2,17},{3,16},{4,23},{5,22},{6,21},{7,20},{8,27},{9,... | collective-permute-start | bytes 294920 | tf_op jit(solution)/shard_map/ppermute | solution.py:450
  (1 other events, 0.7 us)

commit v12 on v10

--- a/solution.py
+++ b/solution.py
@@ -244,7 +244,7 @@
     return pl.pallas_call(
         functools.partial(conv_kernel, early=early),
         grid=(steps,),
-        in_specs=[pl.BlockSpec(memory_space=pltpu.SMEM), here, *specs],
+        in_specs=[here, here, *specs],
         out_specs=[here] * (3 + len(more)),
         out_shape=[
             pltpu.VMEM((steps, dp, N1, N2), F32),
@@ -256,7 +256,7 @@
         compiler_params=pltpu.CompilerParams(vmem_limit_bytes=VMEM),
         cost_estimate=pl.CostEstimate(flops=steps * dp * 5 * 6 * N1**3, bytes_accessed=4 << 20, transcendentals=0),
         name="conv_early" if early else "conv_late",
-    )(gain, received, *tabs)
+    )(near(gain), received, *tabs)
 
 
 def grad_call(received, kept, cots, send):
@@ -458,6 +458,7 @@
     late, received = lax.optimization_barrier((late, received))
     cots = [exchange(x, hop * plane) for hop, x in enumerate([*early, late])]
     gain = lax.dynamic_slice(skip_gain, ((c * dp + d) * per,), (per,))
+    gain = jnp.broadcast_to(gain[:, None, None], (per, 1, N2))
     outs = conv_call(gain, received, tabs, plane, True)
     kept, held, early = outs[:3], outs[3:6], outs[6:]
     early = [exchange(x, hop * plane) for hop, x in enumerate(early)]

time: 160 us -> 160 us (level)
  no operation moved by 1% of the time
where the time goes in v12:
time: 160 us
  waiting for transfers between devices  71.1 us (44%)
  starting transfers between devices  55.3 us (35%)
  Pallas kernels  25.8 us (16%)
  local copies, waits for them, and re-layouts  7.08 us (4%)
    ppermute x20, waiting for transfers between devices, exchange(): lax.ppermute(x, axes, [(i, i ^ mask) for i in range(count)])  42.4 us
    ppermute x20, starting transfers between devices, exchange(): lax.ppermute(x, axes, [(i, i ^ mask) for i in range(count)])  41.4 us
    all_to_all x1, waiting for transfers between devices, by_channel_body(): lax.all_to_all(first, order, 0, 0, tiled=True)  21.1 us
    pallas_call x2, Pallas kernels, conv_call(): pl.pallas_call(functools.partial(conv_kernel, early=early), grid=(steps,)...  11.4 us
    all_to_all x1, waiting for transfers between devices, by_channel_body(): lax.all_to_all(send.reshape(count, *send.shape[2:]), order, 0, 0, tiled=T...  7.48 us
    all_to_all x1, starting transfers between devices, by_channel_body(): lax.all_to_all(first, order, 0, 0, tiled=True)  7.3 us
    unnamed x20, local copies, waits for them, and re-layouts  6.94 us
    all_to_all x1, starting transfers between devices, by_channel_body(): lax.all_to_all(send.reshape(count, *send.shape[2:]), order, 0, 0, tiled=T...  6.51 us
  transfers between devices with their start and end apart: 22, of which 9 were waited for; matrix products, arithmetic and copies ran while one was open for 0% of the time, Pallas kernels for 12%

profile of v12, /device:TPU:0, one launch (start us, length us, event | category | flops | bytes accessed | tf_op | source)
XLA Modules:
  0.0 160.0 jit_solution(8785416555343263322)
XLA Ops:
  0.6 4.0 %outward.1 = bf16[32,3,4,16,256]{4,3,2,1,0:T(8,128)(2,1)} custom-call(bf16[1,16,256,128]{3,2,1,0:T(8,128)(2,1)} %bitcast.10, bf16[1,16,256,128]{3,2,1,0:T(8,128)(2,1)} %bitcast.11, f32[2,16,256,128]{3,2,1,0:T(8,128)} %refs_2_.1), custom_call_target="tpu_custom_call" | custom-call | bytes 7340032 | tf_op jit(solution)/shard_map/outward/pallas_call | solution.py:314
  4.6 7.3 %all-to-all-start = ((bf16[32,3,4,16,256]{4,3,2,1,0:T(8,128)(2,1)}), bf16[32,3,4,16,256]{4,3,2,1,0:T(8,128)(2,1)S(1)}, u32[]{:S(2)}, u32[]{:S(2)}) async-start(bf16[32,3,4,16,256]{4,3,2,1,0:T(8,128)(2,1)} %outward.1), calls=%async_computation | async-start | bytes 6291456 | tf_op jit(solution)/shard_map/all_to_all | solution.py:453
  11.9 2.4 %outward_near.1 = (bf16[4,4,16,256]{3,2,1,0:T(8,128)(2,1)S(1)}, bf16[4,4,16,256]{3,2,1,0:T(8,128)(2,1)S(1)}, bf16[4,4,16,256]{3,2,1,0:T(8,128)(2,1)S(1)}, bf16[4...) custom-call(bf16[1,16,256,128]{3,2,1,0:T(8,128)(2,1)} %bitcast.12), custom_call_target="tpu_custom_call" | custom-call | bytes 2097152 | tf_op jit(solution)/shard_map/outward_near/pallas_call | solution.py:351
  16.3 1.7 %collective-permute-start.3 = (bf16[4,4,16,256]{3,2,1,0:T(8,128)(2,1)}, bf16[4,4,16,256]{3,2,1,0:T(8,128)(2,1)}, u32[]{:S(2)}, u32[]{:S(2)}) collective-permute-start(bf16[4,4,16,256]{3,2,1,0:T(8,128)(2,1)} %get-tuple-element.58), channel_id=1, source_target_pairs={{0,16},{1,17},{2,18},{3,19},{4,20},{5,21},{6,22},{7,23},{8,24},{9,... | collective-permute-start | bytes 393224 | tf_op jit(solution)/shard_map/ppermute | solution.py:450
  18.8 2.6 %collective-permute-start.5 = (bf16[4,4,16,256]{3,2,1,0:T(8,128)(2,1)}, bf16[4,4,16,256]{3,2,1,0:T(8,128)(2,1)S(1)}, u32[]{:S(2)}, u32[]{:S(2)}) collective-permute-start(bf16[4,4,16,256]{3,2,1,0:T(8,128)(2,1)} %get-tuple-element.60), channel_id=1, source_target_pairs={{0,18},{1,19},{2,16},{3,17},{4,22},{5,23},{6,20},{7,21},{8,26},{9,... | collective-permute-start | bytes 393224 | tf_op jit(solution)/shard_map/ppermute | solution.py:450
  21.4 11.4 %collective-permute-done.1.refs_2_ = bf16[4,4,16,256]{3,2,1,0:T(8,128)(2,1)S(1)} collective-permute-done((bf16[4,4,16,256]{3,2,1,0:T(8,128)(2,1)S(1)}, bf16[4,4,16,256]{3,2,1,0:T(8,128)(2,1)S(1)}, u32[]{:S(2)}, u32[]{:S(2)}) %collective-permute-start.1) | collective-permute-done | bytes 131104 | tf_op jit(solution)/shard_map/ppermute | solution.py:450
  33.4 13.3 %collective-permute-start.6 = (bf16[4,4,16,256]{3,2,1,0:T(8,128)(2,1)}, bf16[4,4,16,256]{3,2,1,0:T(8,128)(2,1)S(1)}, u32[]{:S(2)}, u32[]{:S(2)}) collective-permute-start(bf16[4,4,16,256]{3,2,1,0:T(8,128)(2,1)} %get-tuple-element.61), channel_id=1, source_target_pairs={{0,19},{1,18},{2,17},{3,16},{4,23},{5,22},{6,21},{7,20},{8,27},{9,... | collective-permute-start | bytes 393224 | tf_op jit(solution)/shard_map/ppermute | solution.py:450
  46.8 4.9 %collective-permute-done.5.refs_6_ = bf16[4,4,16,256]{3,2,1,0:T(8,128)(2,1)S(1)} collective-permute-done((bf16[4,4,16,256]{3,2,1,0:T(8,128)(2,1)}, bf16[4,4,16,256]{3,2,1,0:T(8,128)(2,1)S(1)}, u32[]{:S(2)}, u32[]{:S(2)}) %collective-permute-start.5) | collective-permute-done | bytes 131104 | tf_op jit(solution)/shard_map/ppermute | solution.py:450
  52.3 3.6 %collective-permute-done.6.refs_7_ = bf16[4,4,16,256]{3,2,1,0:T(8,128)(2,1)S(1)} collective-permute-done((bf16[4,4,16,256]{3,2,1,0:T(8,128)(2,1)}, bf16[4,4,16,256]{3,2,1,0:T(8,128)(2,1)S(1)}, u32[]{:S(2)}, u32[]{:S(2)}) %collective-permute-start.6) | collective-permute-done | bytes 131104 | tf_op jit(solution)/shard_map/ppermute | solution.py:450
  60.2 1.9 %regroup.2 = (bf16[8,4,16,256]{3,2,1,0:T(8,128)(2,1)S(1)}, bf16[8,4,16,256]{3,2,1,0:T(8,128)(2,1)}, bf16[8,4,16,256]{3,2,1,0:T(8,128)(2,1)}, bf16[8,4,16,256]{3,2,1,0:T(8,128)(2,1)S(1)}) custom-call(bf16[4,4,16,256]{3,2,1,0:T(8,128)(2,1)S(1)} %get-tuple-element.54.refs_0_, bf16[4,4,16,256]{3,2,1,0:T(8,128)(2,1)S(1)} %copy-done.1, ...), custom_call_target="tpu_custom_call" | custom-call | bytes 2097152 | tf_op jit(solution)/shard_map/regroup/pallas_call | solution.py:372
  62.8 5.4 %collective-permute-start.8 = (bf16[8,4,16,256]{3,2,1,0:T(8,128)(2,1)}, bf16[8,4,16,256]{3,2,1,0:T(8,128)(2,1)}, u32[]{:S(2)}, u32[]{:S(2)}) collective-permute-start(bf16[8,4,16,256]{3,2,1,0:T(8,128)(2,1)} %get-tuple-element.75), channel_id=1, source_target_pairs={{0,8},{1,9},{2,10},{3,11},{4,12},{5,13},{6,14},{7,15},{8,0},{9,1},... | collective-permute-start | bytes 786440 | tf_op jit(solution)/shard_map/ppermute | solution.py:450
  68.2 21.1 %all-to-all-done = bf16[32,3,4,16,256]{4,3,2,1,0:T(8,128)(2,1)S(1)} async-done(((bf16[32,3,4,16,256]{4,3,2,1,0:T(8,128)(2,1)}), bf16[32,3,4,16,256]{4,3,2,1,0:T(8,128)(2,1)S(1)}, u32[]{:S(2)}, u32[]{:S(2)}) %all-to-all-start) | async-done | bytes 3145760 | tf_op jit(solution)/shard_map/all_to_all | solution.py:453
  90.3 8.2 %conv_early.1 = (f32[3,2,256,256]{3,2,1,0:T(8,128)S(1)}, f32[3,2,144,512]{3,2,1,0:T(8,128)S(1)}, f32[3,2,144,256]{3,2,1,0:T(8,128)S(1)}, bf16[288,256]{1,0:T(8,1...) custom-call(f32[4,1,256]{2,1,0:T(1,128)S(1)} %broadcast_in_dim.2.gai, ...), custom_call_target="tpu_custom_call" | custom-call | flops 3019898880 | bytes 4194304 | tf_op jit(solution)/shard_map/conv_early/pallas_call | solution.py:244
  98.6 3.4 %collective-permute-start.11 = (bf16[8,3,16,256]{3,2,1,0:T(8,128)(2,1)S(1)}, bf16[8,3,16,256]{3,2,1,0:T(8,128)(2,1)S(1)}, u32[]{:S(2)}, u32[]{:S(2)}) collective-permute-start(bf16[8,3,16,256]{3,2,1,0:T(8,128)(2,1)S(1)} %get-tuple-element.80), channel_id=1, source_target_pairs={{0,8},{1,9},{2,10},{3,11},{4,12},{5,13},{6,14},{7,15},{8,0},{9,1},... | collective-permute-start | bytes 589832 | tf_op jit(solution)/shard_map/ppermute | solution.py:450
  103.0 3.3 %conv_late.1 = (f32[1,2,256,256]{3,2,1,0:T(8,128)S(1)}, f32[1,2,144,512]{3,2,1,0:T(8,128)S(1)}, f32[1,2,144,256]{3,2,1,0:T(8,128)S(1)}, bf16[16,2,1,16,256]{4,3,2,1,0:T(8,128)(2,1)S(1)}) custom-call(f32[4,1,256]{2,1,0:T(1,128)S(1)} %broadcast_in_dim.2.gain_ref, bf16[16,2,3,4,16,256]{5,4,3,2,1,0:T(8,128)(2,1)S(1)} %bitcast.7, ...), custom_call_target="tpu_custom_call" | custom-call | flops 1006632960 | bytes 4194304 | tf_op jit(solution)/shard_map/conv_late/pallas_call | solution.py:244
  106.3 3.3 %grad.1 = bf16[16,2,5,16,256]{4,3,2,1,0:T(8,128)(2,1)} custom-call(bf16[16,2,3,4,16,256]{5,4,3,2,1,0:T(8,128)(2,1)S(1)} %bitcast.8, f32[3,2,256,256]{3,2,1,0:T(8,128)S(1)} %get-tuple-element.64.refs_0_, f32[3,2,144,512]{3,2,1,0:T(8,128)S(1)} %get-tuple-element.65.refs_1_, f32[3,2,144,256]{3,2,1,0:T(8,128)S(1)} %get-tuple-element.66.refs_2_, ...), custom_call_target="tpu_custom_call" | custom-call | flops 805306368 | bytes 8388608 | tf_op jit(solution)/shard_map/grad/pallas_call | solution.py:266
  109.6 9.2 %collective-permute-done.11.refs_2_ = bf16[8,3,16,256]{3,2,1,0:T(8,128)(2,1)S(1)} collective-permute-done((bf16[8,3,16,256]{3,2,1,0:T(8,128)(2,1)S(1)}, bf16[8,3,16,256]{3,2,1,0:T(8,128)(2,1)S(1)}, u32[]{:S(2)}, u32[]{:S(2)}) %collective-permute-start.11) | collective-permute-done | bytes 196640 | tf_op jit(solution)/shard_map/ppermute | solution.py:450
  118.9 6.5 %all-to-all-start.1 = ((bf16[32,5,16,256]{3,2,1,0:T(8,128)(2,1)}), bf16[32,5,16,256]{3,2,1,0:T(8,128)(2,1)S(1)}, u32[]{:S(2)}, u32[]{:S(2)}) async-start(bf16[32,5,16,256]{3,2,1,0:T(8,128)(2,1)} %bitcast.9), calls=%async_computation.1 | async-start | bytes 2621440 | tf_op jit(solution)/shard_map/all_to_all | solution.py:469
  129.2 2.6 %collective-permute-start.18 = (bf16[4,3,16,256]{3,2,1,0:T(8,128)(2,1)S(1)}, bf16[4,3,16,256]{3,2,1,0:T(8,128)(2,1)S(1)}, u32[]{:S(2)}, u32[]{:S(2)}) collective-permute-start(bf16[4,3,16,256]{3,2,1,0:T(8,128)(2,1)S(1)} %get-tuple-element.102), channel_id=1, source_target_pairs={{0,18},{1,19},{2,16},{3,17},{4,22},{5,23},{6,20},{7,21},{8,26},{9,... | collective-permute-start | bytes 294920 | tf_op jit(solution)/shard_map/ppermute | solution.py:450
  131.8 5.5 %collective-permute-done.14.refs_2_ = bf16[4,3,16,256]{3,2,1,0:T(8,128)(2,1)S(1)} collective-permute-done((bf16[4,3,16,256]{3,2,1,0:T(8,128)(2,1)S(1)}, bf16[4,3,16,256]{3,2,1,0:T(8,128)(2,1)S(1)}, u32[]{:S(2)}, u32[]{:S(2)}) %collective-permute-start.14) | collective-permute-done | bytes 98336 | tf_op jit(solution)/shard_map/ppermute | solution.py:450
  137.3 4.7 %collective-permute-start.19 = (bf16[4,3,16,256]{3,2,1,0:T(8,128)(2,1)S(1)}, bf16[4,3,16,256]{3,2,1,0:T(8,128)(2,1)S(1)}, u32[]{:S(2)}, u32[]{:S(2)}) collective-permute-start(bf16[4,3,16,256]{3,2,1,0:T(8,128)(2,1)S(1)} %get-tuple-element.103), channel_id=1, source_target_pairs={{0,19},{1,18},{2,17},{3,16},{4,23},{5,22},{6,21},{7,20},{8,27},{9,... | collective-permute-start | bytes 294920 | tf_op jit(solution)/shard_map/ppermute | solution.py:450
  142.0 6.3 %collective-permute-done.18.refs_6_ = bf16[4,3,16,256]{3,2,1,0:T(8,128)(2,1)S(1)} collective-permute-done((bf16[4,3,16,256]{3,2,1,0:T(8,128)(2,1)S(1)}, bf16[4,3,16,256]{3,2,1,0:T(8,128)(2,1)S(1)}, u32[]{:S(2)}, u32[]{:S(2)}) %collective-permute-start.18) | collective-permute-done | bytes 98336 | tf_op jit(solution)/shard_map/ppermute | solution.py:450
  149.8 7.5 %all-to-all-done.1.last_ref = bf16[32,5,16,256]{3,2,1,0:T(8,128)(2,1)S(1)} async-done(((bf16[32,5,16,256]{3,2,1,0:T(8,128)(2,1)}), bf16[32,5,16,256]{3,2,1,0:T(8,128)(2,1)S(1)}, u32[]{:S(2)}, u32[]{:S(2)}) %all-to-all-start.1) | async-done | bytes 1310752 | tf_op jit(solution)/shard_map/all_to_all | solution.py:469
  157.3 2.7 %homeward.1 = (bf16[16,256,128]{2,1,0:T(8,128)(2,1)}, f32[2,16,128,128]{3,2,1,0:T(8,128)}) custom-call(bf16[32,5,16,256]{3,2,1,0:T(8,128)(2,1)S(1)} %all-to-all-done.1.last_ref, bf16[4,3,16,256]{3,2,1,0:T(8,128)(2,1)S(1)} %get-tuple-element.96.refs_0_, bf16[4,3,16,256]{3,2,1,0:T(8,128)(2,1)S(1)} %collective-permute-done.13.refs_1_, ...), custom_call_target="tpu_custom_call" | custom-call | bytes 5242880 | tf_op jit(solution)/shard_map/homeward/pallas_call | solution.py:415
  (50 shorter events, 16.5 us)
Async XLA Ops:
  4.6 42.1 %copy-start.9 = (f32[128]{0:T(128)S(1)}, f32[128]{0:T(128)}, u32[]{:S(2)}) copy-start(f32[128]{0:T(128)} %param.15) | copy-start | bytes 1540
  4.6 84.7 %all-to-all-start = ((bf16[32,3,4,16,256]{4,3,2,1,0:T(8,128)(2,1)}), bf16[32,3,4,16,256]{4,3,2,1,0:T(8,128)(2,1)S(1)}, u32[]{:S(2)}, u32[]{:S(2)}) async-start(bf16[32,3,4,16,256]{4,3,2,1,0:T(8,128)(2,1)} %outward.1), calls=%async_computation | async-start | bytes 6291456 | tf_op jit(solution)/shard_map/all_to_all | solution.py:453
  14.4 3.8 %collective-permute-start = (bf16[4,4,16,256]{3,2,1,0:T(8,128)(2,1)S(1)}, bf16[4,4,16,256]{3,2,1,0:T(8,128)(2,1)S(1)}, u32[]{:S(2)}, u32[]{:S(2)}) collective-permute-start(bf16[4,4,16,256]{3,2,1,0:T(8,128)(2,1)S(1)} %get-tuple-element.55), channel_id=1, source_target_pairs={{0,1},{1,0},{2,3},{3,2},{4,5},{5,4},{6,7},{7,6},{8,9},{9,8},{10,11... | collective-permute-start | bytes 393224 | tf_op jit(solution)/shard_map/ppermute | solution.py:450
  14.6 18.1 %collective-permute-start.1 = (bf16[4,4,16,256]{3,2,1,0:T(8,128)(2,1)S(1)}, bf16[4,4,16,256]{3,2,1,0:T(8,128)(2,1)S(1)}, u32[]{:S(2)}, u32[]{:S(2)}) collective-permute-start(bf16[4,4,16,256]{3,2,1,0:T(8,128)(2,1)S(1)} %get-tuple-element.56), channel_id=1, source_target_pairs={{0,2},{1,3},{2,0},{3,1},{4,6},{5,7},{6,4},{7,5},{8,10},{9,11},{10,... | collective-permute-start | bytes 393224 | tf_op jit(solution)/shard_map/ppermute | solution.py:450
  16.3 30.4 %collective-permute-start.2 = (bf16[4,4,16,256]{3,2,1,0:T(8,128)(2,1)}, bf16[4,4,16,256]{3,2,1,0:T(8,128)(2,1)}, u32[]{:S(2)}, u32[]{:S(2)}) collective-permute-start(bf16[4,4,16,256]{3,2,1,0:T(8,128)(2,1)} %get-tuple-element.57), channel_id=1, source_target_pairs={{0,3},{1,2},{2,1},{3,0},{4,7},{5,6},{6,5},{7,4},{8,11},{9,10},{10,... | collective-permute-start | bytes 393224 | tf_op jit(solution)/shard_map/ppermute | solution.py:450
  16.3 30.4 %collective-permute-start.3 = (bf16[4,4,16,256]{3,2,1,0:T(8,128)(2,1)}, bf16[4,4,16,256]{3,2,1,0:T(8,128)(2,1)}, u32[]{:S(2)}, u32[]{:S(2)}) collective-permute-start(bf16[4,4,16,256]{3,2,1,0:T(8,128)(2,1)} %get-tuple-element.58), channel_id=1, source_target_pairs={{0,16},{1,17},{2,18},{3,19},{4,20},{5,21},{6,22},{7,23},{8,24},{9,... | collective-permute-start | bytes 393224 | tf_op jit(solution)/shard_map/ppermute | solution.py:450
  18.0 28.8 %collective-permute-start.4 = (bf16[4,4,16,256]{3,2,1,0:T(8,128)(2,1)}, bf16[4,4,16,256]{3,2,1,0:T(8,128)(2,1)}, u32[]{:S(2)}, u32[]{:S(2)}) collective-permute-start(bf16[4,4,16,256]{3,2,1,0:T(8,128)(2,1)} %get-tuple-element.59), channel_id=1, source_target_pairs={{0,17},{1,16},{2,19},{3,18},{4,21},{5,20},{6,23},{7,22},{8,25},{9,... | collective-permute-start | bytes 393224 | tf_op jit(solution)/shard_map/ppermute | solution.py:450
  18.8 32.9 %collective-permute-start.5 = (bf16[4,4,16,256]{3,2,1,0:T(8,128)(2,1)}, bf16[4,4,16,256]{3,2,1,0:T(8,128)(2,1)S(1)}, u32[]{:S(2)}, u32[]{:S(2)}) collective-permute-start(bf16[4,4,16,256]{3,2,1,0:T(8,128)(2,1)} %get-tuple-element.60), channel_id=1, source_target_pairs={{0,18},{1,19},{2,16},{3,17},{4,22},{5,23},{6,20},{7,21},{8,26},{9,... | collective-permute-start | bytes 393224 | tf_op jit(solution)/shard_map/ppermute | solution.py:450
  33.4 22.5 %collective-permute-start.6 = (bf16[4,4,16,256]{3,2,1,0:T(8,128)(2,1)}, bf16[4,4,16,256]{3,2,1,0:T(8,128)(2,1)S(1)}, u32[]{:S(2)}, u32[]{:S(2)}) collective-permute-start(bf16[4,4,16,256]{3,2,1,0:T(8,128)(2,1)} %get-tuple-element.61), channel_id=1, source_target_pairs={{0,19},{1,18},{2,17},{3,16},{4,23},{5,22},{6,21},{7,20},{8,27},{9,... | collective-permute-start | bytes 393224 | tf_op jit(solution)/shard_map/ppermute | solution.py:450
  56.6 0.9 copy-start.1
  62.8 39.2 %collective-permute-start.7 = (bf16[8,4,16,256]{3,2,1,0:T(8,128)(2,1)}, bf16[8,4,16,256]{3,2,1,0:T(8,128)(2,1)}, u32[]{:S(2)}, u32[]{:S(2)}) collective-permute-start(bf16[8,4,16,256]{3,2,1,0:T(8,128)(2,1)} %get-tuple-element.74), channel_id=1, source_target_pairs={{0,4},{1,5},{2,6},{3,7},{4,0},{5,1},{6,2},{7,3},{8,12},{9,13},{10,... | collective-permute-start | bytes 786440 | tf_op jit(solution)/shard_map/ppermute | solution.py:450
  62.8 43.5 %collective-permute-start.8 = (bf16[8,4,16,256]{3,2,1,0:T(8,128)(2,1)}, bf16[8,4,16,256]{3,2,1,0:T(8,128)(2,1)}, u32[]{:S(2)}, u32[]{:S(2)}) collective-permute-start(bf16[8,4,16,256]{3,2,1,0:T(8,128)(2,1)} %get-tuple-element.75), channel_id=1, source_target_pairs={{0,8},{1,9},{2,10},{3,11},{4,12},{5,13},{6,14},{7,15},{8,0},{9,1},... | collective-permute-start | bytes 786440 | tf_op jit(solution)/shard_map/ppermute | solution.py:450
  89.3 16.9 %collective-permute-start.9 = (bf16[8,4,16,256]{3,2,1,0:T(8,128)(2,1)}, bf16[8,4,16,256]{3,2,1,0:T(8,128)(2,1)S(1)}, u32[]{:S(2)}, u32[]{:S(2)}) collective-permute-start(bf16[8,4,16,256]{3,2,1,0:T(8,128)(2,1)} %copy-done.8), channel_id=1, source_target_pairs={{0,12},{1,13},{2,14},{3,15},{4,8},{5,9},{6,10},{7,11},{8,4},{9,5},... | collective-permute-start | bytes 786440 | tf_op jit(solution)/shard_map/ppermute | solution.py:450
  98.5 11.1 %collective-permute-start.10 = (bf16[8,3,16,256]{3,2,1,0:T(8,128)(2,1)S(1)}, bf16[8,3,16,256]{3,2,1,0:T(8,128)(2,1)S(1)}, u32[]{:S(2)}, u32[]{:S(2)}) collective-permute-start(bf16[8,3,16,256]{3,2,1,0:T(8,128)(2,1)S(1)} %get-tuple-element.79), channel_id=1, source_target_pairs={{0,4},{1,5},{2,6},{3,7},{4,0},{5,1},{6,2},{7,3},{8,12},{9,13},{10,... | collective-permute-start | bytes 589832 | tf_op jit(solution)/shard_map/ppermute | solution.py:450
  98.6 20.2 %collective-permute-start.11 = (bf16[8,3,16,256]{3,2,1,0:T(8,128)(2,1)S(1)}, bf16[8,3,16,256]{3,2,1,0:T(8,128)(2,1)S(1)}, u32[]{:S(2)}, u32[]{:S(2)}) collective-permute-start(bf16[8,3,16,256]{3,2,1,0:T(8,128)(2,1)S(1)} %get-tuple-element.80), channel_id=1, source_target_pairs={{0,8},{1,9},{2,10},{3,11},{4,12},{5,13},{6,14},{7,15},{8,0},{9,1},... | collective-permute-start | bytes 589832 | tf_op jit(solution)/shard_map/ppermute | solution.py:450
  102.0 16.8 %collective-permute-start.12 = (bf16[8,3,16,256]{3,2,1,0:T(8,128)(2,1)S(1)}, bf16[8,3,16,256]{3,2,1,0:T(8,128)(2,1)S(1)}, u32[]{:S(2)}, u32[]{:S(2)}) collective-permute-start(bf16[8,3,16,256]{3,2,1,0:T(8,128)(2,1)S(1)} %get-tuple-element.81), channel_id=1, source_target_pairs={{0,12},{1,13},{2,14},{3,15},{4,8},{5,9},{6,10},{7,11},{8,4},{9,5},... | collective-permute-start | bytes 589832 | tf_op jit(solution)/shard_map/ppermute | solution.py:450
  118.9 38.4 %all-to-all-start.1 = ((bf16[32,5,16,256]{3,2,1,0:T(8,128)(2,1)}), bf16[32,5,16,256]{3,2,1,0:T(8,128)(2,1)S(1)}, u32[]{:S(2)}, u32[]{:S(2)}) async-start(bf16[32,5,16,256]{3,2,1,0:T(8,128)(2,1)} %bitcast.9), calls=%async_computation.1 | async-start | bytes 2621440 | tf_op jit(solution)/shard_map/all_to_all | solution.py:469
  125.4 3.8 %collective-permute-start.13 = (bf16[4,3,16,256]{3,2,1,0:T(8,128)(2,1)S(1)}, bf16[4,3,16,256]{3,2,1,0:T(8,128)(2,1)S(1)}, u32[]{:S(2)}, u32[]{:S(2)}) collective-permute-start(bf16[4,3,16,256]{3,2,1,0:T(8,128)(2,1)S(1)} %get-tuple-element.97), channel_id=1, source_target_pairs={{0,1},{1,0},{2,3},{3,2},{4,5},{5,4},{6,7},{7,6},{8,9},{9,8},{10,11... | collective-permute-start | bytes 294920 | tf_op jit(solution)/shard_map/ppermute | solution.py:450
  125.7 11.6 %collective-permute-start.14 = (bf16[4,3,16,256]{3,2,1,0:T(8,128)(2,1)S(1)}, bf16[4,3,16,256]{3,2,1,0:T(8,128)(2,1)S(1)}, u32[]{:S(2)}, u32[]{:S(2)}) collective-permute-start(bf16[4,3,16,256]{3,2,1,0:T(8,128)(2,1)S(1)} %get-tuple-element.98), channel_id=1, source_target_pairs={{0,2},{1,3},{2,0},{3,1},{4,6},{5,7},{6,4},{7,5},{8,10},{9,11},{10,... | collective-permute-start | bytes 294920 | tf_op jit(solution)/shard_map/ppermute | solution.py:450
  127.4 14.6 %collective-permute-start.15 = (bf16[4,3,16,256]{3,2,1,0:T(8,128)(2,1)S(1)}, bf16[4,3,16,256]{3,2,1,0:T(8,128)(2,1)S(1)}, u32[]{:S(2)}, u32[]{:S(2)}) collective-permute-start(bf16[4,3,16,256]{3,2,1,0:T(8,128)(2,1)S(1)} %get-tuple-element.99), channel_id=1, source_target_pairs={{0,3},{1,2},{2,1},{3,0},{4,7},{5,6},{6,5},{7,4},{8,11},{9,10},{10,... | collective-permute-start | bytes 294920 | tf_op jit(solution)/shard_map/ppermute | solution.py:450
  127.4 14.6 %collective-permute-start.16 = (bf16[4,3,16,256]{3,2,1,0:T(8,128)(2,1)S(1)}, bf16[4,3,16,256]{3,2,1,0:T(8,128)(2,1)S(1)}, u32[]{:S(2)}, u32[]{:S(2)}) collective-permute-start(bf16[4,3,16,256]{3,2,1,0:T(8,128)(2,1)S(1)} %get-tuple-element.100), channel_id=1, source_target_pairs={{0,16},{1,17},{2,18},{3,19},{4,20},{5,21},{6,22},{7,23},{8,24},{9,... | collective-permute-start | bytes 294920 | tf_op jit(solution)/shard_map/ppermute | solution.py:450
  129.1 12.9 %collective-permute-start.17 = (bf16[4,3,16,256]{3,2,1,0:T(8,128)(2,1)S(1)}, bf16[4,3,16,256]{3,2,1,0:T(8,128)(2,1)S(1)}, u32[]{:S(2)}, u32[]{:S(2)}) collective-permute-start(bf16[4,3,16,256]{3,2,1,0:T(8,128)(2,1)S(1)} %get-tuple-element.101), channel_id=1, source_target_pairs={{0,17},{1,16},{2,19},{3,18},{4,21},{5,20},{6,23},{7,22},{8,25},{9,... | collective-permute-start | bytes 294920 | tf_op jit(solution)/shard_map/ppermute | solution.py:450
  129.2 19.1 %collective-permute-start.18 = (bf16[4,3,16,256]{3,2,1,0:T(8,128)(2,1)S(1)}, bf16[4,3,16,256]{3,2,1,0:T(8,128)(2,1)S(1)}, u32[]{:S(2)}, u32[]{:S(2)}) collective-permute-start(bf16[4,3,16,256]{3,2,1,0:T(8,128)(2,1)S(1)} %get-tuple-element.102), channel_id=1, source_target_pairs={{0,18},{1,19},{2,16},{3,17},{4,22},{5,23},{6,20},{7,21},{8,26},{9,... | collective-permute-start | bytes 294920 | tf_op jit(solution)/shard_map/ppermute | solution.py:450
  137.3 12.4 %collective-permute-start.19 = (bf16[4,3,16,256]{3,2,1,0:T(8,128)(2,1)S(1)}, bf16[4,3,16,256]{3,2,1,0:T(8,128)(2,1)S(1)}, u32[]{:S(2)}, u32[]{:S(2)}) collective-permute-start(bf16[4,3,16,256]{3,2,1,0:T(8,128)(2,1)S(1)} %get-tuple-element.103), channel_id=1, source_target_pairs={{0,19},{1,18},{2,17},{3,16},{4,23},{5,22},{6,21},{7,20},{8,27},{9,... | collective-permute-start | bytes 294920 | tf_op jit(solution)/shard_map/ppermute | solution.py:450
  (8 other events, 6.0 us)

commit v13 on v11

--- a/solution.py
+++ b/solution.py
@@ -244,7 +244,7 @@
     return pl.pallas_call(
         functools.partial(conv_kernel, early=early),
         grid=(steps,),
-        in_specs=[pl.BlockSpec(memory_space=pltpu.SMEM), here, *specs],
+        in_specs=[here, here, *specs],
         out_specs=[here] * (3 + len(more)),
         out_shape=[
             pltpu.VMEM((steps, dp, N1, N2), F32),
@@ -256,7 +256,7 @@
         compiler_params=pltpu.CompilerParams(vmem_limit_bytes=VMEM),
         cost_estimate=pl.CostEstimate(flops=steps * dp * 5 * 6 * N1**3, bytes_accessed=4 << 20, transcendentals=0),
         name="conv_early" if early else "conv_late",
-    )(gain, received, *tabs)
+    )(near(gain), received, *tabs)
 
 
 def grad_call(received, kept, cots, send):
@@ -460,6 +460,7 @@
     cots[3], received = lax.optimization_barrier((cots[3], received))
     cots[2:] = [exchange(x, (2 + i) * plane) for i, x in enumerate(cots[2:])]
     gain = lax.dynamic_slice(skip_gain, ((c * dp + d) * per,), (per,))
+    gain = jnp.broadcast_to(gain[:, None, None], (per, 1, N2))
     outs = conv_call(gain, received, tabs, plane, True)
     kept, held, early = outs[:3], outs[3:6], outs[6:]
     early = [exchange(x, hop * plane) for hop, x in enumerate(early)]

time: 160 us -> 160 us (level)
  no operation moved by 1% of the time
where the time goes in v13:
time: 160 us
  waiting for transfers between devices  79.9 us (50%)
  starting transfers between devices  53.6 us (34%)
  Pallas kernels  24.2 us (15%)
    ppermute x20, waiting for transfers between devices, exchange(): lax.ppermute(x, axes, [(i, i ^ mask) for i in range(count)])  57.9 us
    ppermute x20, starting transfers between devices, exchange(): lax.ppermute(x, axes, [(i, i ^ mask) for i in range(count)])  39.8 us
    all_to_all x1, waiting for transfers between devices, by_channel_body(): lax.all_to_all(first, order, 0, 0, tiled=True)  14.5 us
    pallas_call x2, Pallas kernels, conv_call(): pl.pallas_call(functools.partial(conv_kernel, early=early), grid=(steps,)...  11.4 us
    all_to_all x1, waiting for transfers between devices, by_channel_body(): lax.all_to_all(send.reshape(count, *send.shape[2:]), order, 0, 0, tiled=T...  7.48 us
    all_to_all x1, starting transfers between devices, by_channel_body(): lax.all_to_all(first, order, 0, 0, tiled=True)  7.3 us
    all_to_all x1, starting transfers between devices, by_channel_body(): lax.all_to_all(send.reshape(count, *send.shape[2:]), order, 0, 0, tiled=T...  6.47 us
    pallas_call x1, Pallas kernels, outward(): pl.pallas_call(functools.partial(outward_kernel, count=count), in_specs=[...  4.03 us
  transfers between devices with their start and end apart: 22, of which 10 were waited for; matrix products, arithmetic and copies ran while one was open for 0% of the time, Pallas kernels for 11%

profile of v13, /device:TPU:0, one launch (start us, length us, event | category | flops | bytes accessed | tf_op | source)
XLA Modules:
  0.0 160.0 jit_solution(18277060129433865464)
XLA Ops:
  0.6 4.0 %outward.1 = bf16[32,3,4,16,256]{4,3,2,1,0:T(8,128)(2,1)} custom-call(bf16[1,16,256,128]{3,2,1,0:T(8,128)(2,1)} %bitcast.10, bf16[1,16,256,128]{3,2,1,0:T(8,128)(2,1)} %bitcast.11, f32[2,16,256,128]{3,2,1,0:T(8,128)} %refs_2_.1), custom_call_target="tpu_custom_call" | custom-call | bytes 7340032 | tf_op jit(solution)/shard_map/outward/pallas_call | solution.py:314
  4.7 7.3 %all-to-all-start = ((bf16[32,3,4,16,256]{4,3,2,1,0:T(8,128)(2,1)}), bf16[32,3,4,16,256]{4,3,2,1,0:T(8,128)(2,1)S(1)}, u32[]{:S(2)}, u32[]{:S(2)}) async-start(bf16[32,3,4,16,256]{4,3,2,1,0:T(8,128)(2,1)} %outward.1), calls=%async_computation | async-start | bytes 6291456 | tf_op jit(solution)/shard_map/all_to_all | solution.py:453
  12.0 1.9 %outward_near.1 = (bf16[4,4,16,256]{3,2,1,0:T(8,128)(2,1)S(1)}, bf16[4,4,16,256]{3,2,1,0:T(8,128)(2,1)S(1)}, bf16[4,4,16,256]{3,2,1,0:T(8,128)(2,1)S(1)}, bf16[4...) custom-call(bf16[1,16,256,128]{3,2,1,0:T(8,128)(2,1)} %bitcast.12), custom_call_target="tpu_custom_call" | custom-call | bytes 2097152 | tf_op jit(solution)/shard_map/outward_near/pallas_call | solution.py:351
  15.9 1.7 %collective-permute-start.3 = (bf16[4,4,16,256]{3,2,1,0:T(8,128)(2,1)S(1)}, bf16[4,4,16,256]{3,2,1,0:T(8,128)(2,1)S(1)}, u32[]{:S(2)}, u32[]{:S(2)}) collective-permute-start(bf16[4,4,16,256]{3,2,1,0:T(8,128)(2,1)S(1)} %get-tuple-element.60), channel_id=1, source_target_pairs={{0,16},{1,17},{2,18},{3,19},{4,20},{5,21},{6,22},{7,23},{8,24},{9,... | collective-permute-start | bytes 393224 | tf_op jit(solution)/shard_map/ppermute | solution.py:450
  17.7 2.6 %collective-permute-start.5 = (bf16[4,4,16,256]{3,2,1,0:T(8,128)(2,1)S(1)}, bf16[4,4,16,256]{3,2,1,0:T(8,128)(2,1)S(1)}, u32[]{:S(2)}, u32[]{:S(2)}) collective-permute-start(bf16[4,4,16,256]{3,2,1,0:T(8,128)(2,1)S(1)} %get-tuple-element.62), channel_id=1, source_target_pairs={{0,18},{1,19},{2,16},{3,17},{4,22},{5,23},{6,20},{7,21},{8,26},{9,... | collective-permute-start | bytes 393224 | tf_op jit(solution)/shard_map/ppermute | solution.py:450
  20.3 12.6 %collective-permute-done.1.refs_2_ = bf16[4,4,16,256]{3,2,1,0:T(8,128)(2,1)S(1)} collective-permute-done((bf16[4,4,16,256]{3,2,1,0:T(8,128)(2,1)S(1)}, bf16[4,4,16,256]{3,2,1,0:T(8,128)(2,1)S(1)}, u32[]{:S(2)}, u32[]{:S(2)}) %collective-permute-start.1) | collective-permute-done | bytes 131104 | tf_op jit(solution)/shard_map/ppermute | solution.py:450
  32.8 13.1 %collective-permute-start.6 = (bf16[4,4,16,256]{3,2,1,0:T(8,128)(2,1)S(1)}, bf16[4,4,16,256]{3,2,1,0:T(8,128)(2,1)S(1)}, u32[]{:S(2)}, u32[]{:S(2)}) collective-permute-start(bf16[4,4,16,256]{3,2,1,0:T(8,128)(2,1)S(1)} %get-tuple-element.63), channel_id=1, source_target_pairs={{0,19},{1,18},{2,17},{3,16},{4,23},{5,22},{6,21},{7,20},{8,27},{9,... | collective-permute-start | bytes 393224 | tf_op jit(solution)/shard_map/ppermute | solution.py:450
  46.0 5.7 %collective-permute-done.5.refs_6_ = bf16[4,4,16,256]{3,2,1,0:T(8,128)(2,1)S(1)} collective-permute-done((bf16[4,4,16,256]{3,2,1,0:T(8,128)(2,1)S(1)}, bf16[4,4,16,256]{3,2,1,0:T(8,128)(2,1)S(1)}, u32[]{:S(2)}, u32[]{:S(2)}) %collective-permute-start.5) | collective-permute-done | bytes 131104 | tf_op jit(solution)/shard_map/ppermute | solution.py:450
  51.7 4.3 %collective-permute-done.6.refs_7_ = bf16[4,4,16,256]{3,2,1,0:T(8,128)(2,1)S(1)} collective-permute-done((bf16[4,4,16,256]{3,2,1,0:T(8,128)(2,1)S(1)}, bf16[4,4,16,256]{3,2,1,0:T(8,128)(2,1)S(1)}, u32[]{:S(2)}, u32[]{:S(2)}) %collective-permute-start.6) | collective-permute-done | bytes 131104 | tf_op jit(solution)/shard_map/ppermute | solution.py:450
  58.2 12.8 %collective-permute-done.7.refs_7_ = bf16[8,4,16,256]{3,2,1,0:T(8,128)(2,1)} collective-permute-done((bf16[8,4,16,256]{3,2,1,0:T(8,128)(2,1)}, bf16[8,4,16,256]{3,2,1,0:T(8,128)(2,1)}, u32[]{:S(2)}, u32[]{:S(2)}) %collective-permute-start.7) | collective-permute-done | bytes 262176 | tf_op jit(solution)/shard_map/ppermute | solution.py:450
  71.1 3.8 %collective-permute-start.8 = (bf16[8,4,16,256]{3,2,1,0:T(8,128)(2,1)}, bf16[8,4,16,256]{3,2,1,0:T(8,128)(2,1)}, u32[]{:S(2)}, u32[]{:S(2)}) collective-permute-start(bf16[8,4,16,256]{3,2,1,0:T(8,128)(2,1)} %copy-done.1), channel_id=1, source_target_pairs={{0,8},{1,9},{2,10},{3,11},{4,12},{5,13},{6,14},{7,15},{8,0},{9,1},... | collective-permute-start | bytes 786440 | tf_op jit(solution)/shard_map/ppermute | solution.py:450
  74.9 14.5 %all-to-all-done = bf16[32,3,4,16,256]{4,3,2,1,0:T(8,128)(2,1)S(1)} async-done(((bf16[32,3,4,16,256]{4,3,2,1,0:T(8,128)(2,1)}), bf16[32,3,4,16,256]{4,3,2,1,0:T(8,128)(2,1)S(1)}, u32[]{:S(2)}, u32[]{:S(2)}) %all-to-all-start) | async-done | bytes 3145760 | tf_op jit(solution)/shard_map/all_to_all | solution.py:453
  90.4 8.2 %conv_early.1 = (f32[3,2,256,256]{3,2,1,0:T(8,128)S(1)}, f32[3,2,144,512]{3,2,1,0:T(8,128)S(1)}, f32[3,2,144,256]{3,2,1,0:T(8,128)S(1)}, bf16[288,256]{1,0:T(8,1...) custom-call(f32[4,1,256]{2,1,0:T(1,128)S(1)} %broadcast_in_dim.2.gai, ...), custom_call_target="tpu_custom_call" | custom-call | flops 3019898880 | bytes 4194304 | tf_op jit(solution)/shard_map/conv_early/pallas_call | solution.py:244
  98.7 3.4 %collective-permute-start.11 = (bf16[8,3,16,256]{3,2,1,0:T(8,128)(2,1)S(1)}, bf16[8,3,16,256]{3,2,1,0:T(8,128)(2,1)S(1)}, u32[]{:S(2)}, u32[]{:S(2)}) collective-permute-start(bf16[8,3,16,256]{3,2,1,0:T(8,128)(2,1)S(1)} %get-tuple-element.84), channel_id=1, source_target_pairs={{0,8},{1,9},{2,10},{3,11},{4,12},{5,13},{6,14},{7,15},{8,0},{9,1},... | collective-permute-start | bytes 589832 | tf_op jit(solution)/shard_map/ppermute | solution.py:450
  103.1 3.3 %conv_late.1 = (f32[1,2,256,256]{3,2,1,0:T(8,128)S(1)}, f32[1,2,144,512]{3,2,1,0:T(8,128)S(1)}, f32[1,2,144,256]{3,2,1,0:T(8,128)S(1)}, bf16[16,2,1,16,256]{4,3,2,1,0:T(8,128)(2,1)S(1)}) custom-call(f32[4,1,256]{2,1,0:T(1,128)S(1)} %broadcast_in_dim.2.gain_ref, bf16[16,2,3,4,16,256]{5,4,3,2,1,0:T(8,128)(2,1)S(1)} %bitcast.7, ...), custom_call_target="tpu_custom_call" | custom-call | flops 1006632960 | bytes 4194304 | tf_op jit(solution)/shard_map/conv_late/pallas_call | solution.py:244
  106.4 3.3 %grad.1 = bf16[16,2,5,16,256]{4,3,2,1,0:T(8,128)(2,1)} custom-call(bf16[16,2,3,4,16,256]{5,4,3,2,1,0:T(8,128)(2,1)S(1)} %bitcast.8, f32[3,2,256,256]{3,2,1,0:T(8,128)S(1)} %get-tuple-element.66.refs_0_, f32[3,2,144,512]{3,2,1,0:T(8,128)S(1)} %get-tuple-element.67.refs_1_, f32[3,2,144,256]{3,2,1,0:T(8,128)S(1)} %get-tuple-element.68.refs_2_, ...), custom_call_target="tpu_custom_call" | custom-call | flops 805306368 | bytes 8388608 | tf_op jit(solution)/shard_map/grad/pallas_call | solution.py:266
  109.7 9.2 %collective-permute-done.11.refs_2_ = bf16[8,3,16,256]{3,2,1,0:T(8,128)(2,1)S(1)} collective-permute-done((bf16[8,3,16,256]{3,2,1,0:T(8,128)(2,1)S(1)}, bf16[8,3,16,256]{3,2,1,0:T(8,128)(2,1)S(1)}, u32[]{:S(2)}, u32[]{:S(2)}) %collective-permute-start.11) | collective-permute-done | bytes 196640 | tf_op jit(solution)/shard_map/ppermute | solution.py:450
  118.9 6.5 %all-to-all-start.1 = ((bf16[32,5,16,256]{3,2,1,0:T(8,128)(2,1)}), bf16[32,5,16,256]{3,2,1,0:T(8,128)(2,1)S(1)}, u32[]{:S(2)}, u32[]{:S(2)}) async-start(bf16[32,5,16,256]{3,2,1,0:T(8,128)(2,1)} %bitcast.9), calls=%async_computation.1 | async-start | bytes 2621440 | tf_op jit(solution)/shard_map/all_to_all | solution.py:471
  129.2 2.6 %collective-permute-start.18 = (bf16[4,3,16,256]{3,2,1,0:T(8,128)(2,1)S(1)}, bf16[4,3,16,256]{3,2,1,0:T(8,128)(2,1)S(1)}, u32[]{:S(2)}, u32[]{:S(2)}) collective-permute-start(bf16[4,3,16,256]{3,2,1,0:T(8,128)(2,1)S(1)} %get-tuple-element.106), channel_id=1, source_target_pairs={{0,18},{1,19},{2,16},{3,17},{4,22},{5,23},{6,20},{7,21},{8,26},{9,... | collective-permute-start | bytes 294920 | tf_op jit(solution)/shard_map/ppermute | solution.py:450
  131.8 5.5 %collective-permute-done.14.refs_2_ = bf16[4,3,16,256]{3,2,1,0:T(8,128)(2,1)S(1)} collective-permute-done((bf16[4,3,16,256]{3,2,1,0:T(8,128)(2,1)S(1)}, bf16[4,3,16,256]{3,2,1,0:T(8,128)(2,1)S(1)}, u32[]{:S(2)}, u32[]{:S(2)}) %collective-permute-start.14) | collective-permute-done | bytes 98336 | tf_op jit(solution)/shard_map/ppermute | solution.py:450
  137.3 4.7 %collective-permute-start.19 = (bf16[4,3,16,256]{3,2,1,0:T(8,128)(2,1)S(1)}, bf16[4,3,16,256]{3,2,1,0:T(8,128)(2,1)S(1)}, u32[]{:S(2)}, u32[]{:S(2)}) collective-permute-start(bf16[4,3,16,256]{3,2,1,0:T(8,128)(2,1)S(1)} %get-tuple-element.107), channel_id=1, source_target_pairs={{0,19},{1,18},{2,17},{3,16},{4,23},{5,22},{6,21},{7,20},{8,27},{9,... | collective-permute-start | bytes 294920 | tf_op jit(solution)/shard_map/ppermute | solution.py:450
  142.0 6.3 %collective-permute-done.18.refs_6_ = bf16[4,3,16,256]{3,2,1,0:T(8,128)(2,1)S(1)} collective-permute-done((bf16[4,3,16,256]{3,2,1,0:T(8,128)(2,1)S(1)}, bf16[4,3,16,256]{3,2,1,0:T(8,128)(2,1)S(1)}, u32[]{:S(2)}, u32[]{:S(2)}) %collective-permute-start.18) | collective-permute-done | bytes 98336 | tf_op jit(solution)/shard_map/ppermute | solution.py:450
  149.8 7.5 %all-to-all-done.1.last_ref = bf16[32,5,16,256]{3,2,1,0:T(8,128)(2,1)S(1)} async-done(((bf16[32,5,16,256]{3,2,1,0:T(8,128)(2,1)}), bf16[32,5,16,256]{3,2,1,0:T(8,128)(2,1)S(1)}, u32[]{:S(2)}, u32[]{:S(2)}) %all-to-all-start.1) | async-done | bytes 1310752 | tf_op jit(solution)/shard_map/all_to_all | solution.py:471
  157.3 2.7 %homeward.1 = (bf16[16,256,128]{2,1,0:T(8,128)(2,1)}, f32[2,16,128,128]{3,2,1,0:T(8,128)}) custom-call(bf16[32,5,16,256]{3,2,1,0:T(8,128)(2,1)S(1)} %all-to-all-done.1.last_ref, bf16[4,3,16,256]{3,2,1,0:T(8,128)(2,1)S(1)} %get-tuple-element.100.refs_0_, bf16[4,3,16,256]{3,2,1,0:T(8,128)(2,1)S(1)} %collective-permute-done.13.refs_1_, ...), custom_call_target="tpu_custom_call" | custom-call | bytes 5242880 | tf_op jit(solution)/shard_map/homeward/pallas_call | solution.py:415
  (36 shorter events, 11.8 us)
Async XLA Ops:
  4.7 84.7 %all-to-all-start = ((bf16[32,3,4,16,256]{4,3,2,1,0:T(8,128)(2,1)}), bf16[32,3,4,16,256]{4,3,2,1,0:T(8,128)(2,1)S(1)}, u32[]{:S(2)}, u32[]{:S(2)}) async-start(bf16[32,3,4,16,256]{4,3,2,1,0:T(8,128)(2,1)} %outward.1), calls=%async_computation | async-start | bytes 6291456 | tf_op jit(solution)/shard_map/all_to_all | solution.py:453
  12.0 46.2 %copy-start.2 = (f32[128]{0:T(128)S(1)}, f32[128]{0:T(128)}, u32[]{:S(2)}) copy-start(f32[128]{0:T(128)} %param.15) | copy-start | bytes 1540
  13.9 3.8 %collective-permute-start = (bf16[4,4,16,256]{3,2,1,0:T(8,128)(2,1)S(1)}, bf16[4,4,16,256]{3,2,1,0:T(8,128)(2,1)S(1)}, u32[]{:S(2)}, u32[]{:S(2)}) collective-permute-start(bf16[4,4,16,256]{3,2,1,0:T(8,128)(2,1)S(1)} %get-tuple-element.57), channel_id=1, source_target_pairs={{0,1},{1,0},{2,3},{3,2},{4,5},{5,4},{6,7},{7,6},{8,9},{9,8},{10,11... | collective-permute-start | bytes 393224 | tf_op jit(solution)/shard_map/ppermute | solution.py:450
  14.2 18.7 %collective-permute-start.1 = (bf16[4,4,16,256]{3,2,1,0:T(8,128)(2,1)S(1)}, bf16[4,4,16,256]{3,2,1,0:T(8,128)(2,1)S(1)}, u32[]{:S(2)}, u32[]{:S(2)}) collective-permute-start(bf16[4,4,16,256]{3,2,1,0:T(8,128)(2,1)S(1)} %get-tuple-element.58), channel_id=1, source_target_pairs={{0,2},{1,3},{2,0},{3,1},{4,6},{5,7},{6,4},{7,5},{8,10},{9,11},{10,... | collective-permute-start | bytes 393224 | tf_op jit(solution)/shard_map/ppermute | solution.py:450
  15.9 30.1 %collective-permute-start.2 = (bf16[4,4,16,256]{3,2,1,0:T(8,128)(2,1)S(1)}, bf16[4,4,16,256]{3,2,1,0:T(8,128)(2,1)S(1)}, u32[]{:S(2)}, u32[]{:S(2)}) collective-permute-start(bf16[4,4,16,256]{3,2,1,0:T(8,128)(2,1)S(1)} %get-tuple-element.59), channel_id=1, source_target_pairs={{0,3},{1,2},{2,1},{3,0},{4,7},{5,6},{6,5},{7,4},{8,11},{9,10},{10,... | collective-permute-start | bytes 393224 | tf_op jit(solution)/shard_map/ppermute | solution.py:450
  15.9 30.1 %collective-permute-start.3 = (bf16[4,4,16,256]{3,2,1,0:T(8,128)(2,1)S(1)}, bf16[4,4,16,256]{3,2,1,0:T(8,128)(2,1)S(1)}, u32[]{:S(2)}, u32[]{:S(2)}) collective-permute-start(bf16[4,4,16,256]{3,2,1,0:T(8,128)(2,1)S(1)} %get-tuple-element.60), channel_id=1, source_target_pairs={{0,16},{1,17},{2,18},{3,19},{4,20},{5,21},{6,22},{7,23},{8,24},{9,... | collective-permute-start | bytes 393224 | tf_op jit(solution)/shard_map/ppermute | solution.py:450
  17.6 28.4 %collective-permute-start.4 = (bf16[4,4,16,256]{3,2,1,0:T(8,128)(2,1)S(1)}, bf16[4,4,16,256]{3,2,1,0:T(8,128)(2,1)S(1)}, u32[]{:S(2)}, u32[]{:S(2)}) collective-permute-start(bf16[4,4,16,256]{3,2,1,0:T(8,128)(2,1)S(1)} %get-tuple-element.61), channel_id=1, source_target_pairs={{0,17},{1,16},{2,19},{3,18},{4,21},{5,20},{6,23},{7,22},{8,25},{9,... | collective-permute-start | bytes 393224 | tf_op jit(solution)/shard_map/ppermute | solution.py:450
  17.7 34.0 %collective-permute-start.5 = (bf16[4,4,16,256]{3,2,1,0:T(8,128)(2,1)S(1)}, bf16[4,4,16,256]{3,2,1,0:T(8,128)(2,1)S(1)}, u32[]{:S(2)}, u32[]{:S(2)}) collective-permute-start(bf16[4,4,16,256]{3,2,1,0:T(8,128)(2,1)S(1)} %get-tuple-element.62), channel_id=1, source_target_pairs={{0,18},{1,19},{2,16},{3,17},{4,22},{5,23},{6,20},{7,21},{8,26},{9,... | collective-permute-start | bytes 393224 | tf_op jit(solution)/shard_map/ppermute | solution.py:450
  32.8 23.2 %collective-permute-start.6 = (bf16[4,4,16,256]{3,2,1,0:T(8,128)(2,1)S(1)}, bf16[4,4,16,256]{3,2,1,0:T(8,128)(2,1)S(1)}, u32[]{:S(2)}, u32[]{:S(2)}) collective-permute-start(bf16[4,4,16,256]{3,2,1,0:T(8,128)(2,1)S(1)} %get-tuple-element.63), channel_id=1, source_target_pairs={{0,19},{1,18},{2,17},{3,16},{4,23},{5,22},{6,21},{7,20},{8,27},{9,... | collective-permute-start | bytes 393224 | tf_op jit(solution)/shard_map/ppermute | solution.py:450
  57.5 0.7 copy-start.1
  58.2 12.9 %collective-permute-start.7 = (bf16[8,4,16,256]{3,2,1,0:T(8,128)(2,1)}, bf16[8,4,16,256]{3,2,1,0:T(8,128)(2,1)}, u32[]{:S(2)}, u32[]{:S(2)}) collective-permute-start(bf16[8,4,16,256]{3,2,1,0:T(8,128)(2,1)} %get-tuple-element.76), channel_id=1, source_target_pairs={{0,4},{1,5},{2,6},{3,7},{4,0},{5,1},{6,2},{7,3},{8,12},{9,13},{10,... | collective-permute-start | bytes 786440 | tf_op jit(solution)/shard_map/ppermute | solution.py:450
  71.1 35.3 %collective-permute-start.8 = (bf16[8,4,16,256]{3,2,1,0:T(8,128)(2,1)}, bf16[8,4,16,256]{3,2,1,0:T(8,128)(2,1)}, u32[]{:S(2)}, u32[]{:S(2)}) collective-permute-start(bf16[8,4,16,256]{3,2,1,0:T(8,128)(2,1)} %copy-done.1), channel_id=1, source_target_pairs={{0,8},{1,9},{2,10},{3,11},{4,12},{5,13},{6,14},{7,15},{8,0},{9,1},... | collective-permute-start | bytes 786440 | tf_op jit(solution)/shard_map/ppermute | solution.py:450
  89.4 17.0 %collective-permute-start.9 = (bf16[8,4,16,256]{3,2,1,0:T(8,128)(2,1)}, bf16[8,4,16,256]{3,2,1,0:T(8,128)(2,1)S(1)}, u32[]{:S(2)}, u32[]{:S(2)}) collective-permute-start(bf16[8,4,16,256]{3,2,1,0:T(8,128)(2,1)} %copy-done), channel_id=1, source_target_pairs={{0,12},{1,13},{2,14},{3,15},{4,8},{5,9},{6,10},{7,11},{8,4},{9,5},... | collective-permute-start | bytes 786440 | tf_op jit(solution)/shard_map/ppermute | solution.py:450
  98.6 11.1 %collective-permute-start.10 = (bf16[8,3,16,256]{3,2,1,0:T(8,128)(2,1)S(1)}, bf16[8,3,16,256]{3,2,1,0:T(8,128)(2,1)S(1)}, u32[]{:S(2)}, u32[]{:S(2)}) collective-permute-start(bf16[8,3,16,256]{3,2,1,0:T(8,128)(2,1)S(1)} %get-tuple-element.83), channel_id=1, source_target_pairs={{0,4},{1,5},{2,6},{3,7},{4,0},{5,1},{6,2},{7,3},{8,12},{9,13},{10,... | collective-permute-start | bytes 589832 | tf_op jit(solution)/shard_map/ppermute | solution.py:450
  98.7 20.2 %collective-permute-start.11 = (bf16[8,3,16,256]{3,2,1,0:T(8,128)(2,1)S(1)}, bf16[8,3,16,256]{3,2,1,0:T(8,128)(2,1)S(1)}, u32[]{:S(2)}, u32[]{:S(2)}) collective-permute-start(bf16[8,3,16,256]{3,2,1,0:T(8,128)(2,1)S(1)} %get-tuple-element.84), channel_id=1, source_target_pairs={{0,8},{1,9},{2,10},{3,11},{4,12},{5,13},{6,14},{7,15},{8,0},{9,1},... | collective-permute-start | bytes 589832 | tf_op jit(solution)/shard_map/ppermute | solution.py:450
  102.1 16.8 %collective-permute-start.12 = (bf16[8,3,16,256]{3,2,1,0:T(8,128)(2,1)S(1)}, bf16[8,3,16,256]{3,2,1,0:T(8,128)(2,1)S(1)}, u32[]{:S(2)}, u32[]{:S(2)}) collective-permute-start(bf16[8,3,16,256]{3,2,1,0:T(8,128)(2,1)S(1)} %get-tuple-element.85), channel_id=1, source_target_pairs={{0,12},{1,13},{2,14},{3,15},{4,8},{5,9},{6,10},{7,11},{8,4},{9,5},... | collective-permute-start | bytes 589832 | tf_op jit(solution)/shard_map/ppermute | solution.py:450
  118.9 38.3 %all-to-all-start.1 = ((bf16[32,5,16,256]{3,2,1,0:T(8,128)(2,1)}), bf16[32,5,16,256]{3,2,1,0:T(8,128)(2,1)S(1)}, u32[]{:S(2)}, u32[]{:S(2)}) async-start(bf16[32,5,16,256]{3,2,1,0:T(8,128)(2,1)} %bitcast.9), calls=%async_computation.1 | async-start | bytes 2621440 | tf_op jit(solution)/shard_map/all_to_all | solution.py:471
  125.4 3.8 %collective-permute-start.13 = (bf16[4,3,16,256]{3,2,1,0:T(8,128)(2,1)S(1)}, bf16[4,3,16,256]{3,2,1,0:T(8,128)(2,1)S(1)}, u32[]{:S(2)}, u32[]{:S(2)}) collective-permute-start(bf16[4,3,16,256]{3,2,1,0:T(8,128)(2,1)S(1)} %get-tuple-element.101), channel_id=1, source_target_pairs={{0,1},{1,0},{2,3},{3,2},{4,5},{5,4},{6,7},{7,6},{8,9},{9,8},{10,11... | collective-permute-start | bytes 294920 | tf_op jit(solution)/shard_map/ppermute | solution.py:450
  125.7 11.6 %collective-permute-start.14 = (bf16[4,3,16,256]{3,2,1,0:T(8,128)(2,1)S(1)}, bf16[4,3,16,256]{3,2,1,0:T(8,128)(2,1)S(1)}, u32[]{:S(2)}, u32[]{:S(2)}) collective-permute-start(bf16[4,3,16,256]{3,2,1,0:T(8,128)(2,1)S(1)} %get-tuple-element.102), channel_id=1, source_target_pairs={{0,2},{1,3},{2,0},{3,1},{4,6},{5,7},{6,4},{7,5},{8,10},{9,11},{10,... | collective-permute-start | bytes 294920 | tf_op jit(solution)/shard_map/ppermute | solution.py:450
  127.4 14.6 %collective-permute-start.15 = (bf16[4,3,16,256]{3,2,1,0:T(8,128)(2,1)S(1)}, bf16[4,3,16,256]{3,2,1,0:T(8,128)(2,1)S(1)}, u32[]{:S(2)}, u32[]{:S(2)}) collective-permute-start(bf16[4,3,16,256]{3,2,1,0:T(8,128)(2,1)S(1)} %get-tuple-element.103), channel_id=1, source_target_pairs={{0,3},{1,2},{2,1},{3,0},{4,7},{5,6},{6,5},{7,4},{8,11},{9,10},{10,... | collective-permute-start | bytes 294920 | tf_op jit(solution)/shard_map/ppermute | solution.py:450
  127.4 14.6 %collective-permute-start.16 = (bf16[4,3,16,256]{3,2,1,0:T(8,128)(2,1)S(1)}, bf16[4,3,16,256]{3,2,1,0:T(8,128)(2,1)S(1)}, u32[]{:S(2)}, u32[]{:S(2)}) collective-permute-start(bf16[4,3,16,256]{3,2,1,0:T(8,128)(2,1)S(1)} %get-tuple-element.104), channel_id=1, source_target_pairs={{0,16},{1,17},{2,18},{3,19},{4,20},{5,21},{6,22},{7,23},{8,24},{9,... | collective-permute-start | bytes 294920 | tf_op jit(solution)/shard_map/ppermute | solution.py:450
  129.1 12.9 %collective-permute-start.17 = (bf16[4,3,16,256]{3,2,1,0:T(8,128)(2,1)S(1)}, bf16[4,3,16,256]{3,2,1,0:T(8,128)(2,1)S(1)}, u32[]{:S(2)}, u32[]{:S(2)}) collective-permute-start(bf16[4,3,16,256]{3,2,1,0:T(8,128)(2,1)S(1)} %get-tuple-element.105), channel_id=1, source_target_pairs={{0,17},{1,16},{2,19},{3,18},{4,21},{5,20},{6,23},{7,22},{8,25},{9,... | collective-permute-start | bytes 294920 | tf_op jit(solution)/shard_map/ppermute | solution.py:450
  129.2 19.1 %collective-permute-start.18 = (bf16[4,3,16,256]{3,2,1,0:T(8,128)(2,1)S(1)}, bf16[4,3,16,256]{3,2,1,0:T(8,128)(2,1)S(1)}, u32[]{:S(2)}, u32[]{:S(2)}) collective-permute-start(bf16[4,3,16,256]{3,2,1,0:T(8,128)(2,1)S(1)} %get-tuple-element.106), channel_id=1, source_target_pairs={{0,18},{1,19},{2,16},{3,17},{4,22},{5,23},{6,20},{7,21},{8,26},{9,... | collective-permute-start | bytes 294920 | tf_op jit(solution)/shard_map/ppermute | solution.py:450
  137.3 12.4 %collective-permute-start.19 = (bf16[4,3,16,256]{3,2,1,0:T(8,128)(2,1)S(1)}, bf16[4,3,16,256]{3,2,1,0:T(8,128)(2,1)S(1)}, u32[]{:S(2)}, u32[]{:S(2)}) collective-permute-start(bf16[4,3,16,256]{3,2,1,0:T(8,128)(2,1)S(1)} %get-tuple-element.107), channel_id=1, source_target_pairs={{0,19},{1,18},{2,17},{3,16},{4,23},{5,22},{6,21},{7,20},{8,27},{9,... | collective-permute-start | bytes 294920 | tf_op jit(solution)/shard_map/ppermute | solution.py:450
  (1 other events, 0.7 us)
